TPU v7x, 32 devices: a whole 2x2x4 slice. The times are simulated.
32 devices in a mesh: parts: 2 (over y), tm: 16 (over z, x, core).
Axes of the slice: x: 2, y: 2, z: 4, core: 2. Of those that a mesh axis runs over, the one named last changes fastest.
Arguments:
- frames: bfloat16 [2048, 2048], P('tm', 'parts'), parts along dimension 1, may hold values from -6 to 6
- levels: int32 [2048], P(('parts', 'tm')), parts along dimension 0, may hold values from 0 to 15
- initial_state: float32 [256], P('parts'), parts along dimension 0, may hold values from -6 to 6
- transitions: float32 [16, 128, 128], replicated, may hold values from -1 to 1
- gain: bfloat16 [128, 128], replicated, may hold values from -1 to 1
- pixel_mode: int32 [2048], replicated, may hold values from 0 to 127
- pixel_weight: bfloat16 [2048], replicated, may hold values from 0.099609375 to 0.5
Outputs:
- estimates: float32 [2048, 128], P(('parts', 'tm')), parts along dimension 0
There are 2 independent parts, one for each index of `parts`. A program takes and returns all parts, laid end to end along the dimension named above; an argument that names none is the same for every part. Nothing has to cross between parts.
All inputs are finite; a program needn't handle non-finite values.
Results may differ from a plain program's by a relative error of at most 0.0026.
Values may be sent and summed in bfloat16 or wider, within the bound.
No kernel may reach another device: no remote copies, remote signals or barrier semaphores. Data moves between devices by JAX's collectives and lax.ppermute only.
A program may use at most 128 MiB of HBM per device.

v0:
```python
import functools

import jax
import jax.numpy as jnp
from jax import lax
from jax.experimental import pallas as pl
from jax.experimental.pallas import tpu as pltpu
from jax.sharding import PartitionSpec as P

F32 = jnp.float32
BF16 = jnp.bfloat16
MIB = 1 << 20
NT = (((1,), (1,)), ((), ()))
VMEM = pl.BlockSpec(memory_space=pltpu.VMEM)
SMEM = pl.BlockSpec(memory_space=pltpu.SMEM)
HBM = pl.BlockSpec(memory_space=pltpu.HBM)
ANY = pl.BlockSpec(memory_space=pl.ANY)
shape = jax.ShapeDtypeStruct


def call(kernel, name, mib, flops, moved, **kw):
    return pl.pallas_call(
        kernel,
        name=name,
        compiler_params=pltpu.CompilerParams(vmem_limit_bytes=mib * MIB),
        cost_estimate=pl.CostEstimate(flops=flops, bytes_accessed=moved, transcendentals=0),
        **kw,
    )


def pair(x):
    high = x.astype(BF16)
    mid = (x - high.astype(F32)).astype(BF16)
    return jnp.concatenate([high, mid], axis=1)


def mm(left, right):
    n = right.shape[0]
    out = jnp.dot(left, jnp.concatenate([right, right], axis=0), preferred_element_type=F32)
    return out[:, :n] + out[:, n:]


def mm3(left, left_low, right, right_low):
    n = right.shape[0]
    rest = jnp.dot(
        jnp.concatenate([left[:, :n], left_low], axis=1),
        jnp.concatenate([right_low, right[:, :n]], axis=0),
        preferred_element_type=F32,
    )
    return mm(left, right) + rest


def vm(vec, mat):
    high = vec.astype(BF16).astype(F32)
    rows = jnp.concatenate([high, vec - high], axis=0).astype(BF16)
    out = jnp.dot(rows, mat, preferred_element_type=F32)
    n = vec.shape[1]
    out = out[:, :n] + out[:, n:]
    return out[:8] + out[8:]


def row(ref, t):
    return jnp.broadcast_to(ref[pl.ds(t, 1), :], (8, ref.shape[1]))


def front_kernel(turn, trans_ref, *refs):
    if turn:
        frames_ref, table_ref, low_ref, turned_ref, trans, frames, turned, sems = refs
        into = pltpu.make_async_copy(frames_ref, frames, sems.at[0])
        into.start()
    else:
        table_ref, low_ref, trans, sems = refs
    maps = pltpu.make_async_copy(trans_ref, trans, sems.at[1])
    maps.start()
    if turn:
        into.wait()
        turned[...] = frames[...].T
        out = pltpu.make_async_copy(turned, turned_ref, sems.at[2])
        out.start()
    maps.wait()

    def prepare(k, c):
        x = trans[k].T
        both = pair(x)
        n = x.shape[0]
        table_ref[k] = both
        low_ref[k] = (x - both[:, :n].astype(F32) - both[:, n:].astype(F32)).astype(BF16)
        return c

    lax.fori_loop(0, trans.shape[0], prepare, 0)
    if turn:
        out.wait()


def tree_kernel(steps, levels_ref, table_ref, low_ref, left_hbm, right_hbm, total_ref, left_ref, right_ref, sems):
    base = steps // 4

    def first(t):
        a, b = levels_ref[0, t], levels_ref[0, t + 1]
        return mm3(table_ref[a], low_ref[a], table_ref[b], low_ref[b])

    def node(k):
        return mm(left_ref[k], right_ref[k])

    def first_pairs(ks):
        made = [(first(4 * k), first(4 * k + 2)) for k in ks]
        for k, (a, b) in zip(ks, made):
            left_ref[k] = pair(a)
            right_ref[k] = pair(b)

    def later_pairs(ks):
        made = [(node(2 * (k - base)), node(2 * (k - base) + 1)) for k in ks]
        for k, (a, b) in zip(ks, made):
            left_ref[k] = pair(a)
            right_ref[k] = pair(b)

    def loop(fn, start, count):
        def body(i, c):
            fn([start + 2 * i, start + 2 * i + 1])
            return c

        lax.fori_loop(0, count // 2, body, 0)

    def store(start, count, k):
        copies = [
            pltpu.make_async_copy(ref.at[pl.ds(start, count)], hbm.at[pl.ds(start, count)], sems.at[k + i])
            for i, (ref, hbm) in enumerate([(left_ref, left_hbm), (right_ref, right_hbm)])
        ]
        for copy in copies:
            copy.start()
        return copies

    loop(first_pairs, 0, base)
    copies = store(0, base, 0)
    count, start = base // 2, base
    while count >= 2:
        loop(later_pairs, start, count)
        start += count
        count //= 2
    later_pairs([start])
    copies += store(base, base - 1, 2)
    total_ref[...] = pair(node(start))
    for copy in copies:
        copy.wait()


def local_kernel(pos_ref, levels_ref, x_ref, mode_ref, weight_ref, gain_ref, init_ref, table_ref, total_ref, right_hbm, lefts_ref, shift_ref, drive_ref, right_ref, sems):
    segments, steps, width = x_ref.shape
    n = gain_ref.shape[0]
    base = steps // 4
    copies = [
        pltpu.make_async_copy(right_hbm.at[pl.ds(a, b)], right_ref.at[pl.ds(a, b)], sems.at[i])
        for i, (a, b) in enumerate([(0, base), (base, base - 1)])
    ]
    for copy in copies:
        copy.start()
    channel = lax.broadcasted_iota(jnp.int32, (n, width), 0)
    measured = jnp.zeros((steps, n), F32)
    for k in range(segments):
        weight = jnp.broadcast_to(weight_ref[pl.ds(k, 1), :].astype(F32), (n, width))
        projector = jnp.where(mode_ref[pl.ds(k, 1), :] == channel, weight, 0.0).astype(BF16)
        measured += lax.dot_general(x_ref[k], projector, NT, preferred_element_type=F32)
    drive_ref[...] = lax.dot_general(measured.astype(BF16), gain_ref[...], NT, preferred_element_type=F32)

    states = [row(drive_ref, t) for t in range(steps)]
    at, offset = 0, 0
    for level in range(steps.bit_length() - 1):
        if level in (1, 2):
            copies[level - 1].wait()
        later = []
        for i in range(len(states) // 2):
            mat = table_ref[levels_ref[0, 2 * i + 1]] if level == 0 else right_ref[offset + i]
            lefts_ref[pl.ds(at + i, 1), :] = states[2 * i][:1]
            later.append(vm(states[2 * i], mat) + states[2 * i + 1])
        at += len(later)
        if level > 0:
            offset += len(later)
        states = later
    lefts_ref[pl.ds(at, 1), :] = states[0][:1]
    first = jnp.where(pos_ref[0] == 0, row(init_ref, 0), 0.0)
    shift_ref[...] = states[0] + vm(first, total_ref[...])


def group_kernel(size, pos_ref, *refs):
    maps = refs[:size]
    all_ref, prefix_ref, whole_ref = refs[size:]
    n = whole_ref.shape[0]
    member = pos_ref[0] % size
    for r in range(size):
        all_ref[(member + r) % size] = maps[r][...]
    rows, cols = (lax.broadcasted_iota(jnp.int32, (n, n), d) for d in (0, 1))
    prefix_ref[...] = pair((rows == cols).astype(F32))
    run = all_ref[0]
    for q in range(1, size):
        @pl.when(member == q)
        def _(run=run):
            prefix_ref[...] = run
        run = pair(mm(run, all_ref[q]))
    whole_ref[...] = run


def beside_kernel(size, pos_ref, all_ref, *refs):
    shifts = refs[:size]
    before_ref, whole_ref, held_ref = refs[size:]
    member = pos_ref[0] % size
    for r in range(size):
        held_ref[(member + r) % size] = shifts[r][...]
    before_ref[...] = jnp.zeros_like(before_ref)
    run = held_ref[0]
    for q in range(1, size):
        @pl.when(member == q)
        def _(run=run):
            before_ref[...] = run
        run = vm(run, all_ref[q]) + held_ref[q]
    whole_ref[...] = run


def hop_kernel(got_ref, map_ref, shift_ref, out_ref):
    out_ref[...] = vm(got_ref[...], map_ref[...]) + shift_ref[...]


def final_kernel(pos_ref, levels_ref, got_ref, before_ref, init_ref, prefix_ref, table_ref, total_ref, lefts_ref, left_hbm, out_ref, left_ref, sems):
    steps, n = lefts_ref.shape
    base = steps // 4
    copies = [
        pltpu.make_async_copy(left_hbm.at[pl.ds(a, b)], left_ref.at[pl.ds(a, b)], sems.at[i])
        for i, (a, b) in enumerate([(base, base - 1), (0, base)])
    ]
    for copy in copies:
        copy.start()
    first = jnp.where(pos_ref[0] == 0, row(init_ref, 0), 0.0)
    state = vm(got_ref[...], prefix_ref[...]) + before_ref[...] + first
    out_ref[pl.ds(steps - 1, 1), :] = (vm(state, total_ref[...]) + row(lefts_ref, steps - 1))[:1]
    levels = steps.bit_length() - 1
    starts = [state]
    sizes = [steps >> (level + 1) for level in range(levels)]
    for level in reversed(range(levels)):
        if level == levels - 1:
            copies[0].wait()
        if level == 1:
            copies[1].wait()
        at, offset = sum(sizes[:level]), sum(sizes[1:level])
        later = []
        for i, x in enumerate(starts):
            mat = table_ref[levels_ref[0, 2 * i]] if level == 0 else left_ref[offset + i]
            later += [x, vm(x, mat) + row(lefts_ref, at + i)]
        starts = later
    for t in range(1, steps):
        out_ref[pl.ds(t - 1, 1), :] = starts[t][:1]


def shards(count, frames, levels, initial_state, transitions, gain, pixel_mode, pixel_weight):
    n = gain.shape[0]
    kinds = transitions.shape[0]
    pixels, length = frames.shape
    steps = length // count
    size = 1
    while count % (2 * size) == 0 and 4 * size * size <= count:
        size *= 2
    groups = count // size
    position = lax.axis_index("tm").astype(jnp.int32)[None]
    initial_state = initial_state[None]
    levels = levels[None]
    pairs = steps // 2 - 1
    turn = pixels % 128 == 0

    tables = [shape((kinds, n, 2 * n), BF16), shape((kinds, n, n), BF16)]
    trans = pltpu.VMEM(transitions.shape, F32)
    dma = pltpu.SemaphoreType.DMA
    if turn:
        table, low, turned = call(
            functools.partial(front_kernel, turn), "front", 5, 0, 6 * MIB,
            out_shape=tables + [shape((length, pixels), BF16)],
            in_specs=[HBM, HBM],
            out_specs=[VMEM, VMEM, HBM],
            scratch_shapes=[trans, pltpu.VMEM(frames.shape, BF16), pltpu.VMEM((length, pixels), BF16), dma((3,))],
        )(transitions, frames)
        turned = turned.reshape(count, steps, pixels)
        x = lax.all_to_all(turned, "tm", split_axis=0, concat_axis=0, tiled=True)
    else:
        table, low = call(
            functools.partial(front_kernel, turn), "front", 5, 0, 6 * MIB,
            out_shape=tables,
            in_specs=[HBM],
            out_specs=[VMEM, VMEM],
            scratch_shapes=[trans, dma((2,))],
        )(transitions)
        x = lax.all_to_all(frames, "tm", split_axis=1, concat_axis=0, tiled=True).T[None]
    mode = pixel_mode.reshape(x.shape[0], x.shape[2])
    weight = pixel_weight.reshape(x.shape[0], x.shape[2])

    tree = pltpu.VMEM((pairs, n, 2 * n), BF16)
    left, right, total = call(
        functools.partial(tree_kernel, steps), "tree_of_maps", 8, 2 * steps * n**3 * 6, 8 * MIB,
        out_shape=[shape((pairs, n, 2 * n), BF16), shape((pairs, n, 2 * n), BF16), shape((n, 2 * n), BF16)],
        in_specs=[SMEM, VMEM, VMEM],
        out_specs=[HBM, HBM, VMEM],
        scratch_shapes=[tree, tree, dma((4,))],
    )(levels, table, low)

    def around(x):
        return [
            lax.ppermute(x, "tm", [(j // size * size + (j + r) % size, j) for j in range(count)])
            for r in range(1, size)
        ]

    members = around(total)
    lefts, shift = call(
        local_kernel, "local_states", 6, 1 << 27, 6 * MIB,
        out_shape=[shape((steps, n), F32), shape((8, n), F32)],
        in_specs=[SMEM, SMEM] + [VMEM] * 7 + [HBM],
        out_specs=[VMEM] * 2,
        scratch_shapes=[pltpu.VMEM((steps, n), F32), tree, dma((2,))],
    )(position, levels, x, mode, weight, gain, initial_state, table, total, right)

    vector = shape((8, n), F32)
    maps, prefix, whole = call(
        functools.partial(group_kernel, size), "group_maps", 2, 1 << 24, MIB,
        out_shape=[shape((size, n, 2 * n), BF16), shape((n, 2 * n), BF16), shape((n, 2 * n), BF16)],
        in_specs=[SMEM] + [VMEM] * size,
        out_specs=[VMEM] * 3,
    )(position, total, *members)
    before, carried = call(
        functools.partial(beside_kernel, size), "group_states", 2, 1 << 20, MIB // 4,
        out_shape=[vector, vector],
        in_specs=[SMEM] + [VMEM] * (1 + size),
        out_specs=[VMEM] * 2,
        scratch_shapes=[pltpu.VMEM((size, 8, n), F32)],
    )(position, maps, shift, *around(shift))
    sent = carried
    for hop in range(groups - 1):
        got = lax.ppermute(sent, "tm", [(j, j + size) for j in range(count - size)])
        if hop < groups - 2:
            sent = call(
                hop_kernel, "next_group", 2, 1 << 18, 1 << 16,
                out_shape=vector,
                in_specs=[VMEM] * 3,
                out_specs=VMEM,
            )(got, whole, carried)

    return call(
        final_kernel, "estimates", 5, 1 << 23, 5 * MIB,
        out_shape=shape((steps, n), F32),
        in_specs=[SMEM, SMEM] + [VMEM] * 7 + [HBM],
        out_specs=VMEM,
        scratch_shapes=[tree, dma((2,))],
    )(position, levels, got, before, initial_state, prefix, table, total, lefts, left)


def solution(mesh):
    in_specs = (P("tm", "parts"), P(("parts", "tm")), P("parts"), P(), P(), P(), P())
    out_specs = P(("parts", "tm"), None)
    return jax.shard_map(
        functools.partial(shards, mesh.shape["tm"]),
        mesh=mesh,
        in_specs=in_specs,
        out_specs=out_specs,
        check_vma=False,
    )
```

profile of v0, /device:TPU:0, one launch (start us, length us, event | category | flops | bytes accessed | tf_op | source)
XLA Modules:
  0.0 53.5 jit_solution(14387629795308628833)
XLA Ops:
  0.0 0.0 copy-start.2
  0.0 1.2 %copy-done.2 = f32[16,128,128]{2,1,0:T(8,128)S(1)} copy-done((f32[16,128,128]{2,1,0:T(8,128)S(1)}, f32[16,128,128]{2,1,0:T(8,128)}, u32[]{:S(2)}) %copy-start.2) | copy-done | bytes 1048600
  1.2 0.0 copy-start.3
  1.2 0.9 %copy-done.3 = bf16[128,1024]{1,0:T(8,128)(2,1)S(1)} copy-done((bf16[128,1024]{1,0:T(8,128)(2,1)S(1)}, bf16[128,1024]{1,0:T(8,128)(2,1)}, u32[]{:S(2)}) %copy-start.3) | copy-done | bytes 262168
  2.2 2.0 %front.1 = (bf16[16,128,256]{2,1,0:T(8,128)(2,1)S(1)}, bf16[16,128,128]{2,1,0:T(8,128)(2,1)S(1)}, bf16[1024,128]{1,0:T(8,128)(2,1)}) custom-call(f32[16,128,128]{2,1,0:T(8,128)S(1)} %copy-done.2, bf16[128,1024]{1,0:T(8,128)(2,1)S(1)} %copy-done.3), custom_call_target="tpu_custom_call" | custom-call | bytes 6291456 | tf_op jit(solution)/shard_map/front/pallas_call | solution.py:271
  4.1 0.0 copy-start.10
  4.2 0.8 %copy-done.10 = bf16[16,128,128]{2,1,0:T(8,128)(2,1)} copy-done((bf16[16,128,128]{2,1,0:T(8,128)(2,1)}, bf16[16,128,128]{2,1,0:T(8,128)(2,1)S(1)}, u32[]{:S(2)}) %copy-start.10) | copy-done | bytes 524312
  5.0 7.4 %all-to-all-start = ((bf16[16,64,128]{2,1,0:T(8,128)(2,1)}), bf16[16,64,128]{2,1,0:T(8,128)(2,1)S(1)}, u32[]{:S(2)}, u32[]{:S(2)}) async-start(bf16[16,64,128]{2,1,0:T(8,128)(2,1)} %bitcast.2), calls=%async_computation | async-start | bytes 524288 | tf_op jit(solution)/shard_map/all_to_all | solution.py:279
  12.3 0.0 copy-start.7
  12.3 0.6 %copy-done.7 = s32[64]{0:T(128)S(1)} copy-done((s32[64]{0:T(128)S(1)}, s32[64]{0:T(128)}, u32[]{:S(2)}) %copy-start.7) | copy-done | bytes 280
  13.0 0.0 copy-start.11
  13.0 1.0 %copy-done.11 = bf16[16,128,128]{2,1,0:T(8,128)(2,1)S(1)} copy-done((bf16[16,128,128]{2,1,0:T(8,128)(2,1)S(1)}, bf16[16,128,128]{2,1,0:T(8,128)(2,1)}, u32[]{:S(2)}) %copy-start.11) | copy-done | bytes 524312
  14.0 0.0 copy-start.5
  14.0 0.0 copy-start.6
  14.0 0.0 copy-start.8
  14.0 5.7 %tree_of_maps.1 = (bf16[31,128,256]{2,1,0:T(8,128)(2,1)S(1)}, bf16[31,128,256]{2,1,0:T(8,128)(2,1)S(1)}, bf16[128,256]{1,0:T(8,128)(2,1)S(1)}) custom-call(s32[1,64]{1,0:T(1,128)S(1)} %bitcast.8, bf16[16,128,256]{2,1,0:T(8,128)(2,1)S(1)} %get-tuple-element.18.table_ref, bf16[16,128,128]{2,1,0:T(8,128)(2,1)S(1)} %copy-done.11), custom_call_target="tpu_custom_call" | custom-call | flops 1610612736 | bytes 8388608 | tf_op jit(solution)/shard_map/tree_of_maps/pallas_call | solution.py:293
  19.8 0.0 copy-start
  19.8 1.3 %copy-done = bf16[31,128,256]{2,1,0:T(8,128)(2,1)} copy-done((bf16[31,128,256]{2,1,0:T(8,128)(2,1)}, bf16[31,128,256]{2,1,0:T(8,128)(2,1)S(1)}, u32[]{:S(2)}) %copy-start) | copy-done | bytes 2031640
  21.1 0.4 collective-permute-start.2
  21.5 1.7 %collective-permute-start.1 = (bf16[128,256]{1,0:T(8,128)(2,1)S(1)}, bf16[128,256]{1,0:T(8,128)(2,1)S(1)}, u32[]{:S(2)}, u32[]{:S(2)}) collective-permute-start(bf16[128,256]{1,0:T(8,128)(2,1)S(1)} %get-tuple-element.20.refs_0_.total_ref), channel_id=1, source_target_pairs={{2,0},{3,1},{0,2},{1,3},{6,4},{7,5},{4,6},{5,7},{10,8},{11,9},{8,1... | collective-permute-start | bytes 196616 | tf_op jit(solution)/shard_map/ppermute | solution.py:303
  23.2 1.3 %collective-permute-start = (bf16[128,256]{1,0:T(8,128)(2,1)S(1)}, bf16[128,256]{1,0:T(8,128)(2,1)}, u32[]{:S(2)}, u32[]{:S(2)}) collective-permute-start(bf16[128,256]{1,0:T(8,128)(2,1)S(1)} %get-tuple-element.20.refs_0_.total_ref), channel_id=1, source_target_pairs={{1,0},{2,1},{3,2},{0,3},{5,4},{6,5},{7,6},{4,7},{9,8},{10,9},{11,1... | collective-permute-start | bytes 196616 | tf_op jit(solution)/shard_map/ppermute | solution.py:303
  24.5 0.0 all-to-all-done.x_ref
  24.5 0.0 copy-done.5
  24.5 0.0 copy-done.6
  24.5 0.0 copy-done.8
  24.5 0.0 copy-start.1
  24.5 1.6 %copy-done.1 = bf16[31,128,256]{2,1,0:T(8,128)(2,1)S(1)} copy-done((bf16[31,128,256]{2,1,0:T(8,128)(2,1)S(1)}, bf16[31,128,256]{2,1,0:T(8,128)(2,1)}, u32[]{:S(2)}) %copy-start.1) | copy-done | bytes 2031640
  26.1 0.0 copy-start.4
  26.1 0.8 %copy-done.4 = bf16[128,128]{1,0:T(8,128)(2,1)S(1)} copy-done((bf16[128,128]{1,0:T(8,128)(2,1)S(1)}, bf16[128,128]{1,0:T(8,128)(2,1)}, u32[]{:S(2)}) %copy-start.4) | copy-done | bytes 32792
  26.8 0.0 copy-start.9
  26.8 0.7 %copy-done.9 = f32[128]{0:T(128)S(1)} copy-done((f32[128]{0:T(128)S(1)}, f32[128]{0:T(128)}, u32[]{:S(2)}) %copy-start.9) | copy-done | bytes 536
  27.5 3.1 %local_states.1 = (f32[64,128]{1,0:T(8,128)S(1)}, f32[8,128]{1,0:T(8,128)S(1)}) custom-call(s32[1]{0:T(128)} %bitcast.pos_ref, s32[1,64]{1,0:T(1,128)S(1)} %bitcast.9, bf16[16,64,128]{2,1,0:T(8,128)(2,1)S(1)} %all-to-all-done.x_ref, s32[16,128]{1,0:T(8,128)S(1)} %bitcast.6, bf16[16,128]{1,0:T(8,128)(2,1)S(1)} %bitcast.7, bf16[128,128]{1,0:T(8,128)(2,1)S(1)} %copy-done.4, ...), custom_call_target="tpu_custom_call" | custom-call | flops 134217728 | bytes 6291456 | tf_op jit(solution)/shard_map/local_states/pallas_call | solution.py:308
  30.6 0.1 collective-permute-start.5
  30.7 0.4 collective-permute-start.4
  31.1 0.0 collective-permute-done.2.refs_3_
  31.1 1.4 %collective-permute-start.3 = (f32[8,128]{1,0:T(8,128)S(1)}, f32[8,128]{1,0:T(8,128)S(1)}, u32[]{:S(2)}, u32[]{:S(2)}) collective-permute-start(f32[8,128]{1,0:T(8,128)S(1)} %get-tuple-element.24.refs_0_), channel_id=1, source_target_pairs={{1,0},{2,1},{3,2},{0,3},{5,4},{6,5},{7,6},{4,7},{9,8},{10,9},{11,1... | collective-permute-start | bytes 12296 | tf_op jit(solution)/shard_map/ppermute | solution.py:303
  32.5 0.0 collective-permute-done.1.refs_2_
  32.5 0.0 collective-permute-done.refs_1_
  32.5 1.4 %group_maps.1 = (bf16[4,128,256]{2,1,0:T(8,128)(2,1)S(1)}, bf16[128,256]{1,0:T(8,128)(2,1)S(1)}, bf16[128,256]{1,0:T(8,128)(2,1)S(1)}) custom-call(s32[1]{0:T(128)} %bitcast.pos_ref, bf16[128,256]{1,0:T(8,128)(2,1)S(1)} %get-tuple-element.20.refs_0_.total_ref, bf16[128,256]{1,0:T(8,128)(2,1)} %collective-permute-done.refs_1_, ...), custom_call_target="tpu_custom_call" | custom-call | flops 16777216 | bytes 1048576 | tf_op jit(solution)/shard_map/group_maps/pallas_call | solution.py:317
  33.9 0.0 collective-permute-done.5.refs_3_
  33.9 0.5 collective-permute-done.4.refs_2_
  34.3 0.0 collective-permute-done.3.refs_1_
  34.4 0.4 group_states.1
  34.8 3.4 %collective-permute-start.6 = (f32[8,128]{1,0:T(8,128)S(1)}, f32[8,128]{1,0:T(8,128)S(1)}, u32[]{:S(2)}, u32[]{:S(2)}) collective-permute-start(f32[8,128]{1,0:T(8,128)S(1)} %get-tuple-element.25.shift_ref), channel_id=1, source_target_pairs={{0,4},{1,5},{2,6},{3,7},{4,8},{5,9},{6,10},{7,11},{8,12},{9,13},{1... | collective-permute-start | bytes 12296 | tf_op jit(solution)/shard_map/ppermute | solution.py:332
  38.1 1.3 %collective-permute-done.6.got_ref = f32[8,128]{1,0:T(8,128)S(1)} collective-permute-done((f32[8,128]{1,0:T(8,128)S(1)}, f32[8,128]{1,0:T(8,128)S(1)}, u32[]{:S(2)}, u32[]{:S(2)}) %collective-permute-start.6) | collective-permute-done | bytes 4128 | tf_op jit(solution)/shard_map/ppermute | solution.py:332
  39.4 0.1 next_group.2
  39.6 4.2 %collective-permute-start.7 = (f32[8,128]{1,0:T(8,128)S(1)}, f32[8,128]{1,0:T(8,128)S(1)}, u32[]{:S(2)}, u32[]{:S(2)}) collective-permute-start(f32[8,128]{1,0:T(8,128)S(1)} %next_group.2), channel_id=1, source_target_pairs={{0,4},{1,5},{2,6},{3,7},{4,8},{5,9},{6,10},{7,11},{8,12},{9,13},{1... | collective-permute-start | bytes 12296 | tf_op jit(solution)/shard_map/ppermute | solution.py:332
  43.8 1.3 %collective-permute-done.7.got_ref = f32[8,128]{1,0:T(8,128)S(1)} collective-permute-done((f32[8,128]{1,0:T(8,128)S(1)}, f32[8,128]{1,0:T(8,128)S(1)}, u32[]{:S(2)}, u32[]{:S(2)}) %collective-permute-start.7) | collective-permute-done | bytes 4128 | tf_op jit(solution)/shard_map/ppermute | solution.py:332
  45.1 0.1 next_group.3
  45.2 4.2 %collective-permute-start.8 = (f32[8,128]{1,0:T(8,128)S(1)}, f32[8,128]{1,0:T(8,128)S(1)}, u32[]{:S(2)}, u32[]{:S(2)}) collective-permute-start(f32[8,128]{1,0:T(8,128)S(1)} %next_group.3), channel_id=1, source_target_pairs={{0,4},{1,5},{2,6},{3,7},{4,8},{5,9},{6,10},{7,11},{8,12},{9,13},{1... | collective-permute-start | bytes 12296 | tf_op jit(solution)/shard_map/ppermute | solution.py:332
  49.4 1.3 %collective-permute-done.8.got_ref = f32[8,128]{1,0:T(8,128)S(1)} collective-permute-done((f32[8,128]{1,0:T(8,128)S(1)}, f32[8,128]{1,0:T(8,128)S(1)}, u32[]{:S(2)}, u32[]{:S(2)}) %collective-permute-start.8) | collective-permute-done | bytes 4128 | tf_op jit(solution)/shard_map/ppermute | solution.py:332
  50.7 2.8 %estimates.1 = f32[64,128]{1,0:T(8,128)} custom-call(s32[1]{0:T(128)} %bitcast.pos_ref, s32[1,64]{1,0:T(1,128)S(1)} %bitcast.10, f32[8,128]{1,0:T(8,128)S(1)} %collective-permute-done.8.got_ref, f32[8,128]{1,0:T(8,128)S(1)} %get-tuple-element.27.before_ref, f32[1,128]{1,0:T(1,128)S(1)} %bitcast.12, bf16[128,256]{1,0:T(8,128)(2,1)S(1)} %get-tuple-element.28.prefix_ref, ...), custom_call_target="tpu_custom_call" | custom-call | flops 8388608 | bytes 5242880 | tf_op jit(solution)/shard_map/estimates/pallas_call | solution.py:341
Async XLA Ops:
  0.0 1.2 %copy-start.2 = (f32[16,128,128]{2,1,0:T(8,128)S(1)}, f32[16,128,128]{2,1,0:T(8,128)}, u32[]{:S(2)}) copy-start(f32[16,128,128]{2,1,0:T(8,128)} %trans_ref.1) | copy-start | bytes 3145732
  1.2 0.9 %copy-start.3 = (bf16[128,1024]{1,0:T(8,128)(2,1)S(1)}, bf16[128,1024]{1,0:T(8,128)(2,1)}, u32[]{:S(2)}) copy-start(bf16[128,1024]{1,0:T(8,128)(2,1)} %refs_0_.1) | copy-start | bytes 786436
  4.1 0.8 %copy-start.10 = (bf16[16,128,128]{2,1,0:T(8,128)(2,1)}, bf16[16,128,128]{2,1,0:T(8,128)(2,1)S(1)}, u32[]{:S(2)}) copy-start(bf16[16,128,128]{2,1,0:T(8,128)(2,1)S(1)} %get-tuple-element.19.low_ref) | copy-start | bytes 1572868
  5.0 19.5 %all-to-all-start = ((bf16[16,64,128]{2,1,0:T(8,128)(2,1)}), bf16[16,64,128]{2,1,0:T(8,128)(2,1)S(1)}, u32[]{:S(2)}, u32[]{:S(2)}) async-start(bf16[16,64,128]{2,1,0:T(8,128)(2,1)} %bitcast.2), calls=%async_computation | async-start | bytes 524288 | tf_op jit(solution)/shard_map/all_to_all | solution.py:279
  12.3 0.7 %copy-start.7 = (s32[64]{0:T(128)S(1)}, s32[64]{0:T(128)}, u32[]{:S(2)}) copy-start(s32[64]{0:T(128)} %param.8) | copy-start | bytes 772
  13.0 1.0 %copy-start.11 = (bf16[16,128,128]{2,1,0:T(8,128)(2,1)S(1)}, bf16[16,128,128]{2,1,0:T(8,128)(2,1)}, u32[]{:S(2)}) copy-start(bf16[16,128,128]{2,1,0:T(8,128)(2,1)} %copy-done.10) | copy-start | bytes 1572868
  14.0 10.5 %copy-start.5 = (s32[2048]{0:T(1024)S(1)}, s32[2048]{0:T(1024)}, u32[]{:S(2)}) copy-start(s32[2048]{0:T(1024)} %param.12) | copy-start | bytes 24580
  14.0 10.5 %copy-start.6 = (bf16[2048]{0:T(1024)(128)(2,1)S(1)}, bf16[2048]{0:T(1024)(128)(2,1)}, u32[]{:S(2)}) copy-start(bf16[2048]{0:T(1024)(128)(2,1)} %param.13) | copy-start | bytes 12292
  14.0 10.5 %copy-start.8 = (s32[64]{0:T(128)S(1)}, s32[64]{0:T(128)}, u32[]{:S(2)}) copy-start(s32[64]{0:T(128)} %param.8) | copy-start | bytes 772
  19.8 1.3 %copy-start = (bf16[31,128,256]{2,1,0:T(8,128)(2,1)}, bf16[31,128,256]{2,1,0:T(8,128)(2,1)S(1)}, u32[]{:S(2)}) copy-start(bf16[31,128,256]{2,1,0:T(8,128)(2,1)S(1)} %get-tuple-element.23.right_hbm) | copy-start | bytes 6094852
  21.1 10.0 %collective-permute-start.2 = (bf16[128,256]{1,0:T(8,128)(2,1)S(1)}, bf16[128,256]{1,0:T(8,128)(2,1)S(1)}, u32[]{:S(2)}, u32[]{:S(2)}) collective-permute-start(bf16[128,256]{1,0:T(8,128)(2,1)S(1)} %get-tuple-element.20.refs_0_.total_ref), channel_id=1, source_target_pairs={{3,0},{0,1},{1,2},{2,3},{7,4},{4,5},{5,6},{6,7},{11,8},{8,9},{9,10... | collective-permute-start | bytes 196616 | tf_op jit(solution)/shard_map/ppermute | solution.py:303
  21.5 11.0 %collective-permute-start.1 = (bf16[128,256]{1,0:T(8,128)(2,1)S(1)}, bf16[128,256]{1,0:T(8,128)(2,1)S(1)}, u32[]{:S(2)}, u32[]{:S(2)}) collective-permute-start(bf16[128,256]{1,0:T(8,128)(2,1)S(1)} %get-tuple-element.20.refs_0_.total_ref), channel_id=1, source_target_pairs={{2,0},{3,1},{0,2},{1,3},{6,4},{7,5},{4,6},{5,7},{10,8},{11,9},{8,1... | collective-permute-start | bytes 196616 | tf_op jit(solution)/shard_map/ppermute | solution.py:303
  23.2 9.3 %collective-permute-start = (bf16[128,256]{1,0:T(8,128)(2,1)S(1)}, bf16[128,256]{1,0:T(8,128)(2,1)}, u32[]{:S(2)}, u32[]{:S(2)}) collective-permute-start(bf16[128,256]{1,0:T(8,128)(2,1)S(1)} %get-tuple-element.20.refs_0_.total_ref), channel_id=1, source_target_pairs={{1,0},{2,1},{3,2},{0,3},{5,4},{6,5},{7,6},{4,7},{9,8},{10,9},{11,1... | collective-permute-start | bytes 196616 | tf_op jit(solution)/shard_map/ppermute | solution.py:303
  24.5 1.6 %copy-start.1 = (bf16[31,128,256]{2,1,0:T(8,128)(2,1)S(1)}, bf16[31,128,256]{2,1,0:T(8,128)(2,1)}, u32[]{:S(2)}) copy-start(bf16[31,128,256]{2,1,0:T(8,128)(2,1)} %copy-done) | copy-start | bytes 6094852
  26.1 0.8 %copy-start.4 = (bf16[128,128]{1,0:T(8,128)(2,1)S(1)}, bf16[128,128]{1,0:T(8,128)(2,1)}, u32[]{:S(2)}) copy-start(bf16[128,128]{1,0:T(8,128)(2,1)} %gain_ref.1) | copy-start | bytes 98308
  26.8 0.7 %copy-start.9 = (f32[128]{0:T(128)S(1)}, f32[128]{0:T(128)}, u32[]{:S(2)}) copy-start(f32[128]{0:T(128)} %param.9) | copy-start | bytes 1540
  30.6 3.3 %collective-permute-start.5 = (f32[8,128]{1,0:T(8,128)S(1)}, f32[8,128]{1,0:T(8,128)S(1)}, u32[]{:S(2)}, u32[]{:S(2)}) collective-permute-start(f32[8,128]{1,0:T(8,128)S(1)} %get-tuple-element.24.refs_0_), channel_id=1, source_target_pairs={{3,0},{0,1},{1,2},{2,3},{7,4},{4,5},{5,6},{6,7},{11,8},{8,9},{9,10... | collective-permute-start | bytes 12296 | tf_op jit(solution)/shard_map/ppermute | solution.py:303
  30.7 3.7 %collective-permute-start.4 = (f32[8,128]{1,0:T(8,128)S(1)}, f32[8,128]{1,0:T(8,128)S(1)}, u32[]{:S(2)}, u32[]{:S(2)}) collective-permute-start(f32[8,128]{1,0:T(8,128)S(1)} %get-tuple-element.24.refs_0_), channel_id=1, source_target_pairs={{2,0},{3,1},{0,2},{1,3},{6,4},{7,5},{4,6},{5,7},{10,8},{11,9},{8,1... | collective-permute-start | bytes 12296 | tf_op jit(solution)/shard_map/ppermute | solution.py:303
  31.1 3.3 %collective-permute-start.3 = (f32[8,128]{1,0:T(8,128)S(1)}, f32[8,128]{1,0:T(8,128)S(1)}, u32[]{:S(2)}, u32[]{:S(2)}) collective-permute-start(f32[8,128]{1,0:T(8,128)S(1)} %get-tuple-element.24.refs_0_), channel_id=1, source_target_pairs={{1,0},{2,1},{3,2},{0,3},{5,4},{6,5},{7,6},{4,7},{9,8},{10,9},{11,1... | collective-permute-start | bytes 12296 | tf_op jit(solution)/shard_map/ppermute | solution.py:303
  34.8 4.7 %collective-permute-start.6 = (f32[8,128]{1,0:T(8,128)S(1)}, f32[8,128]{1,0:T(8,128)S(1)}, u32[]{:S(2)}, u32[]{:S(2)}) collective-permute-start(f32[8,128]{1,0:T(8,128)S(1)} %get-tuple-element.25.shift_ref), channel_id=1, source_target_pairs={{0,4},{1,5},{2,6},{3,7},{4,8},{5,9},{6,10},{7,11},{8,12},{9,13},{1... | collective-permute-start | bytes 12296 | tf_op jit(solution)/shard_map/ppermute | solution.py:332
  39.6 5.5 %collective-permute-start.7 = (f32[8,128]{1,0:T(8,128)S(1)}, f32[8,128]{1,0:T(8,128)S(1)}, u32[]{:S(2)}, u32[]{:S(2)}) collective-permute-start(f32[8,128]{1,0:T(8,128)S(1)} %next_group.2), channel_id=1, source_target_pairs={{0,4},{1,5},{2,6},{3,7},{4,8},{5,9},{6,10},{7,11},{8,12},{9,13},{1... | collective-permute-start | bytes 12296 | tf_op jit(solution)/shard_map/ppermute | solution.py:332
  45.2 5.5 %collective-permute-start.8 = (f32[8,128]{1,0:T(8,128)S(1)}, f32[8,128]{1,0:T(8,128)S(1)}, u32[]{:S(2)}, u32[]{:S(2)}) collective-permute-start(f32[8,128]{1,0:T(8,128)S(1)} %next_group.3), channel_id=1, source_target_pairs={{0,4},{1,5},{2,6},{3,7},{4,8},{5,9},{6,10},{7,11},{8,12},{9,13},{1... | collective-permute-start | bytes 12296 | tf_op jit(solution)/shard_map/ppermute | solution.py:332
where the time goes:
time: 54.1 us; the launch traced here: 53.5 us
  starting transfers between devices  24.3 us (45%)
  Pallas kernels  15.7 us (29%)
  local copies, waits for them, and re-layouts  8.95 us (17%)
  waiting for transfers between devices  4.4 us (8%)
    ppermute x3, starting transfers between devices, shards(): got = lax.ppermute(sent, 'tm', [(j, j + size) for j in range(count - size)])  11.7 us
    unnamed x24, local copies, waits for them, and re-layouts  8.95 us
    all_to_all x1, starting transfers between devices, shards(): x = lax.all_to_all(turned, 'tm', split_axis=0, concat_axis=0, tiled=True)  7.36 us
    pallas_call x1, Pallas kernels, shards(): call(functools.partial(tree_kernel, steps), 'tree_of_maps', 8, 2 * steps...  5.75 us
    ppermute x6, starting transfers between devices, around(): lax.ppermute(x, 'tm', [(j // size * size + (j + r) % size, j) for j in ra...  5.23 us
    ppermute x3, waiting for transfers between devices, shards(): got = lax.ppermute(sent, 'tm', [(j, j + size) for j in range(count - size)])  3.93 us
    pallas_call x1, Pallas kernels, shards(): call(local_kernel, 'local_states', 6, 1 << 27, 6 * MIB, out_shape=[shape(...  3.11 us
    pallas_call x1, Pallas kernels, shards(): call(final_kernel, 'estimates', 5, 1 << 23, 5 * MIB, out_shape=shape((ste...  2.84 us
  transfers between devices with their start and end apart: 10, of which 4 were waited for; matrix products, arithmetic and copies ran while one was open for 0% of the time, Pallas kernels for 19%

commit v1 on v0

v1 whole, which is shorter than its diff:
```python
import functools

import jax
import jax.numpy as jnp
from jax import lax
from jax.experimental import pallas as pl
from jax.experimental.pallas import tpu as pltpu
from jax.sharding import PartitionSpec as P

F32 = jnp.float32
BF16 = jnp.bfloat16
MIB = 1 << 20
BIG, SMALL = 60, 2
NT = (((1,), (1,)), ((), ()))
VMEM = pl.BlockSpec(memory_space=pltpu.VMEM)
SMEM = pl.BlockSpec(memory_space=pltpu.SMEM)
HBM = pl.BlockSpec(memory_space=pltpu.HBM)
shape = jax.ShapeDtypeStruct


def call(kernel, name, mib, flops, moved, **kw):
    return pl.pallas_call(
        kernel,
        name=name,
        compiler_params=pltpu.CompilerParams(vmem_limit_bytes=mib * MIB),
        cost_estimate=pl.CostEstimate(flops=flops, bytes_accessed=moved, transcendentals=0),
        **kw,
    )


def pair(x):
    high = x.astype(BF16)
    mid = (x - high.astype(F32)).astype(BF16)
    return jnp.concatenate([high, mid], axis=1)


def mm(left, right):
    n = right.shape[0]
    out = jnp.dot(left, jnp.concatenate([right, right], axis=0), preferred_element_type=F32)
    return out[:, :n] + out[:, n:]


def vm(vec, mat):
    high = vec.astype(BF16).astype(F32)
    rows = jnp.concatenate([high, vec - high], axis=0).astype(BF16)
    out = jnp.dot(rows, mat, preferred_element_type=F32)
    n = vec.shape[1]
    out = out[:, :n] + out[:, n:]
    return out[:8] + out[8:]


def row(ref, t):
    return jnp.broadcast_to(ref[pl.ds(t, 1), :], (8, ref.shape[1]))


def front_kernel(frames_ref, turned_ref, frames, turned, sems):
    into = pltpu.make_async_copy(frames_ref, frames, sems.at[0])
    into.start()
    into.wait()
    turned[...] = frames[...].T
    out = pltpu.make_async_copy(turned, turned_ref, sems.at[1])
    out.start()
    out.wait()


def tree_kernel(steps, levels_ref, trans_ref, left_hbm, right_hbm, table_hbm, total_ref, trans, table_ref, left_ref, right_ref, sems):
    base = steps // 4
    kinds = trans_ref.shape[0]
    cuts = [(k, kinds // 4) for k in range(0, kinds, kinds // 4)]
    ins = [
        pltpu.make_async_copy(trans_ref.at[pl.ds(a, b)], trans.at[pl.ds(a, b)], sems.at[5 + i])
        for i, (a, b) in enumerate(cuts)
    ]
    for copy in ins:
        copy.start()

    def prepare(k, c):
        table_ref[k] = pair(trans[k].T)
        return c

    for copy, (a, b) in zip(ins, cuts):
        copy.wait()
        lax.fori_loop(a, a + b, prepare, 0)

    def first(t):
        return mm(table_ref[levels_ref[0, t]], table_ref[levels_ref[0, t + 1]])

    def node(k):
        return mm(left_ref[k], right_ref[k])

    def first_pairs(ks):
        made = [(first(4 * k), first(4 * k + 2)) for k in ks]
        for k, (a, b) in zip(ks, made):
            left_ref[k] = pair(a)
            right_ref[k] = pair(b)

    def later_pairs(ks):
        made = [(node(2 * (k - base)), node(2 * (k - base) + 1)) for k in ks]
        for k, (a, b) in zip(ks, made):
            left_ref[k] = pair(a)
            right_ref[k] = pair(b)

    def loop(fn, start, count):
        def body(i, c):
            fn([start + 2 * i, start + 2 * i + 1])
            return c

        lax.fori_loop(0, count // 2, body, 0)

    def store(start, count, k):
        copies = [
            pltpu.make_async_copy(ref.at[pl.ds(start, count)], hbm.at[pl.ds(start, count)], sems.at[k + i])
            for i, (ref, hbm) in enumerate([(left_ref, left_hbm), (right_ref, right_hbm)])
        ]
        for copy in copies:
            copy.start()
        return copies

    keep = pltpu.make_async_copy(table_ref, table_hbm, sems.at[4])
    keep.start()
    loop(first_pairs, 0, base)
    copies = store(0, base, 0)
    count, start = base // 2, base
    while count >= 2:
        loop(later_pairs, start, count)
        start += count
        count //= 2
    later_pairs([start])
    copies += store(base, base - 1, 2)
    total_ref[...] = pair(node(start))
    for copy in copies + [keep]:
        copy.wait()


def fetch(pieces, sems):
    copies = [
        pltpu.make_async_copy(hbm.at[pl.ds(a, b)], ref.at[pl.ds(a, b)], sems.at[i])
        for i, (hbm, ref, a, b) in enumerate(pieces)
    ]
    for copy in copies:
        copy.start()
    return copies


def local_kernel(pos_ref, levels_ref, x_ref, mode_ref, weight_ref, gain_ref, init_ref, total_ref, table_hbm, right_hbm, lefts_ref, own_ref, drive_ref, table_ref, right_ref, sems):
    segments, steps, width = x_ref.shape
    n = gain_ref.shape[0]
    base = steps // 4
    copies = fetch(
        [(table_hbm, table_ref, 0, table_ref.shape[0]), (right_hbm, right_ref, 0, base), (right_hbm, right_ref, base, base - 1)],
        sems,
    )
    channel = lax.broadcasted_iota(jnp.int32, (n, width), 0)
    measured = jnp.zeros((steps, n), F32)
    for k in range(segments):
        weight = jnp.broadcast_to(weight_ref[pl.ds(k, 1), :].astype(F32), (n, width))
        projector = jnp.where(mode_ref[pl.ds(k, 1), :] == channel, weight, 0.0).astype(BF16)
        measured += lax.dot_general(x_ref[k], projector, NT, preferred_element_type=F32)
    drive_ref[...] = lax.dot_general(measured.astype(BF16), gain_ref[...], NT, preferred_element_type=F32)

    states = [row(drive_ref, t) for t in range(steps)]
    at, offset = 0, 0
    for level in range(steps.bit_length() - 1):
        if level < 3:
            copies[level].wait()
        later = []
        for i in range(len(states) // 2):
            mat = table_ref[levels_ref[0, 2 * i + 1]] if level == 0 else right_ref[offset + i]
            lefts_ref[pl.ds(at + i, 1), :] = states[2 * i][:1]
            later.append(vm(states[2 * i], mat) + states[2 * i + 1])
        at += len(later)
        if level > 0:
            offset += len(later)
        states = later
    lefts_ref[pl.ds(at, 1), :] = states[0][:1]
    first = jnp.where(pos_ref[0] == 0, row(init_ref, 0), 0.0)
    total = total_ref[...]
    own_ref[pl.ds(0, n), :] = total
    own_ref[pl.ds(n, 16), :] = rows16(states[0] + vm(first, total))


def rows16(vec):
    high = vec.astype(BF16).astype(F32)
    both = jnp.concatenate([high, vec - high], axis=1)
    return jnp.concatenate([both, both], axis=0).astype(BF16)


def rows8(ref, start, n):
    both = ref[pl.ds(start, 16), :].astype(F32)
    return both[:8, :n] + both[:8, n:]


def join_kernel(bit, pos_ref, own_ref, got_ref, *refs):
    out_ref, map_ref, before_ref = refs[-3:]
    n = own_ref.shape[1] // 2
    upper = pos_ref[0] & bit != 0
    own, got = own_ref[pl.ds(0, n), :], got_ref[pl.ds(0, n), :]
    own_shift, got_shift = rows8(own_ref, n, n), rows8(got_ref, n, n)
    early, late = jnp.where(upper, got, own), jnp.where(upper, own, got)
    early_shift, late_shift = jnp.where(upper, got_shift, own_shift), jnp.where(upper, own_shift, got_shift)
    out_ref[pl.ds(0, n), :] = pair(mm(early, late))
    out_ref[pl.ds(n, 16), :] = rows16(vm(early_shift, late) + late_shift)
    if bit == 1:
        rows, cols = (lax.broadcasted_iota(jnp.int32, (n, n), d) for d in (0, 1))
        eye = pair((rows == cols).astype(F32))
        map_ref[...] = jnp.where(upper, got, eye)
        before_ref[...] = jnp.where(upper, got_shift, 0.0)
    else:
        last_map, last_before = refs[0][...], refs[1][...]
        map_ref[...] = jnp.where(upper, pair(mm(got, last_map)), last_map)
        before_ref[...] = last_before + jnp.where(upper, vm(got_shift, last_map), 0.0)


def final_kernel(bit, pos_ref, levels_ref, got_ref, before_ref, init_ref, map_ref, total_ref, lefts_ref, left_hbm, table_hbm, out_ref, left_ref, table_ref, sems):
    steps, n = lefts_ref.shape
    base = steps // 4
    copies = fetch(
        [(left_hbm, left_ref, base, base - 1), (left_hbm, left_ref, 0, base), (table_hbm, table_ref, 0, table_ref.shape[0])],
        sems,
    )
    first = jnp.where(pos_ref[0] == 0, row(init_ref, 0), 0.0)
    moved = vm(rows8(got_ref, 0, n), map_ref[...])
    state = before_ref[...] + first + jnp.where(pos_ref[0] & bit != 0, moved, 0.0)
    out_ref[pl.ds(steps - 1, 1), :] = (vm(state, total_ref[...]) + row(lefts_ref, steps - 1))[:1]
    levels = steps.bit_length() - 1
    starts = [state]
    sizes = [steps >> (level + 1) for level in range(levels)]
    for level in reversed(range(levels)):
        if level == levels - 1:
            copies[0].wait()
        if level < 2:
            copies[2 - level].wait()
        at, offset = sum(sizes[:level]), sum(sizes[1:level])
        later = []
        for i, x in enumerate(starts):
            mat = table_ref[levels_ref[0, 2 * i]] if level == 0 else left_ref[offset + i]
            later += [x, vm(x, mat) + row(lefts_ref, at + i)]
        starts = later
    for t in range(1, steps):
        out_ref[pl.ds(t - 1, 1), :] = starts[t][:1]


def shards(count, frames, levels, initial_state, transitions, gain, pixel_mode, pixel_weight):
    n = gain.shape[0]
    kinds = transitions.shape[0]
    pixels, length = frames.shape
    steps = length // count
    position = lax.axis_index("tm").astype(jnp.int32)[None]
    initial_state = initial_state[None]
    levels = levels[None]
    pairs = steps // 2 - 1
    dma = pltpu.SemaphoreType.DMA

    if pixels % 128 == 0:
        turned = call(
            front_kernel, "turn_frames", BIG, 0, MIB,
            out_shape=shape((length, pixels), BF16),
            in_specs=[HBM],
            out_specs=HBM,
            scratch_shapes=[pltpu.VMEM(frames.shape, BF16), pltpu.VMEM((length, pixels), BF16), dma((2,))],
        )(frames).reshape(count, steps, pixels)
        x = lax.all_to_all(turned, "tm", split_axis=0, concat_axis=0, tiled=True)
    else:
        x = lax.all_to_all(frames, "tm", split_axis=1, concat_axis=0, tiled=True).T[None]
    mode = pixel_mode.reshape(x.shape[0], x.shape[2])
    weight = pixel_weight.reshape(x.shape[0], x.shape[2])

    tree = pltpu.VMEM((pairs, n, 2 * n), BF16)
    table_vmem = pltpu.VMEM((kinds, n, 2 * n), BF16)
    maps = shape((pairs, n, 2 * n), BF16)
    one_map = shape((n, 2 * n), BF16)
    left, right, table, total = call(
        functools.partial(tree_kernel, steps), "tree_of_maps", BIG, 2 * steps * n**3 * 4, 8 * MIB,
        out_shape=[maps, maps, shape((kinds, n, 2 * n), BF16), one_map],
        in_specs=[SMEM, HBM],
        out_specs=[HBM, HBM, HBM, VMEM],
        scratch_shapes=[pltpu.VMEM(transitions.shape, F32), table_vmem, tree, tree, dma((9,))],
    )(levels, transitions)

    lefts, own = call(
        local_kernel, "local_states", BIG, 1 << 27, 6 * MIB,
        out_shape=[shape((steps, n), F32), shape((n + 16, 2 * n), BF16)],
        in_specs=[SMEM, SMEM] + [VMEM] * 6 + [HBM] * 2,
        out_specs=[VMEM] * 2,
        scratch_shapes=[pltpu.VMEM((steps, n), F32), table_vmem, tree, dma((3,))],
    )(position, levels, x, mode, weight, gain, initial_state, total, table, right)

    def swap(x, bit):
        return lax.ppermute(x, "tm", [(j, j ^ bit) for j in range(count)])

    bit, kept = 1, []
    while 2 * bit < count:
        own, *kept = call(
            functools.partial(join_kernel, bit), "join_halves", SMALL, 1 << 25, MIB // 2,
            out_shape=[shape((n + 16, 2 * n), BF16), one_map, shape((8, n), F32)],
            in_specs=[SMEM] + [VMEM] * (2 + len(kept)),
            out_specs=[VMEM] * 3,
        )(position, own, swap(own, bit), *kept)
        bit *= 2
    got = swap(own[n:], bit)
    prefix, before = kept

    return call(
        functools.partial(final_kernel, bit), "estimates", BIG, 1 << 23, 5 * MIB,
        out_shape=shape((steps, n), F32),
        in_specs=[SMEM, SMEM] + [VMEM] * 6 + [HBM] * 2,
        out_specs=VMEM,
        scratch_shapes=[tree, table_vmem, dma((3,))],
    )(position, levels, got, before, initial_state, prefix, total, lefts, left, table)


def solution(mesh):
    in_specs = (P("tm", "parts"), P(("parts", "tm")), P("parts"), P(), P(), P(), P())
    out_specs = P(("parts", "tm"), None)
    return jax.shard_map(
        functools.partial(shards, mesh.shape["tm"]),
        mesh=mesh,
        in_specs=in_specs,
        out_specs=out_specs,
        check_vma=False,
    )
```

time: 54.1 us -> 46.9 us (0.87)
  starting transfers between devices: 24.3 us -> 11.2 us
  waiting for transfers between devices: 4.4 us -> 12.1 us
  local copies, waits for them, and re-layouts: 8.95 us -> 3.38 us
  Pallas kernels: 15.7 us -> 19.7 us
    ppermute x9 -> x4, starting transfers between devices: 17 us -> 3.85 us  [swap(): return lax.ppermute(x, 'tm', [(j, j ^ bit) for j in range(count)])]
    ppermute x9 -> x4, waiting for transfers between devices: 4.4 us -> 11.1 us  [swap(): return lax.ppermute(x, 'tm', [(j, j ^ bit) for j in range(count)])]
    unnamed x24 -> x10, local copies, waits for them, and re-layouts: 8.95 us -> 3.38 us
    pallas_call x8 -> x7, Pallas kernels: 15.7 us -> 19.7 us  [the longest x1 9.02 us: shards(): call(functools.partial(tree_kernel, steps), 'tree_of_maps', BIG, 2 * step...]
    all_to_all x1, waiting for transfers between devices: 0.01 us -> 1.01 us  [shards(): x = lax.all_to_all(turned, 'tm', split_axis=0, concat_axis=0, tiled=True)]
  transfers between devices with their start and end apart: 10 -> 5, of which waited for: 4 -> 5; matrix products, arithmetic and copies ran while one was open for 0% -> 0% of each run, Pallas kernels for 19% -> 19%
where the time goes in v1:
time: 46.9 us; the launch traced here: 46.4 us
  Pallas kernels  19.7 us (42%)
  waiting for transfers between devices  12.1 us (26%)
  starting transfers between devices  11.2 us (24%)
  local copies, waits for them, and re-layouts  3.38 us (7%)
    ppermute x4, waiting for transfers between devices, swap(): return lax.ppermute(x, 'tm', [(j, j ^ bit) for j in range(count)])  11.1 us
    pallas_call x1, Pallas kernels, shards(): call(functools.partial(tree_kernel, steps), 'tree_of_maps', BIG, 2 * step...  9.02 us
    all_to_all x1, starting transfers between devices, shards(): x = lax.all_to_all(turned, 'tm', split_axis=0, concat_axis=0, tiled=True)  7.37 us
    pallas_call x1, Pallas kernels, shards(): call(local_kernel, 'local_states', BIG, 1 << 27, 6 * MIB, out_shape=[shap...  4.34 us
    pallas_call x1, Pallas kernels, shards(): call(functools.partial(final_kernel, bit), 'estimates', BIG, 1 << 23, 5 *...  3.92 us
    ppermute x4, starting transfers between devices, swap(): return lax.ppermute(x, 'tm', [(j, j ^ bit) for j in range(count)])  3.85 us
    unnamed x10, local copies, waits for them, and re-layouts  3.38 us
    pallas_call x1, Pallas kernels, shards(): call(front_kernel, 'turn_frames', BIG, 0, MIB, out_shape=shape((length, p...  1.79 us
  transfers between devices with their start and end apart: 5, of which 5 were waited for; matrix products, arithmetic and copies ran while one was open for 0% of the time, Pallas kernels for 19%

profile of v1, /device:TPU:0, one launch (start us, length us, event | category | flops | bytes accessed | tf_op | source)
XLA Modules:
  0.0 46.4 jit_solution(6506966933401448813)
XLA Ops:
  0.0 1.8 %turn_frames.1 = bf16[1024,128]{1,0:T(8,128)(2,1)} custom-call(bf16[128,1024]{1,0:T(8,128)(2,1)} %frames_ref.1), custom_call_target="tpu_custom_call" | custom-call | bytes 1048576 | tf_op jit(solution)/shard_map/turn_frames/pallas_call | solution.py:255
  1.8 7.4 %all-to-all-start = ((bf16[16,64,128]{2,1,0:T(8,128)(2,1)}), bf16[16,64,128]{2,1,0:T(8,128)(2,1)S(1)}, u32[]{:S(2)}, u32[]{:S(2)}) async-start(bf16[16,64,128]{2,1,0:T(8,128)(2,1)} %bitcast.6), calls=%async_computation | async-start | bytes 524288 | tf_op jit(solution)/shard_map/all_to_all | solution.py:262
  9.2 9.0 %tree_of_maps.1 = (bf16[31,128,256]{2,1,0:T(8,128)(2,1)}, bf16[31,128,256]{2,1,0:T(8,128)(2,1)}, bf16[16,128,256]{2,1,0:T(8,128)(2,1)}, bf16[128,256]{1,0:T(8,128)(2,1)}) custom-call(s32[1,64]{1,0:T(1,128)} %bitcast.9, f32[16,128,128]{2,1,0:T(8,128)} %trans_ref.1), custom_call_target="tpu_custom_call" | custom-call | flops 1073741824 | bytes 8388608 | tf_op jit(solution)/shard_map/tree_of_maps/pallas_call | solution.py:272
  18.2 1.0 %all-to-all-done.x_ref = bf16[16,64,128]{2,1,0:T(8,128)(2,1)S(1)} async-done(((bf16[16,64,128]{2,1,0:T(8,128)(2,1)}), bf16[16,64,128]{2,1,0:T(8,128)(2,1)S(1)}, u32[]{:S(2)}, u32[]{:S(2)}) %all-to-all-start) | async-done | bytes 262176 | tf_op jit(solution)/shard_map/all_to_all | solution.py:262
  19.2 0.0 copy-start.3
  19.2 0.7 %copy-done.3 = bf16[16,64,128]{2,1,0:T(8,128)(2,1)} copy-done((bf16[16,64,128]{2,1,0:T(8,128)(2,1)}, bf16[16,64,128]{2,1,0:T(8,128)(2,1)S(1)}, u32[]{:S(2)}) %copy-start.3) | copy-done | bytes 262168
  19.9 4.3 %local_states.1 = (f32[64,128]{1,0:T(8,128)}, bf16[144,256]{1,0:T(8,128)(2,1)}) custom-call(s32[1]{0:T(128)} %bitcast.pos_ref, s32[1,64]{1,0:T(1,128)} %bitcast.10, bf16[16,64,128]{2,1,0:T(8,128)(2,1)} %copy-done.3, s32[16,128]{1,0:T(8,128)} %bitcast.7, bf16[16,128]{1,0:T(8,128)(2,1)} %bitcast.8, bf16[128,128]{1,0:T(8,128)(2,1)} %gain_ref.1, ...), custom_call_target="tpu_custom_call" | custom-call | flops 134217728 | bytes 6291456 | tf_op jit(solution)/shard_map/local_states/pallas_call | solution.py:280
  24.3 0.1 collective-permute-start
  24.4 1.5 %collective-permute-done.got_ref = bf16[144,256]{1,0:T(8,128)(2,1)S(1)} collective-permute-done((bf16[144,256]{1,0:T(8,128)(2,1)}, bf16[144,256]{1,0:T(8,128)(2,1)S(1)}, u32[]{:S(2)}, u32[]{:S(2)}) %collective-permute-start) | collective-permute-done | bytes 73760 | tf_op jit(solution)/shard_map/ppermute | solution.py:289
  25.8 0.0 copy-start
  25.8 0.9 %copy-done = bf16[144,256]{1,0:T(8,128)(2,1)S(1)} copy-done((bf16[144,256]{1,0:T(8,128)(2,1)S(1)}, bf16[144,256]{1,0:T(8,128)(2,1)}, u32[]{:S(2)}) %copy-start) | copy-done | bytes 73752
  26.7 0.2 join_halves.3
  26.9 1.0 %collective-permute-start.1 = (bf16[144,256]{1,0:T(8,128)(2,1)S(1)}, bf16[144,256]{1,0:T(8,128)(2,1)S(1)}, u32[]{:S(2)}, u32[]{:S(2)}) collective-permute-start(bf16[144,256]{1,0:T(8,128)(2,1)S(1)} %get-tuple-element.24.own_ref), channel_id=1, source_target_pairs={{0,2},{1,3},{2,0},{3,1},{4,6},{5,7},{6,4},{7,5},{8,10},{9,11},{10,... | collective-permute-start | bytes 221192 | tf_op jit(solution)/shard_map/ppermute | solution.py:289
  27.9 3.4 %collective-permute-done.1.got_ref = bf16[144,256]{1,0:T(8,128)(2,1)S(1)} collective-permute-done((bf16[144,256]{1,0:T(8,128)(2,1)S(1)}, bf16[144,256]{1,0:T(8,128)(2,1)S(1)}, u32[]{:S(2)}, u32[]{:S(2)}) %collective-permute-start.1) | collective-permute-done | bytes 73760 | tf_op jit(solution)/shard_map/ppermute | solution.py:289
  31.3 0.2 join_halves.4
  31.5 1.0 %collective-permute-start.2 = (bf16[144,256]{1,0:T(8,128)(2,1)S(1)}, bf16[144,256]{1,0:T(8,128)(2,1)S(1)}, u32[]{:S(2)}, u32[]{:S(2)}) collective-permute-start(bf16[144,256]{1,0:T(8,128)(2,1)S(1)} %get-tuple-element.27.own_ref), channel_id=1, source_target_pairs={{0,4},{1,5},{2,6},{3,7},{4,0},{5,1},{6,2},{7,3},{8,12},{9,13},{10,... | collective-permute-start | bytes 221192 | tf_op jit(solution)/shard_map/ppermute | solution.py:289
  32.5 3.4 %collective-permute-done.2.got_ref = bf16[144,256]{1,0:T(8,128)(2,1)S(1)} collective-permute-done((bf16[144,256]{1,0:T(8,128)(2,1)S(1)}, bf16[144,256]{1,0:T(8,128)(2,1)S(1)}, u32[]{:S(2)}, u32[]{:S(2)}) %collective-permute-start.2) | collective-permute-done | bytes 73760 | tf_op jit(solution)/shard_map/ppermute | solution.py:289
  35.9 0.2 join_halves.5
  36.2 0.0 copy-start.1
  36.2 0.6 %copy-done.1 = bf16[128,256]{1,0:T(8,128)(2,1)} copy-done((bf16[128,256]{1,0:T(8,128)(2,1)}, bf16[128,256]{1,0:T(8,128)(2,1)S(1)}, u32[]{:S(2)}) %copy-start.1) | copy-done | bytes 65560
  36.8 0.0 copy-start.2
  36.8 0.6 %copy-done.2 = f32[8,128]{1,0:T(8,128)} copy-done((f32[8,128]{1,0:T(8,128)}, f32[8,128]{1,0:T(8,128)S(1)}, u32[]{:S(2)}) %copy-start.2) | copy-done | bytes 4120
  37.4 1.8 %collective-permute-start.3 = (bf16[16,256]{1,0:T(8,128)(2,1)S(1)}, bf16[16,256]{1,0:T(8,128)(2,1)S(1)}, u32[]{:S(2)}, u32[]{:S(2)}) collective-permute-start(bf16[16,256]{1,0:T(8,128)(2,1)S(1)} %slice.3), channel_id=1, source_target_pairs={{0,8},{1,9},{2,10},{3,11},{4,12},{5,13},{6,14},{7,15},{8,0},{9,1},... | collective-permute-start | bytes 24584 | tf_op jit(solution)/shard_map/ppermute | solution.py:289
  39.2 2.7 %collective-permute-done.3.got_ref = bf16[16,256]{1,0:T(8,128)(2,1)S(1)} collective-permute-done((bf16[16,256]{1,0:T(8,128)(2,1)S(1)}, bf16[16,256]{1,0:T(8,128)(2,1)S(1)}, u32[]{:S(2)}, u32[]{:S(2)}) %collective-permute-start.3) | collective-permute-done | bytes 8224 | tf_op jit(solution)/shard_map/ppermute | solution.py:289
  41.9 0.0 copy-start.4
  41.9 0.6 %copy-done.4 = bf16[16,256]{1,0:T(8,128)(2,1)} copy-done((bf16[16,256]{1,0:T(8,128)(2,1)}, bf16[16,256]{1,0:T(8,128)(2,1)S(1)}, u32[]{:S(2)}) %copy-start.4) | copy-done | bytes 8216
  42.5 3.9 %estimates.1 = f32[64,128]{1,0:T(8,128)} custom-call(s32[1]{0:T(128)} %bitcast.pos_ref, s32[1,64]{1,0:T(1,128)} %bitcast.11, bf16[16,256]{1,0:T(8,128)(2,1)} %copy-done.4, f32[8,128]{1,0:T(8,128)} %copy-done.2, f32[1,128]{1,0:T(1,128)} %bitcast.13, bf16[128,256]{1,0:T(8,128)(2,1)} %copy-done.1, bf16[128,256]{1,0:T(8,128)(2,1)} %get-tuple-element.20.total_ref, ...), custom_call_target="tpu_custom_call" | custom-call | flops 8388608 | bytes 5242880 | tf_op jit(solution)/shard_map/estimates/pallas_call | solution.py:303
  (1 shorter events, 0.0 us)
Async XLA Ops:
  1.8 17.4 %all-to-all-start = ((bf16[16,64,128]{2,1,0:T(8,128)(2,1)}), bf16[16,64,128]{2,1,0:T(8,128)(2,1)S(1)}, u32[]{:S(2)}, u32[]{:S(2)}) async-start(bf16[16,64,128]{2,1,0:T(8,128)(2,1)} %bitcast.6), calls=%async_computation | async-start | bytes 524288 | tf_op jit(solution)/shard_map/all_to_all | solution.py:262
  19.2 0.7 %copy-start.3 = (bf16[16,64,128]{2,1,0:T(8,128)(2,1)}, bf16[16,64,128]{2,1,0:T(8,128)(2,1)S(1)}, u32[]{:S(2)}) copy-start(bf16[16,64,128]{2,1,0:T(8,128)(2,1)S(1)} %all-to-all-done.x_ref) | copy-start | bytes 786436
  24.3 1.5 %collective-permute-start = (bf16[144,256]{1,0:T(8,128)(2,1)}, bf16[144,256]{1,0:T(8,128)(2,1)S(1)}, u32[]{:S(2)}, u32[]{:S(2)}) collective-permute-start(bf16[144,256]{1,0:T(8,128)(2,1)} %get-tuple-element.23.own_ref), channel_id=1, source_target_pairs={{0,1},{1,0},{2,3},{3,2},{4,5},{5,4},{6,7},{7,6},{8,9},{9,8},{10,11... | collective-permute-start | bytes 221192 | tf_op jit(solution)/shard_map/ppermute | solution.py:289
  25.8 0.9 %copy-start = (bf16[144,256]{1,0:T(8,128)(2,1)S(1)}, bf16[144,256]{1,0:T(8,128)(2,1)}, u32[]{:S(2)}) copy-start(bf16[144,256]{1,0:T(8,128)(2,1)} %get-tuple-element.23.own_ref) | copy-start | bytes 221188
  26.9 4.4 %collective-permute-start.1 = (bf16[144,256]{1,0:T(8,128)(2,1)S(1)}, bf16[144,256]{1,0:T(8,128)(2,1)S(1)}, u32[]{:S(2)}, u32[]{:S(2)}) collective-permute-start(bf16[144,256]{1,0:T(8,128)(2,1)S(1)} %get-tuple-element.24.own_ref), channel_id=1, source_target_pairs={{0,2},{1,3},{2,0},{3,1},{4,6},{5,7},{6,4},{7,5},{8,10},{9,11},{10,... | collective-permute-start | bytes 221192 | tf_op jit(solution)/shard_map/ppermute | solution.py:289
  31.5 4.4 %collective-permute-start.2 = (bf16[144,256]{1,0:T(8,128)(2,1)S(1)}, bf16[144,256]{1,0:T(8,128)(2,1)S(1)}, u32[]{:S(2)}, u32[]{:S(2)}) collective-permute-start(bf16[144,256]{1,0:T(8,128)(2,1)S(1)} %get-tuple-element.27.own_ref), channel_id=1, source_target_pairs={{0,4},{1,5},{2,6},{3,7},{4,0},{5,1},{6,2},{7,3},{8,12},{9,13},{10,... | collective-permute-start | bytes 221192 | tf_op jit(solution)/shard_map/ppermute | solution.py:289
  36.2 0.6 %copy-start.1 = (bf16[128,256]{1,0:T(8,128)(2,1)}, bf16[128,256]{1,0:T(8,128)(2,1)S(1)}, u32[]{:S(2)}) copy-start(bf16[128,256]{1,0:T(8,128)(2,1)S(1)} %get-tuple-element.32.map_ref) | copy-start | bytes 196612
  36.8 0.6 %copy-start.2 = (f32[8,128]{1,0:T(8,128)}, f32[8,128]{1,0:T(8,128)S(1)}, u32[]{:S(2)}) copy-start(f32[8,128]{1,0:T(8,128)S(1)} %get-tuple-element.31.before_ref) | copy-start | bytes 12292
  37.4 4.5 %collective-permute-start.3 = (bf16[16,256]{1,0:T(8,128)(2,1)S(1)}, bf16[16,256]{1,0:T(8,128)(2,1)S(1)}, u32[]{:S(2)}, u32[]{:S(2)}) collective-permute-start(bf16[16,256]{1,0:T(8,128)(2,1)S(1)} %slice.3), channel_id=1, source_target_pairs={{0,8},{1,9},{2,10},{3,11},{4,12},{5,13},{6,14},{7,15},{8,0},{9,1},... | collective-permute-start | bytes 24584 | tf_op jit(solution)/shard_map/ppermute | solution.py:289
  41.9 0.6 %copy-start.4 = (bf16[16,256]{1,0:T(8,128)(2,1)}, bf16[16,256]{1,0:T(8,128)(2,1)S(1)}, u32[]{:S(2)}) copy-start(bf16[16,256]{1,0:T(8,128)(2,1)S(1)} %collective-permute-done.3.got_ref) | copy-start | bytes 24580

commit v2 on v1

v2 whole, which is shorter than its diff:
```python
import functools

import jax
import jax.numpy as jnp
from jax import lax
from jax.experimental import pallas as pl
from jax.experimental.pallas import tpu as pltpu
from jax.sharding import PartitionSpec as P

F32 = jnp.float32
BF16 = jnp.bfloat16
MIB = 1 << 20
BIG, SMALL = 60, 2
NT = (((1,), (1,)), ((), ()))
VMEM = pl.BlockSpec(memory_space=pltpu.VMEM)
SMEM = pl.BlockSpec(memory_space=pltpu.SMEM)
HBM = pl.BlockSpec(memory_space=pltpu.HBM)
shape = jax.ShapeDtypeStruct


def call(kernel, name, mib, flops, moved, **kw):
    return pl.pallas_call(
        kernel,
        name=name,
        compiler_params=pltpu.CompilerParams(vmem_limit_bytes=mib * MIB),
        cost_estimate=pl.CostEstimate(flops=flops, bytes_accessed=moved, transcendentals=0),
        **kw,
    )


def pair(x):
    high = x.astype(BF16)
    mid = (x - high.astype(F32)).astype(BF16)
    return jnp.concatenate([high, mid], axis=1)


def mm(left, right):
    n = right.shape[0]
    out = jnp.dot(left, jnp.concatenate([right, right], axis=0), preferred_element_type=F32)
    return out[:, :n] + out[:, n:]


def vm(vec, mat):
    high = vec.astype(BF16).astype(F32)
    rows = jnp.concatenate([high, vec - high], axis=0).astype(BF16)
    out = jnp.dot(rows, mat, preferred_element_type=F32)
    n = vec.shape[1]
    out = out[:, :n] + out[:, n:]
    return out[:8] + out[8:]


def row(ref, t):
    return jnp.broadcast_to(ref[pl.ds(t, 1), :], (8, ref.shape[1]))


def front_kernel(frames_ref, turned_ref, frames, turned, sems):
    into = pltpu.make_async_copy(frames_ref, frames, sems.at[0])
    into.start()
    into.wait()
    turned[...] = frames[...].T
    out = pltpu.make_async_copy(turned, turned_ref, sems.at[1])
    out.start()
    out.wait()


def tree_kernel(steps, levels_ref, trans_ref, left_hbm, right_hbm, table_hbm, total_ref, trans, table_ref, left_ref, right_ref, sems):
    base = steps // 4
    kinds = trans_ref.shape[0]
    cuts = [(k, kinds // 4) for k in range(0, kinds, kinds // 4)]
    ins = [
        pltpu.make_async_copy(trans_ref.at[pl.ds(a, b)], trans.at[pl.ds(a, b)], sems.at[7 + i])
        for i, (a, b) in enumerate(cuts)
    ]
    for copy in ins:
        copy.start()

    for copy, (a, b) in zip(ins, cuts):
        copy.wait()
        for k in range(a, a + b):
            table_ref[k] = pair(trans[k].T)

    def first(t):
        return mm(table_ref[levels_ref[0, t]], table_ref[levels_ref[0, t + 1]])

    def node(k):
        return mm(left_ref[k], right_ref[k])

    def first_pairs(ks):
        made = [(first(4 * k), first(4 * k + 2)) for k in ks]
        for k, (a, b) in zip(ks, made):
            left_ref[k] = pair(a)
            right_ref[k] = pair(b)

    def later_pairs(ks):
        made = [(node(2 * (k - base)), node(2 * (k - base) + 1)) for k in ks]
        for k, (a, b) in zip(ks, made):
            left_ref[k] = pair(a)
            right_ref[k] = pair(b)

    def run(fn, start, count):
        if count <= 4:
            fn(list(range(start, start + count)))
            return

        def body(i, c):
            fn([start + 4 * i + k for k in range(4)])
            return c

        lax.fori_loop(0, count // 4, body, 0)

    copies = [pltpu.make_async_copy(table_ref, table_hbm, sems.at[0])]
    copies[0].start()

    def store(start, count):
        for ref, hbm in ((right_ref, right_hbm), (left_ref, left_hbm)):
            part = pl.ds(start, count)
            copies.append(pltpu.make_async_copy(ref.at[part], hbm.at[part], sems.at[len(copies)]))
            copies[-1].start()

    run(first_pairs, 0, base)
    store(0, base)
    run(later_pairs, base, base // 2)
    store(base, base // 2)
    count, start = base // 4, base + base // 2
    while count >= 1:
        run(later_pairs, start, count)
        start += count
        count //= 2
    store(base + base // 2, base // 2 - 1)
    total_ref[...] = pair(node(start - 1))
    for copy in copies:
        copy.wait()


def fetch(pieces, sems):
    copies = [
        pltpu.make_async_copy(hbm.at[pl.ds(a, b)], ref.at[pl.ds(a, b)], sems.at[i])
        for i, (hbm, ref, a, b) in enumerate(pieces)
    ]
    for copy in copies:
        copy.start()
    return copies


def local_kernel(pos_ref, levels_ref, *refs):
    hbm, (lefts_ref, shift_ref), (drive_ref, sems), vmem = refs[:8], refs[8:10], refs[10:12], refs[12:]
    x_ref, mode_ref, weight_ref, gain_ref, init_ref, total_ref, table_ref, right_ref = vmem
    segments, steps, width = x_ref.shape
    n = gain_ref.shape[0]
    base = steps // 4
    whole = [(a, b, 0, b.shape[0]) for a, b in zip(hbm[:7], vmem[:7])]
    copies = fetch(whole + [(hbm[7], right_ref, 0, base), (hbm[7], right_ref, base, base - 1)], sems)
    for copy in copies[:6]:
        copy.wait()
    channel = lax.broadcasted_iota(jnp.int32, (n, width), 0)
    measured = jnp.zeros((steps, n), F32)
    for k in range(segments):
        weight = jnp.broadcast_to(weight_ref[pl.ds(k, 1), :].astype(F32), (n, width))
        projector = jnp.where(mode_ref[pl.ds(k, 1), :] == channel, weight, 0.0).astype(BF16)
        measured += lax.dot_general(x_ref[k], projector, NT, preferred_element_type=F32)
    drive_ref[...] = lax.dot_general(measured.astype(BF16), gain_ref[...], NT, preferred_element_type=F32)

    states = [row(drive_ref, t) for t in range(steps)]
    at, offset = 0, 0
    for level in range(steps.bit_length() - 1):
        if level < 3:
            copies[6 + level].wait()
        later = []
        for i in range(len(states) // 2):
            mat = table_ref[levels_ref[0, 2 * i + 1]] if level == 0 else right_ref[offset + i]
            lefts_ref[pl.ds(at + i, 1), :] = states[2 * i][:1]
            later.append(vm(states[2 * i], mat) + states[2 * i + 1])
        at += len(later)
        if level > 0:
            offset += len(later)
        states = later
    lefts_ref[pl.ds(at, 1), :] = states[0][:1]
    first = jnp.where(pos_ref[0] == 0, row(init_ref, 0), 0.0)
    shift_ref[...] = states[0] + vm(first, total_ref[...])


def group_kernel(size, pos_ref, shift_ref, *refs):
    maps = refs[:size]
    prefix_ref, whole_ref, sent_ref, all_ref = refs[size:]
    n = whole_ref.shape[0]
    position = pos_ref[0]
    member = position % size
    for r in range(size):
        all_ref[(member + r) % size] = maps[r][...]
    rows, cols = (lax.broadcasted_iota(jnp.int32, (n, n), d) for d in (0, 1))
    sent_ref[...] = jnp.zeros_like(sent_ref)
    prefix = pair((rows == cols).astype(F32))
    run, vec = all_ref[0], shift_ref[...]
    for q in range(1, size):
        prefix = jnp.where(member == q, run, prefix)
        sent_ref[position - member + q] = jnp.where(member < q, vec, 0.0)[:1]
        vec = jnp.where(member < q, vm(vec, all_ref[q]), vec)
        run = pair(mm(run, all_ref[q]))
    prefix_ref[...] = prefix
    whole_ref[...] = run
    last = position - member + size
    for d in range(size, sent_ref.shape[0]):
        @pl.when(d >= last)
        def _(d=d):
            sent_ref[d] = vec[:1]


def final_kernel(size, pos_ref, levels_ref, got_ref, init_ref, prefix_ref, total_ref, lefts_ref, left_ref, table_ref, *refs):
    wholes, (out_ref, sums_ref) = refs[:-2], refs[-2:]
    steps, n = lefts_ref.shape
    groups = got_ref.shape[0] // size
    position = pos_ref[0]
    group = position // size
    for g in range(groups):
        sums_ref[g] = jnp.broadcast_to(jnp.sum(got_ref[pl.ds(g * size, size)], axis=0), (8, n))
    state = jnp.zeros((8, n), F32)
    for r in range(groups - 1, 0, -1):
        if r <= len(wholes):
            state = vm(state, wholes[r - 1][...])
        state += jnp.where(group >= r, sums_ref[jnp.maximum(group - r, 0)], 0.0)
    first = jnp.where(position == 0, row(init_ref, 0), 0.0)
    state = vm(state, prefix_ref[...]) + sums_ref[group] + first
    out_ref[pl.ds(steps - 1, 1), :] = (vm(state, total_ref[...]) + row(lefts_ref, steps - 1))[:1]
    levels = steps.bit_length() - 1
    starts = [state]
    sizes = [steps >> (level + 1) for level in range(levels)]
    for level in reversed(range(levels)):
        at, offset = sum(sizes[:level]), sum(sizes[1:level])
        later = []
        for i, x in enumerate(starts):
            mat = table_ref[levels_ref[0, 2 * i]] if level == 0 else left_ref[offset + i]
            later += [x, vm(x, mat) + row(lefts_ref, at + i)]
        starts = later
    for t in range(1, steps):
        out_ref[pl.ds(t - 1, 1), :] = starts[t][:1]


def shards(count, frames, levels, initial_state, transitions, gain, pixel_mode, pixel_weight):
    n = gain.shape[0]
    kinds = transitions.shape[0]
    pixels, length = frames.shape
    steps = length // count
    position = lax.axis_index("tm").astype(jnp.int32)[None]
    initial_state = initial_state[None]
    levels = levels[None]
    pairs = steps // 2 - 1
    dma = pltpu.SemaphoreType.DMA

    if pixels % 128 == 0:
        turned = call(
            front_kernel, "turn_frames", BIG, 0, MIB,
            out_shape=shape((length, pixels), BF16),
            in_specs=[HBM],
            out_specs=HBM,
            scratch_shapes=[pltpu.VMEM(frames.shape, BF16), pltpu.VMEM((length, pixels), BF16), dma((2,))],
        )(frames).reshape(count, steps, pixels)
        x = lax.all_to_all(turned, "tm", split_axis=0, concat_axis=0, tiled=True)
    else:
        x = lax.all_to_all(frames, "tm", split_axis=1, concat_axis=0, tiled=True).T[None]
    mode = pixel_mode.reshape(x.shape[0], x.shape[2])
    weight = pixel_weight.reshape(x.shape[0], x.shape[2])

    tree = pltpu.VMEM((pairs, n, 2 * n), BF16)
    table_vmem = pltpu.VMEM((kinds, n, 2 * n), BF16)
    maps = shape((pairs, n, 2 * n), BF16)
    one_map = shape((n, 2 * n), BF16)
    left, right, table, total = call(
        functools.partial(tree_kernel, steps), "tree_of_maps", BIG, 2 * steps * n**3 * 4, 8 * MIB,
        out_shape=[maps, maps, shape((kinds, n, 2 * n), BF16), one_map],
        in_specs=[SMEM, HBM],
        out_specs=[HBM, HBM, HBM, VMEM],
        scratch_shapes=[pltpu.VMEM(transitions.shape, F32), table_vmem, tree, tree, dma((11,))],
    )(levels, transitions)

    size = 1
    while count % (2 * size) == 0 and 4 * size * size <= count:
        size *= 2
    groups = count // size
    members = [
        lax.ppermute(total, "tm", [(j // size * size + (j + r) % size, j) for j in range(count)])
        for r in range(1, size)
    ]
    inputs = (x, mode, weight, gain, initial_state, total, table, right)
    lefts, shift = call(
        local_kernel, "local_states", BIG, 1 << 27, 6 * MIB,
        out_shape=[shape((steps, n), F32), shape((8, n), F32)],
        in_specs=[SMEM, SMEM] + [HBM] * 8,
        out_specs=[VMEM] * 2,
        scratch_shapes=[pltpu.VMEM((steps, n), F32), dma((9,))] + [pltpu.VMEM(a.shape, a.dtype) for a in inputs],
    )(position, levels, *inputs)

    prefix, whole, sent = call(
        functools.partial(group_kernel, size), "group_maps", SMALL, 1 << 24, MIB,
        out_shape=[one_map, one_map, shape((count, 1, n), F32)],
        in_specs=[SMEM] + [VMEM] * (1 + size),
        out_specs=[VMEM] * 3,
        scratch_shapes=[pltpu.VMEM((size, n, 2 * n), BF16)],
    )(position, shift, total, *members)
    wholes = [
        lax.ppermute(whole, "tm", [(j, j + r * size) for j in range(count - r * size)])
        for r in range(1, groups - 1)
    ]
    got = lax.all_to_all(sent, "tm", split_axis=0, concat_axis=0, tiled=True)

    return call(
        functools.partial(final_kernel, size), "estimates", 6, 1 << 23, 5 * MIB,
        out_shape=shape((steps, n), F32),
        in_specs=[SMEM, SMEM] + [VMEM] * (7 + len(wholes)),
        out_specs=VMEM,
        scratch_shapes=[pltpu.VMEM((groups, 8, n), F32)],
    )(position, levels, got, initial_state, prefix, total, lefts, left, table, *wholes)


def solution(mesh):
    in_specs = (P("tm", "parts"), P(("parts", "tm")), P("parts"), P(), P(), P(), P())
    out_specs = P(("parts", "tm"), None)
    return jax.shard_map(
        functools.partial(shards, mesh.shape["tm"]),
        mesh=mesh,
        in_specs=in_specs,
        out_specs=out_specs,
        check_vma=False,
    )
```

time: 46.9 us -> 45.2 us (0.964)
  waiting for transfers between devices: 12.1 us -> 0.38 us
  blocking collectives: 0 us -> 8.98 us
  starting transfers between devices: 11.2 us -> 18.1 us
  Pallas kernels: 19.7 us -> 15.6 us
  local copies, waits for them, and re-layouts: 3.38 us -> 1.46 us
    ppermute x4 -> x5, waiting for transfers between devices: 11.1 us -> 0.01 us  [the longest x3 0.01 us: shards(): lax.ppermute(total, 'tm', [(j // size * size + (j + r) % size, j) for j i...]
    all_to_all x0 -> x1, blocking collectives: none -> 8.98 us  [shards(): got = lax.all_to_all(sent, 'tm', split_axis=0, concat_axis=0, tiled=True)]
    ppermute x4 -> x5, starting transfers between devices: 3.85 us -> 10.7 us  [the longest x2 7.31 us: shards(): lax.ppermute(whole, 'tm', [(j, j + r * size) for j in range(count - r * s...]
    pallas_call x1, Pallas kernels: 9.02 us -> 6.39 us  [shards(): call(functools.partial(tree_kernel, steps), 'tree_of_maps', BIG, 2 * step...]
    unnamed x10 -> x14, local copies, waits for them, and re-layouts: 3.38 us -> 1.46 us
    pallas_call x4 -> x2, Pallas kernels: 4.53 us -> 2.91 us  [the longest x1 2.44 us: shards(): call(functools.partial(final_kernel, size), 'estimates', 6, 1 << 23, 5 *...]
    all_to_all x1, waiting for transfers between devices: 1.01 us -> 0.37 us  [shards(): x = lax.all_to_all(turned, 'tm', split_axis=0, concat_axis=0, tiled=True)]
  transfers between devices with their start and end apart: 5 -> 6, of which waited for: 5 -> 1; matrix products, arithmetic and copies ran while one was open for 0% -> 0% of each run, Pallas kernels for 19% -> 24%
where the time goes in v2:
time: 45.2 us; the launch traced here: 44.8 us
  starting transfers between devices  18.1 us (40%)
  Pallas kernels  15.6 us (35%)
  blocking collectives  8.98 us (20%)
  local copies, waits for them, and re-layouts  1.46 us (3%)
    all_to_all x1, blocking collectives, shards(): got = lax.all_to_all(sent, 'tm', split_axis=0, concat_axis=0, tiled=True)  8.98 us
    all_to_all x1, starting transfers between devices, shards(): x = lax.all_to_all(turned, 'tm', split_axis=0, concat_axis=0, tiled=True)  7.42 us
    ppermute x2, starting transfers between devices, shards(): lax.ppermute(whole, 'tm', [(j, j + r * size) for j in range(count - r * s...  7.31 us
    pallas_call x1, Pallas kernels, shards(): call(functools.partial(tree_kernel, steps), 'tree_of_maps', BIG, 2 * step...  6.39 us
    pallas_call x1, Pallas kernels, shards(): call(local_kernel, 'local_states', BIG, 1 << 27, 6 * MIB, out_shape=[shap...  4.55 us
    ppermute x3, starting transfers between devices, shards(): lax.ppermute(total, 'tm', [(j // size * size + (j + r) % size, j) for j i...  3.38 us
    pallas_call x1, Pallas kernels, shards(): call(functools.partial(final_kernel, size), 'estimates', 6, 1 << 23, 5 *...  2.44 us
    pallas_call x1, Pallas kernels, shards(): call(front_kernel, 'turn_frames', BIG, 0, MIB, out_shape=shape((length, p...  1.8 us
  transfers between devices with their start and end apart: 6, of which 1 were waited for; matrix products, arithmetic and copies ran while one was open for 0% of the time, Pallas kernels for 24%

profile of v2, /device:TPU:0, one launch (start us, length us, event | category | flops | bytes accessed | tf_op | source)
XLA Modules:
  0.0 44.8 jit_solution(17031856794089308692)
XLA Ops:
  0.0 1.8 %turn_frames.1 = bf16[1024,128]{1,0:T(8,128)(2,1)} custom-call(bf16[128,1024]{1,0:T(8,128)(2,1)} %frames_ref.1), custom_call_target="tpu_custom_call" | custom-call | bytes 1048576 | tf_op jit(solution)/shard_map/turn_frames/pallas_call | solution.py:250
  1.8 7.4 %all-to-all-start = ((bf16[16,64,128]{2,1,0:T(8,128)(2,1)}), bf16[16,64,128]{2,1,0:T(8,128)(2,1)}, u32[]{:S(2)}, u32[]{:S(2)}) async-start(bf16[16,64,128]{2,1,0:T(8,128)(2,1)} %bitcast.11), calls=%async_computation | async-start | bytes 524288 | tf_op jit(solution)/shard_map/all_to_all | solution.py:257
  9.2 6.4 %tree_of_maps.1 = (bf16[31,128,256]{2,1,0:T(8,128)(2,1)}, bf16[31,128,256]{2,1,0:T(8,128)(2,1)}, bf16[16,128,256]{2,1,0:T(8,128)(2,1)}, bf16[128,256]{1,0:T(8,128)(2,1)}) custom-call(s32[1,64]{1,0:T(1,128)} %bitcast.6, f32[16,128,128]{2,1,0:T(8,128)} %trans_ref.1), custom_call_target="tpu_custom_call" | custom-call | flops 1073741824 | bytes 8388608 | tf_op jit(solution)/shard_map/tree_of_maps/pallas_call | solution.py:267
  15.6 0.0 copy-start.2
  15.6 0.0 copy-start
  15.7 0.0 copy-start.1
  15.7 0.0 copy-start.5
  15.7 0.0 copy-start.6
  15.7 0.4 collective-permute-start.2
  16.1 1.7 %collective-permute-start.1 = (bf16[128,256]{1,0:T(8,128)(2,1)}, bf16[128,256]{1,0:T(8,128)(2,1)S(1)}, u32[]{:S(2)}, u32[]{:S(2)}) collective-permute-start(bf16[128,256]{1,0:T(8,128)(2,1)} %get-tuple-element.14.refs_5_.refs_0_.total_ref), channel_id=1, source_target_pairs={{2,0},{3,1},{0,2},{1,3},{6,4},{7,5},{4,6},{5,7},{10,8},{11,9},{8,1... | collective-permute-start | bytes 196616 | tf_op jit(solution)/shard_map/ppermute | solution.py:280
  17.7 1.3 %collective-permute-start = (bf16[128,256]{1,0:T(8,128)(2,1)}, bf16[128,256]{1,0:T(8,128)(2,1)S(1)}, u32[]{:S(2)}, u32[]{:S(2)}) collective-permute-start(bf16[128,256]{1,0:T(8,128)(2,1)} %get-tuple-element.14.refs_5_.refs_0_.total_ref), channel_id=1, source_target_pairs={{1,0},{2,1},{3,2},{0,3},{5,4},{6,5},{7,6},{4,7},{9,8},{10,9},{11,1... | collective-permute-start | bytes 196616 | tf_op jit(solution)/shard_map/ppermute | solution.py:280
  19.1 0.4 all-to-all-done.refs_0_
  19.4 4.5 %local_states.1 = (f32[64,128]{1,0:T(8,128)}, f32[8,128]{1,0:T(8,128)}) custom-call(s32[1]{0:T(128)} %bitcast.pos_ref, s32[1,64]{1,0:T(1,128)} %bitcast.7, bf16[16,64,128]{2,1,0:T(8,128)(2,1)} %all-to-all-done.refs_0_, s32[16,128]{1,0:T(8,128)} %bitcast.12, bf16[16,128]{1,0:T(8,128)(2,1)} %bitcast.13, bf16[128,128]{1,0:T(8,128)(2,1)} %refs_3_.1, ...), custom_call_target="tpu_custom_call" | custom-call | flops 134217728 | bytes 6291456 | tf_op jit(solution)/shard_map/local_states/pallas_call | solution.py:284
  24.0 0.0 collective-permute-done.2.refs_3_
  24.0 0.0 collective-permute-done.1.refs_2_
  24.0 0.0 collective-permute-done.refs_1_
  24.0 0.0 copy-done.2
  24.0 0.0 copy-start.4
  24.0 0.7 %copy-done.4 = f32[8,128]{1,0:T(8,128)S(1)} copy-done((f32[8,128]{1,0:T(8,128)S(1)}, f32[8,128]{1,0:T(8,128)}, u32[]{:S(2)}) %copy-start.4) | copy-done | bytes 4120
  24.7 0.5 %group_maps.1 = (bf16[128,256]{1,0:T(8,128)(2,1)S(1)}, bf16[128,256]{1,0:T(8,128)(2,1)S(1)}, f32[16,1,128]{2,1,0:T(1,128)S(1)}) custom-call(s32[1]{0:T(128)} %bitcast.pos_ref, f32[8,128]{1,0:T(8,128)S(1)} %copy-done.4, bf16[128,256]{1,0:T(8,128)(2,1)S(1)} %copy-done.2, bf16[128,256]{1,0:T(8,128)(2,1)S(1)} %collective-permute-done.refs_1_, ...), custom_call_target="tpu_custom_call" | custom-call | flops 16777216 | bytes 1048576 | tf_op jit(solution)/shard_map/group_maps/pallas_call | solution.py:292
  25.2 3.9 %collective-permute-start.4 = (bf16[128,256]{1,0:T(8,128)(2,1)S(1)}, bf16[128,256]{1,0:T(8,128)(2,1)S(1)}, u32[]{:S(2)}, u32[]{:S(2)}) collective-permute-start(bf16[128,256]{1,0:T(8,128)(2,1)S(1)} %get-tuple-element.22), channel_id=1, source_target_pairs={{0,8},{1,9},{2,10},{3,11},{4,12},{5,13},{6,14},{7,15},{16,24},{17,... | collective-permute-start | bytes 196616 | tf_op jit(solution)/shard_map/ppermute | solution.py:300
  29.1 3.4 %collective-permute-start.3 = (bf16[128,256]{1,0:T(8,128)(2,1)S(1)}, bf16[128,256]{1,0:T(8,128)(2,1)S(1)}, u32[]{:S(2)}, u32[]{:S(2)}) collective-permute-start(bf16[128,256]{1,0:T(8,128)(2,1)S(1)} %get-tuple-element.22), channel_id=1, source_target_pairs={{0,4},{1,5},{2,6},{3,7},{4,8},{5,9},{6,10},{7,11},{8,12},{9,13},{1... | collective-permute-start | bytes 196616 | tf_op jit(solution)/shard_map/ppermute | solution.py:300
  32.5 9.0 %all_to_all.10.got_ref = f32[16,1,128]{2,1,0:T(1,128)S(1)} all-to-all(f32[16,1,128]{2,1,0:T(1,128)S(1)} %get-tuple-element.18), channel_id=1, replica_groups=mesh['parts'=2,'tm'=16] {'tm'}, dimensions={0} | all-to-all | bytes 16384 | tf_op jit(solution)/shard_map/all_to_all | solution.py:303
  41.5 0.0 collective-permute-done.4.refs_1_
  41.5 0.0 collective-permute-done.3.refs_0_
  41.5 0.0 copy-done
  41.5 0.0 copy-done.1
  41.5 0.0 copy-done.5
  41.5 0.0 copy-done.6
  41.6 0.0 copy-start.3
  41.6 0.7 %copy-done.3 = f32[64,128]{1,0:T(8,128)S(1)} copy-done((f32[64,128]{1,0:T(8,128)S(1)}, f32[64,128]{1,0:T(8,128)}, u32[]{:S(2)}) %copy-start.3) | copy-done | bytes 32792
  42.3 2.4 %estimates.1 = f32[64,128]{1,0:T(8,128)} custom-call(s32[1]{0:T(128)} %bitcast.pos_ref, s32[1,64]{1,0:T(1,128)S(1)} %bitcast.8, f32[16,1,128]{2,1,0:T(1,128)S(1)} %all_to_all.10.got_ref, f32[1,128]{1,0:T(1,128)S(1)} %bitcast.10, bf16[128,256]{1,0:T(8,128)(2,1)S(1)} %get-tuple-element.19.prefix_ref, bf16[128,256]{1,0:T(8,128)(2,1)S(1)} %copy-done.2, ...), custom_call_target="tpu_custom_call" | custom-call | flops 8388608 | bytes 5242880 | tf_op jit(solution)/shard_map/estimates/pallas_call | solution.py:305
Async XLA Ops:
  1.8 17.6 %all-to-all-start = ((bf16[16,64,128]{2,1,0:T(8,128)(2,1)}), bf16[16,64,128]{2,1,0:T(8,128)(2,1)}, u32[]{:S(2)}, u32[]{:S(2)}) async-start(bf16[16,64,128]{2,1,0:T(8,128)(2,1)} %bitcast.11), calls=%async_computation | async-start | bytes 524288 | tf_op jit(solution)/shard_map/all_to_all | solution.py:257
  15.6 8.4 %copy-start.2 = (bf16[128,256]{1,0:T(8,128)(2,1)S(1)}, bf16[128,256]{1,0:T(8,128)(2,1)}, u32[]{:S(2)}) copy-start(bf16[128,256]{1,0:T(8,128)(2,1)} %get-tuple-element.14.refs_5_.refs_0_.total_ref) | copy-start | bytes 196612
  15.6 25.9 %copy-start = (bf16[16,128,256]{2,1,0:T(8,128)(2,1)S(1)}, bf16[16,128,256]{2,1,0:T(8,128)(2,1)}, u32[]{:S(2)}) copy-start(bf16[16,128,256]{2,1,0:T(8,128)(2,1)} %get-tuple-element.15.refs_6_.table_ref) | copy-start | bytes 3145732
  15.7 25.9 %copy-start.1 = (bf16[31,128,256]{2,1,0:T(8,128)(2,1)S(1)}, bf16[31,128,256]{2,1,0:T(8,128)(2,1)}, u32[]{:S(2)}) copy-start(bf16[31,128,256]{2,1,0:T(8,128)(2,1)} %get-tuple-element.21.left_ref) | copy-start | bytes 6094852
  15.7 25.9 %copy-start.5 = (s32[64]{0:T(128)S(1)}, s32[64]{0:T(128)}, u32[]{:S(2)}) copy-start(s32[64]{0:T(128)} %param.8) | copy-start | bytes 772
  15.7 25.9 %copy-start.6 = (f32[128]{0:T(128)S(1)}, f32[128]{0:T(128)}, u32[]{:S(2)}) copy-start(f32[128]{0:T(128)} %param.9) | copy-start | bytes 1540
  15.7 8.3 %collective-permute-start.2 = (bf16[128,256]{1,0:T(8,128)(2,1)}, bf16[128,256]{1,0:T(8,128)(2,1)S(1)}, u32[]{:S(2)}, u32[]{:S(2)}) collective-permute-start(bf16[128,256]{1,0:T(8,128)(2,1)} %get-tuple-element.14.refs_5_.refs_0_.total_ref), channel_id=1, source_target_pairs={{3,0},{0,1},{1,2},{2,3},{7,4},{4,5},{5,6},{6,7},{11,8},{8,9},{9,10... | collective-permute-start | bytes 196616 | tf_op jit(solution)/shard_map/ppermute | solution.py:280
  16.1 7.9 %collective-permute-start.1 = (bf16[128,256]{1,0:T(8,128)(2,1)}, bf16[128,256]{1,0:T(8,128)(2,1)S(1)}, u32[]{:S(2)}, u32[]{:S(2)}) collective-permute-start(bf16[128,256]{1,0:T(8,128)(2,1)} %get-tuple-element.14.refs_5_.refs_0_.total_ref), channel_id=1, source_target_pairs={{2,0},{3,1},{0,2},{1,3},{6,4},{7,5},{4,6},{5,7},{10,8},{11,9},{8,1... | collective-permute-start | bytes 196616 | tf_op jit(solution)/shard_map/ppermute | solution.py:280
  17.7 6.3 %collective-permute-start = (bf16[128,256]{1,0:T(8,128)(2,1)}, bf16[128,256]{1,0:T(8,128)(2,1)S(1)}, u32[]{:S(2)}, u32[]{:S(2)}) collective-permute-start(bf16[128,256]{1,0:T(8,128)(2,1)} %get-tuple-element.14.refs_5_.refs_0_.total_ref), channel_id=1, source_target_pairs={{1,0},{2,1},{3,2},{0,3},{5,4},{6,5},{7,6},{4,7},{9,8},{10,9},{11,1... | collective-permute-start | bytes 196616 | tf_op jit(solution)/shard_map/ppermute | solution.py:280
  24.0 0.7 %copy-start.4 = (f32[8,128]{1,0:T(8,128)S(1)}, f32[8,128]{1,0:T(8,128)}, u32[]{:S(2)}) copy-start(f32[8,128]{1,0:T(8,128)} %get-tuple-element.17.shift_ref) | copy-start | bytes 12292
  25.2 16.3 %collective-permute-start.4 = (bf16[128,256]{1,0:T(8,128)(2,1)S(1)}, bf16[128,256]{1,0:T(8,128)(2,1)S(1)}, u32[]{:S(2)}, u32[]{:S(2)}) collective-permute-start(bf16[128,256]{1,0:T(8,128)(2,1)S(1)} %get-tuple-element.22), channel_id=1, source_target_pairs={{0,8},{1,9},{2,10},{3,11},{4,12},{5,13},{6,14},{7,15},{16,24},{17,... | collective-permute-start | bytes 196616 | tf_op jit(solution)/shard_map/ppermute | solution.py:300
  29.1 12.4 %collective-permute-start.3 = (bf16[128,256]{1,0:T(8,128)(2,1)S(1)}, bf16[128,256]{1,0:T(8,128)(2,1)S(1)}, u32[]{:S(2)}, u32[]{:S(2)}) collective-permute-start(bf16[128,256]{1,0:T(8,128)(2,1)S(1)} %get-tuple-element.22), channel_id=1, source_target_pairs={{0,4},{1,5},{2,6},{3,7},{4,8},{5,9},{6,10},{7,11},{8,12},{9,13},{1... | collective-permute-start | bytes 196616 | tf_op jit(solution)/shard_map/ppermute | solution.py:300
  41.6 0.8 %copy-start.3 = (f32[64,128]{1,0:T(8,128)S(1)}, f32[64,128]{1,0:T(8,128)}, u32[]{:S(2)}) copy-start(f32[64,128]{1,0:T(8,128)} %get-tuple-element.20.lefts_ref) | copy-start | bytes 98308

commit v3 on v2

--- a/solution.py
+++ b/solution.py
@@ -10,7 +10,7 @@
 F32 = jnp.float32
 BF16 = jnp.bfloat16
 MIB = 1 << 20
-BIG, SMALL = 60, 2
+BIG, ROOMY, SMALL = 60, 52, 2
 NT = (((1,), (1,)), ((), ()))
 VMEM = pl.BlockSpec(memory_space=pltpu.VMEM)
 SMEM = pl.BlockSpec(memory_space=pltpu.SMEM)
@@ -143,7 +143,7 @@
 
 
 def local_kernel(pos_ref, levels_ref, *refs):
-    hbm, (lefts_ref, shift_ref), (drive_ref, sems), vmem = refs[:8], refs[8:10], refs[10:12], refs[12:]
+    hbm, (lefts_ref, own_ref), (drive_ref, sems), vmem = refs[:8], refs[8:10], refs[10:12], refs[12:]
     x_ref, mode_ref, weight_ref, gain_ref, init_ref, total_ref, table_ref, right_ref = vmem
     segments, steps, width = x_ref.shape
     n = gain_ref.shape[0]
@@ -176,50 +176,63 @@
         states = later
     lefts_ref[pl.ds(at, 1), :] = states[0][:1]
     first = jnp.where(pos_ref[0] == 0, row(init_ref, 0), 0.0)
-    shift_ref[...] = states[0] + vm(first, total_ref[...])
-
-
-def group_kernel(size, pos_ref, shift_ref, *refs):
-    maps = refs[:size]
-    prefix_ref, whole_ref, sent_ref, all_ref = refs[size:]
-    n = whole_ref.shape[0]
-    position = pos_ref[0]
-    member = position % size
+    total = total_ref[...]
+    own_ref[pl.ds(0, n), :] = total
+    own_ref[pl.ds(n, 16), :] = rows16(states[0] + vm(first, total))
+
+
+def rows16(vec):
+    high = vec.astype(BF16).astype(F32)
+    both = jnp.concatenate([high, vec - high], axis=1)
+    return jnp.concatenate([both, both], axis=0).astype(BF16)
+
+
+def rows8(rows):
+    both = rows.astype(F32)
+    n = rows.shape[1] // 2
+    return both[:8, :n] + both[:8, n:]
+
+
+def group_kernel(size, pos_ref, *refs):
+    blocks = refs[:size]
+    prefix_ref, before_ref, mine_ref, shift_ref, all_ref = refs[size:]
+    n = prefix_ref.shape[0]
+    member = pos_ref[0] % size
     for r in range(size):
-        all_ref[(member + r) % size] = maps[r][...]
+        all_ref[(member + r) % size] = blocks[r][...]
+
+    def block(q):
+        return all_ref[q, :n, :], rows8(all_ref[q, n:, :])
+
     rows, cols = (lax.broadcasted_iota(jnp.int32, (n, n), d) for d in (0, 1))
-    sent_ref[...] = jnp.zeros_like(sent_ref)
-    prefix = pair((rows == cols).astype(F32))
-    run, vec = all_ref[0], shift_ref[...]
+    prefix, before = pair((rows == cols).astype(F32)), jnp.zeros((8, n), F32)
+    run, vec = block(0)
     for q in range(1, size):
-        prefix = jnp.where(member == q, run, prefix)
-        sent_ref[position - member + q] = jnp.where(member < q, vec, 0.0)[:1]
-        vec = jnp.where(member < q, vm(vec, all_ref[q]), vec)
-        run = pair(mm(run, all_ref[q]))
+        here = member == q
+        prefix, before = jnp.where(here, run, prefix), jnp.where(here, vec, before)
+        step, shift = block(q)
+        vec = vm(vec, step) + shift
+        run = pair(mm(run, step))
     prefix_ref[...] = prefix
-    whole_ref[...] = run
-    last = position - member + size
-    for d in range(size, sent_ref.shape[0]):
-        @pl.when(d >= last)
-        def _(d=d):
-            sent_ref[d] = vec[:1]
-
-
-def final_kernel(size, pos_ref, levels_ref, got_ref, init_ref, prefix_ref, total_ref, lefts_ref, left_ref, table_ref, *refs):
-    wholes, (out_ref, sums_ref) = refs[:-2], refs[-2:]
+    before_ref[...] = before
+    mine_ref[pl.ds(0, n), :] = run
+    mine_ref[pl.ds(n, 16), :] = rows16(vec)
+    shift_ref[...] = rows16(vec)
+
+
+def final_kernel(size, pos_ref, levels_ref, init_ref, prefix_ref, before_ref, total_ref, lefts_ref, left_ref, table_ref, *refs):
+    got, out_ref = refs[:-1], refs[-1]
     steps, n = lefts_ref.shape
-    groups = got_ref.shape[0] // size
     position = pos_ref[0]
     group = position // size
-    for g in range(groups):
-        sums_ref[g] = jnp.broadcast_to(jnp.sum(got_ref[pl.ds(g * size, size)], axis=0), (8, n))
     state = jnp.zeros((8, n), F32)
-    for r in range(groups - 1, 0, -1):
-        if r <= len(wholes):
-            state = vm(state, wholes[r - 1][...])
-        state += jnp.where(group >= r, sums_ref[jnp.maximum(group - r, 0)], 0.0)
+    for r in range(len(got), 0, -1):
+        rows = got[r - 1].shape[0]
+        if rows > 16:
+            state = jnp.where(group > r, vm(state, got[r - 1][pl.ds(0, n), :]), 0.0)
+        state += jnp.where(group >= r, rows8(got[r - 1][pl.ds(rows - 16, 16), :]), 0.0)
     first = jnp.where(position == 0, row(init_ref, 0), 0.0)
-    state = vm(state, prefix_ref[...]) + sums_ref[group] + first
+    state = vm(state, prefix_ref[...]) + before_ref[...] + first
     out_ref[pl.ds(steps - 1, 1), :] = (vm(state, total_ref[...]) + row(lefts_ref, steps - 1))[:1]
     levels = steps.bit_length() - 1
     starts = [state]
@@ -265,7 +278,7 @@
     maps = shape((pairs, n, 2 * n), BF16)
     one_map = shape((n, 2 * n), BF16)
     left, right, table, total = call(
-        functools.partial(tree_kernel, steps), "tree_of_maps", BIG, 2 * steps * n**3 * 4, 8 * MIB,
+        functools.partial(tree_kernel, steps), "tree_of_maps", ROOMY, 2 * steps * n**3 * 4, 8 * MIB,
         out_shape=[maps, maps, shape((kinds, n, 2 * n), BF16), one_map],
         in_specs=[SMEM, HBM],
         out_specs=[HBM, HBM, HBM, VMEM],
@@ -276,39 +289,38 @@
     while count % (2 * size) == 0 and 4 * size * size <= count:
         size *= 2
     groups = count // size
-    members = [
-        lax.ppermute(total, "tm", [(j // size * size + (j + r) % size, j) for j in range(count)])
-        for r in range(1, size)
-    ]
+    block = shape((n + 16, 2 * n), BF16)
     inputs = (x, mode, weight, gain, initial_state, total, table, right)
-    lefts, shift = call(
-        local_kernel, "local_states", BIG, 1 << 27, 6 * MIB,
-        out_shape=[shape((steps, n), F32), shape((8, n), F32)],
+    lefts, own = call(
+        local_kernel, "local_states", ROOMY, 1 << 27, 6 * MIB,
+        out_shape=[shape((steps, n), F32), block],
         in_specs=[SMEM, SMEM] + [HBM] * 8,
         out_specs=[VMEM] * 2,
         scratch_shapes=[pltpu.VMEM((steps, n), F32), dma((9,))] + [pltpu.VMEM(a.shape, a.dtype) for a in inputs],
     )(position, levels, *inputs)
 
-    prefix, whole, sent = call(
+    others = [
+        lax.ppermute(own, "tm", [(j // size * size + (j + r) % size, j) for j in range(count)])
+        for r in range(1, size)
+    ]
+    prefix, before, mine, shift = call(
         functools.partial(group_kernel, size), "group_maps", SMALL, 1 << 24, MIB,
-        out_shape=[one_map, one_map, shape((count, 1, n), F32)],
-        in_specs=[SMEM] + [VMEM] * (1 + size),
-        out_specs=[VMEM] * 3,
-        scratch_shapes=[pltpu.VMEM((size, n, 2 * n), BF16)],
-    )(position, shift, total, *members)
-    wholes = [
-        lax.ppermute(whole, "tm", [(j, j + r * size) for j in range(count - r * size)])
-        for r in range(1, groups - 1)
+        out_shape=[one_map, shape((8, n), F32), block, shape((16, 2 * n), BF16)],
+        in_specs=[SMEM] + [VMEM] * size,
+        out_specs=[VMEM] * 4,
+        scratch_shapes=[pltpu.VMEM((size, n + 16, 2 * n), BF16)],
+    )(position, own, *others)
+    got = [
+        lax.ppermute(mine if r < groups - 1 else shift, "tm", [(j, (j + r * size) % count) for j in range(count)])
+        for r in range(1, groups)
     ]
-    got = lax.all_to_all(sent, "tm", split_axis=0, concat_axis=0, tiled=True)
 
     return call(
         functools.partial(final_kernel, size), "estimates", 6, 1 << 23, 5 * MIB,
         out_shape=shape((steps, n), F32),
-        in_specs=[SMEM, SMEM] + [VMEM] * (7 + len(wholes)),
+        in_specs=[SMEM, SMEM] + [VMEM] * (7 + len(got)),
         out_specs=VMEM,
-        scratch_shapes=[pltpu.VMEM((groups, 8, n), F32)],
-    )(position, levels, got, initial_state, prefix, total, lefts, left, table, *wholes)
+    )(position, levels, initial_state, prefix, before, total, lefts, left, table, *got)
 
 
 def solution(mesh):

time: 45.2 us -> 39.4 us (0.87)
  waiting for transfers between devices: 0.38 us -> 10.7 us
  blocking collectives: 8.98 us -> 0 us
  starting transfers between devices: 18.1 us -> 14.1 us
  Pallas kernels: 15.6 us -> 13.5 us
  local copies, waits for them, and re-layouts: 1.46 us -> 0.69 us
    all_to_all x1 -> x0, blocking collectives: 8.98 us -> none  [shards(): got = lax.all_to_all(sent, 'tm', split_axis=0, concat_axis=0, tiled=True)]
    ppermute x5 -> x6, waiting for transfers between devices: 0.01 us -> 7.06 us  [the longest x3 3.67 us: shards(): lax.ppermute(mine if r < groups - 1 else shift, 'tm', [(j, (j + r * size)...]
    ppermute x5 -> x6, starting transfers between devices: 10.7 us -> 6.77 us  [the longest x3 4.95 us: shards(): lax.ppermute(mine if r < groups - 1 else shift, 'tm', [(j, (j + r * size)...]
    all_to_all x1, waiting for transfers between devices: 0.37 us -> 3.61 us  [shards(): x = lax.all_to_all(turned, 'tm', split_axis=0, concat_axis=0, tiled=True)]
    pallas_call x2, Pallas kernels: 10.9 us -> 8.8 us  [the longest x1 5.72 us: shards(): call(functools.partial(tree_kernel, steps), 'tree_of_maps', ROOMY, 2 * st...]
    unnamed x14, local copies, waits for them, and re-layouts: 1.46 us -> 0.69 us
  transfers between devices with their start and end apart: 6 -> 7, of which waited for: 1 -> 5; matrix products, arithmetic and copies ran while one was open for 0% -> 0% of each run, Pallas kernels for 24% -> 15%
where the time goes in v3:
time: 39.4 us; the launch traced here: 39.1 us
  starting transfers between devices  14.1 us (36%)
  Pallas kernels  13.5 us (34%)
  waiting for transfers between devices  10.7 us (27%)
  local copies, waits for them, and re-layouts  0.69 us (2%)
    all_to_all x1, starting transfers between devices, shards(): x = lax.all_to_all(turned, 'tm', split_axis=0, concat_axis=0, tiled=True)  7.37 us
    pallas_call x1, Pallas kernels, shards(): call(functools.partial(tree_kernel, steps), 'tree_of_maps', ROOMY, 2 * st...  5.72 us
    ppermute x3, starting transfers between devices, shards(): lax.ppermute(mine if r < groups - 1 else shift, 'tm', [(j, (j + r * size)...  4.95 us
    ppermute x3, waiting for transfers between devices, shards(): lax.ppermute(mine if r < groups - 1 else shift, 'tm', [(j, (j + r * size)...  3.67 us
    all_to_all x1, waiting for transfers between devices, shards(): x = lax.all_to_all(turned, 'tm', split_axis=0, concat_axis=0, tiled=True)  3.61 us
    ppermute x3, waiting for transfers between devices, shards(): lax.ppermute(own, 'tm', [(j // size * size + (j + r) % size, j) for j in...  3.39 us
    pallas_call x1, Pallas kernels, shards(): call(local_kernel, 'local_states', ROOMY, 1 << 27, 6 * MIB, out_shape=[sh...  3.08 us
    pallas_call x1, Pallas kernels, shards(): call(functools.partial(final_kernel, size), 'estimates', 6, 1 << 23, 5 *...  2.44 us
  transfers between devices with their start and end apart: 7, of which 5 were waited for; matrix products, arithmetic and copies ran while one was open for 0% of the time, Pallas kernels for 15%

profile of v3, /device:TPU:0, one launch (start us, length us, event | category | flops | bytes accessed | tf_op | source)
XLA Modules:
  0.0 39.1 jit_solution(11078045401028012451)
XLA Ops:
  0.0 1.8 %turn_frames.1 = bf16[1024,128]{1,0:T(8,128)(2,1)} custom-call(bf16[128,1024]{1,0:T(8,128)(2,1)} %frames_ref.1), custom_call_target="tpu_custom_call" | custom-call | bytes 1048576 | tf_op jit(solution)/shard_map/turn_frames/pallas_call | solution.py:263
  1.8 0.0 copy-start.5
  1.8 0.0 copy-start.6
  1.8 7.4 %all-to-all-start = ((bf16[16,64,128]{2,1,0:T(8,128)(2,1)}), bf16[16,64,128]{2,1,0:T(8,128)(2,1)S(1)}, u32[]{:S(2)}, u32[]{:S(2)}) async-start(bf16[16,64,128]{2,1,0:T(8,128)(2,1)} %bitcast.13), calls=%async_computation | async-start | bytes 524288 | tf_op jit(solution)/shard_map/all_to_all | solution.py:270
  9.2 0.0 copy-start.1
  9.2 0.0 copy-start.2
  9.2 0.0 copy-start.3
  9.2 0.0 copy-start.4
  9.2 0.7 %copy-done.4 = s32[64]{0:T(128)S(1)} copy-done((s32[64]{0:T(128)S(1)}, s32[64]{0:T(128)}, u32[]{:S(2)}) %copy-start.4) | copy-done | bytes 280
  9.9 5.7 %tree_of_maps.1 = (bf16[31,128,256]{2,1,0:T(8,128)(2,1)}, bf16[31,128,256]{2,1,0:T(8,128)(2,1)}, bf16[16,128,256]{2,1,0:T(8,128)(2,1)S(1)}, bf16[128,256]{1,0:T(8,128)(2,1)S(1)}) custom-call(s32[1,64]{1,0:T(1,128)S(1)} %bitcast.8, f32[16,128,128]{2,1,0:T(8,128)} %trans_ref.1), custom_call_target="tpu_custom_call" | custom-call | flops 1073741824 | bytes 8388608 | tf_op jit(solution)/shard_map/tree_of_maps/pallas_call | solution.py:280
  15.6 0.0 copy-start
  15.6 3.6 %all-to-all-done.refs_0_ = bf16[16,64,128]{2,1,0:T(8,128)(2,1)S(1)} async-done(((bf16[16,64,128]{2,1,0:T(8,128)(2,1)}), bf16[16,64,128]{2,1,0:T(8,128)(2,1)S(1)}, u32[]{:S(2)}, u32[]{:S(2)}) %all-to-all-start) | async-done | bytes 262176 | tf_op jit(solution)/shard_map/all_to_all | solution.py:270
  19.2 0.0 copy-done.5
  19.2 0.0 copy-done.6
  19.2 0.0 copy-done.1
  19.3 0.0 copy-done.2
  19.3 0.0 copy-done.3
  19.3 3.1 %local_states.1 = (f32[64,128]{1,0:T(8,128)S(1)}, bf16[144,256]{1,0:T(8,128)(2,1)S(1)}) custom-call(s32[1]{0:T(128)} %bitcast.pos_ref, s32[1,64]{1,0:T(1,128)S(1)} %bitcast.9, bf16[16,64,128]{2,1,0:T(8,128)(2,1)S(1)} %all-to-all-done.refs_0_, s32[16,128]{1,0:T(8,128)S(1)} %bitcast.6, bf16[16,128]{1,0:T(8,128)(2,1)S(1)} %bitcast.7, ...), custom_call_target="tpu_custom_call" | custom-call | flops 134217728 | bytes 6291456 | tf_op jit(solution)/shard_map/local_states/pallas_call | solution.py:294
  22.4 0.1 collective-permute-start.2
  22.4 0.5 %collective-permute-start.1 = (bf16[144,256]{1,0:T(8,128)(2,1)S(1)}, bf16[144,256]{1,0:T(8,128)(2,1)S(1)}, u32[]{:S(2)}, u32[]{:S(2)}) collective-permute-start(bf16[144,256]{1,0:T(8,128)(2,1)S(1)} %get-tuple-element.18.refs_0_), channel_id=1, source_target_pairs={{2,0},{3,1},{0,2},{1,3},{6,4},{7,5},{4,6},{5,7},{10,8},{11,9},{8,1... | collective-permute-start | bytes 221192 | tf_op jit(solution)/shard_map/ppermute | solution.py:303
  22.9 1.2 %collective-permute-start = (bf16[144,256]{1,0:T(8,128)(2,1)S(1)}, bf16[144,256]{1,0:T(8,128)(2,1)S(1)}, u32[]{:S(2)}, u32[]{:S(2)}) collective-permute-start(bf16[144,256]{1,0:T(8,128)(2,1)S(1)} %get-tuple-element.18.refs_0_), channel_id=1, source_target_pairs={{1,0},{2,1},{3,2},{0,3},{5,4},{6,5},{7,6},{4,7},{9,8},{10,9},{11,1... | collective-permute-start | bytes 221192 | tf_op jit(solution)/shard_map/ppermute | solution.py:303
  24.2 2.2 %collective-permute-done.2.refs_3_ = bf16[144,256]{1,0:T(8,128)(2,1)S(1)} collective-permute-done((bf16[144,256]{1,0:T(8,128)(2,1)S(1)}, bf16[144,256]{1,0:T(8,128)(2,1)S(1)}, u32[]{:S(2)}, u32[]{:S(2)}) %collective-permute-start.2) | collective-permute-done | bytes 73760 | tf_op jit(solution)/shard_map/ppermute | solution.py:303
  26.4 1.2 %collective-permute-done.1.refs_2_ = bf16[144,256]{1,0:T(8,128)(2,1)S(1)} collective-permute-done((bf16[144,256]{1,0:T(8,128)(2,1)S(1)}, bf16[144,256]{1,0:T(8,128)(2,1)S(1)}, u32[]{:S(2)}, u32[]{:S(2)}) %collective-permute-start.1) | collective-permute-done | bytes 73760 | tf_op jit(solution)/shard_map/ppermute | solution.py:303
  27.6 0.0 collective-permute-done.refs_1_
  27.6 0.4 %group_maps.1 = (bf16[128,256]{1,0:T(8,128)(2,1)S(1)}, f32[8,128]{1,0:T(8,128)S(1)}, bf16[144,256]{1,0:T(8,128)(2,1)S(1)}, bf16[16,256]{1,0:T(8,128)(2,1)S(1)}) custom-call(s32[1]{0:T(128)} %bitcast.pos_ref, bf16[144,256]{1,0:T(8,128)(2,1)S(1)} %get-tuple-element.18.refs_0_, bf16[144,256]{1,0:T(8,128)(2,1)S(1)} %collective-permute-done.refs_1_, ...), custom_call_target="tpu_custom_call" | custom-call | flops 16777216 | bytes 1048576 | tf_op jit(solution)/shard_map/group_maps/pallas_call | solution.py:306
  28.0 1.1 %collective-permute-start.4 = (bf16[144,256]{1,0:T(8,128)(2,1)S(1)}, bf16[144,256]{1,0:T(8,128)(2,1)S(1)}, u32[]{:S(2)}, u32[]{:S(2)}) collective-permute-start(bf16[144,256]{1,0:T(8,128)(2,1)S(1)} %get-tuple-element.23), channel_id=1, source_target_pairs={{0,8},{1,9},{2,10},{3,11},{4,12},{5,13},{6,14},{7,15},{8,0},{9,1},... | collective-permute-start | bytes 221192 | tf_op jit(solution)/shard_map/ppermute | solution.py:314
  29.2 0.8 %collective-permute-start.3 = (bf16[144,256]{1,0:T(8,128)(2,1)S(1)}, bf16[144,256]{1,0:T(8,128)(2,1)S(1)}, u32[]{:S(2)}, u32[]{:S(2)}) collective-permute-start(bf16[144,256]{1,0:T(8,128)(2,1)S(1)} %get-tuple-element.23), channel_id=1, source_target_pairs={{0,4},{1,5},{2,6},{3,7},{4,8},{5,9},{6,10},{7,11},{8,12},{9,13},{1... | collective-permute-start | bytes 221192 | tf_op jit(solution)/shard_map/ppermute | solution.py:314
  30.0 3.0 %collective-permute-start.5 = (bf16[16,256]{1,0:T(8,128)(2,1)S(1)}, bf16[16,256]{1,0:T(8,128)(2,1)S(1)}, u32[]{:S(2)}, u32[]{:S(2)}) collective-permute-start(bf16[16,256]{1,0:T(8,128)(2,1)S(1)} %get-tuple-element.24), channel_id=1, source_target_pairs={{0,12},{1,13},{2,14},{3,15},{4,0},{5,1},{6,2},{7,3},{8,4},{9,5},{1... | collective-permute-start | bytes 24584 | tf_op jit(solution)/shard_map/ppermute | solution.py:314
  33.0 1.4 %collective-permute-done.5.refs_2_ = bf16[16,256]{1,0:T(8,128)(2,1)S(1)} collective-permute-done((bf16[16,256]{1,0:T(8,128)(2,1)S(1)}, bf16[16,256]{1,0:T(8,128)(2,1)S(1)}, u32[]{:S(2)}, u32[]{:S(2)}) %collective-permute-start.5) | collective-permute-done | bytes 8224 | tf_op jit(solution)/shard_map/ppermute | solution.py:314
  34.4 2.3 %collective-permute-done.4.refs_1_ = bf16[144,256]{1,0:T(8,128)(2,1)S(1)} collective-permute-done((bf16[144,256]{1,0:T(8,128)(2,1)S(1)}, bf16[144,256]{1,0:T(8,128)(2,1)S(1)}, u32[]{:S(2)}, u32[]{:S(2)}) %collective-permute-start.4) | collective-permute-done | bytes 73760 | tf_op jit(solution)/shard_map/ppermute | solution.py:314
  36.7 0.0 collective-permute-done.3.refs_0_
  36.7 0.0 copy-done
  36.7 2.4 %estimates.1 = f32[64,128]{1,0:T(8,128)} custom-call(s32[1]{0:T(128)} %bitcast.pos_ref, s32[1,64]{1,0:T(1,128)S(1)} %bitcast.10, f32[1,128]{1,0:T(1,128)S(1)} %bitcast.12, bf16[128,256]{1,0:T(8,128)(2,1)S(1)} %get-tuple-element.19.prefix_ref, f32[8,128]{1,0:T(8,128)S(1)} %get-tuple-element.20.before_ref, ...), custom_call_target="tpu_custom_call" | custom-call | flops 8388608 | bytes 5242880 | tf_op jit(solution)/shard_map/estimates/pallas_call | solution.py:318
Async XLA Ops:
  1.8 17.5 %copy-start.5 = (s32[64]{0:T(128)S(1)}, s32[64]{0:T(128)}, u32[]{:S(2)}) copy-start(s32[64]{0:T(128)} %param.8) | copy-start | bytes 772
  1.8 17.4 %copy-start.6 = (f32[128]{0:T(128)S(1)}, f32[128]{0:T(128)}, u32[]{:S(2)}) copy-start(f32[128]{0:T(128)} %param.9) | copy-start | bytes 1540
  1.8 17.4 %all-to-all-start = ((bf16[16,64,128]{2,1,0:T(8,128)(2,1)}), bf16[16,64,128]{2,1,0:T(8,128)(2,1)S(1)}, u32[]{:S(2)}, u32[]{:S(2)}) async-start(bf16[16,64,128]{2,1,0:T(8,128)(2,1)} %bitcast.13), calls=%async_computation | async-start | bytes 524288 | tf_op jit(solution)/shard_map/all_to_all | solution.py:270
  9.2 10.1 %copy-start.1 = (bf16[128,128]{1,0:T(8,128)(2,1)S(1)}, bf16[128,128]{1,0:T(8,128)(2,1)}, u32[]{:S(2)}) copy-start(bf16[128,128]{1,0:T(8,128)(2,1)} %refs_3_.1) | copy-start | bytes 98308
  9.2 10.0 %copy-start.2 = (s32[2048]{0:T(1024)S(1)}, s32[2048]{0:T(1024)}, u32[]{:S(2)}) copy-start(s32[2048]{0:T(1024)} %param.12) | copy-start | bytes 24580
  9.2 10.0 %copy-start.3 = (bf16[2048]{0:T(1024)(128)(2,1)S(1)}, bf16[2048]{0:T(1024)(128)(2,1)}, u32[]{:S(2)}) copy-start(bf16[2048]{0:T(1024)(128)(2,1)} %param.13) | copy-start | bytes 12292
  9.2 0.7 %copy-start.4 = (s32[64]{0:T(128)S(1)}, s32[64]{0:T(128)}, u32[]{:S(2)}) copy-start(s32[64]{0:T(128)} %param.8) | copy-start | bytes 772
  15.6 21.0 %copy-start = (bf16[31,128,256]{2,1,0:T(8,128)(2,1)S(1)}, bf16[31,128,256]{2,1,0:T(8,128)(2,1)}, u32[]{:S(2)}) copy-start(bf16[31,128,256]{2,1,0:T(8,128)(2,1)} %get-tuple-element.22.left_ref) | copy-start | bytes 6094852
  22.4 4.0 %collective-permute-start.2 = (bf16[144,256]{1,0:T(8,128)(2,1)S(1)}, bf16[144,256]{1,0:T(8,128)(2,1)S(1)}, u32[]{:S(2)}, u32[]{:S(2)}) collective-permute-start(bf16[144,256]{1,0:T(8,128)(2,1)S(1)} %get-tuple-element.18.refs_0_), channel_id=1, source_target_pairs={{3,0},{0,1},{1,2},{2,3},{7,4},{4,5},{5,6},{6,7},{11,8},{8,9},{9,10... | collective-permute-start | bytes 221192 | tf_op jit(solution)/shard_map/ppermute | solution.py:303
  22.4 5.2 %collective-permute-start.1 = (bf16[144,256]{1,0:T(8,128)(2,1)S(1)}, bf16[144,256]{1,0:T(8,128)(2,1)S(1)}, u32[]{:S(2)}, u32[]{:S(2)}) collective-permute-start(bf16[144,256]{1,0:T(8,128)(2,1)S(1)} %get-tuple-element.18.refs_0_), channel_id=1, source_target_pairs={{2,0},{3,1},{0,2},{1,3},{6,4},{7,5},{4,6},{5,7},{10,8},{11,9},{8,1... | collective-permute-start | bytes 221192 | tf_op jit(solution)/shard_map/ppermute | solution.py:303
  22.9 4.6 %collective-permute-start = (bf16[144,256]{1,0:T(8,128)(2,1)S(1)}, bf16[144,256]{1,0:T(8,128)(2,1)S(1)}, u32[]{:S(2)}, u32[]{:S(2)}) collective-permute-start(bf16[144,256]{1,0:T(8,128)(2,1)S(1)} %get-tuple-element.18.refs_0_), channel_id=1, source_target_pairs={{1,0},{2,1},{3,2},{0,3},{5,4},{6,5},{7,6},{4,7},{9,8},{10,9},{11,1... | collective-permute-start | bytes 221192 | tf_op jit(solution)/shard_map/ppermute | solution.py:303
  28.0 8.6 %collective-permute-start.4 = (bf16[144,256]{1,0:T(8,128)(2,1)S(1)}, bf16[144,256]{1,0:T(8,128)(2,1)S(1)}, u32[]{:S(2)}, u32[]{:S(2)}) collective-permute-start(bf16[144,256]{1,0:T(8,128)(2,1)S(1)} %get-tuple-element.23), channel_id=1, source_target_pairs={{0,8},{1,9},{2,10},{3,11},{4,12},{5,13},{6,14},{7,15},{8,0},{9,1},... | collective-permute-start | bytes 221192 | tf_op jit(solution)/shard_map/ppermute | solution.py:314
  29.2 7.5 %collective-permute-start.3 = (bf16[144,256]{1,0:T(8,128)(2,1)S(1)}, bf16[144,256]{1,0:T(8,128)(2,1)S(1)}, u32[]{:S(2)}, u32[]{:S(2)}) collective-permute-start(bf16[144,256]{1,0:T(8,128)(2,1)S(1)} %get-tuple-element.23), channel_id=1, source_target_pairs={{0,4},{1,5},{2,6},{3,7},{4,8},{5,9},{6,10},{7,11},{8,12},{9,13},{1... | collective-permute-start | bytes 221192 | tf_op jit(solution)/shard_map/ppermute | solution.py:314
  30.0 4.4 %collective-permute-start.5 = (bf16[16,256]{1,0:T(8,128)(2,1)S(1)}, bf16[16,256]{1,0:T(8,128)(2,1)S(1)}, u32[]{:S(2)}, u32[]{:S(2)}) collective-permute-start(bf16[16,256]{1,0:T(8,128)(2,1)S(1)} %get-tuple-element.24), channel_id=1, source_target_pairs={{0,12},{1,13},{2,14},{3,15},{4,0},{5,1},{6,2},{7,3},{8,4},{9,5},{1... | collective-permute-start | bytes 24584 | tf_op jit(solution)/shard_map/ppermute | solution.py:314

commit v4 on v2

v4 whole, which is shorter than its diff:
```python
import functools

import jax
import jax.numpy as jnp
from jax import lax
from jax.experimental import pallas as pl
from jax.experimental.pallas import tpu as pltpu
from jax.sharding import PartitionSpec as P

F32 = jnp.float32
BF16 = jnp.bfloat16
MIB = 1 << 20
NT = (((1,), (1,)), ((), ()))
VMEM = pl.BlockSpec(memory_space=pltpu.VMEM)
SMEM = pl.BlockSpec(memory_space=pltpu.SMEM)
HBM = pl.BlockSpec(memory_space=pltpu.HBM)
shape = jax.ShapeDtypeStruct


def hbm(x):
    return pltpu.with_memory_space_constraint(x, pltpu.HBM)


def call(kernel, name, mib, flops, moved, **kw):
    return pl.pallas_call(
        kernel,
        name=name,
        compiler_params=pltpu.CompilerParams(vmem_limit_bytes=mib * MIB),
        cost_estimate=pl.CostEstimate(flops=flops, bytes_accessed=moved, transcendentals=0),
        **kw,
    )


def pair(x):
    high = x.astype(BF16)
    mid = (x - high.astype(F32)).astype(BF16)
    return jnp.concatenate([high, mid], axis=1)


def mm(left, right):
    n = right.shape[0]
    out = jnp.dot(left, jnp.concatenate([right, right], axis=0), preferred_element_type=F32)
    return out[:, :n] + out[:, n:]


def vm(vec, mat):
    high = vec.astype(BF16).astype(F32)
    rows = jnp.concatenate([high, vec - high], axis=0).astype(BF16)
    out = jnp.dot(rows, mat, preferred_element_type=F32)
    n = vec.shape[1]
    out = out[:, :n] + out[:, n:]
    return out[:8] + out[8:]


def row(ref, t):
    return jnp.broadcast_to(ref[pl.ds(t, 1), :], (8, ref.shape[1]))


def front_kernel(cuts, trans_ref, *refs):
    turn = len(refs) > 3
    if turn:
        frames_ref, table_ref, turned_ref, trans, frames, turned, sems = refs
        width = frames.shape[1] // cuts
        parts = [pl.ds(k * width, width) for k in range(cuts)]
        ins = [
            pltpu.make_async_copy(frames_ref.at[:, part], frames.at[:, part], sems.at[k])
            for k, part in enumerate(parts)
        ]
        outs = [
            pltpu.make_async_copy(turned.at[part], turned_ref.at[part], sems.at[cuts + k])
            for k, part in enumerate(parts)
        ]
        for copy in ins:
            copy.start()
    else:
        table_ref, trans, sems = refs
    kinds = trans.shape[0]
    few = kinds // 4
    maps = [
        pltpu.make_async_copy(trans_ref.at[pl.ds(k * few, few)], trans.at[pl.ds(k * few, few)], sems.at[2 * cuts + k])
        for k in range(4)
    ]
    for copy in maps:
        copy.start()
    if turn:
        for k in range(cuts):
            ins[k].wait()
            turned[parts[k], :] = frames[:, parts[k]].T
            outs[k].start()
    for k in range(4):
        maps[k].wait()
        for q in range(k * few, (k + 1) * few):
            table_ref[q] = pair(trans[q].T)
    if turn:
        for copy in outs:
            copy.wait()


def tree_kernel(steps, levels_ref, table_ref, left_hbm, right_hbm, total_ref, left_ref, right_ref, sems):
    base = steps // 4

    def first(t):
        return mm(table_ref[levels_ref[0, t]], table_ref[levels_ref[0, t + 1]])

    def node(k):
        return mm(left_ref[k], right_ref[k])

    def first_pairs(ks):
        made = [(first(4 * k), first(4 * k + 2)) for k in ks]
        for k, (a, b) in zip(ks, made):
            left_ref[k] = pair(a)
            right_ref[k] = pair(b)

    def later_pairs(ks):
        made = [(node(2 * (k - base)), node(2 * (k - base) + 1)) for k in ks]
        for k, (a, b) in zip(ks, made):
            left_ref[k] = pair(a)
            right_ref[k] = pair(b)

    def run(fn, start, count):
        if count <= 4:
            fn(list(range(start, start + count)))
            return

        def body(i, c):
            fn([start + 4 * i + k for k in range(4)])
            return c

        lax.fori_loop(0, count // 4, body, 0)

    copies = []

    def store(start, count):
        for ref, hbm in ((right_ref, right_hbm), (left_ref, left_hbm)):
            part = pl.ds(start, count)
            copies.append(pltpu.make_async_copy(ref.at[part], hbm.at[part], sems.at[len(copies)]))
            copies[-1].start()

    run(first_pairs, 0, base)
    store(0, base)
    run(later_pairs, base, base // 2)
    store(base, base // 2)
    count, start = base // 4, base + base // 2
    while count >= 1:
        run(later_pairs, start, count)
        start += count
        count //= 2
    store(base + base // 2, base // 2 - 1)
    total_ref[...] = pair(node(start - 1))
    for copy in copies:
        copy.wait()


def local_kernel(pos_ref, levels_ref, x_ref, mode_ref, weight_ref, gain_ref, init_ref, table_ref, maps_ref, right_hbm, lefts_ref, sent_ref, drive_ref, right_ref, sems):
    segments, steps, width = x_ref.shape
    n = gain_ref.shape[0]
    base = steps // 4
    copies = [
        pltpu.make_async_copy(right_hbm.at[pl.ds(a, b)], right_ref.at[pl.ds(a, b)], sems.at[i])
        for i, (a, b) in enumerate([(0, base), (base, base - 1)])
    ]
    for copy in copies:
        copy.start()
    channel = lax.broadcasted_iota(jnp.int32, (n, width), 0)
    measured = jnp.zeros((steps, n), F32)
    for k in range(segments):
        weight = jnp.broadcast_to(weight_ref[pl.ds(k, 1), :].astype(F32), (n, width))
        projector = jnp.where(mode_ref[pl.ds(k, 1), :] == channel, weight, 0.0).astype(BF16)
        measured += lax.dot_general(x_ref[k], projector, NT, preferred_element_type=F32)
    drive_ref[...] = lax.dot_general(measured.astype(BF16), gain_ref[...], NT, preferred_element_type=F32)

    states = [row(drive_ref, t) for t in range(steps)]
    at, offset = 0, 0
    for level in range(steps.bit_length() - 1):
        if level in (1, 2):
            copies[level - 1].wait()
        later = []
        for i in range(len(states) // 2):
            mat = table_ref[levels_ref[0, 2 * i + 1]] if level == 0 else right_ref[offset + i]
            lefts_ref[pl.ds(at + i, 1), :] = states[2 * i][:1]
            later.append(vm(states[2 * i], mat) + states[2 * i + 1])
        at += len(later)
        if level > 0:
            offset += len(later)
        states = later
    lefts_ref[pl.ds(at, 1), :] = states[0][:1]
    position, size = pos_ref[0], maps_ref.shape[0]
    member = position % size
    start = position - member
    first = jnp.where(position == 0, row(init_ref, 0), 0.0)
    shift = states[0] + vm(first, maps_ref[member])
    sent_ref[...] = jnp.zeros_like(sent_ref)
    for q in range(1, size):
        sent_ref[start + q] = jnp.where(member < q, shift, 0.0)[:1]
        shift = jnp.where(member < q, vm(shift, maps_ref[q]), shift)
    for d in range(size, sent_ref.shape[0]):
        sent_ref[d] = jnp.where(d >= start + size, shift[:1], sent_ref[d])


def group_kernel(size, pos_ref, *refs):
    blocks = refs[:size]
    all_ref, prefix_ref, whole_ref = refs[size:]
    n = whole_ref.shape[0]
    member = pos_ref[0] % size
    for r in range(size):
        all_ref[member ^ r] = blocks[r][...]
    rows, cols = (lax.broadcasted_iota(jnp.int32, (n, n), d) for d in (0, 1))
    prefix = pair((rows == cols).astype(F32))
    run = all_ref[0]
    for q in range(1, size):
        prefix = jnp.where(member == q, run, prefix)
        run = pair(mm(run, all_ref[q]))
    prefix_ref[...] = prefix
    whole_ref[...] = run


def final_kernel(size, pos_ref, levels_ref, got_ref, init_ref, prefix_ref, total_ref, lefts_ref, left_ref, table_ref, *refs):
    wholes, (out_ref, sums_ref) = refs[:-2], refs[-2:]
    steps, n = lefts_ref.shape
    groups = got_ref.shape[0] // size
    position = pos_ref[0]
    group = position // size
    for g in range(groups):
        sums_ref[g] = jnp.broadcast_to(jnp.sum(got_ref[pl.ds(g * size, size)], axis=0), (8, n))
    state = jnp.zeros((8, n), F32)
    for r in range(groups - 1, 0, -1):
        if r <= len(wholes):
            state = jnp.where(group > r, vm(state, wholes[r - 1][...]), 0.0)
        state += jnp.where(group >= r, sums_ref[jnp.maximum(group - r, 0)], 0.0)
    first = jnp.where(position == 0, row(init_ref, 0), 0.0)
    state = vm(state, prefix_ref[...]) + sums_ref[group] + first
    out_ref[pl.ds(steps - 1, 1), :] = (vm(state, total_ref[...]) + row(lefts_ref, steps - 1))[:1]
    levels = steps.bit_length() - 1
    starts = [state]
    sizes = [steps >> (level + 1) for level in range(levels)]
    for level in reversed(range(levels)):
        at, offset = sum(sizes[:level]), sum(sizes[1:level])
        later = []
        for i, x in enumerate(starts):
            mat = table_ref[levels_ref[0, 2 * i]] if level == 0 else left_ref[offset + i]
            later += [x, vm(x, mat) + row(lefts_ref, at + i)]
        starts = later
    for t in range(1, steps):
        out_ref[pl.ds(t - 1, 1), :] = starts[t][:1]


def shards(count, frames, levels, initial_state, transitions, gain, pixel_mode, pixel_weight):
    n = gain.shape[0]
    kinds = transitions.shape[0]
    pixels, length = frames.shape
    steps = length // count
    position = lax.axis_index("tm").astype(jnp.int32)[None]
    initial_state = initial_state[None]
    levels = levels[None]
    pairs = steps // 2 - 1
    dma = pltpu.SemaphoreType.DMA

    one_map = shape((n, 2 * n), BF16)
    table_shape = shape((kinds, n, 2 * n), BF16)
    cuts = 4
    trans_vmem = pltpu.VMEM(transitions.shape, F32)
    front = functools.partial(front_kernel, cuts)
    if pixels % 128 == 0 and length % (128 * cuts) == 0:
        table, turned = call(
            front, "front", 5, 0, 4 * MIB,
            out_shape=[table_shape, pltpu.HBM((length, pixels), BF16)],
            in_specs=[HBM, HBM],
            out_specs=[VMEM, HBM],
            scratch_shapes=[trans_vmem, pltpu.VMEM(frames.shape, BF16), pltpu.VMEM((length, pixels), BF16), dma((2 * cuts + 4,))],
        )(hbm(transitions), hbm(frames))
        turned = turned.reshape(count, steps, pixels)
        x = lax.all_to_all(turned, "tm", split_axis=0, concat_axis=0, tiled=True)
    else:
        table = call(
            front, "front", 5, 0, 4 * MIB,
            out_shape=table_shape,
            in_specs=[HBM],
            out_specs=VMEM,
            scratch_shapes=[trans_vmem, dma((2 * cuts + 4,))],
        )(hbm(transitions))
        x = lax.all_to_all(frames, "tm", split_axis=1, concat_axis=0, tiled=True).T[None]
    mode = pixel_mode.reshape(x.shape[0], x.shape[2])
    weight = pixel_weight.reshape(x.shape[0], x.shape[2])

    tree = pltpu.VMEM((pairs, n, 2 * n), BF16)
    maps = pltpu.HBM((pairs, n, 2 * n), BF16)
    left, right, total = call(
        functools.partial(tree_kernel, steps), "tree_of_maps", 8, 2 * steps * n**3 * 4, 8 * MIB,
        out_shape=[maps, maps, one_map],
        in_specs=[SMEM, VMEM],
        out_specs=[HBM, HBM, VMEM],
        scratch_shapes=[tree, tree, dma((6,))],
    )(levels, table)

    size = 1
    while count % (2 * size) == 0 and 4 * size * size <= count:
        size *= 2
    groups = count // size

    members = [lax.ppermute(total, "tm", [(j, j ^ r) for j in range(count)]) for r in range(1, size)]
    group_maps, prefix, whole = call(
        functools.partial(group_kernel, size), "group_maps", 2, 1 << 24, MIB,
        out_shape=[shape((size, n, 2 * n), BF16), one_map, one_map],
        in_specs=[SMEM] + [VMEM] * size,
        out_specs=[VMEM] * 3,
    )(position, total, *members)
    wholes = [
        lax.ppermute(whole, "tm", [(j, (j + r * size) % count) for j in range(count)]) for r in range(1, groups - 1)
    ]

    lefts, sent = call(
        local_kernel, "local_states", 8, 1 << 27, 6 * MIB,
        out_shape=[shape((steps, n), F32), shape((count, 1, n), F32)],
        in_specs=[SMEM, SMEM] + [VMEM] * 7 + [HBM],
        out_specs=[VMEM] * 2,
        scratch_shapes=[pltpu.VMEM((steps, n), F32), tree, dma((2,))],
    )(position, levels, x, mode, weight, gain, initial_state, table, group_maps, hbm(right))
    got = lax.all_to_all(sent, "tm", split_axis=0, concat_axis=0, tiled=True)

    return call(
        functools.partial(final_kernel, size), "estimates", 6, 1 << 23, 5 * MIB,
        out_shape=shape((steps, n), F32),
        in_specs=[SMEM, SMEM] + [VMEM] * (7 + len(wholes)),
        out_specs=VMEM,
        scratch_shapes=[pltpu.VMEM((groups, 8, n), F32)],
    )(position, levels, got, initial_state, prefix, total, lefts, left, table, *wholes)


def solution(mesh):
    in_specs = (P("tm", "parts"), P(("parts", "tm")), P("parts"), P(), P(), P(), P())
    out_specs = P(("parts", "tm"), None)
    return jax.shard_map(
        functools.partial(shards, mesh.shape["tm"]),
        mesh=mesh,
        in_specs=in_specs,
        out_specs=out_specs,
        check_vma=False,
    )
```

time: 45.2 us -> 51.9 us (1.15)
  waiting for transfers between devices: 0.38 us -> 10.8 us
  blocking collectives: 8.98 us -> 0 us
  local copies, waits for them, and re-layouts: 1.46 us -> 7.21 us
    all_to_all x1 -> x0, blocking collectives: 8.98 us -> none  [shards(): got = lax.all_to_all(sent, 'tm', split_axis=0, concat_axis=0, tiled=True)]
    all_to_all x0 -> x1, waiting for transfers between devices: none -> 6.38 us  [shards(): got = lax.all_to_all(sent, 'tm', split_axis=0, concat_axis=0, tiled=True)]
    unnamed x14 -> x28, local copies, waits for them, and re-layouts: 1.46 us -> 7.21 us
    ppermute x5, starting transfers between devices: 10.7 us -> 5.74 us  [the longest x2 3.61 us: shards(): lax.ppermute(whole, 'tm', [(j, (j + r * size) % count) for j in range(cou...]
    all_to_all x0 -> x1, starting transfers between devices: none -> 4.62 us  [shards(): got = lax.all_to_all(sent, 'tm', split_axis=0, concat_axis=0, tiled=True)]
    ppermute x5, waiting for transfers between devices: 0.01 us -> 4.44 us  [the longest x3 4.44 us: shards(): lax.ppermute(total, 'tm', [(j, j ^ r) for j in range(count)])]
    pallas_call x4, Pallas kernels: 13.2 us -> 12.6 us  [the longest x1 4.75 us: shards(): call(local_kernel, 'local_states', 8, 1 << 27, 6 * MIB, out_shape=[shape(...]
  transfers between devices with their start and end apart: 6 -> 7, of which waited for: 1 -> 3; matrix products, arithmetic and copies ran while one was open for 0% -> 0% of each run, Pallas kernels for 24% -> 21%
where the time goes in v4:
time: 51.9 us; the launch traced here: 51.2 us
  starting transfers between devices  17.7 us (34%)
  Pallas kernels  15.4 us (30%)
  waiting for transfers between devices  10.8 us (21%)
  local copies, waits for them, and re-layouts  7.21 us (14%)
    all_to_all x1, starting transfers between devices, shards(): x = lax.all_to_all(turned, 'tm', split_axis=0, concat_axis=0, tiled=True)  7.37 us
    unnamed x28, local copies, waits for them, and re-layouts  7.21 us
    all_to_all x1, waiting for transfers between devices, shards(): got = lax.all_to_all(sent, 'tm', split_axis=0, concat_axis=0, tiled=True)  6.38 us
    pallas_call x1, Pallas kernels, shards(): call(local_kernel, 'local_states', 8, 1 << 27, 6 * MIB, out_shape=[shape(...  4.75 us
    all_to_all x1, starting transfers between devices, shards(): got = lax.all_to_all(sent, 'tm', split_axis=0, concat_axis=0, tiled=True)  4.62 us
    ppermute x3, waiting for transfers between devices, shards(): lax.ppermute(total, 'tm', [(j, j ^ r) for j in range(count)])  4.44 us
    pallas_call x1, Pallas kernels, shards(): call(functools.partial(tree_kernel, steps), 'tree_of_maps', 8, 2 * steps...  4.08 us
    ppermute x2, starting transfers between devices, shards(): lax.ppermute(whole, 'tm', [(j, (j + r * size) % count) for j in range(cou...  3.61 us
  transfers between devices with their start and end apart: 7, of which 3 were waited for; matrix products, arithmetic and copies ran while one was open for 0% of the time, Pallas kernels for 21%

profile of v4, /device:TPU:0, one launch (start us, length us, event | category | flops | bytes accessed | tf_op | source)
XLA Modules:
  0.0 51.2 jit_solution(5437605885595862778)
XLA Ops:
  0.0 1.9 %front.1 = (bf16[16,128,256]{2,1,0:T(8,128)(2,1)S(1)}, bf16[1024,128]{1,0:T(8,128)(2,1)}) custom-call(f32[16,128,128]{2,1,0:T(8,128)} %trans_ref.1, bf16[128,1024]{1,0:T(8,128)(2,1)} %refs_0_.1), custom_call_target="tpu_custom_call" | custom-call | bytes 4194304 | tf_op jit(solution)/shard_map/front/pallas_call | solution.py:264
  1.9 7.4 %all-to-all-start = ((bf16[16,64,128]{2,1,0:T(8,128)(2,1)}), bf16[16,64,128]{2,1,0:T(8,128)(2,1)S(1)}, u32[]{:S(2)}, u32[]{:S(2)}) async-start(bf16[16,64,128]{2,1,0:T(8,128)(2,1)} %bitcast.13), calls=%async_computation | async-start | bytes 524288 | tf_op jit(solution)/shard_map/all_to_all | solution.py:272
  9.2 0.0 copy-start.10
  9.3 0.6 %copy-done.10 = s32[64]{0:T(128)S(1)} copy-done((s32[64]{0:T(128)S(1)}, s32[64]{0:T(128)}, u32[]{:S(2)}) %copy-start.10) | copy-done | bytes 280
  9.9 0.0 copy-start.8
  9.9 0.0 copy-start.9
  9.9 0.0 copy-start.11
  9.9 4.1 %tree_of_maps.1 = (bf16[31,128,256]{2,1,0:T(8,128)(2,1)}, bf16[31,128,256]{2,1,0:T(8,128)(2,1)}, bf16[128,256]{1,0:T(8,128)(2,1)S(1)}) custom-call(s32[1,64]{1,0:T(1,128)S(1)} %bitcast.8, bf16[16,128,256]{2,1,0:T(8,128)(2,1)S(1)} %get-tuple-element.16.table_ref), custom_call_target="tpu_custom_call" | custom-call | flops 1073741824 | bytes 8388608 | tf_op jit(solution)/shard_map/tree_of_maps/pallas_call | solution.py:287
  14.0 0.0 copy-start
  14.0 1.8 %collective-permute-start.2 = (bf16[128,256]{1,0:T(8,128)(2,1)S(1)}, bf16[128,256]{1,0:T(8,128)(2,1)S(1)}, u32[]{:S(2)}, u32[]{:S(2)}) collective-permute-start(bf16[128,256]{1,0:T(8,128)(2,1)S(1)} %get-tuple-element.17.refs_0_.total_ref), channel_id=1, source_target_pairs={{0,3},{1,2},{2,1},{3,0},{4,7},{5,6},{6,5},{7,4},{8,11},{9,10},{10,... | collective-permute-start | bytes 196616 | tf_op jit(solution)/shard_map/ppermute | solution.py:300
  15.8 0.4 collective-permute-start.1
  16.1 0.0 collective-permute-start
  16.1 2.1 %collective-permute-done.2.refs_3_ = bf16[128,256]{1,0:T(8,128)(2,1)S(1)} collective-permute-done((bf16[128,256]{1,0:T(8,128)(2,1)S(1)}, bf16[128,256]{1,0:T(8,128)(2,1)S(1)}, u32[]{:S(2)}, u32[]{:S(2)}) %collective-permute-start.2) | collective-permute-done | bytes 65568 | tf_op jit(solution)/shard_map/ppermute | solution.py:300
  18.3 2.3 %collective-permute-done.1.refs_2_ = bf16[128,256]{1,0:T(8,128)(2,1)S(1)} collective-permute-done((bf16[128,256]{1,0:T(8,128)(2,1)S(1)}, bf16[128,256]{1,0:T(8,128)(2,1)S(1)}, u32[]{:S(2)}, u32[]{:S(2)}) %collective-permute-start.1) | collective-permute-done | bytes 65568 | tf_op jit(solution)/shard_map/ppermute | solution.py:300
  20.6 0.0 copy-start.3
  20.6 0.6 %copy-done.3 = bf16[128,256]{1,0:T(8,128)(2,1)} copy-done((bf16[128,256]{1,0:T(8,128)(2,1)}, bf16[128,256]{1,0:T(8,128)(2,1)S(1)}, u32[]{:S(2)}) %copy-start.3) | copy-done | bytes 65560
  21.2 0.0 collective-permute-done.refs_1_
  21.2 0.0 copy-start.4
  21.2 0.8 %copy-done.4 = bf16[128,256]{1,0:T(8,128)(2,1)S(1)} copy-done((bf16[128,256]{1,0:T(8,128)(2,1)S(1)}, bf16[128,256]{1,0:T(8,128)(2,1)}, u32[]{:S(2)}) %copy-start.4) | copy-done | bytes 65560
  22.0 1.9 %group_maps.1 = (bf16[4,128,256]{2,1,0:T(8,128)(2,1)S(1)}, bf16[128,256]{1,0:T(8,128)(2,1)S(1)}, bf16[128,256]{1,0:T(8,128)(2,1)}) custom-call(s32[1]{0:T(128)} %bitcast.pos_ref, bf16[128,256]{1,0:T(8,128)(2,1)S(1)} %get-tuple-element.17.refs_0_.total_ref, bf16[128,256]{1,0:T(8,128)(2,1)} %collective-permute-done.refs_1_, bf16[128,256]{1,0:T(8,128)(2,1)S(1)} %copy-done.4, ...), custom_call_target="tpu_custom_call" | custom-call | flops 16777216 | bytes 1048576 | tf_op jit(solution)/shard_map/group_maps/pallas_call | solution.py:301
  24.0 0.0 copy-start.1
  24.0 0.7 %copy-done.1 = bf16[4,128,256]{2,1,0:T(8,128)(2,1)} copy-done((bf16[4,128,256]{2,1,0:T(8,128)(2,1)}, bf16[4,128,256]{2,1,0:T(8,128)(2,1)S(1)}, u32[]{:S(2)}) %copy-start.1) | copy-done | bytes 262168
  24.7 2.4 %collective-permute-start.4 = (bf16[128,256]{1,0:T(8,128)(2,1)}, bf16[128,256]{1,0:T(8,128)(2,1)S(1)}, u32[]{:S(2)}, u32[]{:S(2)}) collective-permute-start(bf16[128,256]{1,0:T(8,128)(2,1)} %get-tuple-element.24), channel_id=1, source_target_pairs={{0,8},{1,9},{2,10},{3,11},{4,12},{5,13},{6,14},{7,15},{8,0},{9,1},... | collective-permute-start | bytes 196616 | tf_op jit(solution)/shard_map/ppermute | solution.py:308
  27.1 1.2 %collective-permute-start.3 = (bf16[128,256]{1,0:T(8,128)(2,1)}, bf16[128,256]{1,0:T(8,128)(2,1)}, u32[]{:S(2)}, u32[]{:S(2)}) collective-permute-start(bf16[128,256]{1,0:T(8,128)(2,1)} %get-tuple-element.24), channel_id=1, source_target_pairs={{0,4},{1,5},{2,6},{3,7},{4,8},{5,9},{6,10},{7,11},{8,12},{9,13},{1... | collective-permute-start | bytes 196616 | tf_op jit(solution)/shard_map/ppermute | solution.py:308
  28.3 0.0 all-to-all-done.x_ref
  28.3 0.0 copy-done.8
  28.3 0.0 copy-done.9
  28.3 0.0 copy-done.11
  28.3 0.0 copy-start.2
  28.3 0.9 %copy-done.2 = bf16[4,128,256]{2,1,0:T(8,128)(2,1)S(1)} copy-done((bf16[4,128,256]{2,1,0:T(8,128)(2,1)S(1)}, bf16[4,128,256]{2,1,0:T(8,128)(2,1)}, u32[]{:S(2)}) %copy-start.2) | copy-done | bytes 262168
  29.2 0.0 copy-start.5
  29.2 0.8 %copy-done.5 = bf16[128,128]{1,0:T(8,128)(2,1)S(1)} copy-done((bf16[128,128]{1,0:T(8,128)(2,1)S(1)}, bf16[128,128]{1,0:T(8,128)(2,1)}, u32[]{:S(2)}) %copy-start.5) | copy-done | bytes 32792
  30.0 0.0 copy-start.12
  30.0 0.7 %copy-done.12 = f32[128]{0:T(128)S(1)} copy-done((f32[128]{0:T(128)S(1)}, f32[128]{0:T(128)}, u32[]{:S(2)}) %copy-start.12) | copy-done | bytes 536
  30.7 4.7 %local_states.1 = (f32[64,128]{1,0:T(8,128)S(1)}, f32[16,1,128]{2,1,0:T(1,128)}) custom-call(s32[1]{0:T(128)} %bitcast.pos_ref, s32[1,64]{1,0:T(1,128)S(1)} %bitcast.9, bf16[16,64,128]{2,1,0:T(8,128)(2,1)S(1)} %all-to-all-done.x_ref, s32[16,128]{1,0:T(8,128)S(1)} %bitcast.6, bf16[16,128]{1,0:T(8,128)(2,1)S(1)} %bitcast.7, bf16[128,128]{1,0:T(8,128)(2,1)S(1)} %copy-done.5, ...), custom_call_target="tpu_custom_call" | custom-call | flops 134217728 | bytes 6291456 | tf_op jit(solution)/shard_map/local_states/pallas_call | solution.py:311
  35.4 0.0 copy-start.6
  35.4 0.6 %copy-done.6 = f32[64,128]{1,0:T(8,128)} copy-done((f32[64,128]{1,0:T(8,128)}, f32[64,128]{1,0:T(8,128)S(1)}, u32[]{:S(2)}) %copy-start.6) | copy-done | bytes 32792
  36.0 4.6 %all-to-all-start.1 = ((f32[16,1,128]{2,1,0:T(1,128)}), f32[16,1,128]{2,1,0:T(1,128)S(1)}, u32[]{:S(2)}, u32[]{:S(2)}) async-start(f32[16,1,128]{2,1,0:T(1,128)} %get-tuple-element.20), calls=%async_computation.1 | async-start | bytes 16384 | tf_op jit(solution)/shard_map/all_to_all | solution.py:318
  40.7 0.0 collective-permute-done.4.refs_1_
  40.7 0.0 collective-permute-done.3.refs_0_
  40.7 6.4 %all-to-all-done.1.got_ref = f32[16,1,128]{2,1,0:T(1,128)S(1)} async-done(((f32[16,1,128]{2,1,0:T(1,128)}), f32[16,1,128]{2,1,0:T(1,128)S(1)}, u32[]{:S(2)}, u32[]{:S(2)}) %all-to-all-start.1) | async-done | bytes 8224 | tf_op jit(solution)/shard_map/all_to_all | solution.py:318
  47.1 0.0 copy-done
  47.1 0.0 copy-start.7
  47.1 0.8 %copy-done.7 = f32[64,128]{1,0:T(8,128)S(1)} copy-done((f32[64,128]{1,0:T(8,128)S(1)}, f32[64,128]{1,0:T(8,128)}, u32[]{:S(2)}) %copy-start.7) | copy-done | bytes 32792
  47.8 0.0 copy-start.13
  47.8 0.7 %copy-done.13 = f32[128]{0:T(128)S(1)} copy-done((f32[128]{0:T(128)S(1)}, f32[128]{0:T(128)}, u32[]{:S(2)}) %copy-start.13) | copy-done | bytes 536
  48.5 2.8 %estimates.1 = f32[64,128]{1,0:T(8,128)} custom-call(s32[1]{0:T(128)} %bitcast.pos_ref, s32[1,64]{1,0:T(1,128)S(1)} %bitcast.10, f32[16,1,128]{2,1,0:T(1,128)S(1)} %all-to-all-done.1.got_ref, f32[1,128]{1,0:T(1,128)S(1)} %bitcast.12, bf16[128,256]{1,0:T(8,128)(2,1)S(1)} %get-tuple-element.21.prefix_ref, ...), custom_call_target="tpu_custom_call" | custom-call | flops 8388608 | bytes 5242880 | tf_op jit(solution)/shard_map/estimates/pallas_call | solution.py:320
Async XLA Ops:
  1.9 26.4 %all-to-all-start = ((bf16[16,64,128]{2,1,0:T(8,128)(2,1)}), bf16[16,64,128]{2,1,0:T(8,128)(2,1)S(1)}, u32[]{:S(2)}, u32[]{:S(2)}) async-start(bf16[16,64,128]{2,1,0:T(8,128)(2,1)} %bitcast.13), calls=%async_computation | async-start | bytes 524288 | tf_op jit(solution)/shard_map/all_to_all | solution.py:272
  9.2 0.7 %copy-start.10 = (s32[64]{0:T(128)S(1)}, s32[64]{0:T(128)}, u32[]{:S(2)}) copy-start(s32[64]{0:T(128)} %param.8) | copy-start | bytes 772
  9.9 18.4 %copy-start.8 = (s32[2048]{0:T(1024)S(1)}, s32[2048]{0:T(1024)}, u32[]{:S(2)}) copy-start(s32[2048]{0:T(1024)} %param.12) | copy-start | bytes 24580
  9.9 18.4 %copy-start.9 = (bf16[2048]{0:T(1024)(128)(2,1)S(1)}, bf16[2048]{0:T(1024)(128)(2,1)}, u32[]{:S(2)}) copy-start(bf16[2048]{0:T(1024)(128)(2,1)} %param.13) | copy-start | bytes 12292
  9.9 18.4 %copy-start.11 = (s32[64]{0:T(128)S(1)}, s32[64]{0:T(128)}, u32[]{:S(2)}) copy-start(s32[64]{0:T(128)} %param.8) | copy-start | bytes 772
  14.0 33.1 %copy-start = (bf16[31,128,256]{2,1,0:T(8,128)(2,1)S(1)}, bf16[31,128,256]{2,1,0:T(8,128)(2,1)}, u32[]{:S(2)}) copy-start(bf16[31,128,256]{2,1,0:T(8,128)(2,1)} %get-tuple-element.23.left_ref) | copy-start | bytes 6094852
  14.0 4.3 %collective-permute-start.2 = (bf16[128,256]{1,0:T(8,128)(2,1)S(1)}, bf16[128,256]{1,0:T(8,128)(2,1)S(1)}, u32[]{:S(2)}, u32[]{:S(2)}) collective-permute-start(bf16[128,256]{1,0:T(8,128)(2,1)S(1)} %get-tuple-element.17.refs_0_.total_ref), channel_id=1, source_target_pairs={{0,3},{1,2},{2,1},{3,0},{4,7},{5,6},{6,5},{7,4},{8,11},{9,10},{10,... | collective-permute-start | bytes 196616 | tf_op jit(solution)/shard_map/ppermute | solution.py:300
  15.8 4.8 %collective-permute-start.1 = (bf16[128,256]{1,0:T(8,128)(2,1)S(1)}, bf16[128,256]{1,0:T(8,128)(2,1)S(1)}, u32[]{:S(2)}, u32[]{:S(2)}) collective-permute-start(bf16[128,256]{1,0:T(8,128)(2,1)S(1)} %get-tuple-element.17.refs_0_.total_ref), channel_id=1, source_target_pairs={{0,2},{1,3},{2,0},{3,1},{4,6},{5,7},{6,4},{7,5},{8,10},{9,11},{10,... | collective-permute-start | bytes 196616 | tf_op jit(solution)/shard_map/ppermute | solution.py:300
  16.1 5.1 %collective-permute-start = (bf16[128,256]{1,0:T(8,128)(2,1)S(1)}, bf16[128,256]{1,0:T(8,128)(2,1)}, u32[]{:S(2)}, u32[]{:S(2)}) collective-permute-start(bf16[128,256]{1,0:T(8,128)(2,1)S(1)} %get-tuple-element.17.refs_0_.total_ref), channel_id=1, source_target_pairs={{0,1},{1,0},{2,3},{3,2},{4,5},{5,4},{6,7},{7,6},{8,9},{9,8},{10,11... | collective-permute-start | bytes 196616 | tf_op jit(solution)/shard_map/ppermute | solution.py:300
  20.6 0.6 %copy-start.3 = (bf16[128,256]{1,0:T(8,128)(2,1)}, bf16[128,256]{1,0:T(8,128)(2,1)S(1)}, u32[]{:S(2)}) copy-start(bf16[128,256]{1,0:T(8,128)(2,1)S(1)} %collective-permute-done.1.refs_2_) | copy-start | bytes 196612
  21.2 0.8 %copy-start.4 = (bf16[128,256]{1,0:T(8,128)(2,1)S(1)}, bf16[128,256]{1,0:T(8,128)(2,1)}, u32[]{:S(2)}) copy-start(bf16[128,256]{1,0:T(8,128)(2,1)} %copy-done.3) | copy-start | bytes 196612
  24.0 0.7 %copy-start.1 = (bf16[4,128,256]{2,1,0:T(8,128)(2,1)}, bf16[4,128,256]{2,1,0:T(8,128)(2,1)S(1)}, u32[]{:S(2)}) copy-start(bf16[4,128,256]{2,1,0:T(8,128)(2,1)S(1)} %get-tuple-element.18.maps_ref) | copy-start | bytes 786436
  24.7 16.0 %collective-permute-start.4 = (bf16[128,256]{1,0:T(8,128)(2,1)}, bf16[128,256]{1,0:T(8,128)(2,1)S(1)}, u32[]{:S(2)}, u32[]{:S(2)}) collective-permute-start(bf16[128,256]{1,0:T(8,128)(2,1)} %get-tuple-element.24), channel_id=1, source_target_pairs={{0,8},{1,9},{2,10},{3,11},{4,12},{5,13},{6,14},{7,15},{8,0},{9,1},... | collective-permute-start | bytes 196616 | tf_op jit(solution)/shard_map/ppermute | solution.py:308
  27.1 13.6 %collective-permute-start.3 = (bf16[128,256]{1,0:T(8,128)(2,1)}, bf16[128,256]{1,0:T(8,128)(2,1)}, u32[]{:S(2)}, u32[]{:S(2)}) collective-permute-start(bf16[128,256]{1,0:T(8,128)(2,1)} %get-tuple-element.24), channel_id=1, source_target_pairs={{0,4},{1,5},{2,6},{3,7},{4,8},{5,9},{6,10},{7,11},{8,12},{9,13},{1... | collective-permute-start | bytes 196616 | tf_op jit(solution)/shard_map/ppermute | solution.py:308
  28.3 1.0 %copy-start.2 = (bf16[4,128,256]{2,1,0:T(8,128)(2,1)S(1)}, bf16[4,128,256]{2,1,0:T(8,128)(2,1)}, u32[]{:S(2)}) copy-start(bf16[4,128,256]{2,1,0:T(8,128)(2,1)} %copy-done.1) | copy-start | bytes 786436
  29.2 0.8 %copy-start.5 = (bf16[128,128]{1,0:T(8,128)(2,1)S(1)}, bf16[128,128]{1,0:T(8,128)(2,1)}, u32[]{:S(2)}) copy-start(bf16[128,128]{1,0:T(8,128)(2,1)} %gain_ref.1) | copy-start | bytes 98308
  30.0 0.7 %copy-start.12 = (f32[128]{0:T(128)S(1)}, f32[128]{0:T(128)}, u32[]{:S(2)}) copy-start(f32[128]{0:T(128)} %param.9) | copy-start | bytes 1540
  35.4 0.6 %copy-start.6 = (f32[64,128]{1,0:T(8,128)}, f32[64,128]{1,0:T(8,128)S(1)}, u32[]{:S(2)}) copy-start(f32[64,128]{1,0:T(8,128)S(1)} %get-tuple-element.22.lefts_ref) | copy-start | bytes 98308
  36.0 11.0 %all-to-all-start.1 = ((f32[16,1,128]{2,1,0:T(1,128)}), f32[16,1,128]{2,1,0:T(1,128)S(1)}, u32[]{:S(2)}, u32[]{:S(2)}) async-start(f32[16,1,128]{2,1,0:T(1,128)} %get-tuple-element.20), calls=%async_computation.1 | async-start | bytes 16384 | tf_op jit(solution)/shard_map/all_to_all | solution.py:318
  47.1 0.8 %copy-start.7 = (f32[64,128]{1,0:T(8,128)S(1)}, f32[64,128]{1,0:T(8,128)}, u32[]{:S(2)}) copy-start(f32[64,128]{1,0:T(8,128)} %copy-done.6) | copy-start | bytes 98308
  47.8 0.7 %copy-start.13 = (f32[128]{0:T(128)S(1)}, f32[128]{0:T(128)}, u32[]{:S(2)}) copy-start(f32[128]{0:T(128)} %param.9) | copy-start | bytes 1540

commit v5 on v4

--- a/solution.py
+++ b/solution.py
@@ -56,10 +56,11 @@
     return jnp.broadcast_to(ref[pl.ds(t, 1), :], (8, ref.shape[1]))
 
 
-def front_kernel(cuts, trans_ref, *refs):
-    turn = len(refs) > 3
+def front_kernel(cuts, extra, trans_ref, *refs):
+    given, refs = refs[:extra], refs[extra:]
+    turn = len(refs) > extra + 3
     if turn:
-        frames_ref, table_ref, turned_ref, trans, frames, turned, sems = refs
+        frames_ref, table_ref, *moved, turned_ref, trans, frames, turned, sems = refs
         width = frames.shape[1] // cuts
         parts = [pl.ds(k * width, width) for k in range(cuts)]
         ins = [
@@ -73,14 +74,18 @@
         for copy in ins:
             copy.start()
     else:
-        table_ref, trans, sems = refs
+        table_ref, *moved, trans, sems = refs
+        outs = []
     kinds = trans.shape[0]
     few = kinds // 4
     maps = [
         pltpu.make_async_copy(trans_ref.at[pl.ds(k * few, few)], trans.at[pl.ds(k * few, few)], sems.at[2 * cuts + k])
         for k in range(4)
     ]
-    for copy in maps:
+    moves = [
+        pltpu.make_async_copy(a, b, sems.at[2 * cuts + 4 + k]) for k, (a, b) in enumerate(zip(given, moved))
+    ]
+    for copy in maps + moves:
         copy.start()
     if turn:
         for k in range(cuts):
@@ -91,12 +96,11 @@
         maps[k].wait()
         for q in range(k * few, (k + 1) * few):
             table_ref[q] = pair(trans[q].T)
-    if turn:
-        for copy in outs:
-            copy.wait()
-
-
-def tree_kernel(steps, levels_ref, table_ref, left_hbm, right_hbm, total_ref, left_ref, right_ref, sems):
+    for copy in moves + outs:
+        copy.wait()
+
+
+def tree_kernel(steps, levels_ref, table_ref, left_hbm, right_hbm, table_hbm, total_ref, left_ref, right_ref, sems):
     base = steps // 4
 
     def first(t):
@@ -128,7 +132,8 @@
 
         lax.fori_loop(0, count // 4, body, 0)
 
-    copies = []
+    copies = [pltpu.make_async_copy(table_ref, table_hbm, sems.at[0])]
+    copies[0].start()
 
     def store(start, count):
         for ref, hbm in ((right_ref, right_hbm), (left_ref, left_hbm)):
@@ -151,13 +156,14 @@
         copy.wait()
 
 
-def local_kernel(pos_ref, levels_ref, x_ref, mode_ref, weight_ref, gain_ref, init_ref, table_ref, maps_ref, right_hbm, lefts_ref, sent_ref, drive_ref, right_ref, sems):
+def local_kernel(pos_ref, levels_ref, x_ref, mode_ref, weight_ref, gain_ref, init_ref, total_ref, table_hbm, right_hbm, lefts_ref, shift_ref, drive_ref, table_ref, right_ref, sems):
     segments, steps, width = x_ref.shape
     n = gain_ref.shape[0]
     base = steps // 4
     copies = [
-        pltpu.make_async_copy(right_hbm.at[pl.ds(a, b)], right_ref.at[pl.ds(a, b)], sems.at[i])
-        for i, (a, b) in enumerate([(0, base), (base, base - 1)])
+        pltpu.make_async_copy(table_hbm, table_ref, sems.at[0]),
+        pltpu.make_async_copy(right_hbm.at[pl.ds(0, base)], right_ref.at[pl.ds(0, base)], sems.at[1]),
+        pltpu.make_async_copy(right_hbm.at[pl.ds(base, base - 1)], right_ref.at[pl.ds(base, base - 1)], sems.at[2]),
     ]
     for copy in copies:
         copy.start()
@@ -172,8 +178,8 @@
     states = [row(drive_ref, t) for t in range(steps)]
     at, offset = 0, 0
     for level in range(steps.bit_length() - 1):
-        if level in (1, 2):
-            copies[level - 1].wait()
+        if level < 3:
+            copies[level].wait()
         later = []
         for i in range(len(states) // 2):
             mat = table_ref[levels_ref[0, 2 * i + 1]] if level == 0 else right_ref[offset + i]
@@ -184,17 +190,8 @@
             offset += len(later)
         states = later
     lefts_ref[pl.ds(at, 1), :] = states[0][:1]
-    position, size = pos_ref[0], maps_ref.shape[0]
-    member = position % size
-    start = position - member
-    first = jnp.where(position == 0, row(init_ref, 0), 0.0)
-    shift = states[0] + vm(first, maps_ref[member])
-    sent_ref[...] = jnp.zeros_like(sent_ref)
-    for q in range(1, size):
-        sent_ref[start + q] = jnp.where(member < q, shift, 0.0)[:1]
-        shift = jnp.where(member < q, vm(shift, maps_ref[q]), shift)
-    for d in range(size, sent_ref.shape[0]):
-        sent_ref[d] = jnp.where(d >= start + size, shift[:1], sent_ref[d])
+    first = jnp.where(pos_ref[0] == 0, row(init_ref, 0), 0.0)
+    shift_ref[...] = states[0] + vm(first, total_ref[...])
 
 
 def group_kernel(size, pos_ref, *refs):
@@ -214,26 +211,44 @@
     whole_ref[...] = run
 
 
-def final_kernel(size, pos_ref, levels_ref, got_ref, init_ref, prefix_ref, total_ref, lefts_ref, left_ref, table_ref, *refs):
-    wholes, (out_ref, sums_ref) = refs[:-2], refs[-2:]
+def beside_kernel(size, pos_ref, all_ref, *refs):
+    shifts = refs[:size]
+    before_ref, whole_ref, held_ref = refs[size:]
+    member = pos_ref[0] % size
+    for r in range(size):
+        held_ref[member ^ r] = shifts[r][...]
+    run, before = held_ref[0], jnp.zeros(before_ref.shape, F32)
+    for q in range(1, size):
+        before = jnp.where(member == q, run, before)
+        run = vm(run, all_ref[q]) + held_ref[q]
+    before_ref[...] = before
+    whole_ref[...] = run
+
+
+def final_kernel(size, groups, pos_ref, levels_ref, init_ref, prefix_ref, before_ref, total_ref, lefts_ref, left_ref, table_hbm, *refs):
+    shifts, wholes = refs[: groups - 1], refs[groups - 1 : 2 * groups - 3]
+    out_ref, sums_ref, table_ref, sem = refs[2 * groups - 3 :]
+    copy = pltpu.make_async_copy(table_hbm, table_ref, sem)
+    copy.start()
     steps, n = lefts_ref.shape
-    groups = got_ref.shape[0] // size
     position = pos_ref[0]
     group = position // size
-    for g in range(groups):
-        sums_ref[g] = jnp.broadcast_to(jnp.sum(got_ref[pl.ds(g * size, size)], axis=0), (8, n))
+    for r in range(1, groups):
+        sums_ref[group ^ r] = shifts[r - 1][...]
     state = jnp.zeros((8, n), F32)
     for r in range(groups - 1, 0, -1):
-        if r <= len(wholes):
+        if r < groups - 1:
             state = jnp.where(group > r, vm(state, wholes[r - 1][...]), 0.0)
         state += jnp.where(group >= r, sums_ref[jnp.maximum(group - r, 0)], 0.0)
     first = jnp.where(position == 0, row(init_ref, 0), 0.0)
-    state = vm(state, prefix_ref[...]) + sums_ref[group] + first
+    state = vm(state, prefix_ref[...]) + before_ref[...] + first
     out_ref[pl.ds(steps - 1, 1), :] = (vm(state, total_ref[...]) + row(lefts_ref, steps - 1))[:1]
     levels = steps.bit_length() - 1
     starts = [state]
     sizes = [steps >> (level + 1) for level in range(levels)]
     for level in reversed(range(levels)):
+        if level == 0:
+            copy.wait()
         at, offset = sum(sizes[:level]), sum(sizes[1:level])
         later = []
         for i, x in enumerate(starts):
@@ -250,54 +265,70 @@
     pixels, length = frames.shape
     steps = length // count
     position = lax.axis_index("tm").astype(jnp.int32)[None]
-    initial_state = initial_state[None]
-    levels = levels[None]
     pairs = steps // 2 - 1
     dma = pltpu.SemaphoreType.DMA
-
     one_map = shape((n, 2 * n), BF16)
     table_shape = shape((kinds, n, 2 * n), BF16)
     cuts = 4
-    trans_vmem = pltpu.VMEM(transitions.shape, F32)
-    front = functools.partial(front_kernel, cuts)
-    if pixels % 128 == 0 and length % (128 * cuts) == 0:
-        table, turned = call(
-            front, "front", 5, 0, 4 * MIB,
-            out_shape=[table_shape, pltpu.HBM((length, pixels), BF16)],
-            in_specs=[HBM, HBM],
-            out_specs=[VMEM, HBM],
-            scratch_shapes=[trans_vmem, pltpu.VMEM(frames.shape, BF16), pltpu.VMEM((length, pixels), BF16), dma((2 * cuts + 4,))],
-        )(hbm(transitions), hbm(frames))
-        turned = turned.reshape(count, steps, pixels)
-        x = lax.all_to_all(turned, "tm", split_axis=0, concat_axis=0, tiled=True)
+    turn = pixels % 128 == 0 and length % (128 * cuts) == 0
+    segments = count if turn else 1
+    small = [
+        levels[None],
+        initial_state[None],
+        gain,
+        pixel_mode.reshape(segments, -1),
+        pixel_weight.reshape(segments, -1),
+    ]
+    given = [hbm(a) for a in [transitions] + small + [frames] * turn]
+    outs = [table_shape] + [shape(a.shape, a.dtype) for a in small]
+    buffers = [pltpu.VMEM(transitions.shape, F32)]
+    if turn:
+        outs.append(pltpu.HBM((length, pixels), BF16))
+        buffers += [pltpu.VMEM(frames.shape, BF16), pltpu.VMEM((length, pixels), BF16)]
+    table, levels, initial_state, gain, mode, weight, *turned = call(
+        functools.partial(front_kernel, cuts, len(small)), "front", 5, 0, 4 * MIB,
+        out_shape=outs,
+        in_specs=[HBM] * len(given),
+        out_specs=[VMEM] * (1 + len(small)) + [HBM] * turn,
+        scratch_shapes=buffers + [dma((2 * cuts + 4 + len(small),))],
+    )(*given)
+    if turn:
+        x = lax.all_to_all(turned[0].reshape(count, steps, pixels), "tm", split_axis=0, concat_axis=0, tiled=True)
     else:
-        table = call(
-            front, "front", 5, 0, 4 * MIB,
-            out_shape=table_shape,
-            in_specs=[HBM],
-            out_specs=VMEM,
-            scratch_shapes=[trans_vmem, dma((2 * cuts + 4,))],
-        )(hbm(transitions))
         x = lax.all_to_all(frames, "tm", split_axis=1, concat_axis=0, tiled=True).T[None]
-    mode = pixel_mode.reshape(x.shape[0], x.shape[2])
-    weight = pixel_weight.reshape(x.shape[0], x.shape[2])
 
     tree = pltpu.VMEM((pairs, n, 2 * n), BF16)
+    table_vmem = pltpu.VMEM(table_shape.shape, BF16)
     maps = pltpu.HBM((pairs, n, 2 * n), BF16)
-    left, right, total = call(
+    left, right, table, total = call(
         functools.partial(tree_kernel, steps), "tree_of_maps", 8, 2 * steps * n**3 * 4, 8 * MIB,
-        out_shape=[maps, maps, one_map],
+        out_shape=[maps, maps, pltpu.HBM(table_shape.shape, BF16), one_map],
         in_specs=[SMEM, VMEM],
-        out_specs=[HBM, HBM, VMEM],
-        scratch_shapes=[tree, tree, dma((6,))],
+        out_specs=[HBM, HBM, HBM, VMEM],
+        scratch_shapes=[tree, tree, dma((7,))],
     )(levels, table)
+    right, table = hbm(right), hbm(table)
 
     size = 1
     while count % (2 * size) == 0 and 4 * size * size <= count:
         size *= 2
     groups = count // size
 
-    members = [lax.ppermute(total, "tm", [(j, j ^ r) for j in range(count)]) for r in range(1, size)]
+    vector = shape((8, n), F32)
+
+    def swaps(x, step, times):
+        return [lax.ppermute(x, "tm", [(j, j ^ (r * step)) for j in range(count)]) for r in range(1, times)]
+
+    members = swaps(total, 1, size)
+    lefts, shift = call(
+        local_kernel, "local_states", 8, 1 << 27, 6 * MIB,
+        out_shape=[shape((steps, n), F32), vector],
+        in_specs=[SMEM, SMEM] + [VMEM] * 6 + [HBM] * 2,
+        out_specs=[VMEM] * 2,
+        scratch_shapes=[pltpu.VMEM((steps, n), F32), table_vmem, tree, dma((3,))],
+    )(position, levels, x, mode, weight, gain, initial_state, total, table, right)
+    shifts = swaps(shift, 1, size)
+
     group_maps, prefix, whole = call(
         functools.partial(group_kernel, size), "group_maps", 2, 1 << 24, MIB,
         out_shape=[shape((size, n, 2 * n), BF16), one_map, one_map],
@@ -307,23 +338,21 @@
     wholes = [
         lax.ppermute(whole, "tm", [(j, (j + r * size) % count) for j in range(count)]) for r in range(1, groups - 1)
     ]
-
-    lefts, sent = call(
-        local_kernel, "local_states", 8, 1 << 27, 6 * MIB,
-        out_shape=[shape((steps, n), F32), shape((count, 1, n), F32)],
-        in_specs=[SMEM, SMEM] + [VMEM] * 7 + [HBM],
+    before, carried = call(
+        functools.partial(beside_kernel, size), "group_states", 2, 1 << 20, MIB // 4,
+        out_shape=[vector, vector],
+        in_specs=[SMEM] + [VMEM] * (1 + size),
         out_specs=[VMEM] * 2,
-        scratch_shapes=[pltpu.VMEM((steps, n), F32), tree, dma((2,))],
-    )(position, levels, x, mode, weight, gain, initial_state, table, group_maps, hbm(right))
-    got = lax.all_to_all(sent, "tm", split_axis=0, concat_axis=0, tiled=True)
+        scratch_shapes=[pltpu.VMEM((size, 8, n), F32)],
+    )(position, group_maps, shift, *shifts)
 
     return call(
-        functools.partial(final_kernel, size), "estimates", 6, 1 << 23, 5 * MIB,
+        functools.partial(final_kernel, size, groups), "estimates", 6, 1 << 23, 5 * MIB,
         out_shape=shape((steps, n), F32),
-        in_specs=[SMEM, SMEM] + [VMEM] * (7 + len(wholes)),
+        in_specs=[SMEM, SMEM] + [VMEM] * 6 + [HBM] + [VMEM] * (2 * groups - 3),
         out_specs=VMEM,
-        scratch_shapes=[pltpu.VMEM((groups, 8, n), F32)],
-    )(position, levels, got, initial_state, prefix, total, lefts, left, table, *wholes)
+        scratch_shapes=[pltpu.VMEM((groups, 8, n), F32), table_vmem, dma(())],
+    )(position, levels, initial_state, prefix, before, total, lefts, left, table, *swaps(carried, size, groups), *wholes)
 
 
 def solution(mesh):

time: 51.9 us -> 43.3 us (0.83)
  local copies, waits for them, and re-layouts: 7.21 us -> 0.01 us
  Pallas kernels: 15.4 us -> 12.9 us
  starting transfers between devices: 17.7 us -> 19.3 us
    unnamed x28 -> x2, local copies, waits for them, and re-layouts: 7.21 us -> 0.01 us
    all_to_all x2 -> x1, waiting for transfers between devices: 6.38 us -> 0.01 us  [shards(): lax.all_to_all(turned[0].reshape(count, steps, pixels), 'tm', split_axis=...]
    ppermute x3 -> x9, waiting for transfers between devices: 4.44 us -> 10.8 us  [swaps(): lax.ppermute(x, 'tm', [(j, j ^ r * step) for j in range(count)])]
    ppermute x3 -> x9, starting transfers between devices: 2.13 us -> 8.48 us  [swaps(): lax.ppermute(x, 'tm', [(j, j ^ r * step) for j in range(count)])]
    all_to_all x2 -> x1, starting transfers between devices: 12 us -> 7.37 us  [shards(): lax.all_to_all(turned[0].reshape(count, steps, pixels), 'tm', split_axis=...]
    pallas_call x1, Pallas kernels: 4.75 us -> 3.21 us  [shards(): call(local_kernel, 'local_states', 8, 1 << 27, 6 * MIB, out_shape=[shape(...]
    pallas_call x1, Pallas kernels: 1.92 us -> 0.45 us  [shards(): call(functools.partial(group_kernel, size), 'group_maps', 2, 1 << 24, MIB...]
    pallas_call x2 -> x3, Pallas kernels: 4.62 us -> 5.09 us  [the longest x1 2.8 us: shards(): call(functools.partial(final_kernel, size, groups), 'estimates', 6, 1 <<...]
  transfers between devices with their start and end apart: 7 -> 12, of which waited for: 3 -> 6; matrix products, arithmetic and copies ran while one was open for 0% -> 0% of each run, Pallas kernels for 21% -> 19%
where the time goes in v5:
time: 43.3 us; the launch traced here: 43 us
  starting transfers between devices  19.3 us (45%)
  Pallas kernels  12.9 us (30%)
  waiting for transfers between devices  10.8 us (25%)
    ppermute x9, waiting for transfers between devices, swaps(): lax.ppermute(x, 'tm', [(j, j ^ r * step) for j in range(count)])  10.8 us
    ppermute x9, starting transfers between devices, swaps(): lax.ppermute(x, 'tm', [(j, j ^ r * step) for j in range(count)])  8.48 us
    all_to_all x1, starting transfers between devices, shards(): lax.all_to_all(turned[0].reshape(count, steps, pixels), 'tm', split_axis=...  7.37 us
    pallas_call x1, Pallas kernels, shards(): call(functools.partial(tree_kernel, steps), 'tree_of_maps', 8, 2 * steps...  4.12 us
    ppermute x2, starting transfers between devices, shards(): lax.ppermute(whole, 'tm', [(j, (j + r * size) % count) for j in range(cou...  3.47 us
    pallas_call x1, Pallas kernels, shards(): call(local_kernel, 'local_states', 8, 1 << 27, 6 * MIB, out_shape=[shape(...  3.21 us
    pallas_call x1, Pallas kernels, shards(): call(functools.partial(final_kernel, size, groups), 'estimates', 6, 1 <<...  2.8 us
    pallas_call x1, Pallas kernels, shards(): call(functools.partial(front_kernel, cuts, len(small)), 'front', 5, 0, 4...  1.91 us
  transfers between devices with their start and end apart: 12, of which 6 were waited for; matrix products, arithmetic and copies ran while one was open for 0% of the time, Pallas kernels for 19%

profile of v5, /device:TPU:0, one launch (start us, length us, event | category | flops | bytes accessed | tf_op | source)
XLA Modules:
  0.0 43.0 jit_solution(14545216463628807678)
XLA Ops:
  0.0 1.9 %front.1 = (bf16[16,128,256]{2,1,0:T(8,128)(2,1)S(1)}, s32[1,64]{1,0:T(1,128)S(1)}, f32[1,128]{1,0:T(1,128)S(1)}, bf16[128,128]{1,0:T(8,128)(2,1)S(1)}, s32[16,1...) custom-call(f32[16,128,128]{2,1,0:T(8,128)} %trans_ref.1, s32[1,64]{1,0:T(1,128)} %bitcast.9, ...), custom_call_target="tpu_custom_call" | custom-call | bytes 4194304 | tf_op jit(solution)/shard_map/front/pallas_call | solution.py:288
  1.9 7.4 %all-to-all-start = ((bf16[16,64,128]{2,1,0:T(8,128)(2,1)}), bf16[16,64,128]{2,1,0:T(8,128)(2,1)S(1)}, u32[]{:S(2)}, u32[]{:S(2)}) async-start(bf16[16,64,128]{2,1,0:T(8,128)(2,1)} %bitcast.6), calls=%async_computation | async-start | bytes 524288 | tf_op jit(solution)/shard_map/all_to_all | solution.py:296
  9.3 4.1 %tree_of_maps.1 = (bf16[31,128,256]{2,1,0:T(8,128)(2,1)}, bf16[31,128,256]{2,1,0:T(8,128)(2,1)}, bf16[16,128,256]{2,1,0:T(8,128)(2,1)}, bf16[128,256]{1,0:T(8,128)(2,1)S(1)}) custom-call(s32[1,64]{1,0:T(1,128)S(1)} %get-tuple-element.23.levels_ref, bf16[16,128,256]{2,1,0:T(8,128)(2,1)S(1)} %get-tuple-element.25.table_ref), custom_call_target="tpu_custom_call" | custom-call | flops 1073741824 | bytes 8388608 | tf_op jit(solution)/shard_map/tree_of_maps/pallas_call | solution.py:303
  13.4 0.0 copy-start
  13.4 0.5 %collective-permute-start = (bf16[128,256]{1,0:T(8,128)(2,1)S(1)}, bf16[128,256]{1,0:T(8,128)(2,1)S(1)}, u32[]{:S(2)}, u32[]{:S(2)}) collective-permute-start(bf16[128,256]{1,0:T(8,128)(2,1)S(1)} %get-tuple-element.26.refs_0_.total_ref), channel_id=1, source_target_pairs={{0,1},{1,0},{2,3},{3,2},{4,5},{5,4},{6,7},{7,6},{8,9},{9,8},{10,11... | collective-permute-start | bytes 196616 | tf_op jit(solution)/shard_map/ppermute | solution.py:320
  13.9 1.7 %collective-permute-start.1 = (bf16[128,256]{1,0:T(8,128)(2,1)S(1)}, bf16[128,256]{1,0:T(8,128)(2,1)S(1)}, u32[]{:S(2)}, u32[]{:S(2)}) collective-permute-start(bf16[128,256]{1,0:T(8,128)(2,1)S(1)} %get-tuple-element.26.refs_0_.total_ref), channel_id=1, source_target_pairs={{0,2},{1,3},{2,0},{3,1},{4,6},{5,7},{6,4},{7,5},{8,10},{9,11},{10,... | collective-permute-start | bytes 196616 | tf_op jit(solution)/shard_map/ppermute | solution.py:320
  15.6 0.0 collective-permute-start.2
  15.6 0.0 collective-permute-done.refs_1_
  15.6 2.8 %collective-permute-done.1.refs_2_ = bf16[128,256]{1,0:T(8,128)(2,1)S(1)} collective-permute-done((bf16[128,256]{1,0:T(8,128)(2,1)S(1)}, bf16[128,256]{1,0:T(8,128)(2,1)S(1)}, u32[]{:S(2)}, u32[]{:S(2)}) %collective-permute-start.1) | collective-permute-done | bytes 65568 | tf_op jit(solution)/shard_map/ppermute | solution.py:320
  18.4 1.9 %collective-permute-done.2.refs_3_ = bf16[128,256]{1,0:T(8,128)(2,1)S(1)} collective-permute-done((bf16[128,256]{1,0:T(8,128)(2,1)S(1)}, bf16[128,256]{1,0:T(8,128)(2,1)S(1)}, u32[]{:S(2)}, u32[]{:S(2)}) %collective-permute-start.2) | collective-permute-done | bytes 65568 | tf_op jit(solution)/shard_map/ppermute | solution.py:320
  20.3 0.4 %group_maps.1 = (bf16[4,128,256]{2,1,0:T(8,128)(2,1)S(1)}, bf16[128,256]{1,0:T(8,128)(2,1)S(1)}, bf16[128,256]{1,0:T(8,128)(2,1)S(1)}) custom-call(s32[1]{0:T(128)} %bitcast.pos_ref, bf16[128,256]{1,0:T(8,128)(2,1)S(1)} %get-tuple-element.26.refs_0_.total_ref, bf16[128,256]{1,0:T(8,128)(2,1)S(1)} %collective-permute-done.refs_1_, ...), custom_call_target="tpu_custom_call" | custom-call | flops 16777216 | bytes 1048576 | tf_op jit(solution)/shard_map/group_maps/pallas_call | solution.py:332
  20.8 2.2 %collective-permute-start.10 = (bf16[128,256]{1,0:T(8,128)(2,1)S(1)}, bf16[128,256]{1,0:T(8,128)(2,1)S(1)}, u32[]{:S(2)}, u32[]{:S(2)}) collective-permute-start(bf16[128,256]{1,0:T(8,128)(2,1)S(1)} %get-tuple-element.40), channel_id=1, source_target_pairs={{0,8},{1,9},{2,10},{3,11},{4,12},{5,13},{6,14},{7,15},{8,0},{9,1},... | collective-permute-start | bytes 196616 | tf_op jit(solution)/shard_map/ppermute | solution.py:339
  22.9 1.3 %collective-permute-start.9 = (bf16[128,256]{1,0:T(8,128)(2,1)S(1)}, bf16[128,256]{1,0:T(8,128)(2,1)S(1)}, u32[]{:S(2)}, u32[]{:S(2)}) collective-permute-start(bf16[128,256]{1,0:T(8,128)(2,1)S(1)} %get-tuple-element.40), channel_id=1, source_target_pairs={{0,4},{1,5},{2,6},{3,7},{4,8},{5,9},{6,10},{7,11},{8,12},{9,13},{1... | collective-permute-start | bytes 196616 | tf_op jit(solution)/shard_map/ppermute | solution.py:339
  24.2 0.0 all-to-all-done.x_ref
  24.2 3.2 %local_states.1 = (f32[64,128]{1,0:T(8,128)S(1)}, f32[8,128]{1,0:T(8,128)S(1)}) custom-call(s32[1]{0:T(128)} %bitcast.pos_ref, s32[1,64]{1,0:T(1,128)S(1)} %get-tuple-element.23.levels_ref, bf16[16,64,128]{2,1,0:T(8,128)(2,1)S(1)} %all-to-all-done.x_ref, s32[16,128]{1,0:T(8,128)S(1)} %get-tuple-element.30.mode_ref, ...), custom_call_target="tpu_custom_call" | custom-call | flops 134217728 | bytes 6291456 | tf_op jit(solution)/shard_map/local_states/pallas_call | solution.py:323
  27.4 0.1 collective-permute-start.3
  27.5 1.1 %collective-permute-start.4 = (f32[8,128]{1,0:T(8,128)S(1)}, f32[8,128]{1,0:T(8,128)S(1)}, u32[]{:S(2)}, u32[]{:S(2)}) collective-permute-start(f32[8,128]{1,0:T(8,128)S(1)} %get-tuple-element.35.refs_0_), channel_id=1, source_target_pairs={{0,2},{1,3},{2,0},{3,1},{4,6},{5,7},{6,4},{7,5},{8,10},{9,11},{10,... | collective-permute-start | bytes 12296 | tf_op jit(solution)/shard_map/ppermute | solution.py:320
  28.6 0.7 %collective-permute-start.5 = (f32[8,128]{1,0:T(8,128)S(1)}, f32[8,128]{1,0:T(8,128)S(1)}, u32[]{:S(2)}, u32[]{:S(2)}) collective-permute-start(f32[8,128]{1,0:T(8,128)S(1)} %get-tuple-element.35.refs_0_), channel_id=1, source_target_pairs={{0,3},{1,2},{2,1},{3,0},{4,7},{5,6},{6,5},{7,4},{8,11},{9,10},{10,... | collective-permute-start | bytes 12296 | tf_op jit(solution)/shard_map/ppermute | solution.py:320
  29.4 0.0 collective-permute-done.3.refs_1_
  29.4 1.8 %collective-permute-done.4.refs_2_ = f32[8,128]{1,0:T(8,128)S(1)} collective-permute-done((f32[8,128]{1,0:T(8,128)S(1)}, f32[8,128]{1,0:T(8,128)S(1)}, u32[]{:S(2)}, u32[]{:S(2)}) %collective-permute-start.4) | collective-permute-done | bytes 4128 | tf_op jit(solution)/shard_map/ppermute | solution.py:320
  31.2 0.5 %collective-permute-done.5.refs_3_ = f32[8,128]{1,0:T(8,128)S(1)} collective-permute-done((f32[8,128]{1,0:T(8,128)S(1)}, f32[8,128]{1,0:T(8,128)S(1)}, u32[]{:S(2)}, u32[]{:S(2)}) %collective-permute-start.5) | collective-permute-done | bytes 4128 | tf_op jit(solution)/shard_map/ppermute | solution.py:320
  31.7 0.4 group_states.1
  32.0 0.0 collective-permute-start.6
  32.1 2.7 %collective-permute-start.7 = (f32[8,128]{1,0:T(8,128)S(1)}, f32[8,128]{1,0:T(8,128)S(1)}, u32[]{:S(2)}, u32[]{:S(2)}) collective-permute-start(f32[8,128]{1,0:T(8,128)S(1)} %get-tuple-element.39), channel_id=1, source_target_pairs={{0,8},{1,9},{2,10},{3,11},{4,12},{5,13},{6,14},{7,15},{8,0},{9,1},... | collective-permute-start | bytes 12296 | tf_op jit(solution)/shard_map/ppermute | solution.py:320
  34.8 1.6 %collective-permute-start.8 = (f32[8,128]{1,0:T(8,128)S(1)}, f32[8,128]{1,0:T(8,128)S(1)}, u32[]{:S(2)}, u32[]{:S(2)}) collective-permute-start(f32[8,128]{1,0:T(8,128)S(1)} %get-tuple-element.39), channel_id=1, source_target_pairs={{0,12},{1,13},{2,14},{3,15},{4,8},{5,9},{6,10},{7,11},{8,4},{9,5},... | collective-permute-start | bytes 12296 | tf_op jit(solution)/shard_map/ppermute | solution.py:320
  36.4 0.0 collective-permute-done.10.refs_4_
  36.5 0.0 collective-permute-done.9.refs_3_
  36.5 0.0 collective-permute-done.6.refs_0_
  36.5 0.1 collective-permute-done.7.refs_1_
  36.6 3.6 %collective-permute-done.8.refs_2_ = f32[8,128]{1,0:T(8,128)S(1)} collective-permute-done((f32[8,128]{1,0:T(8,128)S(1)}, f32[8,128]{1,0:T(8,128)S(1)}, u32[]{:S(2)}, u32[]{:S(2)}) %collective-permute-start.8) | collective-permute-done | bytes 4128 | tf_op jit(solution)/shard_map/ppermute | solution.py:320
  40.2 0.0 copy-done
  40.2 2.8 %estimates.1 = f32[64,128]{1,0:T(8,128)} custom-call(s32[1]{0:T(128)} %bitcast.pos_ref, s32[1,64]{1,0:T(1,128)S(1)} %get-tuple-element.23.levels_ref, f32[1,128]{1,0:T(1,128)S(1)} %get-tuple-element.24.init_ref, bf16[128,256]{1,0:T(8,128)(2,1)S(1)} %get-tuple-element.27.prefix_ref, f32[8,128]{1,0:T(8,128)S(1)} %get-tuple-element.36.before_ref, ...), custom_call_target="tpu_custom_call" | custom-call | flops 8388608 | bytes 5242880 | tf_op jit(solution)/shard_map/estimates/pallas_call | solution.py:349
Async XLA Ops:
  1.9 22.3 %all-to-all-start = ((bf16[16,64,128]{2,1,0:T(8,128)(2,1)}), bf16[16,64,128]{2,1,0:T(8,128)(2,1)S(1)}, u32[]{:S(2)}, u32[]{:S(2)}) async-start(bf16[16,64,128]{2,1,0:T(8,128)(2,1)} %bitcast.6), calls=%async_computation | async-start | bytes 524288 | tf_op jit(solution)/shard_map/all_to_all | solution.py:296
  13.4 26.8 %copy-start = (bf16[31,128,256]{2,1,0:T(8,128)(2,1)S(1)}, bf16[31,128,256]{2,1,0:T(8,128)(2,1)}, u32[]{:S(2)}) copy-start(bf16[31,128,256]{2,1,0:T(8,128)(2,1)} %get-tuple-element.38.left_ref) | copy-start | bytes 6094852
  13.4 2.2 %collective-permute-start = (bf16[128,256]{1,0:T(8,128)(2,1)S(1)}, bf16[128,256]{1,0:T(8,128)(2,1)S(1)}, u32[]{:S(2)}, u32[]{:S(2)}) collective-permute-start(bf16[128,256]{1,0:T(8,128)(2,1)S(1)} %get-tuple-element.26.refs_0_.total_ref), channel_id=1, source_target_pairs={{0,1},{1,0},{2,3},{3,2},{4,5},{5,4},{6,7},{7,6},{8,9},{9,8},{10,11... | collective-permute-start | bytes 196616 | tf_op jit(solution)/shard_map/ppermute | solution.py:320
  13.9 4.5 %collective-permute-start.1 = (bf16[128,256]{1,0:T(8,128)(2,1)S(1)}, bf16[128,256]{1,0:T(8,128)(2,1)S(1)}, u32[]{:S(2)}, u32[]{:S(2)}) collective-permute-start(bf16[128,256]{1,0:T(8,128)(2,1)S(1)} %get-tuple-element.26.refs_0_.total_ref), channel_id=1, source_target_pairs={{0,2},{1,3},{2,0},{3,1},{4,6},{5,7},{6,4},{7,5},{8,10},{9,11},{10,... | collective-permute-start | bytes 196616 | tf_op jit(solution)/shard_map/ppermute | solution.py:320
  15.6 4.7 %collective-permute-start.2 = (bf16[128,256]{1,0:T(8,128)(2,1)S(1)}, bf16[128,256]{1,0:T(8,128)(2,1)S(1)}, u32[]{:S(2)}, u32[]{:S(2)}) collective-permute-start(bf16[128,256]{1,0:T(8,128)(2,1)S(1)} %get-tuple-element.26.refs_0_.total_ref), channel_id=1, source_target_pairs={{0,3},{1,2},{2,1},{3,0},{4,7},{5,6},{6,5},{7,4},{8,11},{9,10},{10,... | collective-permute-start | bytes 196616 | tf_op jit(solution)/shard_map/ppermute | solution.py:320
  20.8 15.7 %collective-permute-start.10 = (bf16[128,256]{1,0:T(8,128)(2,1)S(1)}, bf16[128,256]{1,0:T(8,128)(2,1)S(1)}, u32[]{:S(2)}, u32[]{:S(2)}) collective-permute-start(bf16[128,256]{1,0:T(8,128)(2,1)S(1)} %get-tuple-element.40), channel_id=1, source_target_pairs={{0,8},{1,9},{2,10},{3,11},{4,12},{5,13},{6,14},{7,15},{8,0},{9,1},... | collective-permute-start | bytes 196616 | tf_op jit(solution)/shard_map/ppermute | solution.py:339
  22.9 13.5 %collective-permute-start.9 = (bf16[128,256]{1,0:T(8,128)(2,1)S(1)}, bf16[128,256]{1,0:T(8,128)(2,1)S(1)}, u32[]{:S(2)}, u32[]{:S(2)}) collective-permute-start(bf16[128,256]{1,0:T(8,128)(2,1)S(1)} %get-tuple-element.40), channel_id=1, source_target_pairs={{0,4},{1,5},{2,6},{3,7},{4,8},{5,9},{6,10},{7,11},{8,12},{9,13},{1... | collective-permute-start | bytes 196616 | tf_op jit(solution)/shard_map/ppermute | solution.py:339
  27.4 1.9 %collective-permute-start.3 = (f32[8,128]{1,0:T(8,128)S(1)}, f32[8,128]{1,0:T(8,128)S(1)}, u32[]{:S(2)}, u32[]{:S(2)}) collective-permute-start(f32[8,128]{1,0:T(8,128)S(1)} %get-tuple-element.35.refs_0_), channel_id=1, source_target_pairs={{0,1},{1,0},{2,3},{3,2},{4,5},{5,4},{6,7},{7,6},{8,9},{9,8},{10,11... | collective-permute-start | bytes 12296 | tf_op jit(solution)/shard_map/ppermute | solution.py:320
  27.5 3.7 %collective-permute-start.4 = (f32[8,128]{1,0:T(8,128)S(1)}, f32[8,128]{1,0:T(8,128)S(1)}, u32[]{:S(2)}, u32[]{:S(2)}) collective-permute-start(f32[8,128]{1,0:T(8,128)S(1)} %get-tuple-element.35.refs_0_), channel_id=1, source_target_pairs={{0,2},{1,3},{2,0},{3,1},{4,6},{5,7},{6,4},{7,5},{8,10},{9,11},{10,... | collective-permute-start | bytes 12296 | tf_op jit(solution)/shard_map/ppermute | solution.py:320
  28.6 3.0 %collective-permute-start.5 = (f32[8,128]{1,0:T(8,128)S(1)}, f32[8,128]{1,0:T(8,128)S(1)}, u32[]{:S(2)}, u32[]{:S(2)}) collective-permute-start(f32[8,128]{1,0:T(8,128)S(1)} %get-tuple-element.35.refs_0_), channel_id=1, source_target_pairs={{0,3},{1,2},{2,1},{3,0},{4,7},{5,6},{6,5},{7,4},{8,11},{9,10},{10,... | collective-permute-start | bytes 12296 | tf_op jit(solution)/shard_map/ppermute | solution.py:320
  32.0 4.4 %collective-permute-start.6 = (f32[8,128]{1,0:T(8,128)S(1)}, f32[8,128]{1,0:T(8,128)S(1)}, u32[]{:S(2)}, u32[]{:S(2)}) collective-permute-start(f32[8,128]{1,0:T(8,128)S(1)} %get-tuple-element.39), channel_id=1, source_target_pairs={{0,4},{1,5},{2,6},{3,7},{4,0},{5,1},{6,2},{7,3},{8,12},{9,13},{10,... | collective-permute-start | bytes 12296 | tf_op jit(solution)/shard_map/ppermute | solution.py:320
  32.1 4.5 %collective-permute-start.7 = (f32[8,128]{1,0:T(8,128)S(1)}, f32[8,128]{1,0:T(8,128)S(1)}, u32[]{:S(2)}, u32[]{:S(2)}) collective-permute-start(f32[8,128]{1,0:T(8,128)S(1)} %get-tuple-element.39), channel_id=1, source_target_pairs={{0,8},{1,9},{2,10},{3,11},{4,12},{5,13},{6,14},{7,15},{8,0},{9,1},... | collective-permute-start | bytes 12296 | tf_op jit(solution)/shard_map/ppermute | solution.py:320
  34.8 5.4 %collective-permute-start.8 = (f32[8,128]{1,0:T(8,128)S(1)}, f32[8,128]{1,0:T(8,128)S(1)}, u32[]{:S(2)}, u32[]{:S(2)}) collective-permute-start(f32[8,128]{1,0:T(8,128)S(1)} %get-tuple-element.39), channel_id=1, source_target_pairs={{0,12},{1,13},{2,14},{3,15},{4,8},{5,9},{6,10},{7,11},{8,4},{9,5},... | collective-permute-start | bytes 12296 | tf_op jit(solution)/shard_map/ppermute | solution.py:320

commit v6 on v5

--- a/solution.py
+++ b/solution.py
@@ -194,7 +194,7 @@
     shift_ref[...] = states[0] + vm(first, total_ref[...])
 
 
-def group_kernel(size, pos_ref, *refs):
+def group_kernel(size, pos_ref, after_ref, *refs):
     blocks = refs[:size]
     all_ref, prefix_ref, whole_ref = refs[size:]
     n = whole_ref.shape[0]
@@ -332,9 +332,9 @@
     group_maps, prefix, whole = call(
         functools.partial(group_kernel, size), "group_maps", 2, 1 << 24, MIB,
         out_shape=[shape((size, n, 2 * n), BF16), one_map, one_map],
-        in_specs=[SMEM] + [VMEM] * size,
+        in_specs=[SMEM] + [VMEM] * (1 + size),
         out_specs=[VMEM] * 3,
-    )(position, total, *members)
+    )(position, shift, total, *members)
     wholes = [
         lax.ppermute(whole, "tm", [(j, (j + r * size) % count) for j in range(count)]) for r in range(1, groups - 1)
     ]

time: 43.3 us -> 41.1 us (0.949)
  starting transfers between devices: 19.3 us -> 17.4 us
    ppermute x9, waiting for transfers between devices: 10.8 us -> 6.68 us  [swaps(): lax.ppermute(x, 'tm', [(j, j ^ r * step) for j in range(count)])]
    all_to_all x1, waiting for transfers between devices: 0.01 us -> 3.78 us  [shards(): lax.all_to_all(turned[0].reshape(count, steps, pixels), 'tm', split_axis=...]
    ppermute x2, starting transfers between devices: 3.47 us -> 1.61 us  [shards(): lax.ppermute(whole, 'tm', [(j, (j + r * size) % count) for j in range(cou...]
  transfers between devices with their start and end apart: 12 -> 12, of which waited for: 6 -> 5; matrix products, arithmetic and copies ran while one was open for 0% -> 0% of each run, Pallas kernels for 19% -> 19%
where the time goes in v6:
time: 41.1 us; the launch traced here: 40.8 us
  starting transfers between devices  17.4 us (42%)
  Pallas kernels  12.9 us (31%)
  waiting for transfers between devices  10.5 us (26%)
    ppermute x9, starting transfers between devices, swaps(): lax.ppermute(x, 'tm', [(j, j ^ r * step) for j in range(count)])  8.41 us
    all_to_all x1, starting transfers between devices, shards(): lax.all_to_all(turned[0].reshape(count, steps, pixels), 'tm', split_axis=...  7.37 us
    ppermute x9, waiting for transfers between devices, swaps(): lax.ppermute(x, 'tm', [(j, j ^ r * step) for j in range(count)])  6.68 us
    pallas_call x1, Pallas kernels, shards(): call(functools.partial(tree_kernel, steps), 'tree_of_maps', 8, 2 * steps...  4.12 us
    all_to_all x1, waiting for transfers between devices, shards(): lax.all_to_all(turned[0].reshape(count, steps, pixels), 'tm', split_axis=...  3.78 us
    pallas_call x1, Pallas kernels, shards(): call(local_kernel, 'local_states', 8, 1 << 27, 6 * MIB, out_shape=[shape(...  3.21 us
    pallas_call x1, Pallas kernels, shards(): call(functools.partial(final_kernel, size, groups), 'estimates', 6, 1 <<...  2.81 us
    pallas_call x1, Pallas kernels, shards(): call(functools.partial(front_kernel, cuts, len(small)), 'front', 5, 0, 4...  1.91 us
  transfers between devices with their start and end apart: 12, of which 5 were waited for; matrix products, arithmetic and copies ran while one was open for 0% of the time, Pallas kernels for 19%

profile of v6, /device:TPU:0, one launch (start us, length us, event | category | flops | bytes accessed | tf_op | source)
XLA Modules:
  0.0 40.8 jit_solution(15456601762289283293)
XLA Ops:
  0.0 1.9 %front.1 = (bf16[16,128,256]{2,1,0:T(8,128)(2,1)S(1)}, s32[1,64]{1,0:T(1,128)S(1)}, f32[1,128]{1,0:T(1,128)S(1)}, bf16[128,128]{1,0:T(8,128)(2,1)S(1)}, s32[16,1...) custom-call(f32[16,128,128]{2,1,0:T(8,128)} %trans_ref.1, s32[1,64]{1,0:T(1,128)} %bitcast.9, ...), custom_call_target="tpu_custom_call" | custom-call | bytes 4194304 | tf_op jit(solution)/shard_map/front/pallas_call | solution.py:288
  1.9 7.4 %all-to-all-start = ((bf16[16,64,128]{2,1,0:T(8,128)(2,1)}), bf16[16,64,128]{2,1,0:T(8,128)(2,1)S(1)}, u32[]{:S(2)}, u32[]{:S(2)}) async-start(bf16[16,64,128]{2,1,0:T(8,128)(2,1)} %bitcast.6), calls=%async_computation | async-start | bytes 524288 | tf_op jit(solution)/shard_map/all_to_all | solution.py:296
  9.3 4.1 %tree_of_maps.1 = (bf16[31,128,256]{2,1,0:T(8,128)(2,1)}, bf16[31,128,256]{2,1,0:T(8,128)(2,1)}, bf16[16,128,256]{2,1,0:T(8,128)(2,1)}, bf16[128,256]{1,0:T(8,128)(2,1)S(1)}) custom-call(s32[1,64]{1,0:T(1,128)S(1)} %get-tuple-element.23.levels_ref, bf16[16,128,256]{2,1,0:T(8,128)(2,1)S(1)} %get-tuple-element.29.table_ref), custom_call_target="tpu_custom_call" | custom-call | flops 1073741824 | bytes 8388608 | tf_op jit(solution)/shard_map/tree_of_maps/pallas_call | solution.py:303
  13.4 0.0 copy-start
  13.4 0.5 %collective-permute-start = (bf16[128,256]{1,0:T(8,128)(2,1)S(1)}, bf16[128,256]{1,0:T(8,128)(2,1)S(1)}, u32[]{:S(2)}, u32[]{:S(2)}) collective-permute-start(bf16[128,256]{1,0:T(8,128)(2,1)S(1)} %get-tuple-element.30.total_ref.refs_0_), channel_id=1, source_target_pairs={{0,1},{1,0},{2,3},{3,2},{4,5},{5,4},{6,7},{7,6},{8,9},{9,8},{10,11... | collective-permute-start | bytes 196616 | tf_op jit(solution)/shard_map/ppermute | solution.py:320
  13.9 1.7 %collective-permute-start.1 = (bf16[128,256]{1,0:T(8,128)(2,1)S(1)}, bf16[128,256]{1,0:T(8,128)(2,1)S(1)}, u32[]{:S(2)}, u32[]{:S(2)}) collective-permute-start(bf16[128,256]{1,0:T(8,128)(2,1)S(1)} %get-tuple-element.30.total_ref.refs_0_), channel_id=1, source_target_pairs={{0,2},{1,3},{2,0},{3,1},{4,6},{5,7},{6,4},{7,5},{8,10},{9,11},{10,... | collective-permute-start | bytes 196616 | tf_op jit(solution)/shard_map/ppermute | solution.py:320
  15.6 0.0 collective-permute-start.2
  15.6 3.8 %all-to-all-done.x_ref = bf16[16,64,128]{2,1,0:T(8,128)(2,1)S(1)} async-done(((bf16[16,64,128]{2,1,0:T(8,128)(2,1)}), bf16[16,64,128]{2,1,0:T(8,128)(2,1)S(1)}, u32[]{:S(2)}, u32[]{:S(2)}) %all-to-all-start) | async-done | bytes 262176 | tf_op jit(solution)/shard_map/all_to_all | solution.py:296
  19.4 3.2 %local_states.1 = (f32[64,128]{1,0:T(8,128)S(1)}, f32[8,128]{1,0:T(8,128)S(1)}) custom-call(s32[1]{0:T(128)} %bitcast.pos_ref, s32[1,64]{1,0:T(1,128)S(1)} %get-tuple-element.23.levels_ref, bf16[16,64,128]{2,1,0:T(8,128)(2,1)S(1)} %all-to-all-done.x_ref, s32[16,128]{1,0:T(8,128)S(1)} %get-tuple-element.26.mode_ref, ...), custom_call_target="tpu_custom_call" | custom-call | flops 134217728 | bytes 6291456 | tf_op jit(solution)/shard_map/local_states/pallas_call | solution.py:323
  22.6 0.0 collective-permute-done.refs_1_
  22.6 0.0 collective-permute-done.1.refs_2_
  22.6 0.0 collective-permute-done.2.refs_3_
  22.6 0.5 %group_maps.1 = (bf16[4,128,256]{2,1,0:T(8,128)(2,1)S(1)}, bf16[128,256]{1,0:T(8,128)(2,1)S(1)}, bf16[128,256]{1,0:T(8,128)(2,1)S(1)}) custom-call(s32[1]{0:T(128)} %bitcast.pos_ref, f32[8,128]{1,0:T(8,128)S(1)} %get-tuple-element.33.after_ref.refs_0_, bf16[128,256]{1,0:T(8,128)(2,1)S(1)} %get-tuple-element.30.total_ref.refs_0_, ...), custom_call_target="tpu_custom_call" | custom-call | flops 16777216 | bytes 1048576 | tf_op jit(solution)/shard_map/group_maps/pallas_call | solution.py:332
  23.1 1.1 %collective-permute-start.10 = (bf16[128,256]{1,0:T(8,128)(2,1)S(1)}, bf16[128,256]{1,0:T(8,128)(2,1)S(1)}, u32[]{:S(2)}, u32[]{:S(2)}) collective-permute-start(bf16[128,256]{1,0:T(8,128)(2,1)S(1)} %get-tuple-element.40), channel_id=1, source_target_pairs={{0,8},{1,9},{2,10},{3,11},{4,12},{5,13},{6,14},{7,15},{8,0},{9,1},... | collective-permute-start | bytes 196616 | tf_op jit(solution)/shard_map/ppermute | solution.py:339
  24.2 0.5 %collective-permute-start.9 = (bf16[128,256]{1,0:T(8,128)(2,1)S(1)}, bf16[128,256]{1,0:T(8,128)(2,1)S(1)}, u32[]{:S(2)}, u32[]{:S(2)}) collective-permute-start(bf16[128,256]{1,0:T(8,128)(2,1)S(1)} %get-tuple-element.40), channel_id=1, source_target_pairs={{0,4},{1,5},{2,6},{3,7},{4,8},{5,9},{6,10},{7,11},{8,12},{9,13},{1... | collective-permute-start | bytes 196616 | tf_op jit(solution)/shard_map/ppermute | solution.py:339
  24.7 0.0 collective-permute-start.3
  24.7 1.2 %collective-permute-start.4 = (f32[8,128]{1,0:T(8,128)S(1)}, f32[8,128]{1,0:T(8,128)S(1)}, u32[]{:S(2)}, u32[]{:S(2)}) collective-permute-start(f32[8,128]{1,0:T(8,128)S(1)} %get-tuple-element.33.after_ref.refs_0_), channel_id=1, source_target_pairs={{0,2},{1,3},{2,0},{3,1},{4,6},{5,7},{6,4},{7,5},{8,10},{9,11},{10,... | collective-permute-start | bytes 12296 | tf_op jit(solution)/shard_map/ppermute | solution.py:320
  25.8 0.7 %collective-permute-start.5 = (f32[8,128]{1,0:T(8,128)S(1)}, f32[8,128]{1,0:T(8,128)S(1)}, u32[]{:S(2)}, u32[]{:S(2)}) collective-permute-start(f32[8,128]{1,0:T(8,128)S(1)} %get-tuple-element.33.after_ref.refs_0_), channel_id=1, source_target_pairs={{0,3},{1,2},{2,1},{3,0},{4,7},{5,6},{6,5},{7,4},{8,11},{9,10},{10,... | collective-permute-start | bytes 12296 | tf_op jit(solution)/shard_map/ppermute | solution.py:320
  26.5 0.0 collective-permute-done.3.refs_1_
  26.5 1.7 %collective-permute-done.4.refs_2_ = f32[8,128]{1,0:T(8,128)S(1)} collective-permute-done((f32[8,128]{1,0:T(8,128)S(1)}, f32[8,128]{1,0:T(8,128)S(1)}, u32[]{:S(2)}, u32[]{:S(2)}) %collective-permute-start.4) | collective-permute-done | bytes 4128 | tf_op jit(solution)/shard_map/ppermute | solution.py:320
  28.3 0.6 %collective-permute-done.5.refs_3_ = f32[8,128]{1,0:T(8,128)S(1)} collective-permute-done((f32[8,128]{1,0:T(8,128)S(1)}, f32[8,128]{1,0:T(8,128)S(1)}, u32[]{:S(2)}, u32[]{:S(2)}) %collective-permute-start.5) | collective-permute-done | bytes 4128 | tf_op jit(solution)/shard_map/ppermute | solution.py:320
  28.9 0.4 group_states.1
  29.3 1.4 %collective-permute-start.6 = (f32[8,128]{1,0:T(8,128)S(1)}, f32[8,128]{1,0:T(8,128)S(1)}, u32[]{:S(2)}, u32[]{:S(2)}) collective-permute-start(f32[8,128]{1,0:T(8,128)S(1)} %get-tuple-element.39), channel_id=1, source_target_pairs={{0,4},{1,5},{2,6},{3,7},{4,0},{5,1},{6,2},{7,3},{8,12},{9,13},{10,... | collective-permute-start | bytes 12296 | tf_op jit(solution)/shard_map/ppermute | solution.py:320
  30.6 2.0 %collective-permute-start.7 = (f32[8,128]{1,0:T(8,128)S(1)}, f32[8,128]{1,0:T(8,128)S(1)}, u32[]{:S(2)}, u32[]{:S(2)}) collective-permute-start(f32[8,128]{1,0:T(8,128)S(1)} %get-tuple-element.39), channel_id=1, source_target_pairs={{0,8},{1,9},{2,10},{3,11},{4,12},{5,13},{6,14},{7,15},{8,0},{9,1},... | collective-permute-start | bytes 12296 | tf_op jit(solution)/shard_map/ppermute | solution.py:320
  32.6 1.1 %collective-permute-start.8 = (f32[8,128]{1,0:T(8,128)S(1)}, f32[8,128]{1,0:T(8,128)S(1)}, u32[]{:S(2)}, u32[]{:S(2)}) collective-permute-start(f32[8,128]{1,0:T(8,128)S(1)} %get-tuple-element.39), channel_id=1, source_target_pairs={{0,12},{1,13},{2,14},{3,15},{4,8},{5,9},{6,10},{7,11},{8,4},{9,5},... | collective-permute-start | bytes 12296 | tf_op jit(solution)/shard_map/ppermute | solution.py:320
  33.7 0.0 collective-permute-done.6.refs_0_
  33.7 1.5 %collective-permute-done.7.refs_1_ = f32[8,128]{1,0:T(8,128)S(1)} collective-permute-done((f32[8,128]{1,0:T(8,128)S(1)}, f32[8,128]{1,0:T(8,128)S(1)}, u32[]{:S(2)}, u32[]{:S(2)}) %collective-permute-start.7) | collective-permute-done | bytes 4128 | tf_op jit(solution)/shard_map/ppermute | solution.py:320
  35.1 2.9 %collective-permute-done.8.refs_2_ = f32[8,128]{1,0:T(8,128)S(1)} collective-permute-done((f32[8,128]{1,0:T(8,128)S(1)}, f32[8,128]{1,0:T(8,128)S(1)}, u32[]{:S(2)}, u32[]{:S(2)}) %collective-permute-start.8) | collective-permute-done | bytes 4128 | tf_op jit(solution)/shard_map/ppermute | solution.py:320
  38.0 0.0 collective-permute-done.10.refs_4_
  38.0 0.0 collective-permute-done.9.refs_3_
  38.0 0.0 copy-done
  38.0 2.8 %estimates.1 = f32[64,128]{1,0:T(8,128)} custom-call(s32[1]{0:T(128)} %bitcast.pos_ref, s32[1,64]{1,0:T(1,128)S(1)} %get-tuple-element.23.levels_ref, f32[1,128]{1,0:T(1,128)S(1)} %get-tuple-element.24.init_ref, bf16[128,256]{1,0:T(8,128)(2,1)S(1)} %get-tuple-element.34.prefix_ref, f32[8,128]{1,0:T(8,128)S(1)} %get-tuple-element.36.before_ref, ...), custom_call_target="tpu_custom_call" | custom-call | flops 8388608 | bytes 5242880 | tf_op jit(solution)/shard_map/estimates/pallas_call | solution.py:349
Async XLA Ops:
  1.9 17.4 %all-to-all-start = ((bf16[16,64,128]{2,1,0:T(8,128)(2,1)}), bf16[16,64,128]{2,1,0:T(8,128)(2,1)S(1)}, u32[]{:S(2)}, u32[]{:S(2)}) async-start(bf16[16,64,128]{2,1,0:T(8,128)(2,1)} %bitcast.6), calls=%async_computation | async-start | bytes 524288 | tf_op jit(solution)/shard_map/all_to_all | solution.py:296
  13.4 24.6 %copy-start = (bf16[31,128,256]{2,1,0:T(8,128)(2,1)S(1)}, bf16[31,128,256]{2,1,0:T(8,128)(2,1)}, u32[]{:S(2)}) copy-start(bf16[31,128,256]{2,1,0:T(8,128)(2,1)} %get-tuple-element.38.left_ref) | copy-start | bytes 6094852
  13.4 9.1 %collective-permute-start = (bf16[128,256]{1,0:T(8,128)(2,1)S(1)}, bf16[128,256]{1,0:T(8,128)(2,1)S(1)}, u32[]{:S(2)}, u32[]{:S(2)}) collective-permute-start(bf16[128,256]{1,0:T(8,128)(2,1)S(1)} %get-tuple-element.30.total_ref.refs_0_), channel_id=1, source_target_pairs={{0,1},{1,0},{2,3},{3,2},{4,5},{5,4},{6,7},{7,6},{8,9},{9,8},{10,11... | collective-permute-start | bytes 196616 | tf_op jit(solution)/shard_map/ppermute | solution.py:320
  13.9 8.7 %collective-permute-start.1 = (bf16[128,256]{1,0:T(8,128)(2,1)S(1)}, bf16[128,256]{1,0:T(8,128)(2,1)S(1)}, u32[]{:S(2)}, u32[]{:S(2)}) collective-permute-start(bf16[128,256]{1,0:T(8,128)(2,1)S(1)} %get-tuple-element.30.total_ref.refs_0_), channel_id=1, source_target_pairs={{0,2},{1,3},{2,0},{3,1},{4,6},{5,7},{6,4},{7,5},{8,10},{9,11},{10,... | collective-permute-start | bytes 196616 | tf_op jit(solution)/shard_map/ppermute | solution.py:320
  15.6 7.0 %collective-permute-start.2 = (bf16[128,256]{1,0:T(8,128)(2,1)S(1)}, bf16[128,256]{1,0:T(8,128)(2,1)S(1)}, u32[]{:S(2)}, u32[]{:S(2)}) collective-permute-start(bf16[128,256]{1,0:T(8,128)(2,1)S(1)} %get-tuple-element.30.total_ref.refs_0_), channel_id=1, source_target_pairs={{0,3},{1,2},{2,1},{3,0},{4,7},{5,6},{6,5},{7,4},{8,11},{9,10},{10,... | collective-permute-start | bytes 196616 | tf_op jit(solution)/shard_map/ppermute | solution.py:320
  23.1 14.9 %collective-permute-start.10 = (bf16[128,256]{1,0:T(8,128)(2,1)S(1)}, bf16[128,256]{1,0:T(8,128)(2,1)S(1)}, u32[]{:S(2)}, u32[]{:S(2)}) collective-permute-start(bf16[128,256]{1,0:T(8,128)(2,1)S(1)} %get-tuple-element.40), channel_id=1, source_target_pairs={{0,8},{1,9},{2,10},{3,11},{4,12},{5,13},{6,14},{7,15},{8,0},{9,1},... | collective-permute-start | bytes 196616 | tf_op jit(solution)/shard_map/ppermute | solution.py:339
  24.2 13.8 %collective-permute-start.9 = (bf16[128,256]{1,0:T(8,128)(2,1)S(1)}, bf16[128,256]{1,0:T(8,128)(2,1)S(1)}, u32[]{:S(2)}, u32[]{:S(2)}) collective-permute-start(bf16[128,256]{1,0:T(8,128)(2,1)S(1)} %get-tuple-element.40), channel_id=1, source_target_pairs={{0,4},{1,5},{2,6},{3,7},{4,8},{5,9},{6,10},{7,11},{8,12},{9,13},{1... | collective-permute-start | bytes 196616 | tf_op jit(solution)/shard_map/ppermute | solution.py:339
  24.7 1.9 %collective-permute-start.3 = (f32[8,128]{1,0:T(8,128)S(1)}, f32[8,128]{1,0:T(8,128)S(1)}, u32[]{:S(2)}, u32[]{:S(2)}) collective-permute-start(f32[8,128]{1,0:T(8,128)S(1)} %get-tuple-element.33.after_ref.refs_0_), channel_id=1, source_target_pairs={{0,1},{1,0},{2,3},{3,2},{4,5},{5,4},{6,7},{7,6},{8,9},{9,8},{10,11... | collective-permute-start | bytes 12296 | tf_op jit(solution)/shard_map/ppermute | solution.py:320
  24.7 3.6 %collective-permute-start.4 = (f32[8,128]{1,0:T(8,128)S(1)}, f32[8,128]{1,0:T(8,128)S(1)}, u32[]{:S(2)}, u32[]{:S(2)}) collective-permute-start(f32[8,128]{1,0:T(8,128)S(1)} %get-tuple-element.33.after_ref.refs_0_), channel_id=1, source_target_pairs={{0,2},{1,3},{2,0},{3,1},{4,6},{5,7},{6,4},{7,5},{8,10},{9,11},{10,... | collective-permute-start | bytes 12296 | tf_op jit(solution)/shard_map/ppermute | solution.py:320
  25.8 3.0 %collective-permute-start.5 = (f32[8,128]{1,0:T(8,128)S(1)}, f32[8,128]{1,0:T(8,128)S(1)}, u32[]{:S(2)}, u32[]{:S(2)}) collective-permute-start(f32[8,128]{1,0:T(8,128)S(1)} %get-tuple-element.33.after_ref.refs_0_), channel_id=1, source_target_pairs={{0,3},{1,2},{2,1},{3,0},{4,7},{5,6},{6,5},{7,4},{8,11},{9,10},{10,... | collective-permute-start | bytes 12296 | tf_op jit(solution)/shard_map/ppermute | solution.py:320
  29.3 4.4 %collective-permute-start.6 = (f32[8,128]{1,0:T(8,128)S(1)}, f32[8,128]{1,0:T(8,128)S(1)}, u32[]{:S(2)}, u32[]{:S(2)}) collective-permute-start(f32[8,128]{1,0:T(8,128)S(1)} %get-tuple-element.39), channel_id=1, source_target_pairs={{0,4},{1,5},{2,6},{3,7},{4,0},{5,1},{6,2},{7,3},{8,12},{9,13},{10,... | collective-permute-start | bytes 12296 | tf_op jit(solution)/shard_map/ppermute | solution.py:320
  30.6 4.5 %collective-permute-start.7 = (f32[8,128]{1,0:T(8,128)S(1)}, f32[8,128]{1,0:T(8,128)S(1)}, u32[]{:S(2)}, u32[]{:S(2)}) collective-permute-start(f32[8,128]{1,0:T(8,128)S(1)} %get-tuple-element.39), channel_id=1, source_target_pairs={{0,8},{1,9},{2,10},{3,11},{4,12},{5,13},{6,14},{7,15},{8,0},{9,1},... | collective-permute-start | bytes 12296 | tf_op jit(solution)/shard_map/ppermute | solution.py:320
  32.6 5.4 %collective-permute-start.8 = (f32[8,128]{1,0:T(8,128)S(1)}, f32[8,128]{1,0:T(8,128)S(1)}, u32[]{:S(2)}, u32[]{:S(2)}) collective-permute-start(f32[8,128]{1,0:T(8,128)S(1)} %get-tuple-element.39), channel_id=1, source_target_pairs={{0,12},{1,13},{2,14},{3,15},{4,8},{5,9},{6,10},{7,11},{8,4},{9,5},... | collective-permute-start | bytes 12296 | tf_op jit(solution)/shard_map/ppermute | solution.py:320

commit v7 on v6

--- a/solution.py
+++ b/solution.py
@@ -56,48 +56,66 @@
     return jnp.broadcast_to(ref[pl.ds(t, 1), :], (8, ref.shape[1]))
 
 
-def front_kernel(cuts, extra, trans_ref, *refs):
+def front_kernel(cuts, extra, size, pos_ref, trans_ref, *refs):
     given, refs = refs[:extra], refs[extra:]
     turn = len(refs) > extra + 3
     if turn:
-        frames_ref, table_ref, *moved, turned_ref, trans, frames, turned, sems = refs
+        frames_ref, table_ref, *moved = refs[: 2 + extra]
+        slabs = refs[2 + extra : 2 + extra + size]
+        trans, frames, turned, sems = refs[2 + extra + size :]
         width = frames.shape[1] // cuts
         parts = [pl.ds(k * width, width) for k in range(cuts)]
         ins = [
             pltpu.make_async_copy(frames_ref.at[:, part], frames.at[:, part], sems.at[k])
             for k, part in enumerate(parts)
         ]
-        outs = [
-            pltpu.make_async_copy(turned.at[part], turned_ref.at[part], sems.at[cuts + k])
-            for k, part in enumerate(parts)
-        ]
         for copy in ins:
             copy.start()
     else:
         table_ref, *moved, trans, sems = refs
-        outs = []
     kinds = trans.shape[0]
     few = kinds // 4
     maps = [
-        pltpu.make_async_copy(trans_ref.at[pl.ds(k * few, few)], trans.at[pl.ds(k * few, few)], sems.at[2 * cuts + k])
+        pltpu.make_async_copy(trans_ref.at[pl.ds(k * few, few)], trans.at[pl.ds(k * few, few)], sems.at[cuts + k])
         for k in range(4)
     ]
-    moves = [
-        pltpu.make_async_copy(a, b, sems.at[2 * cuts + 4 + k]) for k, (a, b) in enumerate(zip(given, moved))
-    ]
+    moves = [pltpu.make_async_copy(a, b, sems.at[cuts + 4 + k]) for k, (a, b) in enumerate(zip(given, moved))]
     for copy in maps + moves:
         copy.start()
     if turn:
         for k in range(cuts):
             ins[k].wait()
             turned[parts[k], :] = frames[:, parts[k]].T
-            outs[k].start()
+        member = pos_ref[0] % size
+        groups, steps, _ = slabs[0].shape
+        for r in range(size):
+            for g in range(groups):
+                start = pl.multiple_of((g * size + (member ^ r)) * steps, steps)
+                slabs[r][g] = turned[pl.ds(start, steps), :]
     for k in range(4):
         maps[k].wait()
         for q in range(k * few, (k + 1) * few):
             table_ref[q] = pair(trans[q].T)
-    for copy in moves + outs:
+    for copy in moves:
         copy.wait()
+
+
+def project_kernel(size, pos_ref, mode_ref, weight_ref, *refs):
+    slabs, outs, (sums, weights) = refs[:size], refs[size:-2], refs[-2:]
+    weights[...] = weight_ref[...].astype(F32)
+    groups, steps, width = slabs[0].shape
+    n = sums.shape[2]
+    position = pos_ref[0]
+    channel = lax.broadcasted_iota(jnp.int32, (n, width), 0)
+    total = jnp.zeros((groups * steps, n), F32)
+    for r in range(size):
+        here = pl.ds(position ^ r, 1)
+        weight = jnp.broadcast_to(weights[here, :], (n, width))
+        projector = jnp.where(mode_ref[here, :] == channel, weight, 0.0).astype(BF16)
+        total += lax.dot_general(slabs[r][...].reshape(groups * steps, width), projector, NT, preferred_element_type=F32)
+    sums[...] = total.reshape(groups, steps, n)
+    for r in range(groups):
+        outs[r][...] = sums[(position // size) ^ r]
 
 
 def tree_kernel(steps, levels_ref, table_ref, left_hbm, right_hbm, table_hbm, total_ref, left_ref, right_ref, sems):
@@ -156,9 +174,9 @@
         copy.wait()
 
 
-def local_kernel(pos_ref, levels_ref, x_ref, mode_ref, weight_ref, gain_ref, init_ref, total_ref, table_hbm, right_hbm, lefts_ref, shift_ref, drive_ref, table_ref, right_ref, sems):
-    segments, steps, width = x_ref.shape
-    n = gain_ref.shape[0]
+def local_kernel(pos_ref, levels_ref, gain_ref, init_ref, total_ref, table_hbm, right_hbm, *refs):
+    parts, (lefts_ref, shift_ref, drive_ref, table_ref, right_ref, sems) = refs[:-6], refs[-6:]
+    steps, n = drive_ref.shape
     base = steps // 4
     copies = [
         pltpu.make_async_copy(table_hbm, table_ref, sems.at[0]),
@@ -167,12 +185,9 @@
     ]
     for copy in copies:
         copy.start()
-    channel = lax.broadcasted_iota(jnp.int32, (n, width), 0)
-    measured = jnp.zeros((steps, n), F32)
-    for k in range(segments):
-        weight = jnp.broadcast_to(weight_ref[pl.ds(k, 1), :].astype(F32), (n, width))
-        projector = jnp.where(mode_ref[pl.ds(k, 1), :] == channel, weight, 0.0).astype(BF16)
-        measured += lax.dot_general(x_ref[k], projector, NT, preferred_element_type=F32)
+    measured = parts[0][...]
+    for part in parts[1:]:
+        measured += part[...]
     drive_ref[...] = lax.dot_general(measured.astype(BF16), gain_ref[...], NT, preferred_element_type=F32)
 
     states = [row(drive_ref, t) for t in range(steps)]
@@ -267,35 +282,52 @@
     position = lax.axis_index("tm").astype(jnp.int32)[None]
     pairs = steps // 2 - 1
     dma = pltpu.SemaphoreType.DMA
+    size = 1
+    while count % (2 * size) == 0 and 4 * size * size <= count:
+        size *= 2
+    groups = count // size
+
+    def swaps(x, step, times):
+        x = x if isinstance(x, list) else [x] * (times - 1)
+        return [
+            lax.ppermute(a, "tm", [(j, j ^ (r * step)) for j in range(count)]) for a, r in zip(x, range(1, times))
+        ]
+
     one_map = shape((n, 2 * n), BF16)
     table_shape = shape((kinds, n, 2 * n), BF16)
     cuts = 4
     turn = pixels % 128 == 0 and length % (128 * cuts) == 0
-    segments = count if turn else 1
-    small = [
-        levels[None],
-        initial_state[None],
-        gain,
-        pixel_mode.reshape(segments, -1),
-        pixel_weight.reshape(segments, -1),
-    ]
+    small = [levels[None], initial_state[None], gain]
+    if turn:
+        small += [pixel_mode.reshape(count, pixels), pixel_weight.reshape(count, pixels)]
     given = [hbm(a) for a in [transitions] + small + [frames] * turn]
     outs = [table_shape] + [shape(a.shape, a.dtype) for a in small]
     buffers = [pltpu.VMEM(transitions.shape, F32)]
     if turn:
-        outs.append(pltpu.HBM((length, pixels), BF16))
+        outs += [shape((groups, steps, pixels), BF16)] * size
         buffers += [pltpu.VMEM(frames.shape, BF16), pltpu.VMEM((length, pixels), BF16)]
-    table, levels, initial_state, gain, mode, weight, *turned = call(
-        functools.partial(front_kernel, cuts, len(small)), "front", 5, 0, 4 * MIB,
+    table, levels, initial_state, gain, *rest = call(
+        functools.partial(front_kernel, cuts, len(small), size), "front", 5, 0, 4 * MIB,
         out_shape=outs,
-        in_specs=[HBM] * len(given),
-        out_specs=[VMEM] * (1 + len(small)) + [HBM] * turn,
-        scratch_shapes=buffers + [dma((2 * cuts + 4 + len(small),))],
-    )(*given)
-    if turn:
-        x = lax.all_to_all(turned[0].reshape(count, steps, pixels), "tm", split_axis=0, concat_axis=0, tiled=True)
+        in_specs=[SMEM] + [HBM] * len(given),
+        out_specs=[VMEM] * len(outs),
+        scratch_shapes=buffers + [dma((cuts + 4 + len(small),))],
+    )(position, *given)
+    if turn:
+        mode, weight, slab, *slabs = rest
+        first, *parts = call(
+            functools.partial(project_kernel, size), "project", 4, 1 << 25, MIB,
+            out_shape=[shape((steps, n), F32)] * groups,
+            in_specs=[SMEM] + [VMEM] * (2 + size),
+            out_specs=[VMEM] * groups,
+            scratch_shapes=[pltpu.VMEM((groups, steps, n), F32), pltpu.VMEM((count, pixels), F32)],
+        )(position, mode, weight, slab, *swaps(slabs, 1, size))
+        parts = [first] + swaps(parts, size, groups)
     else:
-        x = lax.all_to_all(frames, "tm", split_axis=1, concat_axis=0, tiled=True).T[None]
+        x = lax.all_to_all(frames, "tm", split_axis=1, concat_axis=0, tiled=True)
+        channels = jnp.arange(n, dtype=jnp.int32)
+        projector = jnp.where(pixel_mode[None, :] == channels[:, None], pixel_weight[None, :], jnp.zeros((), BF16))
+        parts = [lax.dot_general(x, projector, (((0,), (1,)), ((), ())), preferred_element_type=F32)]
 
     tree = pltpu.VMEM((pairs, n, 2 * n), BF16)
     table_vmem = pltpu.VMEM(table_shape.shape, BF16)
@@ -309,24 +341,16 @@
     )(levels, table)
     right, table = hbm(right), hbm(table)
 
-    size = 1
-    while count % (2 * size) == 0 and 4 * size * size <= count:
-        size *= 2
-    groups = count // size
-
     vector = shape((8, n), F32)
-
-    def swaps(x, step, times):
-        return [lax.ppermute(x, "tm", [(j, j ^ (r * step)) for j in range(count)]) for r in range(1, times)]
 
     members = swaps(total, 1, size)
     lefts, shift = call(
         local_kernel, "local_states", 8, 1 << 27, 6 * MIB,
         out_shape=[shape((steps, n), F32), vector],
-        in_specs=[SMEM, SMEM] + [VMEM] * 6 + [HBM] * 2,
+        in_specs=[SMEM, SMEM] + [VMEM] * 3 + [HBM] * 2 + [VMEM] * len(parts),
         out_specs=[VMEM] * 2,
         scratch_shapes=[pltpu.VMEM((steps, n), F32), table_vmem, tree, dma((3,))],
-    )(position, levels, x, mode, weight, gain, initial_state, total, table, right)
+    )(position, levels, gain, initial_state, total, table, right, *parts)
     shifts = swaps(shift, 1, size)
 
     group_maps, prefix, whole = call(
@@ -334,7 +358,7 @@
         out_shape=[shape((size, n, 2 * n), BF16), one_map, one_map],
         in_specs=[SMEM] + [VMEM] * (1 + size),
         out_specs=[VMEM] * 3,
-    )(position, shift, total, *members)
+    )(position, shifts[0], total, *members)
     wholes = [
         lax.ppermute(whole, "tm", [(j, (j + r * size) % count) for j in range(count)]) for r in range(1, groups - 1)
     ]

time: 41.1 us -> 46.2 us (1.12)
  waiting for transfers between devices: 10.5 us -> 16.7 us
  starting transfers between devices: 17.4 us -> 16.4 us
    ppermute x9 -> x15, waiting for transfers between devices: 6.68 us -> 16.7 us  [swaps(): lax.ppermute(a, 'tm', [(j, j ^ r * step) for j in range(count)])]
    all_to_all x1 -> x0, starting transfers between devices: 7.37 us -> none  [shards(): lax.all_to_all(turned[0].reshape(count, steps, pixels), 'tm', split_axis=...]
    ppermute x9 -> x15, starting transfers between devices: 8.41 us -> 15.4 us  [swaps(): lax.ppermute(a, 'tm', [(j, j ^ r * step) for j in range(count)])]
    all_to_all x1 -> x0, waiting for transfers between devices: 3.78 us -> none  [shards(): lax.all_to_all(turned[0].reshape(count, steps, pixels), 'tm', split_axis=...]
    ppermute x2, starting transfers between devices: 1.61 us -> 1.01 us  [shards(): lax.ppermute(whole, 'tm', [(j, (j + r * size) % count) for j in range(cou...]
    pallas_call x1 -> x2, Pallas kernels: 1.91 us -> 2.08 us  [the longest x1 1.83 us: shards(): call(functools.partial(front_kernel, cuts, len(small), size), 'front', 5,...]
  transfers between devices with their start and end apart: 12 -> 17, of which waited for: 5 -> 9; matrix products, arithmetic and copies ran while one was open for 0% -> 0% of each run, Pallas kernels for 19% -> 16%
where the time goes in v7:
time: 46.2 us; the launch traced here: 46 us
  waiting for transfers between devices  16.7 us (36%)
  starting transfers between devices  16.4 us (35%)
  Pallas kernels  12.8 us (28%)
    ppermute x15, waiting for transfers between devices, swaps(): lax.ppermute(a, 'tm', [(j, j ^ r * step) for j in range(count)])  16.7 us
    ppermute x15, starting transfers between devices, swaps(): lax.ppermute(a, 'tm', [(j, j ^ r * step) for j in range(count)])  15.4 us
    pallas_call x1, Pallas kernels, shards(): call(functools.partial(tree_kernel, steps), 'tree_of_maps', 8, 2 * steps...  4.11 us
    pallas_call x1, Pallas kernels, shards(): call(local_kernel, 'local_states', 8, 1 << 27, 6 * MIB, out_shape=[shape(...  2.97 us
    pallas_call x1, Pallas kernels, shards(): call(functools.partial(final_kernel, size, groups), 'estimates', 6, 1 <<...  2.81 us
    pallas_call x1, Pallas kernels, shards(): call(functools.partial(front_kernel, cuts, len(small), size), 'front', 5,...  1.83 us
    ppermute x2, starting transfers between devices, shards(): lax.ppermute(whole, 'tm', [(j, (j + r * size) % count) for j in range(cou...  1.01 us
  transfers between devices with their start and end apart: 17, of which 9 were waited for; matrix products, arithmetic and copies ran while one was open for 0% of the time, Pallas kernels for 16%

profile of v7, /device:TPU:0, one launch (start us, length us, event | category | flops | bytes accessed | tf_op | source)
XLA Modules:
  0.0 46.0 jit_solution(3375983508668155099)
XLA Ops:
  0.0 1.8 %front.1 = (bf16[16,128,256]{2,1,0:T(8,128)(2,1)S(1)}, s32[1,64]{1,0:T(1,128)S(1)}, f32[1,128]{1,0:T(1,128)S(1)}, bf16[128,128]{1,0:T(8,128)(2,1)S(1)}, s32[16,1...) custom-call(s32[1]{0:T(128)} %bitcast.pos_ref, ...), custom_call_target="tpu_custom_call" | custom-call | bytes 4194304 | tf_op jit(solution)/shard_map/front/pallas_call | solution.py:309
  1.8 0.5 %collective-permute-start = (bf16[4,64,128]{2,1,0:T(8,128)(2,1)S(1)}, bf16[4,64,128]{2,1,0:T(8,128)(2,1)S(1)}, u32[]{:S(2)}, u32[]{:S(2)}) collective-permute-start(bf16[4,64,128]{2,1,0:T(8,128)(2,1)S(1)} %get-tuple-element.40), channel_id=1, source_target_pairs={{0,1},{1,0},{2,3},{3,2},{4,5},{5,4},{6,7},{7,6},{8,9},{9,8},{10,11... | collective-permute-start | bytes 196616 | tf_op jit(solution)/shard_map/ppermute | solution.py:293
  2.4 2.6 %collective-permute-start.1 = (bf16[4,64,128]{2,1,0:T(8,128)(2,1)S(1)}, bf16[4,64,128]{2,1,0:T(8,128)(2,1)S(1)}, u32[]{:S(2)}, u32[]{:S(2)}) collective-permute-start(bf16[4,64,128]{2,1,0:T(8,128)(2,1)S(1)} %get-tuple-element.41), channel_id=1, source_target_pairs={{0,2},{1,3},{2,0},{3,1},{4,6},{5,7},{6,4},{7,5},{8,10},{9,11},{10,... | collective-permute-start | bytes 196616 | tf_op jit(solution)/shard_map/ppermute | solution.py:293
  4.9 0.1 collective-permute-start.2
  5.0 0.0 collective-permute-done.refs_1_
  5.0 2.6 %collective-permute-done.1.refs_2_ = bf16[4,64,128]{2,1,0:T(8,128)(2,1)S(1)} collective-permute-done((bf16[4,64,128]{2,1,0:T(8,128)(2,1)S(1)}, bf16[4,64,128]{2,1,0:T(8,128)(2,1)S(1)}, u32[]{:S(2)}, u32[]{:S(2)}) %collective-permute-start.1) | collective-permute-done | bytes 65568 | tf_op jit(solution)/shard_map/ppermute | solution.py:293
  7.6 1.4 %collective-permute-done.2.refs_3_ = bf16[4,64,128]{2,1,0:T(8,128)(2,1)S(1)} collective-permute-done((bf16[4,64,128]{2,1,0:T(8,128)(2,1)S(1)}, bf16[4,64,128]{2,1,0:T(8,128)(2,1)S(1)}, u32[]{:S(2)}, u32[]{:S(2)}) %collective-permute-start.2) | collective-permute-done | bytes 65568 | tf_op jit(solution)/shard_map/ppermute | solution.py:293
  9.0 0.2 project.1
  9.2 1.6 %collective-permute-start.3 = (f32[64,128]{1,0:T(8,128)S(1)}, f32[64,128]{1,0:T(8,128)S(1)}, u32[]{:S(2)}, u32[]{:S(2)}) collective-permute-start(f32[64,128]{1,0:T(8,128)S(1)} %get-tuple-element.44), channel_id=1, source_target_pairs={{0,4},{1,5},{2,6},{3,7},{4,0},{5,1},{6,2},{7,3},{8,12},{9,13},{10,... | collective-permute-start | bytes 98312 | tf_op jit(solution)/shard_map/ppermute | solution.py:293
  10.9 4.1 %tree_of_maps.1 = (bf16[31,128,256]{2,1,0:T(8,128)(2,1)}, bf16[31,128,256]{2,1,0:T(8,128)(2,1)}, bf16[16,128,256]{2,1,0:T(8,128)(2,1)}, bf16[128,256]{1,0:T(8,128)(2,1)S(1)}) custom-call(s32[1,64]{1,0:T(1,128)S(1)} %get-tuple-element.30.levels_ref, bf16[16,128,256]{2,1,0:T(8,128)(2,1)S(1)} %get-tuple-element.33.table_ref), custom_call_target="tpu_custom_call" | custom-call | flops 1073741824 | bytes 8388608 | tf_op jit(solution)/shard_map/tree_of_maps/pallas_call | solution.py:335
  15.0 0.0 copy-start
  15.0 1.0 %collective-permute-start.9 = (bf16[128,256]{1,0:T(8,128)(2,1)S(1)}, bf16[128,256]{1,0:T(8,128)(2,1)S(1)}, u32[]{:S(2)}, u32[]{:S(2)}) collective-permute-start(bf16[128,256]{1,0:T(8,128)(2,1)S(1)} %get-tuple-element.34.total_ref.refs_0_), channel_id=1, source_target_pairs={{0,3},{1,2},{2,1},{3,0},{4,7},{5,6},{6,5},{7,4},{8,11},{9,10},{10,... | collective-permute-start | bytes 196616 | tf_op jit(solution)/shard_map/ppermute | solution.py:293
  16.0 0.6 %collective-permute-start.8 = (bf16[128,256]{1,0:T(8,128)(2,1)S(1)}, bf16[128,256]{1,0:T(8,128)(2,1)S(1)}, u32[]{:S(2)}, u32[]{:S(2)}) collective-permute-start(bf16[128,256]{1,0:T(8,128)(2,1)S(1)} %get-tuple-element.34.total_ref.refs_0_), channel_id=1, source_target_pairs={{0,2},{1,3},{2,0},{3,1},{4,6},{5,7},{6,4},{7,5},{8,10},{9,11},{10,... | collective-permute-start | bytes 196616 | tf_op jit(solution)/shard_map/ppermute | solution.py:293
  16.6 0.4 collective-permute-start.7
  16.9 2.6 %collective-permute-start.4 = (f32[64,128]{1,0:T(8,128)S(1)}, f32[64,128]{1,0:T(8,128)S(1)}, u32[]{:S(2)}, u32[]{:S(2)}) collective-permute-start(f32[64,128]{1,0:T(8,128)S(1)} %get-tuple-element.45), channel_id=1, source_target_pairs={{0,8},{1,9},{2,10},{3,11},{4,12},{5,13},{6,14},{7,15},{8,0},{9,1},... | collective-permute-start | bytes 98312 | tf_op jit(solution)/shard_map/ppermute | solution.py:293
  19.5 0.0 collective-permute-done.3.refs_1_
  19.5 0.2 collective-permute-start.5
  19.7 2.3 %collective-permute-done.4.refs_2_ = f32[64,128]{1,0:T(8,128)S(1)} collective-permute-done((f32[64,128]{1,0:T(8,128)S(1)}, f32[64,128]{1,0:T(8,128)S(1)}, u32[]{:S(2)}, u32[]{:S(2)}) %collective-permute-start.4) | collective-permute-done | bytes 32800 | tf_op jit(solution)/shard_map/ppermute | solution.py:293
  22.0 3.2 %collective-permute-done.5.refs_3_ = f32[64,128]{1,0:T(8,128)S(1)} collective-permute-done((f32[64,128]{1,0:T(8,128)S(1)}, f32[64,128]{1,0:T(8,128)S(1)}, u32[]{:S(2)}, u32[]{:S(2)}) %collective-permute-start.5) | collective-permute-done | bytes 32800 | tf_op jit(solution)/shard_map/ppermute | solution.py:293
  25.2 3.0 %local_states.1 = (f32[64,128]{1,0:T(8,128)S(1)}, f32[8,128]{1,0:T(8,128)S(1)}) custom-call(s32[1]{0:T(128)} %bitcast.pos_ref, s32[1,64]{1,0:T(1,128)S(1)} %get-tuple-element.30.levels_ref, bf16[128,128]{1,0:T(8,128)(2,1)S(1)} %get-tuple-element.32.gain_ref, f32[1,128]{1,0:T(1,128)S(1)} %get-tuple-element.31.init_ref, ...), custom_call_target="tpu_custom_call" | custom-call | flops 134217728 | bytes 6291456 | tf_op jit(solution)/shard_map/local_states/pallas_call | solution.py:347
  28.2 0.1 collective-permute-start.6
  28.3 0.0 collective-permute-done.9.refs_3_
  28.3 0.0 collective-permute-done.8.refs_2_
  28.3 0.0 collective-permute-done.7.refs_1_
  28.3 1.1 %collective-permute-done.6.after_ref.refs_1_ = f32[8,128]{1,0:T(8,128)S(1)} collective-permute-done((f32[8,128]{1,0:T(8,128)S(1)}, f32[8,128]{1,0:T(8,128)S(1)}, u32[]{:S(2)}, u32[]{:S(2)}) %collective-permute-start.6) | collective-permute-done | bytes 4128 | tf_op jit(solution)/shard_map/ppermute | solution.py:293
  29.4 0.4 group_maps.1
  29.9 0.1 collective-permute-start.16
  30.0 0.9 %collective-permute-start.15 = (bf16[128,256]{1,0:T(8,128)(2,1)S(1)}, bf16[128,256]{1,0:T(8,128)(2,1)S(1)}, u32[]{:S(2)}, u32[]{:S(2)}) collective-permute-start(bf16[128,256]{1,0:T(8,128)(2,1)S(1)} %get-tuple-element.54), channel_id=1, source_target_pairs={{0,4},{1,5},{2,6},{3,7},{4,8},{5,9},{6,10},{7,11},{8,12},{9,13},{1... | collective-permute-start | bytes 196616 | tf_op jit(solution)/shard_map/ppermute | solution.py:363
  30.9 0.6 %collective-permute-start.11 = (f32[8,128]{1,0:T(8,128)S(1)}, f32[8,128]{1,0:T(8,128)S(1)}, u32[]{:S(2)}, u32[]{:S(2)}) collective-permute-start(f32[8,128]{1,0:T(8,128)S(1)} %get-tuple-element.47.refs_0_), channel_id=1, source_target_pairs={{0,3},{1,2},{2,1},{3,0},{4,7},{5,6},{6,5},{7,4},{8,11},{9,10},{10,... | collective-permute-start | bytes 12296 | tf_op jit(solution)/shard_map/ppermute | solution.py:293
  31.5 0.8 %collective-permute-start.10 = (f32[8,128]{1,0:T(8,128)S(1)}, f32[8,128]{1,0:T(8,128)S(1)}, u32[]{:S(2)}, u32[]{:S(2)}) collective-permute-start(f32[8,128]{1,0:T(8,128)S(1)} %get-tuple-element.47.refs_0_), channel_id=1, source_target_pairs={{0,2},{1,3},{2,0},{3,1},{4,6},{5,7},{6,4},{7,5},{8,10},{9,11},{10,... | collective-permute-start | bytes 12296 | tf_op jit(solution)/shard_map/ppermute | solution.py:293
  32.4 1.6 %collective-permute-done.11.refs_3_ = f32[8,128]{1,0:T(8,128)S(1)} collective-permute-done((f32[8,128]{1,0:T(8,128)S(1)}, f32[8,128]{1,0:T(8,128)S(1)}, u32[]{:S(2)}, u32[]{:S(2)}) %collective-permute-start.11) | collective-permute-done | bytes 4128 | tf_op jit(solution)/shard_map/ppermute | solution.py:293
  34.0 1.2 %collective-permute-done.10.refs_2_ = f32[8,128]{1,0:T(8,128)S(1)} collective-permute-done((f32[8,128]{1,0:T(8,128)S(1)}, f32[8,128]{1,0:T(8,128)S(1)}, u32[]{:S(2)}, u32[]{:S(2)}) %collective-permute-start.10) | collective-permute-done | bytes 4128 | tf_op jit(solution)/shard_map/ppermute | solution.py:293
  35.1 0.4 group_states.1
  35.5 3.2 %collective-permute-start.14 = (f32[8,128]{1,0:T(8,128)S(1)}, f32[8,128]{1,0:T(8,128)S(1)}, u32[]{:S(2)}, u32[]{:S(2)}) collective-permute-start(f32[8,128]{1,0:T(8,128)S(1)} %get-tuple-element.53), channel_id=1, source_target_pairs={{0,12},{1,13},{2,14},{3,15},{4,8},{5,9},{6,10},{7,11},{8,4},{9,5},... | collective-permute-start | bytes 12296 | tf_op jit(solution)/shard_map/ppermute | solution.py:293
  38.7 0.8 %collective-permute-start.13 = (f32[8,128]{1,0:T(8,128)S(1)}, f32[8,128]{1,0:T(8,128)S(1)}, u32[]{:S(2)}, u32[]{:S(2)}) collective-permute-start(f32[8,128]{1,0:T(8,128)S(1)} %get-tuple-element.53), channel_id=1, source_target_pairs={{0,8},{1,9},{2,10},{3,11},{4,12},{5,13},{6,14},{7,15},{8,0},{9,1},... | collective-permute-start | bytes 12296 | tf_op jit(solution)/shard_map/ppermute | solution.py:293
  39.5 0.5 collective-permute-start.12
  39.9 1.0 %collective-permute-done.14.refs_2_ = f32[8,128]{1,0:T(8,128)S(1)} collective-permute-done((f32[8,128]{1,0:T(8,128)S(1)}, f32[8,128]{1,0:T(8,128)S(1)}, u32[]{:S(2)}, u32[]{:S(2)}) %collective-permute-start.14) | collective-permute-done | bytes 4128 | tf_op jit(solution)/shard_map/ppermute | solution.py:293
  40.9 2.2 %collective-permute-done.13.refs_1_ = f32[8,128]{1,0:T(8,128)S(1)} collective-permute-done((f32[8,128]{1,0:T(8,128)S(1)}, f32[8,128]{1,0:T(8,128)S(1)}, u32[]{:S(2)}, u32[]{:S(2)}) %collective-permute-start.13) | collective-permute-done | bytes 4128 | tf_op jit(solution)/shard_map/ppermute | solution.py:293
  43.2 0.0 collective-permute-done.12.refs_0_
  43.2 0.0 collective-permute-done.16.refs_4_
  43.2 0.0 collective-permute-done.15.refs_3_
  43.2 0.0 copy-done
  43.2 2.8 %estimates.1 = f32[64,128]{1,0:T(8,128)} custom-call(s32[1]{0:T(128)} %bitcast.pos_ref, s32[1,64]{1,0:T(1,128)S(1)} %get-tuple-element.30.levels_ref, f32[1,128]{1,0:T(1,128)S(1)} %get-tuple-element.31.init_ref, bf16[128,256]{1,0:T(8,128)(2,1)S(1)} %get-tuple-element.48.prefix_ref, f32[8,128]{1,0:T(8,128)S(1)} %get-tuple-element.50.before_ref, ...), custom_call_target="tpu_custom_call" | custom-call | flops 8388608 | bytes 5242880 | tf_op jit(solution)/shard_map/estimates/pallas_call | solution.py:373
Async XLA Ops:
  1.8 3.2 %collective-permute-start = (bf16[4,64,128]{2,1,0:T(8,128)(2,1)S(1)}, bf16[4,64,128]{2,1,0:T(8,128)(2,1)S(1)}, u32[]{:S(2)}, u32[]{:S(2)}) collective-permute-start(bf16[4,64,128]{2,1,0:T(8,128)(2,1)S(1)} %get-tuple-element.40), channel_id=1, source_target_pairs={{0,1},{1,0},{2,3},{3,2},{4,5},{5,4},{6,7},{7,6},{8,9},{9,8},{10,11... | collective-permute-start | bytes 196616 | tf_op jit(solution)/shard_map/ppermute | solution.py:293
  2.4 5.2 %collective-permute-start.1 = (bf16[4,64,128]{2,1,0:T(8,128)(2,1)S(1)}, bf16[4,64,128]{2,1,0:T(8,128)(2,1)S(1)}, u32[]{:S(2)}, u32[]{:S(2)}) collective-permute-start(bf16[4,64,128]{2,1,0:T(8,128)(2,1)S(1)} %get-tuple-element.41), channel_id=1, source_target_pairs={{0,2},{1,3},{2,0},{3,1},{4,6},{5,7},{6,4},{7,5},{8,10},{9,11},{10,... | collective-permute-start | bytes 196616 | tf_op jit(solution)/shard_map/ppermute | solution.py:293
  4.9 4.0 %collective-permute-start.2 = (bf16[4,64,128]{2,1,0:T(8,128)(2,1)S(1)}, bf16[4,64,128]{2,1,0:T(8,128)(2,1)S(1)}, u32[]{:S(2)}, u32[]{:S(2)}) collective-permute-start(bf16[4,64,128]{2,1,0:T(8,128)(2,1)S(1)} %get-tuple-element.42), channel_id=1, source_target_pairs={{0,3},{1,2},{2,1},{3,0},{4,7},{5,6},{6,5},{7,4},{8,11},{9,10},{10,... | collective-permute-start | bytes 196616 | tf_op jit(solution)/shard_map/ppermute | solution.py:293
  9.2 10.3 %collective-permute-start.3 = (f32[64,128]{1,0:T(8,128)S(1)}, f32[64,128]{1,0:T(8,128)S(1)}, u32[]{:S(2)}, u32[]{:S(2)}) collective-permute-start(f32[64,128]{1,0:T(8,128)S(1)} %get-tuple-element.44), channel_id=1, source_target_pairs={{0,4},{1,5},{2,6},{3,7},{4,0},{5,1},{6,2},{7,3},{8,12},{9,13},{10,... | collective-permute-start | bytes 98312 | tf_op jit(solution)/shard_map/ppermute | solution.py:293
  15.0 28.2 %copy-start = (bf16[31,128,256]{2,1,0:T(8,128)(2,1)S(1)}, bf16[31,128,256]{2,1,0:T(8,128)(2,1)}, u32[]{:S(2)}) copy-start(bf16[31,128,256]{2,1,0:T(8,128)(2,1)} %get-tuple-element.52.left_ref) | copy-start | bytes 6094852
  15.0 13.3 %collective-permute-start.9 = (bf16[128,256]{1,0:T(8,128)(2,1)S(1)}, bf16[128,256]{1,0:T(8,128)(2,1)S(1)}, u32[]{:S(2)}, u32[]{:S(2)}) collective-permute-start(bf16[128,256]{1,0:T(8,128)(2,1)S(1)} %get-tuple-element.34.total_ref.refs_0_), channel_id=1, source_target_pairs={{0,3},{1,2},{2,1},{3,0},{4,7},{5,6},{6,5},{7,4},{8,11},{9,10},{10,... | collective-permute-start | bytes 196616 | tf_op jit(solution)/shard_map/ppermute | solution.py:293
  16.0 12.3 %collective-permute-start.8 = (bf16[128,256]{1,0:T(8,128)(2,1)S(1)}, bf16[128,256]{1,0:T(8,128)(2,1)S(1)}, u32[]{:S(2)}, u32[]{:S(2)}) collective-permute-start(bf16[128,256]{1,0:T(8,128)(2,1)S(1)} %get-tuple-element.34.total_ref.refs_0_), channel_id=1, source_target_pairs={{0,2},{1,3},{2,0},{3,1},{4,6},{5,7},{6,4},{7,5},{8,10},{9,11},{10,... | collective-permute-start | bytes 196616 | tf_op jit(solution)/shard_map/ppermute | solution.py:293
  16.6 11.7 %collective-permute-start.7 = (bf16[128,256]{1,0:T(8,128)(2,1)S(1)}, bf16[128,256]{1,0:T(8,128)(2,1)S(1)}, u32[]{:S(2)}, u32[]{:S(2)}) collective-permute-start(bf16[128,256]{1,0:T(8,128)(2,1)S(1)} %get-tuple-element.34.total_ref.refs_0_), channel_id=1, source_target_pairs={{0,1},{1,0},{2,3},{3,2},{4,5},{5,4},{6,7},{7,6},{8,9},{9,8},{10,11... | collective-permute-start | bytes 196616 | tf_op jit(solution)/shard_map/ppermute | solution.py:293
  16.9 5.1 %collective-permute-start.4 = (f32[64,128]{1,0:T(8,128)S(1)}, f32[64,128]{1,0:T(8,128)S(1)}, u32[]{:S(2)}, u32[]{:S(2)}) collective-permute-start(f32[64,128]{1,0:T(8,128)S(1)} %get-tuple-element.45), channel_id=1, source_target_pairs={{0,8},{1,9},{2,10},{3,11},{4,12},{5,13},{6,14},{7,15},{8,0},{9,1},... | collective-permute-start | bytes 98312 | tf_op jit(solution)/shard_map/ppermute | solution.py:293
  19.5 5.7 %collective-permute-start.5 = (f32[64,128]{1,0:T(8,128)S(1)}, f32[64,128]{1,0:T(8,128)S(1)}, u32[]{:S(2)}, u32[]{:S(2)}) collective-permute-start(f32[64,128]{1,0:T(8,128)S(1)} %get-tuple-element.46), channel_id=1, source_target_pairs={{0,12},{1,13},{2,14},{3,15},{4,8},{5,9},{6,10},{7,11},{8,4},{9,5},... | collective-permute-start | bytes 98312 | tf_op jit(solution)/shard_map/ppermute | solution.py:293
  28.2 1.2 %collective-permute-start.6 = (f32[8,128]{1,0:T(8,128)S(1)}, f32[8,128]{1,0:T(8,128)S(1)}, u32[]{:S(2)}, u32[]{:S(2)}) collective-permute-start(f32[8,128]{1,0:T(8,128)S(1)} %get-tuple-element.47.refs_0_), channel_id=1, source_target_pairs={{0,1},{1,0},{2,3},{3,2},{4,5},{5,4},{6,7},{7,6},{8,9},{9,8},{10,11... | collective-permute-start | bytes 12296 | tf_op jit(solution)/shard_map/ppermute | solution.py:293
  29.9 13.3 %collective-permute-start.16 = (bf16[128,256]{1,0:T(8,128)(2,1)S(1)}, bf16[128,256]{1,0:T(8,128)(2,1)S(1)}, u32[]{:S(2)}, u32[]{:S(2)}) collective-permute-start(bf16[128,256]{1,0:T(8,128)(2,1)S(1)} %get-tuple-element.54), channel_id=1, source_target_pairs={{0,8},{1,9},{2,10},{3,11},{4,12},{5,13},{6,14},{7,15},{8,0},{9,1},... | collective-permute-start | bytes 196616 | tf_op jit(solution)/shard_map/ppermute | solution.py:363
  30.0 13.2 %collective-permute-start.15 = (bf16[128,256]{1,0:T(8,128)(2,1)S(1)}, bf16[128,256]{1,0:T(8,128)(2,1)S(1)}, u32[]{:S(2)}, u32[]{:S(2)}) collective-permute-start(bf16[128,256]{1,0:T(8,128)(2,1)S(1)} %get-tuple-element.54), channel_id=1, source_target_pairs={{0,4},{1,5},{2,6},{3,7},{4,8},{5,9},{6,10},{7,11},{8,12},{9,13},{1... | collective-permute-start | bytes 196616 | tf_op jit(solution)/shard_map/ppermute | solution.py:363
  30.9 3.0 %collective-permute-start.11 = (f32[8,128]{1,0:T(8,128)S(1)}, f32[8,128]{1,0:T(8,128)S(1)}, u32[]{:S(2)}, u32[]{:S(2)}) collective-permute-start(f32[8,128]{1,0:T(8,128)S(1)} %get-tuple-element.47.refs_0_), channel_id=1, source_target_pairs={{0,3},{1,2},{2,1},{3,0},{4,7},{5,6},{6,5},{7,4},{8,11},{9,10},{10,... | collective-permute-start | bytes 12296 | tf_op jit(solution)/shard_map/ppermute | solution.py:293
  31.5 3.6 %collective-permute-start.10 = (f32[8,128]{1,0:T(8,128)S(1)}, f32[8,128]{1,0:T(8,128)S(1)}, u32[]{:S(2)}, u32[]{:S(2)}) collective-permute-start(f32[8,128]{1,0:T(8,128)S(1)} %get-tuple-element.47.refs_0_), channel_id=1, source_target_pairs={{0,2},{1,3},{2,0},{3,1},{4,6},{5,7},{6,4},{7,5},{8,10},{9,11},{10,... | collective-permute-start | bytes 12296 | tf_op jit(solution)/shard_map/ppermute | solution.py:293
  35.5 5.4 %collective-permute-start.14 = (f32[8,128]{1,0:T(8,128)S(1)}, f32[8,128]{1,0:T(8,128)S(1)}, u32[]{:S(2)}, u32[]{:S(2)}) collective-permute-start(f32[8,128]{1,0:T(8,128)S(1)} %get-tuple-element.53), channel_id=1, source_target_pairs={{0,12},{1,13},{2,14},{3,15},{4,8},{5,9},{6,10},{7,11},{8,4},{9,5},... | collective-permute-start | bytes 12296 | tf_op jit(solution)/shard_map/ppermute | solution.py:293
  38.7 4.5 %collective-permute-start.13 = (f32[8,128]{1,0:T(8,128)S(1)}, f32[8,128]{1,0:T(8,128)S(1)}, u32[]{:S(2)}, u32[]{:S(2)}) collective-permute-start(f32[8,128]{1,0:T(8,128)S(1)} %get-tuple-element.53), channel_id=1, source_target_pairs={{0,8},{1,9},{2,10},{3,11},{4,12},{5,13},{6,14},{7,15},{8,0},{9,1},... | collective-permute-start | bytes 12296 | tf_op jit(solution)/shard_map/ppermute | solution.py:293
  39.5 3.7 %collective-permute-start.12 = (f32[8,128]{1,0:T(8,128)S(1)}, f32[8,128]{1,0:T(8,128)S(1)}, u32[]{:S(2)}, u32[]{:S(2)}) collective-permute-start(f32[8,128]{1,0:T(8,128)S(1)} %get-tuple-element.53), channel_id=1, source_target_pairs={{0,4},{1,5},{2,6},{3,7},{4,0},{5,1},{6,2},{7,3},{8,12},{9,13},{10,... | collective-permute-start | bytes 12296 | tf_op jit(solution)/shard_map/ppermute | solution.py:293

commit v8 on v7

--- a/solution.py
+++ b/solution.py
@@ -21,12 +21,12 @@
     return pltpu.with_memory_space_constraint(x, pltpu.HBM)
 
 
-def call(kernel, name, mib, flops, moved, **kw):
+def call(kernel, name, mib, **kw):
     return pl.pallas_call(
         kernel,
         name=name,
         compiler_params=pltpu.CompilerParams(vmem_limit_bytes=mib * MIB),
-        cost_estimate=pl.CostEstimate(flops=flops, bytes_accessed=moved, transcendentals=0),
+        cost_estimate=pl.CostEstimate(flops=1, bytes_accessed=1, transcendentals=0),
         **kw,
     )
 
@@ -100,7 +100,7 @@
         copy.wait()
 
 
-def project_kernel(size, pos_ref, mode_ref, weight_ref, *refs):
+def project_kernel(size, pos_ref, after_ref, mode_ref, weight_ref, *refs):
     slabs, outs, (sums, weights) = refs[:size], refs[size:-2], refs[-2:]
     weights[...] = weight_ref[...].astype(F32)
     groups, steps, width = slabs[0].shape
@@ -118,7 +118,7 @@
         outs[r][...] = sums[(position // size) ^ r]
 
 
-def tree_kernel(steps, levels_ref, table_ref, left_hbm, right_hbm, table_hbm, total_ref, left_ref, right_ref, sems):
+def tree_kernel(steps, levels_ref, table_ref, left_hbm, right_hbm, total_ref, left_ref, right_ref, sems):
     base = steps // 4
 
     def first(t):
@@ -150,8 +150,7 @@
 
         lax.fori_loop(0, count // 4, body, 0)
 
-    copies = [pltpu.make_async_copy(table_ref, table_hbm, sems.at[0])]
-    copies[0].start()
+    copies = []
 
     def store(start, count):
         for ref, hbm in ((right_ref, right_hbm), (left_ref, left_hbm)):
@@ -174,14 +173,13 @@
         copy.wait()
 
 
-def local_kernel(pos_ref, levels_ref, gain_ref, init_ref, total_ref, table_hbm, right_hbm, *refs):
-    parts, (lefts_ref, shift_ref, drive_ref, table_ref, right_ref, sems) = refs[:-6], refs[-6:]
+def local_kernel(pos_ref, levels_ref, gain_ref, init_ref, total_ref, table_ref, right_hbm, *refs):
+    parts, (lefts_ref, own_ref, drive_ref, right_ref, sems) = refs[:-5], refs[-5:]
     steps, n = drive_ref.shape
     base = steps // 4
     copies = [
-        pltpu.make_async_copy(table_hbm, table_ref, sems.at[0]),
-        pltpu.make_async_copy(right_hbm.at[pl.ds(0, base)], right_ref.at[pl.ds(0, base)], sems.at[1]),
-        pltpu.make_async_copy(right_hbm.at[pl.ds(base, base - 1)], right_ref.at[pl.ds(base, base - 1)], sems.at[2]),
+        pltpu.make_async_copy(right_hbm.at[pl.ds(0, base)], right_ref.at[pl.ds(0, base)], sems.at[0]),
+        pltpu.make_async_copy(right_hbm.at[pl.ds(base, base - 1)], right_ref.at[pl.ds(base, base - 1)], sems.at[1]),
     ]
     for copy in copies:
         copy.start()
@@ -193,8 +191,8 @@
     states = [row(drive_ref, t) for t in range(steps)]
     at, offset = 0, 0
     for level in range(steps.bit_length() - 1):
-        if level < 3:
-            copies[level].wait()
+        if level in (1, 2):
+            copies[level - 1].wait()
         later = []
         for i in range(len(states) // 2):
             mat = table_ref[levels_ref[0, 2 * i + 1]] if level == 0 else right_ref[offset + i]
@@ -206,55 +204,61 @@
         states = later
     lefts_ref[pl.ds(at, 1), :] = states[0][:1]
     first = jnp.where(pos_ref[0] == 0, row(init_ref, 0), 0.0)
-    shift_ref[...] = states[0] + vm(first, total_ref[...])
-
-
-def group_kernel(size, pos_ref, after_ref, *refs):
+    total = total_ref[...]
+    own_ref[pl.ds(0, n), :] = total
+    own_ref[pl.ds(n, 16), :] = rows16(states[0] + vm(first, total))
+
+
+def rows16(vec):
+    high = vec.astype(BF16).astype(F32)
+    both = jnp.concatenate([high, vec - high], axis=1)
+    return jnp.concatenate([both, both], axis=0).astype(BF16)
+
+
+def rows8(rows):
+    both = rows.astype(F32)
+    n = rows.shape[1] // 2
+    return both[:8, :n] + both[:8, n:]
+
+
+def group_kernel(size, pos_ref, *refs):
     blocks = refs[:size]
-    all_ref, prefix_ref, whole_ref = refs[size:]
-    n = whole_ref.shape[0]
+    prefix_ref, before_ref, mine_ref, shift_ref, all_ref = refs[size:]
+    n = prefix_ref.shape[0]
     member = pos_ref[0] % size
     for r in range(size):
         all_ref[member ^ r] = blocks[r][...]
+
+    def block(q):
+        return all_ref[q, :n, :], rows8(all_ref[q, n:, :])
+
     rows, cols = (lax.broadcasted_iota(jnp.int32, (n, n), d) for d in (0, 1))
-    prefix = pair((rows == cols).astype(F32))
-    run = all_ref[0]
+    prefix, before = pair((rows == cols).astype(F32)), jnp.zeros((8, n), F32)
+    run, vec = block(0)
     for q in range(1, size):
-        prefix = jnp.where(member == q, run, prefix)
-        run = pair(mm(run, all_ref[q]))
+        here = member == q
+        prefix, before = jnp.where(here, run, prefix), jnp.where(here, vec, before)
+        step, shift = block(q)
+        vec = vm(vec, step) + shift
+        run = pair(mm(run, step))
     prefix_ref[...] = prefix
-    whole_ref[...] = run
-
-
-def beside_kernel(size, pos_ref, all_ref, *refs):
-    shifts = refs[:size]
-    before_ref, whole_ref, held_ref = refs[size:]
-    member = pos_ref[0] % size
-    for r in range(size):
-        held_ref[member ^ r] = shifts[r][...]
-    run, before = held_ref[0], jnp.zeros(before_ref.shape, F32)
-    for q in range(1, size):
-        before = jnp.where(member == q, run, before)
-        run = vm(run, all_ref[q]) + held_ref[q]
     before_ref[...] = before
-    whole_ref[...] = run
-
-
-def final_kernel(size, groups, pos_ref, levels_ref, init_ref, prefix_ref, before_ref, total_ref, lefts_ref, left_ref, table_hbm, *refs):
-    shifts, wholes = refs[: groups - 1], refs[groups - 1 : 2 * groups - 3]
-    out_ref, sums_ref, table_ref, sem = refs[2 * groups - 3 :]
-    copy = pltpu.make_async_copy(table_hbm, table_ref, sem)
-    copy.start()
+    mine_ref[pl.ds(0, n), :] = run
+    mine_ref[pl.ds(n, 16), :] = rows16(vec)
+    shift_ref[...] = rows16(vec)
+
+
+def final_kernel(size, pos_ref, levels_ref, init_ref, prefix_ref, before_ref, total_ref, lefts_ref, left_ref, table_ref, *refs):
+    got, out_ref = refs[:-1], refs[-1]
     steps, n = lefts_ref.shape
     position = pos_ref[0]
     group = position // size
-    for r in range(1, groups):
-        sums_ref[group ^ r] = shifts[r - 1][...]
     state = jnp.zeros((8, n), F32)
-    for r in range(groups - 1, 0, -1):
-        if r < groups - 1:
-            state = jnp.where(group > r, vm(state, wholes[r - 1][...]), 0.0)
-        state += jnp.where(group >= r, sums_ref[jnp.maximum(group - r, 0)], 0.0)
+    for r in range(len(got), 0, -1):
+        rows = got[r - 1].shape[0]
+        if rows > 16:
+            state = jnp.where(group > r, vm(state, got[r - 1][pl.ds(0, n), :]), 0.0)
+        state += jnp.where(group >= r, rows8(got[r - 1][pl.ds(rows - 16, 16), :]), 0.0)
     first = jnp.where(position == 0, row(init_ref, 0), 0.0)
     state = vm(state, prefix_ref[...]) + before_ref[...] + first
     out_ref[pl.ds(steps - 1, 1), :] = (vm(state, total_ref[...]) + row(lefts_ref, steps - 1))[:1]
@@ -262,8 +266,6 @@
     starts = [state]
     sizes = [steps >> (level + 1) for level in range(levels)]
     for level in reversed(range(levels)):
-        if level == 0:
-            copy.wait()
         at, offset = sum(sizes[:level]), sum(sizes[1:level])
         later = []
         for i, x in enumerate(starts):
@@ -307,21 +309,31 @@
         outs += [shape((groups, steps, pixels), BF16)] * size
         buffers += [pltpu.VMEM(frames.shape, BF16), pltpu.VMEM((length, pixels), BF16)]
     table, levels, initial_state, gain, *rest = call(
-        functools.partial(front_kernel, cuts, len(small), size), "front", 5, 0, 4 * MIB,
+        functools.partial(front_kernel, cuts, len(small), size), "front", 5,
         out_shape=outs,
         in_specs=[SMEM] + [HBM] * len(given),
         out_specs=[VMEM] * len(outs),
         scratch_shapes=buffers + [dma((cuts + 4 + len(small),))],
     )(position, *given)
+    tree = pltpu.VMEM((pairs, n, 2 * n), BF16)
+    maps = pltpu.HBM((pairs, n, 2 * n), BF16)
+    left, right, total = call(
+        functools.partial(tree_kernel, steps), "tree_of_maps", 8,
+        out_shape=[maps, maps, one_map],
+        in_specs=[SMEM, VMEM],
+        out_specs=[HBM, HBM, VMEM],
+        scratch_shapes=[tree, tree, dma((6,))],
+    )(levels, table)
+
     if turn:
         mode, weight, slab, *slabs = rest
         first, *parts = call(
-            functools.partial(project_kernel, size), "project", 4, 1 << 25, MIB,
+            functools.partial(project_kernel, size), "project", 4,
             out_shape=[shape((steps, n), F32)] * groups,
-            in_specs=[SMEM] + [VMEM] * (2 + size),
+            in_specs=[SMEM] + [VMEM] * (3 + size),
             out_specs=[VMEM] * groups,
             scratch_shapes=[pltpu.VMEM((groups, steps, n), F32), pltpu.VMEM((count, pixels), F32)],
-        )(position, mode, weight, slab, *swaps(slabs, 1, size))
+        )(position, total, mode, weight, slab, *swaps(slabs, 1, size))
         parts = [first] + swaps(parts, size, groups)
     else:
         x = lax.all_to_all(frames, "tm", split_axis=1, concat_axis=0, tiled=True)
@@ -329,54 +341,32 @@
         projector = jnp.where(pixel_mode[None, :] == channels[:, None], pixel_weight[None, :], jnp.zeros((), BF16))
         parts = [lax.dot_general(x, projector, (((0,), (1,)), ((), ())), preferred_element_type=F32)]
 
-    tree = pltpu.VMEM((pairs, n, 2 * n), BF16)
-    table_vmem = pltpu.VMEM(table_shape.shape, BF16)
-    maps = pltpu.HBM((pairs, n, 2 * n), BF16)
-    left, right, table, total = call(
-        functools.partial(tree_kernel, steps), "tree_of_maps", 8, 2 * steps * n**3 * 4, 8 * MIB,
-        out_shape=[maps, maps, pltpu.HBM(table_shape.shape, BF16), one_map],
-        in_specs=[SMEM, VMEM],
-        out_specs=[HBM, HBM, HBM, VMEM],
-        scratch_shapes=[tree, tree, dma((7,))],
-    )(levels, table)
-    right, table = hbm(right), hbm(table)
-
-    vector = shape((8, n), F32)
-
-    members = swaps(total, 1, size)
-    lefts, shift = call(
-        local_kernel, "local_states", 8, 1 << 27, 6 * MIB,
-        out_shape=[shape((steps, n), F32), vector],
-        in_specs=[SMEM, SMEM] + [VMEM] * 3 + [HBM] * 2 + [VMEM] * len(parts),
+    block = shape((n + 16, 2 * n), BF16)
+    lefts, own = call(
+        local_kernel, "local_states", 8,
+        out_shape=[shape((steps, n), F32), block],
+        in_specs=[SMEM, SMEM] + [VMEM] * 4 + [HBM] + [VMEM] * len(parts),
         out_specs=[VMEM] * 2,
-        scratch_shapes=[pltpu.VMEM((steps, n), F32), table_vmem, tree, dma((3,))],
-    )(position, levels, gain, initial_state, total, table, right, *parts)
-    shifts = swaps(shift, 1, size)
-
-    group_maps, prefix, whole = call(
-        functools.partial(group_kernel, size), "group_maps", 2, 1 << 24, MIB,
-        out_shape=[shape((size, n, 2 * n), BF16), one_map, one_map],
-        in_specs=[SMEM] + [VMEM] * (1 + size),
-        out_specs=[VMEM] * 3,
-    )(position, shifts[0], total, *members)
-    wholes = [
-        lax.ppermute(whole, "tm", [(j, (j + r * size) % count) for j in range(count)]) for r in range(1, groups - 1)
+        scratch_shapes=[pltpu.VMEM((steps, n), F32), tree, dma((2,))],
+    )(position, levels, gain, initial_state, total, table, hbm(right), *parts)
+    prefix, before, mine, carried = call(
+        functools.partial(group_kernel, size), "group_maps", 2,
+        out_shape=[one_map, shape((8, n), F32), block, shape((16, 2 * n), BF16)],
+        in_specs=[SMEM] + [VMEM] * size,
+        out_specs=[VMEM] * 4,
+        scratch_shapes=[pltpu.VMEM((size, n + 16, 2 * n), BF16)],
+    )(position, own, *swaps(own, 1, size))
+    got = [
+        lax.ppermute(mine if r < groups - 1 else carried, "tm", [(j, (j + r * size) % count) for j in range(count)])
+        for r in range(1, groups)
     ]
-    before, carried = call(
-        functools.partial(beside_kernel, size), "group_states", 2, 1 << 20, MIB // 4,
-        out_shape=[vector, vector],
-        in_specs=[SMEM] + [VMEM] * (1 + size),
-        out_specs=[VMEM] * 2,
-        scratch_shapes=[pltpu.VMEM((size, 8, n), F32)],
-    )(position, group_maps, shift, *shifts)
 
     return call(
-        functools.partial(final_kernel, size, groups), "estimates", 6, 1 << 23, 5 * MIB,
+        functools.partial(final_kernel, size), "estimates", 6,
         out_shape=shape((steps, n), F32),
-        in_specs=[SMEM, SMEM] + [VMEM] * 6 + [HBM] + [VMEM] * (2 * groups - 3),
+        in_specs=[SMEM, SMEM] + [VMEM] * (7 + len(got)),
         out_specs=VMEM,
-        scratch_shapes=[pltpu.VMEM((groups, 8, n), F32), table_vmem, dma(())],
-    )(position, levels, initial_state, prefix, before, total, lefts, left, table, *swaps(carried, size, groups), *wholes)
+    )(position, levels, initial_state, prefix, before, total, lefts, left, table, *got)
 
 
 def solution(mesh):

time: 46.2 us -> 38.8 us (0.84)
  waiting for transfers between devices: 16.7 us -> 13 us
  starting transfers between devices: 16.4 us -> 13.5 us
  Pallas kernels: 12.8 us -> 12 us
    ppermute x15 -> x9, waiting for transfers between devices: 16.7 us -> 10 us  [swaps(): lax.ppermute(a, 'tm', [(j, j ^ r * step) for j in range(count)])]
    ppermute x15 -> x9, starting transfers between devices: 15.4 us -> 9.54 us  [swaps(): lax.ppermute(a, 'tm', [(j, j ^ r * step) for j in range(count)])]
    ppermute x2 -> x3, waiting for transfers between devices: 0.01 us -> 3.03 us  [shards(): lax.ppermute(mine if r < groups - 1 else carried, 'tm', [(j, (j + r * siz...]
    ppermute x2 -> x3, starting transfers between devices: 1.01 us -> 3.95 us  [shards(): lax.ppermute(mine if r < groups - 1 else carried, 'tm', [(j, (j + r * siz...]
    pallas_call x6 -> x5, Pallas kernels: 11 us -> 10.2 us  [the longest x1 4.08 us: shards(): call(functools.partial(tree_kernel, steps), 'tree_of_maps', 8, out_shape=...]
  transfers between devices with their start and end apart: 17 -> 12, of which waited for: 9 -> 6; matrix products, arithmetic and copies ran while one was open for 0% -> 0% of each run, Pallas kernels for 16% -> 11%
where the time goes in v8:
time: 38.8 us; the launch traced here: 38.6 us
  starting transfers between devices  13.5 us (35%)
  waiting for transfers between devices  13 us (34%)
  Pallas kernels  12 us (31%)
    ppermute x9, waiting for transfers between devices, swaps(): lax.ppermute(a, 'tm', [(j, j ^ r * step) for j in range(count)])  10 us
    ppermute x9, starting transfers between devices, swaps(): lax.ppermute(a, 'tm', [(j, j ^ r * step) for j in range(count)])  9.54 us
    pallas_call x1, Pallas kernels, shards(): call(functools.partial(tree_kernel, steps), 'tree_of_maps', 8, out_shape=...  4.08 us
    ppermute x3, starting transfers between devices, shards(): lax.ppermute(mine if r < groups - 1 else carried, 'tm', [(j, (j + r * siz...  3.95 us
    ppermute x3, waiting for transfers between devices, shards(): lax.ppermute(mine if r < groups - 1 else carried, 'tm', [(j, (j + r * siz...  3.03 us
    pallas_call x1, Pallas kernels, shards(): call(local_kernel, 'local_states', 8, out_shape=[shape((steps, n), F32),...  2.95 us
    pallas_call x1, Pallas kernels, shards(): call(functools.partial(final_kernel, size), 'estimates', 6, out_shape=sha...  2.44 us
    pallas_call x1, Pallas kernels, shards(): call(functools.partial(front_kernel, cuts, len(small), size), 'front', 5,...  1.83 us
  transfers between devices with their start and end apart: 12, of which 6 were waited for; matrix products, arithmetic and copies ran while one was open for 0% of the time, Pallas kernels for 11%

profile of v8, /device:TPU:0, one launch (start us, length us, event | category | flops | bytes accessed | tf_op | source)
XLA Modules:
  0.0 38.6 jit_solution(340103111372974007)
XLA Ops:
  0.0 1.8 %front.1 = (bf16[16,128,256]{2,1,0:T(8,128)(2,1)S(1)}, s32[1,64]{1,0:T(1,128)S(1)}, f32[1,128]{1,0:T(1,128)S(1)}, bf16[128,128]{1,0:T(8,128)(2,1)S(1)}, s32[16,1...) custom-call(s32[1]{0:T(128)} %bitcast.pos_ref, ...), custom_call_target="tpu_custom_call" | custom-call | flops 1 | bytes 1 | tf_op jit(solution)/shard_map/front/pallas_call | solution.py:311
  1.8 0.5 %collective-permute-start = (bf16[4,64,128]{2,1,0:T(8,128)(2,1)S(1)}, bf16[4,64,128]{2,1,0:T(8,128)(2,1)S(1)}, u32[]{:S(2)}, u32[]{:S(2)}) collective-permute-start(bf16[4,64,128]{2,1,0:T(8,128)(2,1)S(1)} %get-tuple-element.37), channel_id=1, source_target_pairs={{0,1},{1,0},{2,3},{3,2},{4,5},{5,4},{6,7},{7,6},{8,9},{9,8},{10,11... | collective-permute-start | bytes 196616 | tf_op jit(solution)/shard_map/ppermute | solution.py:295
  2.4 2.6 %collective-permute-start.1 = (bf16[4,64,128]{2,1,0:T(8,128)(2,1)S(1)}, bf16[4,64,128]{2,1,0:T(8,128)(2,1)S(1)}, u32[]{:S(2)}, u32[]{:S(2)}) collective-permute-start(bf16[4,64,128]{2,1,0:T(8,128)(2,1)S(1)} %get-tuple-element.38), channel_id=1, source_target_pairs={{0,2},{1,3},{2,0},{3,1},{4,6},{5,7},{6,4},{7,5},{8,10},{9,11},{10,... | collective-permute-start | bytes 196616 | tf_op jit(solution)/shard_map/ppermute | solution.py:295
  4.9 0.1 collective-permute-start.2
  5.0 4.1 %tree_of_maps.1 = (bf16[31,128,256]{2,1,0:T(8,128)(2,1)}, bf16[31,128,256]{2,1,0:T(8,128)(2,1)}, bf16[128,256]{1,0:T(8,128)(2,1)S(1)}) custom-call(s32[1,64]{1,0:T(1,128)S(1)} %get-tuple-element.28.levels_ref, bf16[16,128,256]{2,1,0:T(8,128)(2,1)S(1)} %get-tuple-element.31.table_ref), custom_call_target="tpu_custom_call" | custom-call | flops 1 | bytes 1 | tf_op jit(solution)/shard_map/tree_of_maps/pallas_call | solution.py:320
  9.1 0.0 copy-start
  9.1 0.0 collective-permute-done.refs_1_
  9.1 0.0 collective-permute-done.1.refs_2_
  9.1 0.0 collective-permute-done.2.refs_3_
  9.1 0.3 project.1
  9.4 1.9 %collective-permute-start.3 = (f32[64,128]{1,0:T(8,128)S(1)}, f32[64,128]{1,0:T(8,128)S(1)}, u32[]{:S(2)}, u32[]{:S(2)}) collective-permute-start(f32[64,128]{1,0:T(8,128)S(1)} %get-tuple-element.41), channel_id=1, source_target_pairs={{0,4},{1,5},{2,6},{3,7},{4,0},{5,1},{6,2},{7,3},{8,12},{9,13},{10,... | collective-permute-start | bytes 98312 | tf_op jit(solution)/shard_map/ppermute | solution.py:295
  11.3 2.6 %collective-permute-start.4 = (f32[64,128]{1,0:T(8,128)S(1)}, f32[64,128]{1,0:T(8,128)S(1)}, u32[]{:S(2)}, u32[]{:S(2)}) collective-permute-start(f32[64,128]{1,0:T(8,128)S(1)} %get-tuple-element.42), channel_id=1, source_target_pairs={{0,8},{1,9},{2,10},{3,11},{4,12},{5,13},{6,14},{7,15},{8,0},{9,1},... | collective-permute-start | bytes 98312 | tf_op jit(solution)/shard_map/ppermute | solution.py:295
  13.9 0.0 collective-permute-start.5
  13.9 0.0 collective-permute-done.3.refs_1_
  13.9 2.8 %collective-permute-done.4.refs_2_ = f32[64,128]{1,0:T(8,128)S(1)} collective-permute-done((f32[64,128]{1,0:T(8,128)S(1)}, f32[64,128]{1,0:T(8,128)S(1)}, u32[]{:S(2)}, u32[]{:S(2)}) %collective-permute-start.4) | collective-permute-done | bytes 32800 | tf_op jit(solution)/shard_map/ppermute | solution.py:295
  16.7 2.9 %collective-permute-done.5.refs_3_ = f32[64,128]{1,0:T(8,128)S(1)} collective-permute-done((f32[64,128]{1,0:T(8,128)S(1)}, f32[64,128]{1,0:T(8,128)S(1)}, u32[]{:S(2)}, u32[]{:S(2)}) %collective-permute-start.5) | collective-permute-done | bytes 32800 | tf_op jit(solution)/shard_map/ppermute | solution.py:295
  19.6 3.0 %local_states.1 = (f32[64,128]{1,0:T(8,128)S(1)}, bf16[144,256]{1,0:T(8,128)(2,1)S(1)}) custom-call(s32[1]{0:T(128)} %bitcast.pos_ref, s32[1,64]{1,0:T(1,128)S(1)} %get-tuple-element.28.levels_ref, bf16[128,128]{1,0:T(8,128)(2,1)S(1)} %get-tuple-element.30.gain_ref, f32[1,128]{1,0:T(1,128)S(1)} %get-tuple-element.29.init_ref, ...), custom_call_target="tpu_custom_call" | custom-call | flops 1 | bytes 1 | tf_op jit(solution)/shard_map/local_states/pallas_call | solution.py:345
  22.5 0.1 collective-permute-start.8
  22.6 1.6 %collective-permute-start.7 = (bf16[144,256]{1,0:T(8,128)(2,1)S(1)}, bf16[144,256]{1,0:T(8,128)(2,1)S(1)}, u32[]{:S(2)}, u32[]{:S(2)}) collective-permute-start(bf16[144,256]{1,0:T(8,128)(2,1)S(1)} %get-tuple-element.44.refs_0_), channel_id=1, source_target_pairs={{0,2},{1,3},{2,0},{3,1},{4,6},{5,7},{6,4},{7,5},{8,10},{9,11},{10,... | collective-permute-start | bytes 221192 | tf_op jit(solution)/shard_map/ppermute | solution.py:295
  24.2 0.3 collective-permute-start.6
  24.5 2.7 %collective-permute-done.8.refs_3_ = bf16[144,256]{1,0:T(8,128)(2,1)S(1)} collective-permute-done((bf16[144,256]{1,0:T(8,128)(2,1)S(1)}, bf16[144,256]{1,0:T(8,128)(2,1)S(1)}, u32[]{:S(2)}, u32[]{:S(2)}) %collective-permute-start.8) | collective-permute-done | bytes 73760 | tf_op jit(solution)/shard_map/ppermute | solution.py:295
  27.1 1.6 %collective-permute-done.7.refs_2_ = bf16[144,256]{1,0:T(8,128)(2,1)S(1)} collective-permute-done((bf16[144,256]{1,0:T(8,128)(2,1)S(1)}, bf16[144,256]{1,0:T(8,128)(2,1)S(1)}, u32[]{:S(2)}, u32[]{:S(2)}) %collective-permute-start.7) | collective-permute-done | bytes 73760 | tf_op jit(solution)/shard_map/ppermute | solution.py:295
  28.7 0.0 collective-permute-done.6.refs_1_
  28.7 0.4 %group_maps.1 = (bf16[128,256]{1,0:T(8,128)(2,1)S(1)}, f32[8,128]{1,0:T(8,128)S(1)}, bf16[144,256]{1,0:T(8,128)(2,1)S(1)}, bf16[16,256]{1,0:T(8,128)(2,1)S(1)}) custom-call(s32[1]{0:T(128)} %bitcast.pos_ref, bf16[144,256]{1,0:T(8,128)(2,1)S(1)} %get-tuple-element.44.refs_0_, bf16[144,256]{1,0:T(8,128)(2,1)S(1)} %collective-permute-done.6.refs_1_, ...), custom_call_target="tpu_custom_call" | custom-call | flops 1 | bytes 1 | tf_op jit(solution)/shard_map/group_maps/pallas_call | solution.py:352
  29.2 0.1 collective-permute-start.10
  29.3 0.9 %collective-permute-start.9 = (bf16[144,256]{1,0:T(8,128)(2,1)S(1)}, bf16[144,256]{1,0:T(8,128)(2,1)S(1)}, u32[]{:S(2)}, u32[]{:S(2)}) collective-permute-start(bf16[144,256]{1,0:T(8,128)(2,1)S(1)} %get-tuple-element.49), channel_id=1, source_target_pairs={{0,4},{1,5},{2,6},{3,7},{4,8},{5,9},{6,10},{7,11},{8,12},{9,13},{1... | collective-permute-start | bytes 221192 | tf_op jit(solution)/shard_map/ppermute | solution.py:360
  30.2 2.9 %collective-permute-start.11 = (bf16[16,256]{1,0:T(8,128)(2,1)S(1)}, bf16[16,256]{1,0:T(8,128)(2,1)S(1)}, u32[]{:S(2)}, u32[]{:S(2)}) collective-permute-start(bf16[16,256]{1,0:T(8,128)(2,1)S(1)} %get-tuple-element.50), channel_id=1, source_target_pairs={{0,12},{1,13},{2,14},{3,15},{4,0},{5,1},{6,2},{7,3},{8,4},{9,5},{1... | collective-permute-start | bytes 24584 | tf_op jit(solution)/shard_map/ppermute | solution.py:360
  33.2 2.5 %collective-permute-done.11.refs_2_ = bf16[16,256]{1,0:T(8,128)(2,1)S(1)} collective-permute-done((bf16[16,256]{1,0:T(8,128)(2,1)S(1)}, bf16[16,256]{1,0:T(8,128)(2,1)S(1)}, u32[]{:S(2)}, u32[]{:S(2)}) %collective-permute-start.11) | collective-permute-done | bytes 8224 | tf_op jit(solution)/shard_map/ppermute | solution.py:360
  35.6 0.5 %collective-permute-done.10.refs_1_ = bf16[144,256]{1,0:T(8,128)(2,1)S(1)} collective-permute-done((bf16[144,256]{1,0:T(8,128)(2,1)S(1)}, bf16[144,256]{1,0:T(8,128)(2,1)S(1)}, u32[]{:S(2)}, u32[]{:S(2)}) %collective-permute-start.10) | collective-permute-done | bytes 73760 | tf_op jit(solution)/shard_map/ppermute | solution.py:360
  36.2 0.0 collective-permute-done.9.refs_0_
  36.2 0.0 copy-done
  36.2 2.4 %estimates.1 = f32[64,128]{1,0:T(8,128)} custom-call(s32[1]{0:T(128)} %bitcast.pos_ref, s32[1,64]{1,0:T(1,128)S(1)} %get-tuple-element.28.levels_ref, f32[1,128]{1,0:T(1,128)S(1)} %get-tuple-element.29.init_ref, bf16[128,256]{1,0:T(8,128)(2,1)S(1)} %get-tuple-element.45.prefix_ref, f32[8,128]{1,0:T(8,128)S(1)} %get-tuple-element.46.before_ref, ...), custom_call_target="tpu_custom_call" | custom-call | flops 1 | bytes 1 | tf_op jit(solution)/shard_map/estimates/pallas_call | solution.py:364
Async XLA Ops:
  1.8 7.3 %collective-permute-start = (bf16[4,64,128]{2,1,0:T(8,128)(2,1)S(1)}, bf16[4,64,128]{2,1,0:T(8,128)(2,1)S(1)}, u32[]{:S(2)}, u32[]{:S(2)}) collective-permute-start(bf16[4,64,128]{2,1,0:T(8,128)(2,1)S(1)} %get-tuple-element.37), channel_id=1, source_target_pairs={{0,1},{1,0},{2,3},{3,2},{4,5},{5,4},{6,7},{7,6},{8,9},{9,8},{10,11... | collective-permute-start | bytes 196616 | tf_op jit(solution)/shard_map/ppermute | solution.py:295
  2.4 6.7 %collective-permute-start.1 = (bf16[4,64,128]{2,1,0:T(8,128)(2,1)S(1)}, bf16[4,64,128]{2,1,0:T(8,128)(2,1)S(1)}, u32[]{:S(2)}, u32[]{:S(2)}) collective-permute-start(bf16[4,64,128]{2,1,0:T(8,128)(2,1)S(1)} %get-tuple-element.38), channel_id=1, source_target_pairs={{0,2},{1,3},{2,0},{3,1},{4,6},{5,7},{6,4},{7,5},{8,10},{9,11},{10,... | collective-permute-start | bytes 196616 | tf_op jit(solution)/shard_map/ppermute | solution.py:295
  4.9 4.2 %collective-permute-start.2 = (bf16[4,64,128]{2,1,0:T(8,128)(2,1)S(1)}, bf16[4,64,128]{2,1,0:T(8,128)(2,1)S(1)}, u32[]{:S(2)}, u32[]{:S(2)}) collective-permute-start(bf16[4,64,128]{2,1,0:T(8,128)(2,1)S(1)} %get-tuple-element.39), channel_id=1, source_target_pairs={{0,3},{1,2},{2,1},{3,0},{4,7},{5,6},{6,5},{7,4},{8,11},{9,10},{10,... | collective-permute-start | bytes 196616 | tf_op jit(solution)/shard_map/ppermute | solution.py:295
  9.1 27.1 %copy-start = (bf16[31,128,256]{2,1,0:T(8,128)(2,1)S(1)}, bf16[31,128,256]{2,1,0:T(8,128)(2,1)}, u32[]{:S(2)}) copy-start(bf16[31,128,256]{2,1,0:T(8,128)(2,1)} %get-tuple-element.48.left_ref) | copy-start | bytes 6094852
  9.4 4.5 %collective-permute-start.3 = (f32[64,128]{1,0:T(8,128)S(1)}, f32[64,128]{1,0:T(8,128)S(1)}, u32[]{:S(2)}, u32[]{:S(2)}) collective-permute-start(f32[64,128]{1,0:T(8,128)S(1)} %get-tuple-element.41), channel_id=1, source_target_pairs={{0,4},{1,5},{2,6},{3,7},{4,0},{5,1},{6,2},{7,3},{8,12},{9,13},{10,... | collective-permute-start | bytes 98312 | tf_op jit(solution)/shard_map/ppermute | solution.py:295
  11.3 5.4 %collective-permute-start.4 = (f32[64,128]{1,0:T(8,128)S(1)}, f32[64,128]{1,0:T(8,128)S(1)}, u32[]{:S(2)}, u32[]{:S(2)}) collective-permute-start(f32[64,128]{1,0:T(8,128)S(1)} %get-tuple-element.42), channel_id=1, source_target_pairs={{0,8},{1,9},{2,10},{3,11},{4,12},{5,13},{6,14},{7,15},{8,0},{9,1},... | collective-permute-start | bytes 98312 | tf_op jit(solution)/shard_map/ppermute | solution.py:295
  13.9 5.7 %collective-permute-start.5 = (f32[64,128]{1,0:T(8,128)S(1)}, f32[64,128]{1,0:T(8,128)S(1)}, u32[]{:S(2)}, u32[]{:S(2)}) collective-permute-start(f32[64,128]{1,0:T(8,128)S(1)} %get-tuple-element.43), channel_id=1, source_target_pairs={{0,12},{1,13},{2,14},{3,15},{4,8},{5,9},{6,10},{7,11},{8,4},{9,5},... | collective-permute-start | bytes 98312 | tf_op jit(solution)/shard_map/ppermute | solution.py:295
  22.5 4.6 %collective-permute-start.8 = (bf16[144,256]{1,0:T(8,128)(2,1)S(1)}, bf16[144,256]{1,0:T(8,128)(2,1)S(1)}, u32[]{:S(2)}, u32[]{:S(2)}) collective-permute-start(bf16[144,256]{1,0:T(8,128)(2,1)S(1)} %get-tuple-element.44.refs_0_), channel_id=1, source_target_pairs={{0,3},{1,2},{2,1},{3,0},{4,7},{5,6},{6,5},{7,4},{8,11},{9,10},{10,... | collective-permute-start | bytes 221192 | tf_op jit(solution)/shard_map/ppermute | solution.py:295
  22.6 6.1 %collective-permute-start.7 = (bf16[144,256]{1,0:T(8,128)(2,1)S(1)}, bf16[144,256]{1,0:T(8,128)(2,1)S(1)}, u32[]{:S(2)}, u32[]{:S(2)}) collective-permute-start(bf16[144,256]{1,0:T(8,128)(2,1)S(1)} %get-tuple-element.44.refs_0_), channel_id=1, source_target_pairs={{0,2},{1,3},{2,0},{3,1},{4,6},{5,7},{6,4},{7,5},{8,10},{9,11},{10,... | collective-permute-start | bytes 221192 | tf_op jit(solution)/shard_map/ppermute | solution.py:295
  24.2 4.6 %collective-permute-start.6 = (bf16[144,256]{1,0:T(8,128)(2,1)S(1)}, bf16[144,256]{1,0:T(8,128)(2,1)S(1)}, u32[]{:S(2)}, u32[]{:S(2)}) collective-permute-start(bf16[144,256]{1,0:T(8,128)(2,1)S(1)} %get-tuple-element.44.refs_0_), channel_id=1, source_target_pairs={{0,1},{1,0},{2,3},{3,2},{4,5},{5,4},{6,7},{7,6},{8,9},{9,8},{10,11... | collective-permute-start | bytes 221192 | tf_op jit(solution)/shard_map/ppermute | solution.py:295
  29.2 7.0 %collective-permute-start.10 = (bf16[144,256]{1,0:T(8,128)(2,1)S(1)}, bf16[144,256]{1,0:T(8,128)(2,1)S(1)}, u32[]{:S(2)}, u32[]{:S(2)}) collective-permute-start(bf16[144,256]{1,0:T(8,128)(2,1)S(1)} %get-tuple-element.49), channel_id=1, source_target_pairs={{0,8},{1,9},{2,10},{3,11},{4,12},{5,13},{6,14},{7,15},{8,0},{9,1},... | collective-permute-start | bytes 221192 | tf_op jit(solution)/shard_map/ppermute | solution.py:360
  29.3 6.9 %collective-permute-start.9 = (bf16[144,256]{1,0:T(8,128)(2,1)S(1)}, bf16[144,256]{1,0:T(8,128)(2,1)S(1)}, u32[]{:S(2)}, u32[]{:S(2)}) collective-permute-start(bf16[144,256]{1,0:T(8,128)(2,1)S(1)} %get-tuple-element.49), channel_id=1, source_target_pairs={{0,4},{1,5},{2,6},{3,7},{4,8},{5,9},{6,10},{7,11},{8,12},{9,13},{1... | collective-permute-start | bytes 221192 | tf_op jit(solution)/shard_map/ppermute | solution.py:360
  30.2 5.4 %collective-permute-start.11 = (bf16[16,256]{1,0:T(8,128)(2,1)S(1)}, bf16[16,256]{1,0:T(8,128)(2,1)S(1)}, u32[]{:S(2)}, u32[]{:S(2)}) collective-permute-start(bf16[16,256]{1,0:T(8,128)(2,1)S(1)} %get-tuple-element.50), channel_id=1, source_target_pairs={{0,12},{1,13},{2,14},{3,15},{4,0},{5,1},{6,2},{7,3},{8,4},{9,5},{1... | collective-permute-start | bytes 24584 | tf_op jit(solution)/shard_map/ppermute | solution.py:360

commit v9 on v8

--- a/solution.py
+++ b/solution.py
@@ -118,68 +118,88 @@
         outs[r][...] = sums[(position // size) ^ r]
 
 
-def tree_kernel(steps, levels_ref, table_ref, left_hbm, right_hbm, total_ref, left_ref, right_ref, sems):
+def each(fn, start, count):
+    if count <= 4:
+        fn(list(range(start, start + count)))
+        return
+
+    def body(i, c):
+        fn([start + 4 * i + k for k in range(4)])
+        return c
+
+    lax.fori_loop(0, count // 4, body, 0)
+
+
+def keep(left_ref, right_ref, ks, made):
+    for k, (a, b) in zip(ks, made):
+        left_ref[k] = pair(a)
+        right_ref[k] = pair(b)
+
+
+def low_tree_kernel(steps, levels_ref, table_ref, left_hbm, right_hbm, mark_ref, left_ref, right_ref, sems):
     base = steps // 4
+    copies = []
 
     def first(t):
         return mm(table_ref[levels_ref[0, t]], table_ref[levels_ref[0, t + 1]])
 
+    def first_pairs(ks):
+        keep(left_ref, right_ref, ks, [(first(4 * k), first(4 * k + 2)) for k in ks])
+
     def node(k):
         return mm(left_ref[k], right_ref[k])
 
-    def first_pairs(ks):
-        made = [(first(4 * k), first(4 * k + 2)) for k in ks]
-        for k, (a, b) in zip(ks, made):
-            left_ref[k] = pair(a)
-            right_ref[k] = pair(b)
-
     def later_pairs(ks):
-        made = [(node(2 * (k - base)), node(2 * (k - base) + 1)) for k in ks]
-        for k, (a, b) in zip(ks, made):
-            left_ref[k] = pair(a)
-            right_ref[k] = pair(b)
-
-    def run(fn, start, count):
-        if count <= 4:
-            fn(list(range(start, start + count)))
-            return
-
-        def body(i, c):
-            fn([start + 4 * i + k for k in range(4)])
-            return c
-
-        lax.fori_loop(0, count // 4, body, 0)
-
-    copies = []
+        keep(left_ref, right_ref, ks, [(node(2 * (k - base)), node(2 * (k - base) + 1)) for k in ks])
 
     def store(start, count):
-        for ref, hbm in ((right_ref, right_hbm), (left_ref, left_hbm)):
+        for ref, hbm_ref in ((right_ref, right_hbm), (left_ref, left_hbm)):
             part = pl.ds(start, count)
-            copies.append(pltpu.make_async_copy(ref.at[part], hbm.at[part], sems.at[len(copies)]))
+            copies.append(pltpu.make_async_copy(ref.at[part], hbm_ref.at[part], sems.at[len(copies)]))
             copies[-1].start()
 
-    run(first_pairs, 0, base)
+    each(first_pairs, 0, base)
     store(0, base)
-    run(later_pairs, base, base // 2)
+    each(later_pairs, base, base // 2)
     store(base, base // 2)
-    count, start = base // 4, base + base // 2
+    mark_ref[...] = jnp.zeros_like(mark_ref)
+    for copy in copies:
+        copy.wait()
+
+
+def high_tree_kernel(base, after_ref, low_left, low_right, left_out, right_out, total_ref, left_ref, right_ref, sems):
+    half = base // 2
+    part = pl.ds(base, half)
+    copies = [
+        pltpu.make_async_copy(low_left.at[part], left_ref.at[pl.ds(0, half)], sems.at[0]),
+        pltpu.make_async_copy(low_right.at[part], right_ref.at[pl.ds(0, half)], sems.at[1]),
+    ]
+    for copy in copies:
+        copy.start()
+    for copy in copies:
+        copy.wait()
+
+    def node(k):
+        return mm(left_ref[k], right_ref[k])
+
+    count, start = half // 2, half
     while count >= 1:
-        run(later_pairs, start, count)
+        ks = list(range(start, start + count))
+        keep(left_ref, right_ref, ks, [(node(2 * (k - half)), node(2 * (k - half) + 1)) for k in ks])
         start += count
         count //= 2
-    store(base + base // 2, base // 2 - 1)
     total_ref[...] = pair(node(start - 1))
-    for copy in copies:
-        copy.wait()
-
-
-def local_kernel(pos_ref, levels_ref, gain_ref, init_ref, total_ref, table_ref, right_hbm, *refs):
+    left_out[...] = left_ref[pl.ds(half, half - 1)]
+    right_out[...] = right_ref[pl.ds(half, half - 1)]
+
+
+def local_kernel(pos_ref, levels_ref, gain_ref, init_ref, total_ref, table_ref, high_ref, right_hbm, *refs):
     parts, (lefts_ref, own_ref, drive_ref, right_ref, sems) = refs[:-5], refs[-5:]
     steps, n = drive_ref.shape
     base = steps // 4
     copies = [
         pltpu.make_async_copy(right_hbm.at[pl.ds(0, base)], right_ref.at[pl.ds(0, base)], sems.at[0]),
-        pltpu.make_async_copy(right_hbm.at[pl.ds(base, base - 1)], right_ref.at[pl.ds(base, base - 1)], sems.at[1]),
+        pltpu.make_async_copy(right_hbm.at[pl.ds(base, base // 2)], right_ref.at[pl.ds(base, base // 2)], sems.at[1]),
     ]
     for copy in copies:
         copy.start()
@@ -195,7 +215,12 @@
             copies[level - 1].wait()
         later = []
         for i in range(len(states) // 2):
-            mat = table_ref[levels_ref[0, 2 * i + 1]] if level == 0 else right_ref[offset + i]
+            if level == 0:
+                mat = table_ref[levels_ref[0, 2 * i + 1]]
+            elif level < 3:
+                mat = right_ref[offset + i]
+            else:
+                mat = high_ref[offset + i - base - base // 2]
             lefts_ref[pl.ds(at + i, 1), :] = states[2 * i][:1]
             later.append(vm(states[2 * i], mat) + states[2 * i + 1])
         at += len(later)
@@ -248,7 +273,7 @@
     shift_ref[...] = rows16(vec)
 
 
-def final_kernel(size, pos_ref, levels_ref, init_ref, prefix_ref, before_ref, total_ref, lefts_ref, left_ref, table_ref, *refs):
+def final_kernel(size, pos_ref, levels_ref, init_ref, prefix_ref, before_ref, total_ref, lefts_ref, left_ref, high_ref, table_ref, *refs):
     got, out_ref = refs[:-1], refs[-1]
     steps, n = lefts_ref.shape
     position = pos_ref[0]
@@ -265,11 +290,17 @@
     levels = steps.bit_length() - 1
     starts = [state]
     sizes = [steps >> (level + 1) for level in range(levels)]
+    low = sizes[1] + sizes[2]
     for level in reversed(range(levels)):
         at, offset = sum(sizes[:level]), sum(sizes[1:level])
         later = []
         for i, x in enumerate(starts):
-            mat = table_ref[levels_ref[0, 2 * i]] if level == 0 else left_ref[offset + i]
+            if level == 0:
+                mat = table_ref[levels_ref[0, 2 * i]]
+            elif level < 3:
+                mat = left_ref[offset + i]
+            else:
+                mat = high_ref[offset + i - low]
             later += [x, vm(x, mat) + row(lefts_ref, at + i)]
         starts = later
     for t in range(1, steps):
@@ -282,7 +313,6 @@
     pixels, length = frames.shape
     steps = length // count
     position = lax.axis_index("tm").astype(jnp.int32)[None]
-    pairs = steps // 2 - 1
     dma = pltpu.SemaphoreType.DMA
     size = 1
     while count % (2 * size) == 0 and 4 * size * size <= count:
@@ -315,14 +345,15 @@
         out_specs=[VMEM] * len(outs),
         scratch_shapes=buffers + [dma((cuts + 4 + len(small),))],
     )(position, *given)
-    tree = pltpu.VMEM((pairs, n, 2 * n), BF16)
-    maps = pltpu.HBM((pairs, n, 2 * n), BF16)
-    left, right, total = call(
-        functools.partial(tree_kernel, steps), "tree_of_maps", 8,
-        out_shape=[maps, maps, one_map],
+    base = steps // 4
+    low = (base + base // 2, n, 2 * n)
+    high = shape((base // 2 - 1, n, 2 * n), BF16)
+    low_left, low_right, mark = call(
+        functools.partial(low_tree_kernel, steps), "low_tree", 8,
+        out_shape=[pltpu.HBM(low, BF16)] * 2 + [shape((8, n), F32)],
         in_specs=[SMEM, VMEM],
         out_specs=[HBM, HBM, VMEM],
-        scratch_shapes=[tree, tree, dma((6,))],
+        scratch_shapes=[pltpu.VMEM(low, BF16)] * 2 + [dma((4,))],
     )(levels, table)
 
     if turn:
@@ -333,22 +364,31 @@
             in_specs=[SMEM] + [VMEM] * (3 + size),
             out_specs=[VMEM] * groups,
             scratch_shapes=[pltpu.VMEM((groups, steps, n), F32), pltpu.VMEM((count, pixels), F32)],
-        )(position, total, mode, weight, slab, *swaps(slabs, 1, size))
-        parts = [first] + swaps(parts, size, groups)
+        )(position, mark, mode, weight, slab, *swaps(slabs, 1, size))
+        far = swaps(parts, size, groups)
+        first, parts = far[0], [first] + far[::-1]
     else:
         x = lax.all_to_all(frames, "tm", split_axis=1, concat_axis=0, tiled=True)
         channels = jnp.arange(n, dtype=jnp.int32)
         projector = jnp.where(pixel_mode[None, :] == channels[:, None], pixel_weight[None, :], jnp.zeros((), BF16))
         parts = [lax.dot_general(x, projector, (((0,), (1,)), ((), ())), preferred_element_type=F32)]
-
+        first = mark
+
+    high_left, high_right, total = call(
+        functools.partial(high_tree_kernel, base), "high_tree", 5,
+        out_shape=[high, high, one_map],
+        in_specs=[VMEM, HBM, HBM],
+        out_specs=[VMEM] * 3,
+        scratch_shapes=[pltpu.VMEM((base, n, 2 * n), BF16)] * 2 + [dma((2,))],
+    )(first, hbm(low_left), hbm(low_right))
     block = shape((n + 16, 2 * n), BF16)
     lefts, own = call(
         local_kernel, "local_states", 8,
         out_shape=[shape((steps, n), F32), block],
-        in_specs=[SMEM, SMEM] + [VMEM] * 4 + [HBM] + [VMEM] * len(parts),
+        in_specs=[SMEM, SMEM] + [VMEM] * 5 + [HBM] + [VMEM] * len(parts),
         out_specs=[VMEM] * 2,
-        scratch_shapes=[pltpu.VMEM((steps, n), F32), tree, dma((2,))],
-    )(position, levels, gain, initial_state, total, table, hbm(right), *parts)
+        scratch_shapes=[pltpu.VMEM((steps, n), F32), pltpu.VMEM(low, BF16), dma((2,))],
+    )(position, levels, gain, initial_state, total, table, high_right, hbm(low_right), *parts)
     prefix, before, mine, carried = call(
         functools.partial(group_kernel, size), "group_maps", 2,
         out_shape=[one_map, shape((8, n), F32), block, shape((16, 2 * n), BF16)],
@@ -364,9 +404,9 @@
     return call(
         functools.partial(final_kernel, size), "estimates", 6,
         out_shape=shape((steps, n), F32),
-        in_specs=[SMEM, SMEM] + [VMEM] * (7 + len(got)),
+        in_specs=[SMEM, SMEM] + [VMEM] * (8 + len(got)),
         out_specs=VMEM,
-    )(position, levels, initial_state, prefix, before, total, lefts, left, table, *got)
+    )(position, levels, initial_state, prefix, before, total, lefts, low_left, high_left, table, *got)
 
 
 def solution(mesh):

time: 38.8 us -> 38.9 us (level)
  waiting for transfers between devices: 13 us -> 11.5 us
  Pallas kernels: 12 us -> 13.4 us
    ppermute x9, waiting for transfers between devices: 10 us -> 7.55 us  [swaps(): lax.ppermute(a, 'tm', [(j, j ^ r * step) for j in range(count)])]
    pallas_call x1 -> x2, Pallas kernels: 4.08 us -> 5.52 us  [the longest x1 3.5 us: shards(): call(functools.partial(low_tree_kernel, steps), 'low_tree', 8, out_shape=...]
    ppermute x3, waiting for transfers between devices: 3.03 us -> 3.98 us  [shards(): lax.ppermute(mine if r < groups - 1 else carried, 'tm', [(j, (j + r * siz...]
    ppermute x3, starting transfers between devices: 3.95 us -> 4.41 us  [shards(): lax.ppermute(mine if r < groups - 1 else carried, 'tm', [(j, (j + r * siz...]
  transfers between devices with their start and end apart: 12 -> 12, of which waited for: 6 -> 7; matrix products, arithmetic and copies ran while one was open for 0% -> 0% of each run, Pallas kernels for 11% -> 14%
where the time goes in v9:
time: 38.9 us; the launch traced here: 38.7 us
  starting transfers between devices  13.7 us (35%)
  Pallas kernels  13.4 us (34%)
  waiting for transfers between devices  11.5 us (30%)
    ppermute x9, starting transfers between devices, swaps(): lax.ppermute(a, 'tm', [(j, j ^ r * step) for j in range(count)])  9.31 us
    ppermute x9, waiting for transfers between devices, swaps(): lax.ppermute(a, 'tm', [(j, j ^ r * step) for j in range(count)])  7.55 us
    ppermute x3, starting transfers between devices, shards(): lax.ppermute(mine if r < groups - 1 else carried, 'tm', [(j, (j + r * siz...  4.41 us
    ppermute x3, waiting for transfers between devices, shards(): lax.ppermute(mine if r < groups - 1 else carried, 'tm', [(j, (j + r * siz...  3.98 us
    pallas_call x1, Pallas kernels, shards(): call(functools.partial(low_tree_kernel, steps), 'low_tree', 8, out_shape=...  3.5 us
    pallas_call x1, Pallas kernels, shards(): call(local_kernel, 'local_states', 8, out_shape=[shape((steps, n), F32),...  2.92 us
    pallas_call x1, Pallas kernels, shards(): call(functools.partial(final_kernel, size), 'estimates', 6, out_shape=sha...  2.44 us
    pallas_call x1, Pallas kernels, shards(): call(functools.partial(high_tree_kernel, base), 'high_tree', 5, out_shape...  2.03 us
  transfers between devices with their start and end apart: 12, of which 7 were waited for; matrix products, arithmetic and copies ran while one was open for 0% of the time, Pallas kernels for 14%

profile of v9, /device:TPU:0, one launch (start us, length us, event | category | flops | bytes accessed | tf_op | source)
XLA Modules:
  0.0 38.7 jit_solution(6620072988852362150)
XLA Ops:
  0.0 1.8 %front.1 = (bf16[16,128,256]{2,1,0:T(8,128)(2,1)S(1)}, s32[1,64]{1,0:T(1,128)S(1)}, f32[1,128]{1,0:T(1,128)S(1)}, bf16[128,128]{1,0:T(8,128)(2,1)S(1)}, s32[16,1...) custom-call(s32[1]{0:T(128)} %bitcast.pos_ref, ...), custom_call_target="tpu_custom_call" | custom-call | flops 1 | bytes 1 | tf_op jit(solution)/shard_map/front/pallas_call | solution.py:341
  1.8 0.5 %collective-permute-start = (bf16[4,64,128]{2,1,0:T(8,128)(2,1)S(1)}, bf16[4,64,128]{2,1,0:T(8,128)(2,1)S(1)}, u32[]{:S(2)}, u32[]{:S(2)}) collective-permute-start(bf16[4,64,128]{2,1,0:T(8,128)(2,1)S(1)} %get-tuple-element.39), channel_id=1, source_target_pairs={{0,1},{1,0},{2,3},{3,2},{4,5},{5,4},{6,7},{7,6},{8,9},{9,8},{10,11... | collective-permute-start | bytes 196616 | tf_op jit(solution)/shard_map/ppermute | solution.py:325
  2.4 2.6 %collective-permute-start.1 = (bf16[4,64,128]{2,1,0:T(8,128)(2,1)S(1)}, bf16[4,64,128]{2,1,0:T(8,128)(2,1)S(1)}, u32[]{:S(2)}, u32[]{:S(2)}) collective-permute-start(bf16[4,64,128]{2,1,0:T(8,128)(2,1)S(1)} %get-tuple-element.40), channel_id=1, source_target_pairs={{0,2},{1,3},{2,0},{3,1},{4,6},{5,7},{6,4},{7,5},{8,10},{9,11},{10,... | collective-permute-start | bytes 196616 | tf_op jit(solution)/shard_map/ppermute | solution.py:325
  4.9 0.1 collective-permute-start.2
  5.0 3.5 %low_tree.1 = (bf16[24,128,256]{2,1,0:T(8,128)(2,1)}, bf16[24,128,256]{2,1,0:T(8,128)(2,1)}, f32[8,128]{1,0:T(8,128)S(1)}) custom-call(s32[1,64]{1,0:T(1,128)S(1)} %get-tuple-element.31.levels_ref, bf16[16,128,256]{2,1,0:T(8,128)(2,1)S(1)} %get-tuple-element.34.table_ref), custom_call_target="tpu_custom_call" | custom-call | flops 1 | bytes 1 | tf_op jit(solution)/shard_map/low_tree/pallas_call | solution.py:351
  8.5 0.0 collective-permute-done.refs_1_
  8.5 0.0 collective-permute-done.1.refs_2_
  8.5 0.5 %collective-permute-done.2.refs_3_ = bf16[4,64,128]{2,1,0:T(8,128)(2,1)S(1)} collective-permute-done((bf16[4,64,128]{2,1,0:T(8,128)(2,1)S(1)}, bf16[4,64,128]{2,1,0:T(8,128)(2,1)S(1)}, u32[]{:S(2)}, u32[]{:S(2)}) %collective-permute-start.2) | collective-permute-done | bytes 65568 | tf_op jit(solution)/shard_map/ppermute | solution.py:325
  9.0 0.2 project.1
  9.2 1.6 %collective-permute-start.3 = (f32[64,128]{1,0:T(8,128)S(1)}, f32[64,128]{1,0:T(8,128)S(1)}, u32[]{:S(2)}, u32[]{:S(2)}) collective-permute-start(f32[64,128]{1,0:T(8,128)S(1)} %get-tuple-element.42), channel_id=1, source_target_pairs={{0,4},{1,5},{2,6},{3,7},{4,0},{5,1},{6,2},{7,3},{8,12},{9,13},{10,... | collective-permute-start | bytes 98312 | tf_op jit(solution)/shard_map/ppermute | solution.py:325
  10.9 2.5 %collective-permute-start.4 = (f32[64,128]{1,0:T(8,128)S(1)}, f32[64,128]{1,0:T(8,128)S(1)}, u32[]{:S(2)}, u32[]{:S(2)}) collective-permute-start(f32[64,128]{1,0:T(8,128)S(1)} %get-tuple-element.48), channel_id=1, source_target_pairs={{0,12},{1,13},{2,14},{3,15},{4,8},{5,9},{6,10},{7,11},{8,4},{9,5},... | collective-permute-start | bytes 98312 | tf_op jit(solution)/shard_map/ppermute | solution.py:325
  13.3 0.1 collective-permute-start.5
  13.5 0.0 collective-permute-done.3.after_ref.refs_3_
  13.5 2.0 %high_tree.1 = (bf16[7,128,256]{2,1,0:T(8,128)(2,1)S(1)}, bf16[7,128,256]{2,1,0:T(8,128)(2,1)S(1)}, bf16[128,256]{1,0:T(8,128)(2,1)S(1)}) custom-call(f32[64,128]{1,0:T(8,128)S(1)} %collective-permute-done.3.after_ref.refs_3_, bf16[24,128,256]{2,1,0:T(8,128)(2,1)} %get-tuple-element.43.low_left.left_ref, ...), custom_call_target="tpu_custom_call" | custom-call | flops 1 | bytes 1 | tf_op jit(solution)/shard_map/high_tree/pallas_call | solution.py:377
  15.5 1.1 %collective-permute-done.4.refs_1_ = f32[64,128]{1,0:T(8,128)S(1)} collective-permute-done((f32[64,128]{1,0:T(8,128)S(1)}, f32[64,128]{1,0:T(8,128)S(1)}, u32[]{:S(2)}, u32[]{:S(2)}) %collective-permute-start.4) | collective-permute-done | bytes 32800 | tf_op jit(solution)/shard_map/ppermute | solution.py:325
  16.6 1.9 %collective-permute-done.5.refs_2_ = f32[64,128]{1,0:T(8,128)S(1)} collective-permute-done((f32[64,128]{1,0:T(8,128)S(1)}, f32[64,128]{1,0:T(8,128)S(1)}, u32[]{:S(2)}, u32[]{:S(2)}) %collective-permute-start.5) | collective-permute-done | bytes 32800 | tf_op jit(solution)/shard_map/ppermute | solution.py:325
  18.5 0.0 copy-start
  18.5 2.9 %local_states.1 = (f32[64,128]{1,0:T(8,128)S(1)}, bf16[144,256]{1,0:T(8,128)(2,1)S(1)}) custom-call(s32[1]{0:T(128)} %bitcast.pos_ref, s32[1,64]{1,0:T(1,128)S(1)} %get-tuple-element.31.levels_ref, bf16[128,128]{1,0:T(8,128)(2,1)S(1)} %get-tuple-element.33.gain_ref, f32[1,128]{1,0:T(1,128)S(1)} %get-tuple-element.32.init_ref, ...), custom_call_target="tpu_custom_call" | custom-call | flops 1 | bytes 1 | tf_op jit(solution)/shard_map/local_states/pallas_call | solution.py:385
  21.4 0.1 collective-permute-start.8
  21.5 1.4 %collective-permute-start.7 = (bf16[144,256]{1,0:T(8,128)(2,1)S(1)}, bf16[144,256]{1,0:T(8,128)(2,1)S(1)}, u32[]{:S(2)}, u32[]{:S(2)}) collective-permute-start(bf16[144,256]{1,0:T(8,128)(2,1)S(1)} %get-tuple-element.50.refs_0_), channel_id=1, source_target_pairs={{0,2},{1,3},{2,0},{3,1},{4,6},{5,7},{6,4},{7,5},{8,10},{9,11},{10,... | collective-permute-start | bytes 221192 | tf_op jit(solution)/shard_map/ppermute | solution.py:325
  22.9 0.4 %collective-permute-start.6 = (bf16[144,256]{1,0:T(8,128)(2,1)S(1)}, bf16[144,256]{1,0:T(8,128)(2,1)S(1)}, u32[]{:S(2)}, u32[]{:S(2)}) collective-permute-start(bf16[144,256]{1,0:T(8,128)(2,1)S(1)} %get-tuple-element.50.refs_0_), channel_id=1, source_target_pairs={{0,1},{1,0},{2,3},{3,2},{4,5},{5,4},{6,7},{7,6},{8,9},{9,8},{10,11... | collective-permute-start | bytes 221192 | tf_op jit(solution)/shard_map/ppermute | solution.py:325
  23.4 2.7 %collective-permute-done.8.refs_3_ = bf16[144,256]{1,0:T(8,128)(2,1)S(1)} collective-permute-done((bf16[144,256]{1,0:T(8,128)(2,1)S(1)}, bf16[144,256]{1,0:T(8,128)(2,1)S(1)}, u32[]{:S(2)}, u32[]{:S(2)}) %collective-permute-start.8) | collective-permute-done | bytes 73760 | tf_op jit(solution)/shard_map/ppermute | solution.py:325
  26.1 1.4 %collective-permute-done.7.refs_2_ = bf16[144,256]{1,0:T(8,128)(2,1)S(1)} collective-permute-done((bf16[144,256]{1,0:T(8,128)(2,1)S(1)}, bf16[144,256]{1,0:T(8,128)(2,1)S(1)}, u32[]{:S(2)}, u32[]{:S(2)}) %collective-permute-start.7) | collective-permute-done | bytes 73760 | tf_op jit(solution)/shard_map/ppermute | solution.py:325
  27.4 0.0 collective-permute-done.6.refs_1_
  27.4 0.4 %group_maps.1 = (bf16[128,256]{1,0:T(8,128)(2,1)S(1)}, f32[8,128]{1,0:T(8,128)S(1)}, bf16[144,256]{1,0:T(8,128)(2,1)S(1)}, bf16[16,256]{1,0:T(8,128)(2,1)S(1)}) custom-call(s32[1]{0:T(128)} %bitcast.pos_ref, bf16[144,256]{1,0:T(8,128)(2,1)S(1)} %get-tuple-element.50.refs_0_, bf16[144,256]{1,0:T(8,128)(2,1)S(1)} %collective-permute-done.6.refs_1_, ...), custom_call_target="tpu_custom_call" | custom-call | flops 1 | bytes 1 | tf_op jit(solution)/shard_map/group_maps/pallas_call | solution.py:392
  27.9 0.6 %collective-permute-start.10 = (bf16[144,256]{1,0:T(8,128)(2,1)S(1)}, bf16[144,256]{1,0:T(8,128)(2,1)S(1)}, u32[]{:S(2)}, u32[]{:S(2)}) collective-permute-start(bf16[144,256]{1,0:T(8,128)(2,1)S(1)} %get-tuple-element.55), channel_id=1, source_target_pairs={{0,8},{1,9},{2,10},{3,11},{4,12},{5,13},{6,14},{7,15},{8,0},{9,1},... | collective-permute-start | bytes 221192 | tf_op jit(solution)/shard_map/ppermute | solution.py:400
  28.5 1.8 %collective-permute-start.9 = (bf16[144,256]{1,0:T(8,128)(2,1)S(1)}, bf16[144,256]{1,0:T(8,128)(2,1)S(1)}, u32[]{:S(2)}, u32[]{:S(2)}) collective-permute-start(bf16[144,256]{1,0:T(8,128)(2,1)S(1)} %get-tuple-element.55), channel_id=1, source_target_pairs={{0,4},{1,5},{2,6},{3,7},{4,8},{5,9},{6,10},{7,11},{8,12},{9,13},{1... | collective-permute-start | bytes 221192 | tf_op jit(solution)/shard_map/ppermute | solution.py:400
  30.3 2.0 %collective-permute-start.11 = (bf16[16,256]{1,0:T(8,128)(2,1)S(1)}, bf16[16,256]{1,0:T(8,128)(2,1)S(1)}, u32[]{:S(2)}, u32[]{:S(2)}) collective-permute-start(bf16[16,256]{1,0:T(8,128)(2,1)S(1)} %get-tuple-element.56), channel_id=1, source_target_pairs={{0,12},{1,13},{2,14},{3,15},{4,0},{5,1},{6,2},{7,3},{8,4},{9,5},{1... | collective-permute-start | bytes 24584 | tf_op jit(solution)/shard_map/ppermute | solution.py:400
  32.3 2.4 %collective-permute-done.11.refs_2_ = bf16[16,256]{1,0:T(8,128)(2,1)S(1)} collective-permute-done((bf16[16,256]{1,0:T(8,128)(2,1)S(1)}, bf16[16,256]{1,0:T(8,128)(2,1)S(1)}, u32[]{:S(2)}, u32[]{:S(2)}) %collective-permute-start.11) | collective-permute-done | bytes 8224 | tf_op jit(solution)/shard_map/ppermute | solution.py:400
  34.7 1.5 %collective-permute-done.10.refs_1_ = bf16[144,256]{1,0:T(8,128)(2,1)S(1)} collective-permute-done((bf16[144,256]{1,0:T(8,128)(2,1)S(1)}, bf16[144,256]{1,0:T(8,128)(2,1)S(1)}, u32[]{:S(2)}, u32[]{:S(2)}) %collective-permute-start.10) | collective-permute-done | bytes 73760 | tf_op jit(solution)/shard_map/ppermute | solution.py:400
  36.3 0.0 collective-permute-done.9.refs_0_
  36.3 0.0 copy-done
  36.3 2.4 %estimates.1 = f32[64,128]{1,0:T(8,128)} custom-call(s32[1]{0:T(128)} %bitcast.pos_ref, s32[1,64]{1,0:T(1,128)S(1)} %get-tuple-element.31.levels_ref, f32[1,128]{1,0:T(1,128)S(1)} %get-tuple-element.32.init_ref, bf16[128,256]{1,0:T(8,128)(2,1)S(1)} %get-tuple-element.51.prefix_ref, f32[8,128]{1,0:T(8,128)S(1)} %get-tuple-element.52.before_ref, ...), custom_call_target="tpu_custom_call" | custom-call | flops 1 | bytes 1 | tf_op jit(solution)/shard_map/estimates/pallas_call | solution.py:404
Async XLA Ops:
  1.8 6.7 %collective-permute-start = (bf16[4,64,128]{2,1,0:T(8,128)(2,1)S(1)}, bf16[4,64,128]{2,1,0:T(8,128)(2,1)S(1)}, u32[]{:S(2)}, u32[]{:S(2)}) collective-permute-start(bf16[4,64,128]{2,1,0:T(8,128)(2,1)S(1)} %get-tuple-element.39), channel_id=1, source_target_pairs={{0,1},{1,0},{2,3},{3,2},{4,5},{5,4},{6,7},{7,6},{8,9},{9,8},{10,11... | collective-permute-start | bytes 196616 | tf_op jit(solution)/shard_map/ppermute | solution.py:325
  2.4 6.2 %collective-permute-start.1 = (bf16[4,64,128]{2,1,0:T(8,128)(2,1)S(1)}, bf16[4,64,128]{2,1,0:T(8,128)(2,1)S(1)}, u32[]{:S(2)}, u32[]{:S(2)}) collective-permute-start(bf16[4,64,128]{2,1,0:T(8,128)(2,1)S(1)} %get-tuple-element.40), channel_id=1, source_target_pairs={{0,2},{1,3},{2,0},{3,1},{4,6},{5,7},{6,4},{7,5},{8,10},{9,11},{10,... | collective-permute-start | bytes 196616 | tf_op jit(solution)/shard_map/ppermute | solution.py:325
  4.9 4.0 %collective-permute-start.2 = (bf16[4,64,128]{2,1,0:T(8,128)(2,1)S(1)}, bf16[4,64,128]{2,1,0:T(8,128)(2,1)S(1)}, u32[]{:S(2)}, u32[]{:S(2)}) collective-permute-start(bf16[4,64,128]{2,1,0:T(8,128)(2,1)S(1)} %get-tuple-element.41), channel_id=1, source_target_pairs={{0,3},{1,2},{2,1},{3,0},{4,7},{5,6},{6,5},{7,4},{8,11},{9,10},{10,... | collective-permute-start | bytes 196616 | tf_op jit(solution)/shard_map/ppermute | solution.py:325
  9.2 4.2 %collective-permute-start.3 = (f32[64,128]{1,0:T(8,128)S(1)}, f32[64,128]{1,0:T(8,128)S(1)}, u32[]{:S(2)}, u32[]{:S(2)}) collective-permute-start(f32[64,128]{1,0:T(8,128)S(1)} %get-tuple-element.42), channel_id=1, source_target_pairs={{0,4},{1,5},{2,6},{3,7},{4,0},{5,1},{6,2},{7,3},{8,12},{9,13},{10,... | collective-permute-start | bytes 98312 | tf_op jit(solution)/shard_map/ppermute | solution.py:325
  10.9 5.7 %collective-permute-start.4 = (f32[64,128]{1,0:T(8,128)S(1)}, f32[64,128]{1,0:T(8,128)S(1)}, u32[]{:S(2)}, u32[]{:S(2)}) collective-permute-start(f32[64,128]{1,0:T(8,128)S(1)} %get-tuple-element.48), channel_id=1, source_target_pairs={{0,12},{1,13},{2,14},{3,15},{4,8},{5,9},{6,10},{7,11},{8,4},{9,5},... | collective-permute-start | bytes 98312 | tf_op jit(solution)/shard_map/ppermute | solution.py:325
  13.3 5.2 %collective-permute-start.5 = (f32[64,128]{1,0:T(8,128)S(1)}, f32[64,128]{1,0:T(8,128)S(1)}, u32[]{:S(2)}, u32[]{:S(2)}) collective-permute-start(f32[64,128]{1,0:T(8,128)S(1)} %get-tuple-element.49), channel_id=1, source_target_pairs={{0,8},{1,9},{2,10},{3,11},{4,12},{5,13},{6,14},{7,15},{8,0},{9,1},... | collective-permute-start | bytes 98312 | tf_op jit(solution)/shard_map/ppermute | solution.py:325
  18.5 17.8 %copy-start = (bf16[24,128,256]{2,1,0:T(8,128)(2,1)S(1)}, bf16[24,128,256]{2,1,0:T(8,128)(2,1)}, u32[]{:S(2)}) copy-start(bf16[24,128,256]{2,1,0:T(8,128)(2,1)} %get-tuple-element.43.low_left.left_ref) | copy-start | bytes 4718596
  21.4 4.6 %collective-permute-start.8 = (bf16[144,256]{1,0:T(8,128)(2,1)S(1)}, bf16[144,256]{1,0:T(8,128)(2,1)S(1)}, u32[]{:S(2)}, u32[]{:S(2)}) collective-permute-start(bf16[144,256]{1,0:T(8,128)(2,1)S(1)} %get-tuple-element.50.refs_0_), channel_id=1, source_target_pairs={{0,3},{1,2},{2,1},{3,0},{4,7},{5,6},{6,5},{7,4},{8,11},{9,10},{10,... | collective-permute-start | bytes 221192 | tf_op jit(solution)/shard_map/ppermute | solution.py:325
  21.5 5.9 %collective-permute-start.7 = (bf16[144,256]{1,0:T(8,128)(2,1)S(1)}, bf16[144,256]{1,0:T(8,128)(2,1)S(1)}, u32[]{:S(2)}, u32[]{:S(2)}) collective-permute-start(bf16[144,256]{1,0:T(8,128)(2,1)S(1)} %get-tuple-element.50.refs_0_), channel_id=1, source_target_pairs={{0,2},{1,3},{2,0},{3,1},{4,6},{5,7},{6,4},{7,5},{8,10},{9,11},{10,... | collective-permute-start | bytes 221192 | tf_op jit(solution)/shard_map/ppermute | solution.py:325
  22.9 4.5 %collective-permute-start.6 = (bf16[144,256]{1,0:T(8,128)(2,1)S(1)}, bf16[144,256]{1,0:T(8,128)(2,1)S(1)}, u32[]{:S(2)}, u32[]{:S(2)}) collective-permute-start(bf16[144,256]{1,0:T(8,128)(2,1)S(1)} %get-tuple-element.50.refs_0_), channel_id=1, source_target_pairs={{0,1},{1,0},{2,3},{3,2},{4,5},{5,4},{6,7},{7,6},{8,9},{9,8},{10,11... | collective-permute-start | bytes 221192 | tf_op jit(solution)/shard_map/ppermute | solution.py:325
  27.9 8.4 %collective-permute-start.10 = (bf16[144,256]{1,0:T(8,128)(2,1)S(1)}, bf16[144,256]{1,0:T(8,128)(2,1)S(1)}, u32[]{:S(2)}, u32[]{:S(2)}) collective-permute-start(bf16[144,256]{1,0:T(8,128)(2,1)S(1)} %get-tuple-element.55), channel_id=1, source_target_pairs={{0,8},{1,9},{2,10},{3,11},{4,12},{5,13},{6,14},{7,15},{8,0},{9,1},... | collective-permute-start | bytes 221192 | tf_op jit(solution)/shard_map/ppermute | solution.py:400
  28.5 7.8 %collective-permute-start.9 = (bf16[144,256]{1,0:T(8,128)(2,1)S(1)}, bf16[144,256]{1,0:T(8,128)(2,1)S(1)}, u32[]{:S(2)}, u32[]{:S(2)}) collective-permute-start(bf16[144,256]{1,0:T(8,128)(2,1)S(1)} %get-tuple-element.55), channel_id=1, source_target_pairs={{0,4},{1,5},{2,6},{3,7},{4,8},{5,9},{6,10},{7,11},{8,12},{9,13},{1... | collective-permute-start | bytes 221192 | tf_op jit(solution)/shard_map/ppermute | solution.py:400
  30.3 4.4 %collective-permute-start.11 = (bf16[16,256]{1,0:T(8,128)(2,1)S(1)}, bf16[16,256]{1,0:T(8,128)(2,1)S(1)}, u32[]{:S(2)}, u32[]{:S(2)}) collective-permute-start(bf16[16,256]{1,0:T(8,128)(2,1)S(1)} %get-tuple-element.56), channel_id=1, source_target_pairs={{0,12},{1,13},{2,14},{3,15},{4,0},{5,1},{6,2},{7,3},{8,4},{9,5},{1... | collective-permute-start | bytes 24584 | tf_op jit(solution)/shard_map/ppermute | solution.py:400

commit v10 on v8

--- a/solution.py
+++ b/solution.py
@@ -21,12 +21,12 @@
     return pltpu.with_memory_space_constraint(x, pltpu.HBM)
 
 
-def call(kernel, name, mib, **kw):
+def call(kernel, name, mib, flops=1, **kw):
     return pl.pallas_call(
         kernel,
         name=name,
         compiler_params=pltpu.CompilerParams(vmem_limit_bytes=mib * MIB),
-        cost_estimate=pl.CostEstimate(flops=1, bytes_accessed=1, transcendentals=0),
+        cost_estimate=pl.CostEstimate(flops=flops, bytes_accessed=1, transcendentals=0),
         **kw,
     )
 
@@ -100,8 +100,9 @@
         copy.wait()
 
 
-def project_kernel(size, pos_ref, after_ref, mode_ref, weight_ref, *refs):
-    slabs, outs, (sums, weights) = refs[:size], refs[size:-2], refs[-2:]
+def project_kernel(size, pos_ref, total_ref, mode_ref, weight_ref, *refs):
+    slabs, (same_ref, *outs), (sums, weights) = refs[:size], refs[size:-2], refs[-2:]
+    same_ref[...] = total_ref[...]
     weights[...] = weight_ref[...].astype(F32)
     groups, steps, width = slabs[0].shape
     n = sums.shape[2]
@@ -174,7 +175,7 @@
 
 
 def local_kernel(pos_ref, levels_ref, gain_ref, init_ref, total_ref, table_ref, right_hbm, *refs):
-    parts, (lefts_ref, own_ref, drive_ref, right_ref, sems) = refs[:-5], refs[-5:]
+    parts, (lefts_ref, shift_ref, drive_ref, right_ref, sems) = refs[:-5], refs[-5:]
     steps, n = drive_ref.shape
     base = steps // 4
     copies = [
@@ -204,61 +205,61 @@
         states = later
     lefts_ref[pl.ds(at, 1), :] = states[0][:1]
     first = jnp.where(pos_ref[0] == 0, row(init_ref, 0), 0.0)
-    total = total_ref[...]
-    own_ref[pl.ds(0, n), :] = total
-    own_ref[pl.ds(n, 16), :] = rows16(states[0] + vm(first, total))
-
-
-def rows16(vec):
-    high = vec.astype(BF16).astype(F32)
-    both = jnp.concatenate([high, vec - high], axis=1)
-    return jnp.concatenate([both, both], axis=0).astype(BF16)
-
-
-def rows8(rows):
-    both = rows.astype(F32)
-    n = rows.shape[1] // 2
-    return both[:8, :n] + both[:8, n:]
-
-
-def group_kernel(size, pos_ref, *refs):
+    shift_ref[...] = states[0] + vm(first, total_ref[...])
+
+
+def map_kernel(size, pos_ref, *refs):
     blocks = refs[:size]
-    prefix_ref, before_ref, mine_ref, shift_ref, all_ref = refs[size:]
-    n = prefix_ref.shape[0]
+    all_ref, prefix_ref, whole_ref = refs[size:]
+    n = whole_ref.shape[0]
     member = pos_ref[0] % size
     for r in range(size):
         all_ref[member ^ r] = blocks[r][...]
-
-    def block(q):
-        return all_ref[q, :n, :], rows8(all_ref[q, n:, :])
-
     rows, cols = (lax.broadcasted_iota(jnp.int32, (n, n), d) for d in (0, 1))
-    prefix, before = pair((rows == cols).astype(F32)), jnp.zeros((8, n), F32)
-    run, vec = block(0)
+    prefix = pair((rows == cols).astype(F32))
+    run = all_ref[0]
     for q in range(1, size):
-        here = member == q
-        prefix, before = jnp.where(here, run, prefix), jnp.where(here, vec, before)
-        step, shift = block(q)
-        vec = vm(vec, step) + shift
-        run = pair(mm(run, step))
+        prefix = jnp.where(member == q, run, prefix)
+        run = pair(mm(run, all_ref[q]))
     prefix_ref[...] = prefix
+    whole_ref[...] = run
+
+
+def shift_kernel(size, pos_ref, all_ref, near_ref, *refs):
+    shifts = refs[:size]
+    before_ref, whole_ref, far_ref, held_ref = refs[size:]
+    member = pos_ref[0] % size
+    for r in range(size):
+        held_ref[member ^ r] = shifts[r][...]
+    run, before = held_ref[0], jnp.zeros(before_ref.shape, F32)
+    for q in range(1, size):
+        before = jnp.where(member == q, run, before)
+        run = vm(run, all_ref[q]) + held_ref[q]
     before_ref[...] = before
-    mine_ref[pl.ds(0, n), :] = run
-    mine_ref[pl.ds(n, 16), :] = rows16(vec)
-    shift_ref[...] = rows16(vec)
-
-
-def final_kernel(size, pos_ref, levels_ref, init_ref, prefix_ref, before_ref, total_ref, lefts_ref, left_ref, table_ref, *refs):
+    whole_ref[...] = run
+    far_ref[...] = jnp.where((pos_ref[0] // size) % 2 == 0, vm(run, near_ref[...]), run)
+
+
+def four_groups(group, near_ref, shift_ref, *far):
+    state = jnp.where(group >= 2, far[0][...] + far[1][...], 0.0)
+    return jnp.where(group % 2 == 1, vm(state, near_ref[...]) + shift_ref[...], state)
+
+
+def any_groups(group, *got):
+    many = (len(got) + 1) // 2
+    state = jnp.zeros(got[0].shape, F32)
+    for r in range(many, 0, -1):
+        if r < many:
+            state = jnp.where(group > r, vm(state, got[many + r - 1][...]), 0.0)
+        state += jnp.where(group >= r, got[r - 1][...], 0.0)
+    return state
+
+
+def final_kernel(size, gather, pos_ref, levels_ref, init_ref, prefix_ref, before_ref, total_ref, lefts_ref, left_ref, table_ref, *refs):
     got, out_ref = refs[:-1], refs[-1]
     steps, n = lefts_ref.shape
     position = pos_ref[0]
-    group = position // size
-    state = jnp.zeros((8, n), F32)
-    for r in range(len(got), 0, -1):
-        rows = got[r - 1].shape[0]
-        if rows > 16:
-            state = jnp.where(group > r, vm(state, got[r - 1][pl.ds(0, n), :]), 0.0)
-        state += jnp.where(group >= r, rows8(got[r - 1][pl.ds(rows - 16, 16), :]), 0.0)
+    state = gather(position // size, *got)
     first = jnp.where(position == 0, row(init_ref, 0), 0.0)
     state = vm(state, prefix_ref[...]) + before_ref[...] + first
     out_ref[pl.ds(steps - 1, 1), :] = (vm(state, total_ref[...]) + row(lefts_ref, steps - 1))[:1]
@@ -282,7 +283,6 @@
     pixels, length = frames.shape
     steps = length // count
     position = lax.axis_index("tm").astype(jnp.int32)[None]
-    pairs = steps // 2 - 1
     dma = pltpu.SemaphoreType.DMA
     size = 1
     while count % (2 * size) == 0 and 4 * size * size <= count:
@@ -315,6 +315,7 @@
         out_specs=[VMEM] * len(outs),
         scratch_shapes=buffers + [dma((cuts + 4 + len(small),))],
     )(position, *given)
+    pairs = steps // 2 - 1
     tree = pltpu.VMEM((pairs, n, 2 * n), BF16)
     maps = pltpu.HBM((pairs, n, 2 * n), BF16)
     left, right, total = call(
@@ -327,42 +328,57 @@
 
     if turn:
         mode, weight, slab, *slabs = rest
-        first, *parts = call(
+        total, first, *parts = call(
             functools.partial(project_kernel, size), "project", 4,
-            out_shape=[shape((steps, n), F32)] * groups,
+            out_shape=[one_map] + [shape((steps, n), F32)] * groups,
             in_specs=[SMEM] + [VMEM] * (3 + size),
-            out_specs=[VMEM] * groups,
+            out_specs=[VMEM] * (1 + groups),
             scratch_shapes=[pltpu.VMEM((groups, steps, n), F32), pltpu.VMEM((count, pixels), F32)],
         )(position, total, mode, weight, slab, *swaps(slabs, 1, size))
-        parts = [first] + swaps(parts, size, groups)
+        far = swaps(parts, size, groups)
+        parts = [first] + far[::-1]
     else:
         x = lax.all_to_all(frames, "tm", split_axis=1, concat_axis=0, tiled=True)
         channels = jnp.arange(n, dtype=jnp.int32)
         projector = jnp.where(pixel_mode[None, :] == channels[:, None], pixel_weight[None, :], jnp.zeros((), BF16))
         parts = [lax.dot_general(x, projector, (((0,), (1,)), ((), ())), preferred_element_type=F32)]
-
-    block = shape((n + 16, 2 * n), BF16)
-    lefts, own = call(
-        local_kernel, "local_states", 8,
-        out_shape=[shape((steps, n), F32), block],
+    members = swaps(total, 1, size)
+    vector = shape((8, n), F32)
+    lefts, shift = call(
+        local_kernel, "local_states", 8, 1 << 40,
+        out_shape=[shape((steps, n), F32), vector],
         in_specs=[SMEM, SMEM] + [VMEM] * 4 + [HBM] + [VMEM] * len(parts),
         out_specs=[VMEM] * 2,
         scratch_shapes=[pltpu.VMEM((steps, n), F32), tree, dma((2,))],
     )(position, levels, gain, initial_state, total, table, hbm(right), *parts)
-    prefix, before, mine, carried = call(
-        functools.partial(group_kernel, size), "group_maps", 2,
-        out_shape=[one_map, shape((8, n), F32), block, shape((16, 2 * n), BF16)],
+    shifts = swaps(shift, 1, size)
+    group_maps, prefix, whole = call(
+        functools.partial(map_kernel, size), "group_maps", 2,
+        out_shape=[shape((size, n, 2 * n), BF16), one_map, one_map],
         in_specs=[SMEM] + [VMEM] * size,
-        out_specs=[VMEM] * 4,
-        scratch_shapes=[pltpu.VMEM((size, n + 16, 2 * n), BF16)],
-    )(position, own, *swaps(own, 1, size))
-    got = [
-        lax.ppermute(mine if r < groups - 1 else carried, "tm", [(j, (j + r * size) % count) for j in range(count)])
-        for r in range(1, groups)
-    ]
+        out_specs=[VMEM] * 3,
+    )(position, total, *members)
+    near = swaps(whole, size, 2)[0]
+    before, carried, sent = call(
+        functools.partial(shift_kernel, size), "group_shifts", 2,
+        out_shape=[vector] * 3,
+        in_specs=[SMEM] + [VMEM] * (2 + size),
+        out_specs=[VMEM] * 3,
+        scratch_shapes=[pltpu.VMEM((size, 8, n), F32)],
+    )(position, group_maps, near, shift, *shifts)
+
+    def back(x, r):
+        return lax.ppermute(x, "tm", [(j, (j + r * size) % count) for j in range(count)])
+
+    if groups == 4:
+        gather = four_groups
+        got = [near] + swaps([carried, sent, sent], size, groups)
+    else:
+        gather = any_groups
+        got = [back(carried, r) for r in range(1, groups)] + [back(whole, r) for r in range(1, groups - 1)]
 
     return call(
-        functools.partial(final_kernel, size), "estimates", 6,
+        functools.partial(final_kernel, size, gather), "estimates", 6,
         out_shape=shape((steps, n), F32),
         in_specs=[SMEM, SMEM] + [VMEM] * (7 + len(got)),
         out_specs=VMEM,

time: 38.8 us -> 39.1 us (level)
  waiting for transfers between devices: 13 us -> 8.11 us
  starting transfers between devices: 13.5 us -> 16.5 us
  Pallas kernels: 12 us -> 14.2 us
    ppermute x9 -> x16, starting transfers between devices: 9.54 us -> 16.5 us  [swaps(): lax.ppermute(a, 'tm', [(j, j ^ r * step) for j in range(count)])]
    ppermute x3 -> x0, starting transfers between devices: 3.95 us -> none  [shards(): lax.ppermute(mine if r < groups - 1 else carried, 'tm', [(j, (j + r * siz...]
    ppermute x3 -> x0, waiting for transfers between devices: 3.03 us -> none  [shards(): lax.ppermute(mine if r < groups - 1 else carried, 'tm', [(j, (j + r * siz...]
    pallas_call x4 -> x5, Pallas kernels: 6.09 us -> 8.25 us  [the longest x1 2.94 us: shards(): call(local_kernel, 'local_states', 8, 1 << 40, out_shape=[shape((steps, n...]
    ppermute x9 -> x16, waiting for transfers between devices: 10 us -> 8.11 us  [swaps(): lax.ppermute(a, 'tm', [(j, j ^ r * step) for j in range(count)])]
  transfers between devices with their start and end apart: 12 -> 16, of which waited for: 6 -> 6; matrix products, arithmetic and copies ran while one was open for 0% -> 0% of each run, Pallas kernels for 11% -> 21%
where the time goes in v10:
time: 39.1 us; the launch traced here: 38.9 us
  starting transfers between devices  16.5 us (42%)
  Pallas kernels  14.2 us (36%)
  waiting for transfers between devices  8.11 us (21%)
    ppermute x16, starting transfers between devices, swaps(): lax.ppermute(a, 'tm', [(j, j ^ r * step) for j in range(count)])  16.5 us
    ppermute x16, waiting for transfers between devices, swaps(): lax.ppermute(a, 'tm', [(j, j ^ r * step) for j in range(count)])  8.11 us
    pallas_call x1, Pallas kernels, shards(): call(functools.partial(tree_kernel, steps), 'tree_of_maps', 8, out_shape=...  4.1 us
    pallas_call x1, Pallas kernels, shards(): call(local_kernel, 'local_states', 8, 1 << 40, out_shape=[shape((steps, n...  2.94 us
    pallas_call x1, Pallas kernels, shards(): call(functools.partial(final_kernel, size, gather), 'estimates', 6, out_s...  2.62 us
    pallas_call x1, Pallas kernels, shards(): call(functools.partial(front_kernel, cuts, len(small), size), 'front', 5,...  1.83 us
    pallas_call x1, Pallas kernels, shards(): call(functools.partial(shift_kernel, size), 'group_shifts', 2, out_shape=...  1.33 us
    pallas_call x1, Pallas kernels, shards(): call(functools.partial(map_kernel, size), 'group_maps', 2, out_shape=[sha...  1.1 us
  transfers between devices with their start and end apart: 16, of which 6 were waited for; matrix products, arithmetic and copies ran while one was open for 0% of the time, Pallas kernels for 21%

profile of v10, /device:TPU:0, one launch (start us, length us, event | category | flops | bytes accessed | tf_op | source)
XLA Modules:
  0.0 38.9 jit_solution(6904322416261408669)
XLA Ops:
  0.0 1.8 %front.1 = (bf16[16,128,256]{2,1,0:T(8,128)(2,1)S(1)}, s32[1,64]{1,0:T(1,128)S(1)}, f32[1,128]{1,0:T(1,128)S(1)}, bf16[128,128]{1,0:T(8,128)(2,1)S(1)}, s32[16,1...) custom-call(s32[1]{0:T(128)} %bitcast.pos_ref, ...), custom_call_target="tpu_custom_call" | custom-call | flops 1 | bytes 1 | tf_op jit(solution)/shard_map/front/pallas_call | solution.py:311
  1.8 0.5 %collective-permute-start = (bf16[4,64,128]{2,1,0:T(8,128)(2,1)S(1)}, bf16[4,64,128]{2,1,0:T(8,128)(2,1)S(1)}, u32[]{:S(2)}, u32[]{:S(2)}) collective-permute-start(bf16[4,64,128]{2,1,0:T(8,128)(2,1)S(1)} %get-tuple-element.38), channel_id=1, source_target_pairs={{0,1},{1,0},{2,3},{3,2},{4,5},{5,4},{6,7},{7,6},{8,9},{9,8},{10,11... | collective-permute-start | bytes 196616 | tf_op jit(solution)/shard_map/ppermute | solution.py:295
  2.4 2.6 %collective-permute-start.1 = (bf16[4,64,128]{2,1,0:T(8,128)(2,1)S(1)}, bf16[4,64,128]{2,1,0:T(8,128)(2,1)S(1)}, u32[]{:S(2)}, u32[]{:S(2)}) collective-permute-start(bf16[4,64,128]{2,1,0:T(8,128)(2,1)S(1)} %get-tuple-element.39), channel_id=1, source_target_pairs={{0,2},{1,3},{2,0},{3,1},{4,6},{5,7},{6,4},{7,5},{8,10},{9,11},{10,... | collective-permute-start | bytes 196616 | tf_op jit(solution)/shard_map/ppermute | solution.py:295
  4.9 0.1 collective-permute-start.2
  5.0 4.1 %tree_of_maps.1 = (bf16[31,128,256]{2,1,0:T(8,128)(2,1)}, bf16[31,128,256]{2,1,0:T(8,128)(2,1)}, bf16[128,256]{1,0:T(8,128)(2,1)S(1)}) custom-call(s32[1,64]{1,0:T(1,128)S(1)} %get-tuple-element.31.levels_ref, bf16[16,128,256]{2,1,0:T(8,128)(2,1)S(1)} %get-tuple-element.33.table_ref), custom_call_target="tpu_custom_call" | custom-call | flops 1 | bytes 1 | tf_op jit(solution)/shard_map/tree_of_maps/pallas_call | solution.py:321
  9.1 0.0 collective-permute-done.refs_1_
  9.1 0.0 collective-permute-done.1.refs_2_
  9.1 0.0 collective-permute-done.2.refs_3_
  9.1 0.3 project.1
  9.4 1.7 %collective-permute-start.5 = (bf16[128,256]{1,0:T(8,128)(2,1)S(1)}, bf16[128,256]{1,0:T(8,128)(2,1)S(1)}, u32[]{:S(2)}, u32[]{:S(2)}) collective-permute-start(bf16[128,256]{1,0:T(8,128)(2,1)S(1)} %get-tuple-element.41.refs_0_.total_ref), channel_id=1, source_target_pairs={{0,3},{1,2},{2,1},{3,0},{4,7},{5,6},{6,5},{7,4},{8,11},{9,10},{10,... | collective-permute-start | bytes 196616 | tf_op jit(solution)/shard_map/ppermute | solution.py:295
  11.1 0.1 collective-permute-start.4
  11.3 0.1 collective-permute-start.3
  11.3 3.9 %collective-permute-start.7 = (f32[64,128]{1,0:T(8,128)S(1)}, f32[64,128]{1,0:T(8,128)S(1)}, u32[]{:S(2)}, u32[]{:S(2)}) collective-permute-start(f32[64,128]{1,0:T(8,128)S(1)} %get-tuple-element.48), channel_id=1, source_target_pairs={{0,12},{1,13},{2,14},{3,15},{4,8},{5,9},{6,10},{7,11},{8,4},{9,5},... | collective-permute-start | bytes 98312 | tf_op jit(solution)/shard_map/ppermute | solution.py:295
  15.3 0.0 collective-permute-start.8
  15.3 0.0 collective-permute-done.5.refs_3_
  15.3 0.6 %collective-permute-start.9 = (f32[64,128]{1,0:T(8,128)S(1)}, f32[64,128]{1,0:T(8,128)S(1)}, u32[]{:S(2)}, u32[]{:S(2)}) collective-permute-start(f32[64,128]{1,0:T(8,128)S(1)} %get-tuple-element.50), channel_id=1, source_target_pairs={{0,4},{1,5},{2,6},{3,7},{4,0},{5,1},{6,2},{7,3},{8,12},{9,13},{10,... | collective-permute-start | bytes 98312 | tf_op jit(solution)/shard_map/ppermute | solution.py:295
  15.9 0.0 collective-permute-done.4.refs_2_
  15.9 0.0 collective-permute-done.3.refs_1_
  15.9 1.1 %group_maps.1 = (bf16[4,128,256]{2,1,0:T(8,128)(2,1)S(1)}, bf16[128,256]{1,0:T(8,128)(2,1)S(1)}, bf16[128,256]{1,0:T(8,128)(2,1)}) custom-call(s32[1]{0:T(128)} %bitcast.pos_ref, bf16[128,256]{1,0:T(8,128)(2,1)S(1)} %get-tuple-element.41.refs_0_.total_ref, bf16[128,256]{1,0:T(8,128)(2,1)S(1)} %collective-permute-done.3.refs_1_, ...), custom_call_target="tpu_custom_call" | custom-call | flops 1 | bytes 1 | tf_op jit(solution)/shard_map/group_maps/pallas_call | solution.py:355
  17.0 1.5 %collective-permute-start.6 = (bf16[128,256]{1,0:T(8,128)(2,1)}, bf16[128,256]{1,0:T(8,128)(2,1)}, u32[]{:S(2)}, u32[]{:S(2)}) collective-permute-start(bf16[128,256]{1,0:T(8,128)(2,1)} %get-tuple-element.44), channel_id=1, source_target_pairs={{0,4},{1,5},{2,6},{3,7},{4,0},{5,1},{6,2},{7,3},{8,12},{9,13},{10,... | collective-permute-start | bytes 196616 | tf_op jit(solution)/shard_map/ppermute | solution.py:295
  18.4 0.0 collective-permute-done.7.refs_1_
  18.4 1.7 %collective-permute-done.8.refs_2_ = f32[64,128]{1,0:T(8,128)S(1)} collective-permute-done((f32[64,128]{1,0:T(8,128)S(1)}, f32[64,128]{1,0:T(8,128)S(1)}, u32[]{:S(2)}, u32[]{:S(2)}) %collective-permute-start.8) | collective-permute-done | bytes 32800 | tf_op jit(solution)/shard_map/ppermute | solution.py:295
  20.1 0.0 collective-permute-done.9.refs_3_
  20.1 0.0 copy-start
  20.1 2.9 %local_states.1 = (f32[64,128]{1,0:T(8,128)S(1)}, f32[8,128]{1,0:T(8,128)S(1)}) custom-call(s32[1]{0:T(128)} %bitcast.pos_ref, s32[1,64]{1,0:T(1,128)S(1)} %get-tuple-element.31.levels_ref, bf16[128,128]{1,0:T(8,128)(2,1)S(1)} %get-tuple-element.45.gain_ref, f32[1,128]{1,0:T(1,128)S(1)} %get-tuple-element.32.init_ref, ...), custom_call_target="tpu_custom_call" | custom-call | flops 1099511627776 | bytes 1 | tf_op jit(solution)/shard_map/local_states/pallas_call | solution.py:347
  23.1 0.4 collective-permute-start.12
  23.5 1.3 %collective-permute-start.11 = (f32[8,128]{1,0:T(8,128)S(1)}, f32[8,128]{1,0:T(8,128)S(1)}, u32[]{:S(2)}, u32[]{:S(2)}) collective-permute-start(f32[8,128]{1,0:T(8,128)S(1)} %get-tuple-element.51.refs_0_), channel_id=1, source_target_pairs={{0,2},{1,3},{2,0},{3,1},{4,6},{5,7},{6,4},{7,5},{8,10},{9,11},{10,... | collective-permute-start | bytes 12296 | tf_op jit(solution)/shard_map/ppermute | solution.py:295
  24.7 0.3 collective-permute-start.10
  25.0 1.2 %collective-permute-done.12.refs_3_ = f32[8,128]{1,0:T(8,128)S(1)} collective-permute-done((f32[8,128]{1,0:T(8,128)S(1)}, f32[8,128]{1,0:T(8,128)S(1)}, u32[]{:S(2)}, u32[]{:S(2)}) %collective-permute-start.12) | collective-permute-done | bytes 4128 | tf_op jit(solution)/shard_map/ppermute | solution.py:295
  26.2 0.9 %collective-permute-done.11.refs_2_ = f32[8,128]{1,0:T(8,128)S(1)} collective-permute-done((f32[8,128]{1,0:T(8,128)S(1)}, f32[8,128]{1,0:T(8,128)S(1)}, u32[]{:S(2)}, u32[]{:S(2)}) %collective-permute-start.11) | collective-permute-done | bytes 4128 | tf_op jit(solution)/shard_map/ppermute | solution.py:295
  27.1 0.0 collective-permute-done.10.refs_1_
  27.1 0.0 collective-permute-done.6.near_ref.refs_0_
  27.1 1.3 %group_shifts.1 = (f32[8,128]{1,0:T(8,128)S(1)}, f32[8,128]{1,0:T(8,128)S(1)}, f32[8,128]{1,0:T(8,128)S(1)}) custom-call(s32[1]{0:T(128)} %bitcast.pos_ref, bf16[4,128,256]{2,1,0:T(8,128)(2,1)S(1)} %get-tuple-element.43.all_ref, bf16[128,256]{1,0:T(8,128)(2,1)} %collective-permute-done.6.near_ref.refs_0_, f32[8,128]{1,0:T(8,128)S(1)} %get-tuple-element.51.refs_0_, ...), custom_call_target="tpu_custom_call" | custom-call | flops 1 | bytes 1 | tf_op jit(solution)/shard_map/group_shifts/pallas_call | solution.py:362
  28.4 0.6 %collective-permute-start.13 = (f32[8,128]{1,0:T(8,128)S(1)}, f32[8,128]{1,0:T(8,128)S(1)}, u32[]{:S(2)}, u32[]{:S(2)}) collective-permute-start(f32[8,128]{1,0:T(8,128)S(1)} %get-tuple-element.55), channel_id=1, source_target_pairs={{0,4},{1,5},{2,6},{3,7},{4,0},{5,1},{6,2},{7,3},{8,12},{9,13},{10,... | collective-permute-start | bytes 12296 | tf_op jit(solution)/shard_map/ppermute | solution.py:295
  29.0 2.7 %collective-permute-start.15 = (f32[8,128]{1,0:T(8,128)S(1)}, f32[8,128]{1,0:T(8,128)S(1)}, u32[]{:S(2)}, u32[]{:S(2)}) collective-permute-start(f32[8,128]{1,0:T(8,128)S(1)} %get-tuple-element.56), channel_id=1, source_target_pairs={{0,12},{1,13},{2,14},{3,15},{4,8},{5,9},{6,10},{7,11},{8,4},{9,5},... | collective-permute-start | bytes 12296 | tf_op jit(solution)/shard_map/ppermute | solution.py:295
  31.7 0.2 collective-permute-start.14
  31.9 0.1 collective-permute-done.13.refs_1_
  32.0 2.4 %collective-permute-done.15.refs_3_ = f32[8,128]{1,0:T(8,128)S(1)} collective-permute-done((f32[8,128]{1,0:T(8,128)S(1)}, f32[8,128]{1,0:T(8,128)S(1)}, u32[]{:S(2)}, u32[]{:S(2)}) %collective-permute-start.15) | collective-permute-done | bytes 4128 | tf_op jit(solution)/shard_map/ppermute | solution.py:295
  34.4 1.8 %collective-permute-done.14.refs_2_ = f32[8,128]{1,0:T(8,128)S(1)} collective-permute-done((f32[8,128]{1,0:T(8,128)S(1)}, f32[8,128]{1,0:T(8,128)S(1)}, u32[]{:S(2)}, u32[]{:S(2)}) %collective-permute-start.14) | collective-permute-done | bytes 4128 | tf_op jit(solution)/shard_map/ppermute | solution.py:295
  36.2 0.0 copy-done
  36.2 2.6 %estimates.1 = f32[64,128]{1,0:T(8,128)} custom-call(s32[1]{0:T(128)} %bitcast.pos_ref, s32[1,64]{1,0:T(1,128)S(1)} %get-tuple-element.31.levels_ref, f32[1,128]{1,0:T(1,128)S(1)} %get-tuple-element.32.init_ref, bf16[128,256]{1,0:T(8,128)(2,1)S(1)} %get-tuple-element.42.prefix_ref, f32[8,128]{1,0:T(8,128)S(1)} %get-tuple-element.52.before_ref, ...), custom_call_target="tpu_custom_call" | custom-call | flops 1 | bytes 1 | tf_op jit(solution)/shard_map/estimates/pallas_call | solution.py:380
Async XLA Ops:
  1.8 7.3 %collective-permute-start = (bf16[4,64,128]{2,1,0:T(8,128)(2,1)S(1)}, bf16[4,64,128]{2,1,0:T(8,128)(2,1)S(1)}, u32[]{:S(2)}, u32[]{:S(2)}) collective-permute-start(bf16[4,64,128]{2,1,0:T(8,128)(2,1)S(1)} %get-tuple-element.38), channel_id=1, source_target_pairs={{0,1},{1,0},{2,3},{3,2},{4,5},{5,4},{6,7},{7,6},{8,9},{9,8},{10,11... | collective-permute-start | bytes 196616 | tf_op jit(solution)/shard_map/ppermute | solution.py:295
  2.4 6.8 %collective-permute-start.1 = (bf16[4,64,128]{2,1,0:T(8,128)(2,1)S(1)}, bf16[4,64,128]{2,1,0:T(8,128)(2,1)S(1)}, u32[]{:S(2)}, u32[]{:S(2)}) collective-permute-start(bf16[4,64,128]{2,1,0:T(8,128)(2,1)S(1)} %get-tuple-element.39), channel_id=1, source_target_pairs={{0,2},{1,3},{2,0},{3,1},{4,6},{5,7},{6,4},{7,5},{8,10},{9,11},{10,... | collective-permute-start | bytes 196616 | tf_op jit(solution)/shard_map/ppermute | solution.py:295
  4.9 4.2 %collective-permute-start.2 = (bf16[4,64,128]{2,1,0:T(8,128)(2,1)S(1)}, bf16[4,64,128]{2,1,0:T(8,128)(2,1)S(1)}, u32[]{:S(2)}, u32[]{:S(2)}) collective-permute-start(bf16[4,64,128]{2,1,0:T(8,128)(2,1)S(1)} %get-tuple-element.40), channel_id=1, source_target_pairs={{0,3},{1,2},{2,1},{3,0},{4,7},{5,6},{6,5},{7,4},{8,11},{9,10},{10,... | collective-permute-start | bytes 196616 | tf_op jit(solution)/shard_map/ppermute | solution.py:295
  9.4 5.9 %collective-permute-start.5 = (bf16[128,256]{1,0:T(8,128)(2,1)S(1)}, bf16[128,256]{1,0:T(8,128)(2,1)S(1)}, u32[]{:S(2)}, u32[]{:S(2)}) collective-permute-start(bf16[128,256]{1,0:T(8,128)(2,1)S(1)} %get-tuple-element.41.refs_0_.total_ref), channel_id=1, source_target_pairs={{0,3},{1,2},{2,1},{3,0},{4,7},{5,6},{6,5},{7,4},{8,11},{9,10},{10,... | collective-permute-start | bytes 196616 | tf_op jit(solution)/shard_map/ppermute | solution.py:295
  11.1 4.7 %collective-permute-start.4 = (bf16[128,256]{1,0:T(8,128)(2,1)S(1)}, bf16[128,256]{1,0:T(8,128)(2,1)S(1)}, u32[]{:S(2)}, u32[]{:S(2)}) collective-permute-start(bf16[128,256]{1,0:T(8,128)(2,1)S(1)} %get-tuple-element.41.refs_0_.total_ref), channel_id=1, source_target_pairs={{0,2},{1,3},{2,0},{3,1},{4,6},{5,7},{6,4},{7,5},{8,10},{9,11},{10,... | collective-permute-start | bytes 196616 | tf_op jit(solution)/shard_map/ppermute | solution.py:295
  11.3 4.6 %collective-permute-start.3 = (bf16[128,256]{1,0:T(8,128)(2,1)S(1)}, bf16[128,256]{1,0:T(8,128)(2,1)S(1)}, u32[]{:S(2)}, u32[]{:S(2)}) collective-permute-start(bf16[128,256]{1,0:T(8,128)(2,1)S(1)} %get-tuple-element.41.refs_0_.total_ref), channel_id=1, source_target_pairs={{0,1},{1,0},{2,3},{3,2},{4,5},{5,4},{6,7},{7,6},{8,9},{9,8},{10,11... | collective-permute-start | bytes 196616 | tf_op jit(solution)/shard_map/ppermute | solution.py:295
  11.3 7.1 %collective-permute-start.7 = (f32[64,128]{1,0:T(8,128)S(1)}, f32[64,128]{1,0:T(8,128)S(1)}, u32[]{:S(2)}, u32[]{:S(2)}) collective-permute-start(f32[64,128]{1,0:T(8,128)S(1)} %get-tuple-element.48), channel_id=1, source_target_pairs={{0,12},{1,13},{2,14},{3,15},{4,8},{5,9},{6,10},{7,11},{8,4},{9,5},... | collective-permute-start | bytes 98312 | tf_op jit(solution)/shard_map/ppermute | solution.py:295
  15.3 4.9 %collective-permute-start.8 = (f32[64,128]{1,0:T(8,128)S(1)}, f32[64,128]{1,0:T(8,128)S(1)}, u32[]{:S(2)}, u32[]{:S(2)}) collective-permute-start(f32[64,128]{1,0:T(8,128)S(1)} %get-tuple-element.49), channel_id=1, source_target_pairs={{0,8},{1,9},{2,10},{3,11},{4,12},{5,13},{6,14},{7,15},{8,0},{9,1},... | collective-permute-start | bytes 98312 | tf_op jit(solution)/shard_map/ppermute | solution.py:295
  15.3 4.9 %collective-permute-start.9 = (f32[64,128]{1,0:T(8,128)S(1)}, f32[64,128]{1,0:T(8,128)S(1)}, u32[]{:S(2)}, u32[]{:S(2)}) collective-permute-start(f32[64,128]{1,0:T(8,128)S(1)} %get-tuple-element.50), channel_id=1, source_target_pairs={{0,4},{1,5},{2,6},{3,7},{4,0},{5,1},{6,2},{7,3},{8,12},{9,13},{10,... | collective-permute-start | bytes 98312 | tf_op jit(solution)/shard_map/ppermute | solution.py:295
  17.0 10.1 %collective-permute-start.6 = (bf16[128,256]{1,0:T(8,128)(2,1)}, bf16[128,256]{1,0:T(8,128)(2,1)}, u32[]{:S(2)}, u32[]{:S(2)}) collective-permute-start(bf16[128,256]{1,0:T(8,128)(2,1)} %get-tuple-element.44), channel_id=1, source_target_pairs={{0,4},{1,5},{2,6},{3,7},{4,0},{5,1},{6,2},{7,3},{8,12},{9,13},{10,... | collective-permute-start | bytes 196616 | tf_op jit(solution)/shard_map/ppermute | solution.py:295
  20.1 16.1 %copy-start = (bf16[31,128,256]{2,1,0:T(8,128)(2,1)S(1)}, bf16[31,128,256]{2,1,0:T(8,128)(2,1)}, u32[]{:S(2)}) copy-start(bf16[31,128,256]{2,1,0:T(8,128)(2,1)} %get-tuple-element.54.left_ref) | copy-start | bytes 6094852
  23.1 3.1 %collective-permute-start.12 = (f32[8,128]{1,0:T(8,128)S(1)}, f32[8,128]{1,0:T(8,128)S(1)}, u32[]{:S(2)}, u32[]{:S(2)}) collective-permute-start(f32[8,128]{1,0:T(8,128)S(1)} %get-tuple-element.51.refs_0_), channel_id=1, source_target_pairs={{0,3},{1,2},{2,1},{3,0},{4,7},{5,6},{6,5},{7,4},{8,11},{9,10},{10,... | collective-permute-start | bytes 12296 | tf_op jit(solution)/shard_map/ppermute | solution.py:295
  23.5 3.6 %collective-permute-start.11 = (f32[8,128]{1,0:T(8,128)S(1)}, f32[8,128]{1,0:T(8,128)S(1)}, u32[]{:S(2)}, u32[]{:S(2)}) collective-permute-start(f32[8,128]{1,0:T(8,128)S(1)} %get-tuple-element.51.refs_0_), channel_id=1, source_target_pairs={{0,2},{1,3},{2,0},{3,1},{4,6},{5,7},{6,4},{7,5},{8,10},{9,11},{10,... | collective-permute-start | bytes 12296 | tf_op jit(solution)/shard_map/ppermute | solution.py:295
  24.7 2.4 %collective-permute-start.10 = (f32[8,128]{1,0:T(8,128)S(1)}, f32[8,128]{1,0:T(8,128)S(1)}, u32[]{:S(2)}, u32[]{:S(2)}) collective-permute-start(f32[8,128]{1,0:T(8,128)S(1)} %get-tuple-element.51.refs_0_), channel_id=1, source_target_pairs={{0,1},{1,0},{2,3},{3,2},{4,5},{5,4},{6,7},{7,6},{8,9},{9,8},{10,11... | collective-permute-start | bytes 12296 | tf_op jit(solution)/shard_map/ppermute | solution.py:295
  28.4 3.6 %collective-permute-start.13 = (f32[8,128]{1,0:T(8,128)S(1)}, f32[8,128]{1,0:T(8,128)S(1)}, u32[]{:S(2)}, u32[]{:S(2)}) collective-permute-start(f32[8,128]{1,0:T(8,128)S(1)} %get-tuple-element.55), channel_id=1, source_target_pairs={{0,4},{1,5},{2,6},{3,7},{4,0},{5,1},{6,2},{7,3},{8,12},{9,13},{10,... | collective-permute-start | bytes 12296 | tf_op jit(solution)/shard_map/ppermute | solution.py:295
  29.0 5.4 %collective-permute-start.15 = (f32[8,128]{1,0:T(8,128)S(1)}, f32[8,128]{1,0:T(8,128)S(1)}, u32[]{:S(2)}, u32[]{:S(2)}) collective-permute-start(f32[8,128]{1,0:T(8,128)S(1)} %get-tuple-element.56), channel_id=1, source_target_pairs={{0,12},{1,13},{2,14},{3,15},{4,8},{5,9},{6,10},{7,11},{8,4},{9,5},... | collective-permute-start | bytes 12296 | tf_op jit(solution)/shard_map/ppermute | solution.py:295
  31.7 4.5 %collective-permute-start.14 = (f32[8,128]{1,0:T(8,128)S(1)}, f32[8,128]{1,0:T(8,128)S(1)}, u32[]{:S(2)}, u32[]{:S(2)}) collective-permute-start(f32[8,128]{1,0:T(8,128)S(1)} %get-tuple-element.56), channel_id=1, source_target_pairs={{0,8},{1,9},{2,10},{3,11},{4,12},{5,13},{6,14},{7,15},{8,0},{9,1},... | collective-permute-start | bytes 12296 | tf_op jit(solution)/shard_map/ppermute | solution.py:295

commit v11 on v10

--- a/solution.py
+++ b/solution.py
@@ -119,7 +119,7 @@
         outs[r][...] = sums[(position // size) ^ r]
 
 
-def tree_kernel(steps, levels_ref, table_ref, left_hbm, right_hbm, total_ref, left_ref, right_ref, sems):
+def tree_kernel(steps, levels_ref, table_ref, left_hbm, right_hbm, table_hbm, total_ref, left_ref, right_ref, sems):
     base = steps // 4
 
     def first(t):
@@ -151,7 +151,8 @@
 
         lax.fori_loop(0, count // 4, body, 0)
 
-    copies = []
+    copies = [pltpu.make_async_copy(table_ref, table_hbm, sems.at[0])]
+    copies[0].start()
 
     def store(start, count):
         for ref, hbm in ((right_ref, right_hbm), (left_ref, left_hbm)):
@@ -174,13 +175,14 @@
         copy.wait()
 
 
-def local_kernel(pos_ref, levels_ref, gain_ref, init_ref, total_ref, table_ref, right_hbm, *refs):
-    parts, (lefts_ref, shift_ref, drive_ref, right_ref, sems) = refs[:-5], refs[-5:]
+def local_kernel(pos_ref, levels_ref, gain_ref, init_ref, total_ref, table_hbm, right_hbm, *refs):
+    parts, (lefts_ref, shift_ref, drive_ref, table_ref, right_ref, sems) = refs[:-6], refs[-6:]
     steps, n = drive_ref.shape
     base = steps // 4
     copies = [
-        pltpu.make_async_copy(right_hbm.at[pl.ds(0, base)], right_ref.at[pl.ds(0, base)], sems.at[0]),
-        pltpu.make_async_copy(right_hbm.at[pl.ds(base, base - 1)], right_ref.at[pl.ds(base, base - 1)], sems.at[1]),
+        pltpu.make_async_copy(table_hbm, table_ref, sems.at[0]),
+        pltpu.make_async_copy(right_hbm.at[pl.ds(0, base)], right_ref.at[pl.ds(0, base)], sems.at[1]),
+        pltpu.make_async_copy(right_hbm.at[pl.ds(base, base - 1)], right_ref.at[pl.ds(base, base - 1)], sems.at[2]),
     ]
     for copy in copies:
         copy.start()
@@ -192,8 +194,8 @@
     states = [row(drive_ref, t) for t in range(steps)]
     at, offset = 0, 0
     for level in range(steps.bit_length() - 1):
-        if level in (1, 2):
-            copies[level - 1].wait()
+        if level < 3:
+            copies[level].wait()
         later = []
         for i in range(len(states) // 2):
             mat = table_ref[levels_ref[0, 2 * i + 1]] if level == 0 else right_ref[offset + i]
@@ -318,12 +320,12 @@
     pairs = steps // 2 - 1
     tree = pltpu.VMEM((pairs, n, 2 * n), BF16)
     maps = pltpu.HBM((pairs, n, 2 * n), BF16)
-    left, right, total = call(
+    left, right, table, total = call(
         functools.partial(tree_kernel, steps), "tree_of_maps", 8,
-        out_shape=[maps, maps, one_map],
+        out_shape=[maps, maps, pltpu.HBM(table_shape.shape, BF16), one_map],
         in_specs=[SMEM, VMEM],
-        out_specs=[HBM, HBM, VMEM],
-        scratch_shapes=[tree, tree, dma((6,))],
+        out_specs=[HBM, HBM, HBM, VMEM],
+        scratch_shapes=[tree, tree, dma((7,))],
     )(levels, table)
 
     if turn:
@@ -347,10 +349,10 @@
     lefts, shift = call(
         local_kernel, "local_states", 8, 1 << 40,
         out_shape=[shape((steps, n), F32), vector],
-        in_specs=[SMEM, SMEM] + [VMEM] * 4 + [HBM] + [VMEM] * len(parts),
+        in_specs=[SMEM, SMEM] + [VMEM] * 3 + [HBM] * 2 + [VMEM] * len(parts),
         out_specs=[VMEM] * 2,
-        scratch_shapes=[pltpu.VMEM((steps, n), F32), tree, dma((2,))],
-    )(position, levels, gain, initial_state, total, table, hbm(right), *parts)
+        scratch_shapes=[pltpu.VMEM((steps, n), F32), pltpu.VMEM(table.shape, BF16), tree, dma((3,))],
+    )(position, levels, gain, initial_state, total, hbm(table), hbm(right), *parts)
     shifts = swaps(shift, 1, size)
     group_maps, prefix, whole = call(
         functools.partial(map_kernel, size), "group_maps", 2,

time: 39.1 us -> 39.4 us (level)
  no operation moved by 1% of the time
where the time goes in v11:
time: 39.4 us; the launch traced here: 39.2 us
  starting transfers between devices  16.5 us (42%)
  Pallas kernels  14.5 us (37%)
  waiting for transfers between devices  8.13 us (21%)
    ppermute x16, starting transfers between devices, swaps(): lax.ppermute(a, 'tm', [(j, j ^ r * step) for j in range(count)])  16.5 us
    ppermute x16, waiting for transfers between devices, swaps(): lax.ppermute(a, 'tm', [(j, j ^ r * step) for j in range(count)])  8.13 us
    pallas_call x1, Pallas kernels, shards(): call(functools.partial(tree_kernel, steps), 'tree_of_maps', 8, out_shape=...  4.11 us
    pallas_call x1, Pallas kernels, shards(): call(local_kernel, 'local_states', 8, 1 << 40, out_shape=[shape((steps, n...  3.24 us
    pallas_call x1, Pallas kernels, shards(): call(functools.partial(final_kernel, size, gather), 'estimates', 6, out_s...  2.62 us
    pallas_call x1, Pallas kernels, shards(): call(functools.partial(front_kernel, cuts, len(small), size), 'front', 5,...  1.83 us
    pallas_call x1, Pallas kernels, shards(): call(functools.partial(shift_kernel, size), 'group_shifts', 2, out_shape=...  1.33 us
    pallas_call x1, Pallas kernels, shards(): call(functools.partial(map_kernel, size), 'group_maps', 2, out_shape=[sha...  1.08 us
  transfers between devices with their start and end apart: 16, of which 6 were waited for; matrix products, arithmetic and copies ran while one was open for 0% of the time, Pallas kernels for 21%

profile of v11, /device:TPU:0, one launch (start us, length us, event | category | flops | bytes accessed | tf_op | source)
XLA Modules:
  0.0 39.2 jit_solution(3595416076597112997)
XLA Ops:
  0.0 1.8 %front.1 = (bf16[16,128,256]{2,1,0:T(8,128)(2,1)S(1)}, s32[1,64]{1,0:T(1,128)S(1)}, f32[1,128]{1,0:T(1,128)S(1)}, bf16[128,128]{1,0:T(8,128)(2,1)S(1)}, s32[16,1...) custom-call(s32[1]{0:T(128)} %bitcast.pos_ref, ...), custom_call_target="tpu_custom_call" | custom-call | flops 1 | bytes 1 | tf_op jit(solution)/shard_map/front/pallas_call | solution.py:313
  1.8 0.5 %collective-permute-start = (bf16[4,64,128]{2,1,0:T(8,128)(2,1)S(1)}, bf16[4,64,128]{2,1,0:T(8,128)(2,1)S(1)}, u32[]{:S(2)}, u32[]{:S(2)}) collective-permute-start(bf16[4,64,128]{2,1,0:T(8,128)(2,1)S(1)} %get-tuple-element.39), channel_id=1, source_target_pairs={{0,1},{1,0},{2,3},{3,2},{4,5},{5,4},{6,7},{7,6},{8,9},{9,8},{10,11... | collective-permute-start | bytes 196616 | tf_op jit(solution)/shard_map/ppermute | solution.py:297
  2.4 2.6 %collective-permute-start.1 = (bf16[4,64,128]{2,1,0:T(8,128)(2,1)S(1)}, bf16[4,64,128]{2,1,0:T(8,128)(2,1)S(1)}, u32[]{:S(2)}, u32[]{:S(2)}) collective-permute-start(bf16[4,64,128]{2,1,0:T(8,128)(2,1)S(1)} %get-tuple-element.40), channel_id=1, source_target_pairs={{0,2},{1,3},{2,0},{3,1},{4,6},{5,7},{6,4},{7,5},{8,10},{9,11},{10,... | collective-permute-start | bytes 196616 | tf_op jit(solution)/shard_map/ppermute | solution.py:297
  4.9 0.1 collective-permute-start.2
  5.0 4.1 %tree_of_maps.1 = (bf16[31,128,256]{2,1,0:T(8,128)(2,1)}, bf16[31,128,256]{2,1,0:T(8,128)(2,1)}, bf16[16,128,256]{2,1,0:T(8,128)(2,1)}, bf16[128,256]{1,0:T(8,128)(2,1)S(1)}) custom-call(s32[1,64]{1,0:T(1,128)S(1)} %get-tuple-element.32.levels_ref, bf16[16,128,256]{2,1,0:T(8,128)(2,1)S(1)} %get-tuple-element.34.table_ref), custom_call_target="tpu_custom_call" | custom-call | flops 1 | bytes 1 | tf_op jit(solution)/shard_map/tree_of_maps/pallas_call | solution.py:323
  9.1 0.0 collective-permute-done.refs_1_
  9.1 0.0 collective-permute-done.1.refs_2_
  9.1 0.0 collective-permute-done.2.refs_3_
  9.1 0.3 project.1
  9.4 1.7 %collective-permute-start.5 = (bf16[128,256]{1,0:T(8,128)(2,1)S(1)}, bf16[128,256]{1,0:T(8,128)(2,1)S(1)}, u32[]{:S(2)}, u32[]{:S(2)}) collective-permute-start(bf16[128,256]{1,0:T(8,128)(2,1)S(1)} %get-tuple-element.42.refs_0_.total_ref), channel_id=1, source_target_pairs={{0,3},{1,2},{2,1},{3,0},{4,7},{5,6},{6,5},{7,4},{8,11},{9,10},{10,... | collective-permute-start | bytes 196616 | tf_op jit(solution)/shard_map/ppermute | solution.py:297
  11.2 0.1 collective-permute-start.4
  11.3 0.1 collective-permute-start.3
  11.4 3.9 %collective-permute-start.7 = (f32[64,128]{1,0:T(8,128)S(1)}, f32[64,128]{1,0:T(8,128)S(1)}, u32[]{:S(2)}, u32[]{:S(2)}) collective-permute-start(f32[64,128]{1,0:T(8,128)S(1)} %get-tuple-element.50), channel_id=1, source_target_pairs={{0,12},{1,13},{2,14},{3,15},{4,8},{5,9},{6,10},{7,11},{8,4},{9,5},... | collective-permute-start | bytes 98312 | tf_op jit(solution)/shard_map/ppermute | solution.py:297
  15.3 0.0 collective-permute-start.8
  15.3 0.0 collective-permute-done.5.refs_3_
  15.3 0.6 %collective-permute-start.9 = (f32[64,128]{1,0:T(8,128)S(1)}, f32[64,128]{1,0:T(8,128)S(1)}, u32[]{:S(2)}, u32[]{:S(2)}) collective-permute-start(f32[64,128]{1,0:T(8,128)S(1)} %get-tuple-element.52), channel_id=1, source_target_pairs={{0,4},{1,5},{2,6},{3,7},{4,0},{5,1},{6,2},{7,3},{8,12},{9,13},{10,... | collective-permute-start | bytes 98312 | tf_op jit(solution)/shard_map/ppermute | solution.py:297
  15.9 0.0 collective-permute-done.4.refs_2_
  15.9 0.0 collective-permute-done.3.refs_1_
  15.9 1.1 %group_maps.1 = (bf16[4,128,256]{2,1,0:T(8,128)(2,1)S(1)}, bf16[128,256]{1,0:T(8,128)(2,1)S(1)}, bf16[128,256]{1,0:T(8,128)(2,1)}) custom-call(s32[1]{0:T(128)} %bitcast.pos_ref, bf16[128,256]{1,0:T(8,128)(2,1)S(1)} %get-tuple-element.42.refs_0_.total_ref, bf16[128,256]{1,0:T(8,128)(2,1)S(1)} %collective-permute-done.3.refs_1_, ...), custom_call_target="tpu_custom_call" | custom-call | flops 1 | bytes 1 | tf_op jit(solution)/shard_map/group_maps/pallas_call | solution.py:357
  16.9 1.5 %collective-permute-start.6 = (bf16[128,256]{1,0:T(8,128)(2,1)}, bf16[128,256]{1,0:T(8,128)(2,1)}, u32[]{:S(2)}, u32[]{:S(2)}) collective-permute-start(bf16[128,256]{1,0:T(8,128)(2,1)} %get-tuple-element.45), channel_id=1, source_target_pairs={{0,4},{1,5},{2,6},{3,7},{4,0},{5,1},{6,2},{7,3},{8,12},{9,13},{10,... | collective-permute-start | bytes 196616 | tf_op jit(solution)/shard_map/ppermute | solution.py:297
  18.4 0.0 collective-permute-done.7.refs_1_
  18.4 1.7 %collective-permute-done.8.refs_2_ = f32[64,128]{1,0:T(8,128)S(1)} collective-permute-done((f32[64,128]{1,0:T(8,128)S(1)}, f32[64,128]{1,0:T(8,128)S(1)}, u32[]{:S(2)}, u32[]{:S(2)}) %collective-permute-start.8) | collective-permute-done | bytes 32800 | tf_op jit(solution)/shard_map/ppermute | solution.py:297
  20.1 0.0 collective-permute-done.9.refs_3_
  20.1 0.0 copy-start
  20.2 0.0 copy-start.1
  20.2 3.2 %local_states.1 = (f32[64,128]{1,0:T(8,128)S(1)}, f32[8,128]{1,0:T(8,128)S(1)}) custom-call(s32[1]{0:T(128)} %bitcast.pos_ref, s32[1,64]{1,0:T(1,128)S(1)} %get-tuple-element.32.levels_ref, bf16[128,128]{1,0:T(8,128)(2,1)S(1)} %get-tuple-element.46.gain_ref, f32[1,128]{1,0:T(1,128)S(1)} %get-tuple-element.33.init_ref, ...), custom_call_target="tpu_custom_call" | custom-call | flops 1099511627776 | bytes 1 | tf_op jit(solution)/shard_map/local_states/pallas_call | solution.py:349
  23.4 0.4 collective-permute-start.12
  23.8 1.3 %collective-permute-start.11 = (f32[8,128]{1,0:T(8,128)S(1)}, f32[8,128]{1,0:T(8,128)S(1)}, u32[]{:S(2)}, u32[]{:S(2)}) collective-permute-start(f32[8,128]{1,0:T(8,128)S(1)} %get-tuple-element.53.refs_0_), channel_id=1, source_target_pairs={{0,2},{1,3},{2,0},{3,1},{4,6},{5,7},{6,4},{7,5},{8,10},{9,11},{10,... | collective-permute-start | bytes 12296 | tf_op jit(solution)/shard_map/ppermute | solution.py:297
  25.0 0.3 collective-permute-start.10
  25.3 1.2 %collective-permute-done.12.refs_3_ = f32[8,128]{1,0:T(8,128)S(1)} collective-permute-done((f32[8,128]{1,0:T(8,128)S(1)}, f32[8,128]{1,0:T(8,128)S(1)}, u32[]{:S(2)}, u32[]{:S(2)}) %collective-permute-start.12) | collective-permute-done | bytes 4128 | tf_op jit(solution)/shard_map/ppermute | solution.py:297
  26.5 0.9 %collective-permute-done.11.refs_2_ = f32[8,128]{1,0:T(8,128)S(1)} collective-permute-done((f32[8,128]{1,0:T(8,128)S(1)}, f32[8,128]{1,0:T(8,128)S(1)}, u32[]{:S(2)}, u32[]{:S(2)}) %collective-permute-start.11) | collective-permute-done | bytes 4128 | tf_op jit(solution)/shard_map/ppermute | solution.py:297
  27.4 0.0 collective-permute-done.10.refs_1_
  27.4 0.0 collective-permute-done.6.near_ref.refs_0_
  27.4 1.3 %group_shifts.1 = (f32[8,128]{1,0:T(8,128)S(1)}, f32[8,128]{1,0:T(8,128)S(1)}, f32[8,128]{1,0:T(8,128)S(1)}) custom-call(s32[1]{0:T(128)} %bitcast.pos_ref, bf16[4,128,256]{2,1,0:T(8,128)(2,1)S(1)} %get-tuple-element.44.all_ref, bf16[128,256]{1,0:T(8,128)(2,1)} %collective-permute-done.6.near_ref.refs_0_, f32[8,128]{1,0:T(8,128)S(1)} %get-tuple-element.53.refs_0_, ...), custom_call_target="tpu_custom_call" | custom-call | flops 1 | bytes 1 | tf_op jit(solution)/shard_map/group_shifts/pallas_call | solution.py:364
  28.7 0.6 %collective-permute-start.13 = (f32[8,128]{1,0:T(8,128)S(1)}, f32[8,128]{1,0:T(8,128)S(1)}, u32[]{:S(2)}, u32[]{:S(2)}) collective-permute-start(f32[8,128]{1,0:T(8,128)S(1)} %get-tuple-element.57), channel_id=1, source_target_pairs={{0,4},{1,5},{2,6},{3,7},{4,0},{5,1},{6,2},{7,3},{8,12},{9,13},{10,... | collective-permute-start | bytes 12296 | tf_op jit(solution)/shard_map/ppermute | solution.py:297
  29.3 2.7 %collective-permute-start.15 = (f32[8,128]{1,0:T(8,128)S(1)}, f32[8,128]{1,0:T(8,128)S(1)}, u32[]{:S(2)}, u32[]{:S(2)}) collective-permute-start(f32[8,128]{1,0:T(8,128)S(1)} %get-tuple-element.58), channel_id=1, source_target_pairs={{0,12},{1,13},{2,14},{3,15},{4,8},{5,9},{6,10},{7,11},{8,4},{9,5},... | collective-permute-start | bytes 12296 | tf_op jit(solution)/shard_map/ppermute | solution.py:297
  32.0 0.2 collective-permute-start.14
  32.2 0.1 collective-permute-done.13.refs_1_
  32.3 2.4 %collective-permute-done.15.refs_3_ = f32[8,128]{1,0:T(8,128)S(1)} collective-permute-done((f32[8,128]{1,0:T(8,128)S(1)}, f32[8,128]{1,0:T(8,128)S(1)}, u32[]{:S(2)}, u32[]{:S(2)}) %collective-permute-start.15) | collective-permute-done | bytes 4128 | tf_op jit(solution)/shard_map/ppermute | solution.py:297
  34.7 1.8 %collective-permute-done.14.refs_2_ = f32[8,128]{1,0:T(8,128)S(1)} collective-permute-done((f32[8,128]{1,0:T(8,128)S(1)}, f32[8,128]{1,0:T(8,128)S(1)}, u32[]{:S(2)}, u32[]{:S(2)}) %collective-permute-start.14) | collective-permute-done | bytes 4128 | tf_op jit(solution)/shard_map/ppermute | solution.py:297
  36.5 0.0 copy-done
  36.5 0.0 copy-done.1
  36.5 2.6 %estimates.1 = f32[64,128]{1,0:T(8,128)} custom-call(s32[1]{0:T(128)} %bitcast.pos_ref, s32[1,64]{1,0:T(1,128)S(1)} %get-tuple-element.32.levels_ref, f32[1,128]{1,0:T(1,128)S(1)} %get-tuple-element.33.init_ref, bf16[128,256]{1,0:T(8,128)(2,1)S(1)} %get-tuple-element.43.prefix_ref, f32[8,128]{1,0:T(8,128)S(1)} %get-tuple-element.54.before_ref, ...), custom_call_target="tpu_custom_call" | custom-call | flops 1 | bytes 1 | tf_op jit(solution)/shard_map/estimates/pallas_call | solution.py:382
Async XLA Ops:
  1.8 7.3 %collective-permute-start = (bf16[4,64,128]{2,1,0:T(8,128)(2,1)S(1)}, bf16[4,64,128]{2,1,0:T(8,128)(2,1)S(1)}, u32[]{:S(2)}, u32[]{:S(2)}) collective-permute-start(bf16[4,64,128]{2,1,0:T(8,128)(2,1)S(1)} %get-tuple-element.39), channel_id=1, source_target_pairs={{0,1},{1,0},{2,3},{3,2},{4,5},{5,4},{6,7},{7,6},{8,9},{9,8},{10,11... | collective-permute-start | bytes 196616 | tf_op jit(solution)/shard_map/ppermute | solution.py:297
  2.4 6.8 %collective-permute-start.1 = (bf16[4,64,128]{2,1,0:T(8,128)(2,1)S(1)}, bf16[4,64,128]{2,1,0:T(8,128)(2,1)S(1)}, u32[]{:S(2)}, u32[]{:S(2)}) collective-permute-start(bf16[4,64,128]{2,1,0:T(8,128)(2,1)S(1)} %get-tuple-element.40), channel_id=1, source_target_pairs={{0,2},{1,3},{2,0},{3,1},{4,6},{5,7},{6,4},{7,5},{8,10},{9,11},{10,... | collective-permute-start | bytes 196616 | tf_op jit(solution)/shard_map/ppermute | solution.py:297
  4.9 4.2 %collective-permute-start.2 = (bf16[4,64,128]{2,1,0:T(8,128)(2,1)S(1)}, bf16[4,64,128]{2,1,0:T(8,128)(2,1)S(1)}, u32[]{:S(2)}, u32[]{:S(2)}) collective-permute-start(bf16[4,64,128]{2,1,0:T(8,128)(2,1)S(1)} %get-tuple-element.41), channel_id=1, source_target_pairs={{0,3},{1,2},{2,1},{3,0},{4,7},{5,6},{6,5},{7,4},{8,11},{9,10},{10,... | collective-permute-start | bytes 196616 | tf_op jit(solution)/shard_map/ppermute | solution.py:297
  9.4 5.9 %collective-permute-start.5 = (bf16[128,256]{1,0:T(8,128)(2,1)S(1)}, bf16[128,256]{1,0:T(8,128)(2,1)S(1)}, u32[]{:S(2)}, u32[]{:S(2)}) collective-permute-start(bf16[128,256]{1,0:T(8,128)(2,1)S(1)} %get-tuple-element.42.refs_0_.total_ref), channel_id=1, source_target_pairs={{0,3},{1,2},{2,1},{3,0},{4,7},{5,6},{6,5},{7,4},{8,11},{9,10},{10,... | collective-permute-start | bytes 196616 | tf_op jit(solution)/shard_map/ppermute | solution.py:297
  11.2 4.7 %collective-permute-start.4 = (bf16[128,256]{1,0:T(8,128)(2,1)S(1)}, bf16[128,256]{1,0:T(8,128)(2,1)S(1)}, u32[]{:S(2)}, u32[]{:S(2)}) collective-permute-start(bf16[128,256]{1,0:T(8,128)(2,1)S(1)} %get-tuple-element.42.refs_0_.total_ref), channel_id=1, source_target_pairs={{0,2},{1,3},{2,0},{3,1},{4,6},{5,7},{6,4},{7,5},{8,10},{9,11},{10,... | collective-permute-start | bytes 196616 | tf_op jit(solution)/shard_map/ppermute | solution.py:297
  11.3 4.6 %collective-permute-start.3 = (bf16[128,256]{1,0:T(8,128)(2,1)S(1)}, bf16[128,256]{1,0:T(8,128)(2,1)S(1)}, u32[]{:S(2)}, u32[]{:S(2)}) collective-permute-start(bf16[128,256]{1,0:T(8,128)(2,1)S(1)} %get-tuple-element.42.refs_0_.total_ref), channel_id=1, source_target_pairs={{0,1},{1,0},{2,3},{3,2},{4,5},{5,4},{6,7},{7,6},{8,9},{9,8},{10,11... | collective-permute-start | bytes 196616 | tf_op jit(solution)/shard_map/ppermute | solution.py:297
  11.4 7.1 %collective-permute-start.7 = (f32[64,128]{1,0:T(8,128)S(1)}, f32[64,128]{1,0:T(8,128)S(1)}, u32[]{:S(2)}, u32[]{:S(2)}) collective-permute-start(f32[64,128]{1,0:T(8,128)S(1)} %get-tuple-element.50), channel_id=1, source_target_pairs={{0,12},{1,13},{2,14},{3,15},{4,8},{5,9},{6,10},{7,11},{8,4},{9,5},... | collective-permute-start | bytes 98312 | tf_op jit(solution)/shard_map/ppermute | solution.py:297
  15.3 4.9 %collective-permute-start.8 = (f32[64,128]{1,0:T(8,128)S(1)}, f32[64,128]{1,0:T(8,128)S(1)}, u32[]{:S(2)}, u32[]{:S(2)}) collective-permute-start(f32[64,128]{1,0:T(8,128)S(1)} %get-tuple-element.51), channel_id=1, source_target_pairs={{0,8},{1,9},{2,10},{3,11},{4,12},{5,13},{6,14},{7,15},{8,0},{9,1},... | collective-permute-start | bytes 98312 | tf_op jit(solution)/shard_map/ppermute | solution.py:297
  15.3 4.9 %collective-permute-start.9 = (f32[64,128]{1,0:T(8,128)S(1)}, f32[64,128]{1,0:T(8,128)S(1)}, u32[]{:S(2)}, u32[]{:S(2)}) collective-permute-start(f32[64,128]{1,0:T(8,128)S(1)} %get-tuple-element.52), channel_id=1, source_target_pairs={{0,4},{1,5},{2,6},{3,7},{4,0},{5,1},{6,2},{7,3},{8,12},{9,13},{10,... | collective-permute-start | bytes 98312 | tf_op jit(solution)/shard_map/ppermute | solution.py:297
  16.9 10.4 %collective-permute-start.6 = (bf16[128,256]{1,0:T(8,128)(2,1)}, bf16[128,256]{1,0:T(8,128)(2,1)}, u32[]{:S(2)}, u32[]{:S(2)}) collective-permute-start(bf16[128,256]{1,0:T(8,128)(2,1)} %get-tuple-element.45), channel_id=1, source_target_pairs={{0,4},{1,5},{2,6},{3,7},{4,0},{5,1},{6,2},{7,3},{8,12},{9,13},{10,... | collective-permute-start | bytes 196616 | tf_op jit(solution)/shard_map/ppermute | solution.py:297
  20.1 16.4 %copy-start = (bf16[31,128,256]{2,1,0:T(8,128)(2,1)S(1)}, bf16[31,128,256]{2,1,0:T(8,128)(2,1)}, u32[]{:S(2)}) copy-start(bf16[31,128,256]{2,1,0:T(8,128)(2,1)} %get-tuple-element.56.left_ref) | copy-start | bytes 6094852
  20.2 16.4 %copy-start.1 = (bf16[16,128,256]{2,1,0:T(8,128)(2,1)S(1)}, bf16[16,128,256]{2,1,0:T(8,128)(2,1)}, u32[]{:S(2)}) copy-start(bf16[16,128,256]{2,1,0:T(8,128)(2,1)} %get-tuple-element.47.table_hbm.table_ref) | copy-start | bytes 3145732
  23.4 3.1 %collective-permute-start.12 = (f32[8,128]{1,0:T(8,128)S(1)}, f32[8,128]{1,0:T(8,128)S(1)}, u32[]{:S(2)}, u32[]{:S(2)}) collective-permute-start(f32[8,128]{1,0:T(8,128)S(1)} %get-tuple-element.53.refs_0_), channel_id=1, source_target_pairs={{0,3},{1,2},{2,1},{3,0},{4,7},{5,6},{6,5},{7,4},{8,11},{9,10},{10,... | collective-permute-start | bytes 12296 | tf_op jit(solution)/shard_map/ppermute | solution.py:297
  23.8 3.6 %collective-permute-start.11 = (f32[8,128]{1,0:T(8,128)S(1)}, f32[8,128]{1,0:T(8,128)S(1)}, u32[]{:S(2)}, u32[]{:S(2)}) collective-permute-start(f32[8,128]{1,0:T(8,128)S(1)} %get-tuple-element.53.refs_0_), channel_id=1, source_target_pairs={{0,2},{1,3},{2,0},{3,1},{4,6},{5,7},{6,4},{7,5},{8,10},{9,11},{10,... | collective-permute-start | bytes 12296 | tf_op jit(solution)/shard_map/ppermute | solution.py:297
  25.0 2.4 %collective-permute-start.10 = (f32[8,128]{1,0:T(8,128)S(1)}, f32[8,128]{1,0:T(8,128)S(1)}, u32[]{:S(2)}, u32[]{:S(2)}) collective-permute-start(f32[8,128]{1,0:T(8,128)S(1)} %get-tuple-element.53.refs_0_), channel_id=1, source_target_pairs={{0,1},{1,0},{2,3},{3,2},{4,5},{5,4},{6,7},{7,6},{8,9},{9,8},{10,11... | collective-permute-start | bytes 12296 | tf_op jit(solution)/shard_map/ppermute | solution.py:297
  28.7 3.6 %collective-permute-start.13 = (f32[8,128]{1,0:T(8,128)S(1)}, f32[8,128]{1,0:T(8,128)S(1)}, u32[]{:S(2)}, u32[]{:S(2)}) collective-permute-start(f32[8,128]{1,0:T(8,128)S(1)} %get-tuple-element.57), channel_id=1, source_target_pairs={{0,4},{1,5},{2,6},{3,7},{4,0},{5,1},{6,2},{7,3},{8,12},{9,13},{10,... | collective-permute-start | bytes 12296 | tf_op jit(solution)/shard_map/ppermute | solution.py:297
  29.3 5.4 %collective-permute-start.15 = (f32[8,128]{1,0:T(8,128)S(1)}, f32[8,128]{1,0:T(8,128)S(1)}, u32[]{:S(2)}, u32[]{:S(2)}) collective-permute-start(f32[8,128]{1,0:T(8,128)S(1)} %get-tuple-element.58), channel_id=1, source_target_pairs={{0,12},{1,13},{2,14},{3,15},{4,8},{5,9},{6,10},{7,11},{8,4},{9,5},... | collective-permute-start | bytes 12296 | tf_op jit(solution)/shard_map/ppermute | solution.py:297
  32.0 4.5 %collective-permute-start.14 = (f32[8,128]{1,0:T(8,128)S(1)}, f32[8,128]{1,0:T(8,128)S(1)}, u32[]{:S(2)}, u32[]{:S(2)}) collective-permute-start(f32[8,128]{1,0:T(8,128)S(1)} %get-tuple-element.58), channel_id=1, source_target_pairs={{0,8},{1,9},{2,10},{3,11},{4,12},{5,13},{6,14},{7,15},{8,0},{9,1},... | collective-permute-start | bytes 12296 | tf_op jit(solution)/shard_map/ppermute | solution.py:297

commit v12 on v10

--- a/solution.py
+++ b/solution.py
@@ -14,6 +14,7 @@
 VMEM = pl.BlockSpec(memory_space=pltpu.VMEM)
 SMEM = pl.BlockSpec(memory_space=pltpu.SMEM)
 HBM = pl.BlockSpec(memory_space=pltpu.HBM)
+ANY = pl.BlockSpec(memory_space=pl.ANY)
 shape = jax.ShapeDtypeStruct
 
 
@@ -166,9 +167,9 @@
     count, start = base // 4, base + base // 2
     while count >= 1:
         run(later_pairs, start, count)
+        store(start, count)
         start += count
         count //= 2
-    store(base + base // 2, base // 2 - 1)
     total_ref[...] = pair(node(start - 1))
     for copy in copies:
         copy.wait()
@@ -227,7 +228,9 @@
 
 def shift_kernel(size, pos_ref, all_ref, near_ref, *refs):
     shifts = refs[:size]
-    before_ref, whole_ref, far_ref, held_ref = refs[size:]
+    before_ref, whole_ref, far_ref, map_ref, held_ref, sem = refs[size:]
+    copy = pltpu.make_async_copy(near_ref, map_ref, sem)
+    copy.start()
     member = pos_ref[0] % size
     for r in range(size):
         held_ref[member ^ r] = shifts[r][...]
@@ -237,7 +240,8 @@
         run = vm(run, all_ref[q]) + held_ref[q]
     before_ref[...] = before
     whole_ref[...] = run
-    far_ref[...] = jnp.where((pos_ref[0] // size) % 2 == 0, vm(run, near_ref[...]), run)
+    copy.wait()
+    far_ref[...] = jnp.where((pos_ref[0] // size) % 2 == 0, vm(run, map_ref[...]), run)
 
 
 def four_groups(group, near_ref, shift_ref, *far):
@@ -323,7 +327,7 @@
         out_shape=[maps, maps, one_map],
         in_specs=[SMEM, VMEM],
         out_specs=[HBM, HBM, VMEM],
-        scratch_shapes=[tree, tree, dma((6,))],
+        scratch_shapes=[tree, tree, dma((2 * steps.bit_length(),))],
     )(levels, table)
 
     if turn:
@@ -336,7 +340,7 @@
             scratch_shapes=[pltpu.VMEM((groups, steps, n), F32), pltpu.VMEM((count, pixels), F32)],
         )(position, total, mode, weight, slab, *swaps(slabs, 1, size))
         far = swaps(parts, size, groups)
-        parts = [first] + far[::-1]
+        parts = [first] + far
     else:
         x = lax.all_to_all(frames, "tm", split_axis=1, concat_axis=0, tiled=True)
         channels = jnp.arange(n, dtype=jnp.int32)
@@ -354,17 +358,17 @@
     shifts = swaps(shift, 1, size)
     group_maps, prefix, whole = call(
         functools.partial(map_kernel, size), "group_maps", 2,
-        out_shape=[shape((size, n, 2 * n), BF16), one_map, one_map],
+        out_shape=[shape((size, n, 2 * n), BF16), one_map, pltpu.VMEM(one_map.shape, BF16)],
         in_specs=[SMEM] + [VMEM] * size,
         out_specs=[VMEM] * 3,
     )(position, total, *members)
     near = swaps(whole, size, 2)[0]
-    before, carried, sent = call(
+    before, carried, sent, near = call(
         functools.partial(shift_kernel, size), "group_shifts", 2,
-        out_shape=[vector] * 3,
-        in_specs=[SMEM] + [VMEM] * (2 + size),
-        out_specs=[VMEM] * 3,
-        scratch_shapes=[pltpu.VMEM((size, 8, n), F32)],
+        out_shape=[vector] * 3 + [one_map],
+        in_specs=[SMEM, VMEM, ANY] + [VMEM] * size,
+        out_specs=[VMEM] * 4,
+        scratch_shapes=[pltpu.VMEM((size, 8, n), F32), dma(())],
     )(position, group_maps, near, shift, *shifts)
 
     def back(x, r):

time: 39.1 us -> 38.6 us (0.987)
  Pallas kernels: 14.2 us -> 13.3 us
  waiting for transfers between devices: 8.11 us -> 8.58 us
    ppermute x16, waiting for transfers between devices: 8.11 us -> 8.58 us  [swaps(): lax.ppermute(a, 'tm', [(j, j ^ r * step) for j in range(count)])]
  transfers between devices with their start and end apart: 16 -> 16, of which waited for: 6 -> 8; matrix products, arithmetic and copies ran while one was open for 0% -> 0% of each run, Pallas kernels for 21% -> 21%
where the time goes in v12:
time: 38.6 us; the launch traced here: 38.4 us
  starting transfers between devices  16.4 us (42%)
  Pallas kernels  13.3 us (34%)
  waiting for transfers between devices  8.58 us (22%)
    ppermute x16, starting transfers between devices, swaps(): lax.ppermute(a, 'tm', [(j, j ^ r * step) for j in range(count)])  16.4 us
    ppermute x16, waiting for transfers between devices, swaps(): lax.ppermute(a, 'tm', [(j, j ^ r * step) for j in range(count)])  8.58 us
    pallas_call x1, Pallas kernels, shards(): call(functools.partial(tree_kernel, steps), 'tree_of_maps', 8, out_shape=...  3.89 us
    pallas_call x1, Pallas kernels, shards(): call(local_kernel, 'local_states', 8, 1 << 40, out_shape=[shape((steps, n...  2.94 us
    pallas_call x1, Pallas kernels, shards(): call(functools.partial(final_kernel, size, gather), 'estimates', 6, out_s...  2.32 us
    pallas_call x1, Pallas kernels, shards(): call(functools.partial(front_kernel, cuts, len(small), size), 'front', 5,...  1.83 us
    pallas_call x1, Pallas kernels, shards(): call(functools.partial(map_kernel, size), 'group_maps', 2, out_shape=[sha...  1.08 us
    pallas_call x1, Pallas kernels, shards(): call(functools.partial(shift_kernel, size), 'group_shifts', 2, out_shape=...  1 us
  transfers between devices with their start and end apart: 16, of which 8 were waited for; matrix products, arithmetic and copies ran while one was open for 0% of the time, Pallas kernels for 21%

profile of v12, /device:TPU:0, one launch (start us, length us, event | category | flops | bytes accessed | tf_op | source)
XLA Modules:
  0.0 38.4 jit_solution(3861710349912561920)
XLA Ops:
  0.0 1.8 %front.1 = (bf16[16,128,256]{2,1,0:T(8,128)(2,1)S(1)}, s32[1,64]{1,0:T(1,128)S(1)}, f32[1,128]{1,0:T(1,128)S(1)}, bf16[128,128]{1,0:T(8,128)(2,1)S(1)}, s32[16,1...) custom-call(s32[1]{0:T(128)} %bitcast.pos_ref, ...), custom_call_target="tpu_custom_call" | custom-call | flops 1 | bytes 1 | tf_op jit(solution)/shard_map/front/pallas_call | solution.py:315
  1.8 0.5 %collective-permute-start = (bf16[4,64,128]{2,1,0:T(8,128)(2,1)S(1)}, bf16[4,64,128]{2,1,0:T(8,128)(2,1)S(1)}, u32[]{:S(2)}, u32[]{:S(2)}) collective-permute-start(bf16[4,64,128]{2,1,0:T(8,128)(2,1)S(1)} %get-tuple-element.39), channel_id=1, source_target_pairs={{0,1},{1,0},{2,3},{3,2},{4,5},{5,4},{6,7},{7,6},{8,9},{9,8},{10,11... | collective-permute-start | bytes 196616 | tf_op jit(solution)/shard_map/ppermute | solution.py:299
  2.4 2.6 %collective-permute-start.1 = (bf16[4,64,128]{2,1,0:T(8,128)(2,1)S(1)}, bf16[4,64,128]{2,1,0:T(8,128)(2,1)S(1)}, u32[]{:S(2)}, u32[]{:S(2)}) collective-permute-start(bf16[4,64,128]{2,1,0:T(8,128)(2,1)S(1)} %get-tuple-element.40), channel_id=1, source_target_pairs={{0,2},{1,3},{2,0},{3,1},{4,6},{5,7},{6,4},{7,5},{8,10},{9,11},{10,... | collective-permute-start | bytes 196616 | tf_op jit(solution)/shard_map/ppermute | solution.py:299
  4.9 0.1 collective-permute-start.2
  5.0 3.9 %tree_of_maps.1 = (bf16[31,128,256]{2,1,0:T(8,128)(2,1)}, bf16[31,128,256]{2,1,0:T(8,128)(2,1)}, bf16[128,256]{1,0:T(8,128)(2,1)S(1)}) custom-call(s32[1,64]{1,0:T(1,128)S(1)} %get-tuple-element.32.levels_ref, bf16[16,128,256]{2,1,0:T(8,128)(2,1)S(1)} %get-tuple-element.34.table_ref), custom_call_target="tpu_custom_call" | custom-call | flops 1 | bytes 1 | tf_op jit(solution)/shard_map/tree_of_maps/pallas_call | solution.py:325
  8.9 0.0 collective-permute-done.refs_1_
  8.9 0.0 collective-permute-done.1.refs_2_
  8.9 0.1 collective-permute-done.2.refs_3_
  9.0 0.3 project.1
  9.2 1.7 %collective-permute-start.5 = (bf16[128,256]{1,0:T(8,128)(2,1)S(1)}, bf16[128,256]{1,0:T(8,128)(2,1)S(1)}, u32[]{:S(2)}, u32[]{:S(2)}) collective-permute-start(bf16[128,256]{1,0:T(8,128)(2,1)S(1)} %get-tuple-element.42.refs_0_.total_ref), channel_id=1, source_target_pairs={{0,3},{1,2},{2,1},{3,0},{4,7},{5,6},{6,5},{7,4},{8,11},{9,10},{10,... | collective-permute-start | bytes 196616 | tf_op jit(solution)/shard_map/ppermute | solution.py:299
  10.9 0.2 collective-permute-start.4
  11.1 0.1 collective-permute-start.3
  11.2 1.9 %collective-permute-start.7 = (f32[64,128]{1,0:T(8,128)S(1)}, f32[64,128]{1,0:T(8,128)S(1)}, u32[]{:S(2)}, u32[]{:S(2)}) collective-permute-start(f32[64,128]{1,0:T(8,128)S(1)} %get-tuple-element.49), channel_id=1, source_target_pairs={{0,4},{1,5},{2,6},{3,7},{4,0},{5,1},{6,2},{7,3},{8,12},{9,13},{10,... | collective-permute-start | bytes 98312 | tf_op jit(solution)/shard_map/ppermute | solution.py:299
  13.0 2.6 %collective-permute-start.8 = (f32[64,128]{1,0:T(8,128)S(1)}, f32[64,128]{1,0:T(8,128)S(1)}, u32[]{:S(2)}, u32[]{:S(2)}) collective-permute-start(f32[64,128]{1,0:T(8,128)S(1)} %get-tuple-element.50), channel_id=1, source_target_pairs={{0,8},{1,9},{2,10},{3,11},{4,12},{5,13},{6,14},{7,15},{8,0},{9,1},... | collective-permute-start | bytes 98312 | tf_op jit(solution)/shard_map/ppermute | solution.py:299
  15.6 0.0 collective-permute-done.5.refs_3_
  15.6 1.4 %collective-permute-start.9 = (f32[64,128]{1,0:T(8,128)S(1)}, f32[64,128]{1,0:T(8,128)S(1)}, u32[]{:S(2)}, u32[]{:S(2)}) collective-permute-start(f32[64,128]{1,0:T(8,128)S(1)} %get-tuple-element.51), channel_id=1, source_target_pairs={{0,12},{1,13},{2,14},{3,15},{4,8},{5,9},{6,10},{7,11},{8,4},{9,5},... | collective-permute-start | bytes 98312 | tf_op jit(solution)/shard_map/ppermute | solution.py:299
  17.0 0.0 collective-permute-done.4.refs_2_
  17.0 0.0 collective-permute-done.3.refs_1_
  17.0 1.1 %group_maps.1 = (bf16[4,128,256]{2,1,0:T(8,128)(2,1)S(1)}, bf16[128,256]{1,0:T(8,128)(2,1)S(1)}, bf16[128,256]{1,0:T(8,128)(2,1)}) custom-call(s32[1]{0:T(128)} %bitcast.pos_ref, bf16[128,256]{1,0:T(8,128)(2,1)S(1)} %get-tuple-element.42.refs_0_.total_ref, bf16[128,256]{1,0:T(8,128)(2,1)S(1)} %collective-permute-done.3.refs_1_, ...), custom_call_target="tpu_custom_call" | custom-call | flops 1 | bytes 1 | tf_op jit(solution)/shard_map/group_maps/pallas_call | solution.py:359
  18.1 0.0 collective-permute-start.6
  18.1 0.0 collective-permute-done.7.refs_1_
  18.1 0.3 collective-permute-done.8.refs_2_
  18.5 3.0 %collective-permute-done.9.refs_3_ = f32[64,128]{1,0:T(8,128)S(1)} collective-permute-done((f32[64,128]{1,0:T(8,128)S(1)}, f32[64,128]{1,0:T(8,128)S(1)}, u32[]{:S(2)}, u32[]{:S(2)}) %collective-permute-start.9) | collective-permute-done | bytes 32800 | tf_op jit(solution)/shard_map/ppermute | solution.py:299
  21.4 0.0 copy-start
  21.4 2.9 %local_states.1 = (f32[64,128]{1,0:T(8,128)S(1)}, f32[8,128]{1,0:T(8,128)S(1)}) custom-call(s32[1]{0:T(128)} %bitcast.pos_ref, s32[1,64]{1,0:T(1,128)S(1)} %get-tuple-element.32.levels_ref, bf16[128,128]{1,0:T(8,128)(2,1)S(1)} %get-tuple-element.46.gain_ref, f32[1,128]{1,0:T(1,128)S(1)} %get-tuple-element.33.init_ref, ...), custom_call_target="tpu_custom_call" | custom-call | flops 1099511627776 | bytes 1 | tf_op jit(solution)/shard_map/local_states/pallas_call | solution.py:351
  24.4 0.1 collective-permute-start.12
  24.5 1.6 %collective-permute-start.11 = (f32[8,128]{1,0:T(8,128)S(1)}, f32[8,128]{1,0:T(8,128)S(1)}, u32[]{:S(2)}, u32[]{:S(2)}) collective-permute-start(f32[8,128]{1,0:T(8,128)S(1)} %get-tuple-element.52.refs_0_), channel_id=1, source_target_pairs={{0,2},{1,3},{2,0},{3,1},{4,6},{5,7},{6,4},{7,5},{8,10},{9,11},{10,... | collective-permute-start | bytes 12296 | tf_op jit(solution)/shard_map/ppermute | solution.py:299
  26.0 0.3 collective-permute-start.10
  26.3 1.2 %collective-permute-done.12.refs_3_ = f32[8,128]{1,0:T(8,128)S(1)} collective-permute-done((f32[8,128]{1,0:T(8,128)S(1)}, f32[8,128]{1,0:T(8,128)S(1)}, u32[]{:S(2)}, u32[]{:S(2)}) %collective-permute-start.12) | collective-permute-done | bytes 4128 | tf_op jit(solution)/shard_map/ppermute | solution.py:299
  27.5 0.7 %collective-permute-done.11.refs_2_ = f32[8,128]{1,0:T(8,128)S(1)} collective-permute-done((f32[8,128]{1,0:T(8,128)S(1)}, f32[8,128]{1,0:T(8,128)S(1)}, u32[]{:S(2)}, u32[]{:S(2)}) %collective-permute-start.11) | collective-permute-done | bytes 4128 | tf_op jit(solution)/shard_map/ppermute | solution.py:299
  28.1 0.0 collective-permute-done.10.refs_1_
  28.1 0.0 collective-permute-done.6.near_ref
  28.1 1.0 %group_shifts.1 = (f32[8,128]{1,0:T(8,128)S(1)}, f32[8,128]{1,0:T(8,128)S(1)}, f32[8,128]{1,0:T(8,128)S(1)}, bf16[128,256]{1,0:T(8,128)(2,1)S(1)}) custom-call(s32[1]{0:T(128)} %bitcast.pos_ref, bf16[4,128,256]{2,1,0:T(8,128)(2,1)S(1)} %get-tuple-element.44.all_ref, bf16[128,256]{1,0:T(8,128)(2,1)} %collective-permute-done.6.near_ref, ...), custom_call_target="tpu_custom_call" | custom-call | flops 1 | bytes 1 | tf_op jit(solution)/shard_map/group_shifts/pallas_call | solution.py:366
  29.1 0.1 collective-permute-start.13
  29.2 2.4 %collective-permute-start.15 = (f32[8,128]{1,0:T(8,128)S(1)}, f32[8,128]{1,0:T(8,128)S(1)}, u32[]{:S(2)}, u32[]{:S(2)}) collective-permute-start(f32[8,128]{1,0:T(8,128)S(1)} %get-tuple-element.58), channel_id=1, source_target_pairs={{0,12},{1,13},{2,14},{3,15},{4,8},{5,9},{6,10},{7,11},{8,4},{9,5},... | collective-permute-start | bytes 12296 | tf_op jit(solution)/shard_map/ppermute | solution.py:299
  31.6 1.1 %collective-permute-start.14 = (f32[8,128]{1,0:T(8,128)S(1)}, f32[8,128]{1,0:T(8,128)S(1)}, u32[]{:S(2)}, u32[]{:S(2)}) collective-permute-start(f32[8,128]{1,0:T(8,128)S(1)} %get-tuple-element.58), channel_id=1, source_target_pairs={{0,8},{1,9},{2,10},{3,11},{4,12},{5,13},{6,14},{7,15},{8,0},{9,1},... | collective-permute-start | bytes 12296 | tf_op jit(solution)/shard_map/ppermute | solution.py:299
  32.7 0.1 collective-permute-done.13.refs_1_
  32.8 1.9 %collective-permute-done.15.refs_3_ = f32[8,128]{1,0:T(8,128)S(1)} collective-permute-done((f32[8,128]{1,0:T(8,128)S(1)}, f32[8,128]{1,0:T(8,128)S(1)}, u32[]{:S(2)}, u32[]{:S(2)}) %collective-permute-start.15) | collective-permute-done | bytes 4128 | tf_op jit(solution)/shard_map/ppermute | solution.py:299
  34.7 1.4 %collective-permute-done.14.refs_2_ = f32[8,128]{1,0:T(8,128)S(1)} collective-permute-done((f32[8,128]{1,0:T(8,128)S(1)}, f32[8,128]{1,0:T(8,128)S(1)}, u32[]{:S(2)}, u32[]{:S(2)}) %collective-permute-start.14) | collective-permute-done | bytes 4128 | tf_op jit(solution)/shard_map/ppermute | solution.py:299
  36.1 0.0 copy-done
  36.1 2.3 %estimates.1 = f32[64,128]{1,0:T(8,128)} custom-call(s32[1]{0:T(128)} %bitcast.pos_ref, s32[1,64]{1,0:T(1,128)S(1)} %get-tuple-element.32.levels_ref, f32[1,128]{1,0:T(1,128)S(1)} %get-tuple-element.33.init_ref, bf16[128,256]{1,0:T(8,128)(2,1)S(1)} %get-tuple-element.43.prefix_ref, f32[8,128]{1,0:T(8,128)S(1)} %get-tuple-element.53.before_ref, ...), custom_call_target="tpu_custom_call" | custom-call | flops 1 | bytes 1 | tf_op jit(solution)/shard_map/estimates/pallas_call | solution.py:384
Async XLA Ops:
  1.8 7.1 %collective-permute-start = (bf16[4,64,128]{2,1,0:T(8,128)(2,1)S(1)}, bf16[4,64,128]{2,1,0:T(8,128)(2,1)S(1)}, u32[]{:S(2)}, u32[]{:S(2)}) collective-permute-start(bf16[4,64,128]{2,1,0:T(8,128)(2,1)S(1)} %get-tuple-element.39), channel_id=1, source_target_pairs={{0,1},{1,0},{2,3},{3,2},{4,5},{5,4},{6,7},{7,6},{8,9},{9,8},{10,11... | collective-permute-start | bytes 196616 | tf_op jit(solution)/shard_map/ppermute | solution.py:299
  2.4 6.5 %collective-permute-start.1 = (bf16[4,64,128]{2,1,0:T(8,128)(2,1)S(1)}, bf16[4,64,128]{2,1,0:T(8,128)(2,1)S(1)}, u32[]{:S(2)}, u32[]{:S(2)}) collective-permute-start(bf16[4,64,128]{2,1,0:T(8,128)(2,1)S(1)} %get-tuple-element.40), channel_id=1, source_target_pairs={{0,2},{1,3},{2,0},{3,1},{4,6},{5,7},{6,4},{7,5},{8,10},{9,11},{10,... | collective-permute-start | bytes 196616 | tf_op jit(solution)/shard_map/ppermute | solution.py:299
  4.9 4.0 %collective-permute-start.2 = (bf16[4,64,128]{2,1,0:T(8,128)(2,1)S(1)}, bf16[4,64,128]{2,1,0:T(8,128)(2,1)S(1)}, u32[]{:S(2)}, u32[]{:S(2)}) collective-permute-start(bf16[4,64,128]{2,1,0:T(8,128)(2,1)S(1)} %get-tuple-element.41), channel_id=1, source_target_pairs={{0,3},{1,2},{2,1},{3,0},{4,7},{5,6},{6,5},{7,4},{8,11},{9,10},{10,... | collective-permute-start | bytes 196616 | tf_op jit(solution)/shard_map/ppermute | solution.py:299
  9.2 6.4 %collective-permute-start.5 = (bf16[128,256]{1,0:T(8,128)(2,1)S(1)}, bf16[128,256]{1,0:T(8,128)(2,1)S(1)}, u32[]{:S(2)}, u32[]{:S(2)}) collective-permute-start(bf16[128,256]{1,0:T(8,128)(2,1)S(1)} %get-tuple-element.42.refs_0_.total_ref), channel_id=1, source_target_pairs={{0,3},{1,2},{2,1},{3,0},{4,7},{5,6},{6,5},{7,4},{8,11},{9,10},{10,... | collective-permute-start | bytes 196616 | tf_op jit(solution)/shard_map/ppermute | solution.py:299
  10.9 6.1 %collective-permute-start.4 = (bf16[128,256]{1,0:T(8,128)(2,1)S(1)}, bf16[128,256]{1,0:T(8,128)(2,1)S(1)}, u32[]{:S(2)}, u32[]{:S(2)}) collective-permute-start(bf16[128,256]{1,0:T(8,128)(2,1)S(1)} %get-tuple-element.42.refs_0_.total_ref), channel_id=1, source_target_pairs={{0,2},{1,3},{2,0},{3,1},{4,6},{5,7},{6,4},{7,5},{8,10},{9,11},{10,... | collective-permute-start | bytes 196616 | tf_op jit(solution)/shard_map/ppermute | solution.py:299
  11.1 6.0 %collective-permute-start.3 = (bf16[128,256]{1,0:T(8,128)(2,1)S(1)}, bf16[128,256]{1,0:T(8,128)(2,1)S(1)}, u32[]{:S(2)}, u32[]{:S(2)}) collective-permute-start(bf16[128,256]{1,0:T(8,128)(2,1)S(1)} %get-tuple-element.42.refs_0_.total_ref), channel_id=1, source_target_pairs={{0,1},{1,0},{2,3},{3,2},{4,5},{5,4},{6,7},{7,6},{8,9},{9,8},{10,11... | collective-permute-start | bytes 196616 | tf_op jit(solution)/shard_map/ppermute | solution.py:299
  11.2 7.0 %collective-permute-start.7 = (f32[64,128]{1,0:T(8,128)S(1)}, f32[64,128]{1,0:T(8,128)S(1)}, u32[]{:S(2)}, u32[]{:S(2)}) collective-permute-start(f32[64,128]{1,0:T(8,128)S(1)} %get-tuple-element.49), channel_id=1, source_target_pairs={{0,4},{1,5},{2,6},{3,7},{4,0},{5,1},{6,2},{7,3},{8,12},{9,13},{10,... | collective-permute-start | bytes 98312 | tf_op jit(solution)/shard_map/ppermute | solution.py:299
  13.0 5.4 %collective-permute-start.8 = (f32[64,128]{1,0:T(8,128)S(1)}, f32[64,128]{1,0:T(8,128)S(1)}, u32[]{:S(2)}, u32[]{:S(2)}) collective-permute-start(f32[64,128]{1,0:T(8,128)S(1)} %get-tuple-element.50), channel_id=1, source_target_pairs={{0,8},{1,9},{2,10},{3,11},{4,12},{5,13},{6,14},{7,15},{8,0},{9,1},... | collective-permute-start | bytes 98312 | tf_op jit(solution)/shard_map/ppermute | solution.py:299
  15.6 5.8 %collective-permute-start.9 = (f32[64,128]{1,0:T(8,128)S(1)}, f32[64,128]{1,0:T(8,128)S(1)}, u32[]{:S(2)}, u32[]{:S(2)}) collective-permute-start(f32[64,128]{1,0:T(8,128)S(1)} %get-tuple-element.51), channel_id=1, source_target_pairs={{0,12},{1,13},{2,14},{3,15},{4,8},{5,9},{6,10},{7,11},{8,4},{9,5},... | collective-permute-start | bytes 98312 | tf_op jit(solution)/shard_map/ppermute | solution.py:299
  18.1 10.0 %collective-permute-start.6 = (bf16[128,256]{1,0:T(8,128)(2,1)}, bf16[128,256]{1,0:T(8,128)(2,1)}, u32[]{:S(2)}, u32[]{:S(2)}) collective-permute-start(bf16[128,256]{1,0:T(8,128)(2,1)} %get-tuple-element.45), channel_id=1, source_target_pairs={{0,4},{1,5},{2,6},{3,7},{4,0},{5,1},{6,2},{7,3},{8,12},{9,13},{10,... | collective-permute-start | bytes 196616 | tf_op jit(solution)/shard_map/ppermute | solution.py:299
  21.4 14.7 %copy-start = (bf16[31,128,256]{2,1,0:T(8,128)(2,1)S(1)}, bf16[31,128,256]{2,1,0:T(8,128)(2,1)}, u32[]{:S(2)}) copy-start(bf16[31,128,256]{2,1,0:T(8,128)(2,1)} %get-tuple-element.55.left_ref) | copy-start | bytes 6094852
  24.4 3.1 %collective-permute-start.12 = (f32[8,128]{1,0:T(8,128)S(1)}, f32[8,128]{1,0:T(8,128)S(1)}, u32[]{:S(2)}, u32[]{:S(2)}) collective-permute-start(f32[8,128]{1,0:T(8,128)S(1)} %get-tuple-element.52.refs_0_), channel_id=1, source_target_pairs={{0,3},{1,2},{2,1},{3,0},{4,7},{5,6},{6,5},{7,4},{8,11},{9,10},{10,... | collective-permute-start | bytes 12296 | tf_op jit(solution)/shard_map/ppermute | solution.py:299
  24.5 3.7 %collective-permute-start.11 = (f32[8,128]{1,0:T(8,128)S(1)}, f32[8,128]{1,0:T(8,128)S(1)}, u32[]{:S(2)}, u32[]{:S(2)}) collective-permute-start(f32[8,128]{1,0:T(8,128)S(1)} %get-tuple-element.52.refs_0_), channel_id=1, source_target_pairs={{0,2},{1,3},{2,0},{3,1},{4,6},{5,7},{6,4},{7,5},{8,10},{9,11},{10,... | collective-permute-start | bytes 12296 | tf_op jit(solution)/shard_map/ppermute | solution.py:299
  26.0 2.1 %collective-permute-start.10 = (f32[8,128]{1,0:T(8,128)S(1)}, f32[8,128]{1,0:T(8,128)S(1)}, u32[]{:S(2)}, u32[]{:S(2)}) collective-permute-start(f32[8,128]{1,0:T(8,128)S(1)} %get-tuple-element.52.refs_0_), channel_id=1, source_target_pairs={{0,1},{1,0},{2,3},{3,2},{4,5},{5,4},{6,7},{7,6},{8,9},{9,8},{10,11... | collective-permute-start | bytes 12296 | tf_op jit(solution)/shard_map/ppermute | solution.py:299
  29.1 3.7 %collective-permute-start.13 = (f32[8,128]{1,0:T(8,128)S(1)}, f32[8,128]{1,0:T(8,128)S(1)}, u32[]{:S(2)}, u32[]{:S(2)}) collective-permute-start(f32[8,128]{1,0:T(8,128)S(1)} %get-tuple-element.57), channel_id=1, source_target_pairs={{0,4},{1,5},{2,6},{3,7},{4,0},{5,1},{6,2},{7,3},{8,12},{9,13},{10,... | collective-permute-start | bytes 12296 | tf_op jit(solution)/shard_map/ppermute | solution.py:299
  29.2 5.5 %collective-permute-start.15 = (f32[8,128]{1,0:T(8,128)S(1)}, f32[8,128]{1,0:T(8,128)S(1)}, u32[]{:S(2)}, u32[]{:S(2)}) collective-permute-start(f32[8,128]{1,0:T(8,128)S(1)} %get-tuple-element.58), channel_id=1, source_target_pairs={{0,12},{1,13},{2,14},{3,15},{4,8},{5,9},{6,10},{7,11},{8,4},{9,5},... | collective-permute-start | bytes 12296 | tf_op jit(solution)/shard_map/ppermute | solution.py:299
  31.6 4.5 %collective-permute-start.14 = (f32[8,128]{1,0:T(8,128)S(1)}, f32[8,128]{1,0:T(8,128)S(1)}, u32[]{:S(2)}, u32[]{:S(2)}) collective-permute-start(f32[8,128]{1,0:T(8,128)S(1)} %get-tuple-element.58), channel_id=1, source_target_pairs={{0,8},{1,9},{2,10},{3,11},{4,12},{5,13},{6,14},{7,15},{8,0},{9,1},... | collective-permute-start | bytes 12296 | tf_op jit(solution)/shard_map/ppermute | solution.py:299

commit v13 on v12

--- a/solution.py
+++ b/solution.py
@@ -209,7 +209,7 @@
     shift_ref[...] = states[0] + vm(first, total_ref[...])
 
 
-def map_kernel(size, pos_ref, *refs):
+def map_kernel(size, pos_ref, after_ref, *refs):
     blocks = refs[:size]
     all_ref, prefix_ref, whole_ref = refs[size:]
     n = whole_ref.shape[0]
@@ -359,9 +359,9 @@
     group_maps, prefix, whole = call(
         functools.partial(map_kernel, size), "group_maps", 2,
         out_shape=[shape((size, n, 2 * n), BF16), one_map, pltpu.VMEM(one_map.shape, BF16)],
-        in_specs=[SMEM] + [VMEM] * size,
+        in_specs=[SMEM] + [VMEM] * (1 + size),
         out_specs=[VMEM] * 3,
-    )(position, total, *members)
+    )(position, shift, total, *members)
     near = swaps(whole, size, 2)[0]
     before, carried, sent, near = call(
         functools.partial(shift_kernel, size), "group_shifts", 2,

time: 38.6 us -> 39.5 us (1.023)
  starting transfers between devices: 16.4 us -> 14.9 us
  waiting for transfers between devices: 8.58 us -> 9.73 us
  Pallas kernels: 13.3 us -> 14.4 us
    ppermute x16, starting transfers between devices: 16.4 us -> 14.9 us  [swaps(): lax.ppermute(a, 'tm', [(j, j ^ r * step) for j in range(count)])]
    ppermute x16, waiting for transfers between devices: 8.58 us -> 9.73 us  [swaps(): lax.ppermute(a, 'tm', [(j, j ^ r * step) for j in range(count)])]
    pallas_call x1, Pallas kernels: 0.25 us -> 0.71 us  [shards(): call(functools.partial(project_kernel, size), 'project', 4, out_shape=[on...]
    pallas_call x1, Pallas kernels: 2.94 us -> 3.4 us  [shards(): call(local_kernel, 'local_states', 8, 1 << 40, out_shape=[shape((steps, n...]
    pallas_call x1, Pallas kernels: 1 us -> 0.58 us  [shards(): call(functools.partial(shift_kernel, size), 'group_shifts', 2, out_shape=...]
  transfers between devices with their start and end apart: 16 -> 16, of which waited for: 8 -> 9; matrix products, arithmetic and copies ran while one was open for 0% -> 0% of each run, Pallas kernels for 21% -> 19%
where the time goes in v13:
time: 39.5 us; the launch traced here: 39.2 us
  starting transfers between devices  14.9 us (38%)
  Pallas kernels  14.4 us (36%)
  waiting for transfers between devices  9.73 us (25%)
    ppermute x16, starting transfers between devices, swaps(): lax.ppermute(a, 'tm', [(j, j ^ r * step) for j in range(count)])  14.9 us
    ppermute x16, waiting for transfers between devices, swaps(): lax.ppermute(a, 'tm', [(j, j ^ r * step) for j in range(count)])  9.73 us
    pallas_call x1, Pallas kernels, shards(): call(functools.partial(tree_kernel, steps), 'tree_of_maps', 8, out_shape=...  3.89 us
    pallas_call x1, Pallas kernels, shards(): call(local_kernel, 'local_states', 8, 1 << 40, out_shape=[shape((steps, n...  3.4 us
    pallas_call x1, Pallas kernels, shards(): call(functools.partial(final_kernel, size, gather), 'estimates', 6, out_s...  2.62 us
    pallas_call x1, Pallas kernels, shards(): call(functools.partial(front_kernel, cuts, len(small), size), 'front', 5,...  1.83 us
    pallas_call x1, Pallas kernels, shards(): call(functools.partial(map_kernel, size), 'group_maps', 2, out_shape=[sha...  1.39 us
  transfers between devices with their start and end apart: 16, of which 9 were waited for; matrix products, arithmetic and copies ran while one was open for 0% of the time, Pallas kernels for 19%

profile of v13, /device:TPU:0, one launch (start us, length us, event | category | flops | bytes accessed | tf_op | source)
XLA Modules:
  0.0 39.2 jit_solution(8756195060566836870)
XLA Ops:
  0.0 1.8 %front.1 = (bf16[16,128,256]{2,1,0:T(8,128)(2,1)S(1)}, s32[1,64]{1,0:T(1,128)S(1)}, f32[1,128]{1,0:T(1,128)S(1)}, bf16[128,128]{1,0:T(8,128)(2,1)S(1)}, s32[16,1...) custom-call(s32[1]{0:T(128)} %bitcast.pos_ref, ...), custom_call_target="tpu_custom_call" | custom-call | flops 1 | bytes 1 | tf_op jit(solution)/shard_map/front/pallas_call | solution.py:315
  1.8 0.5 %collective-permute-start = (bf16[4,64,128]{2,1,0:T(8,128)(2,1)S(1)}, bf16[4,64,128]{2,1,0:T(8,128)(2,1)S(1)}, u32[]{:S(2)}, u32[]{:S(2)}) collective-permute-start(bf16[4,64,128]{2,1,0:T(8,128)(2,1)S(1)} %get-tuple-element.40), channel_id=1, source_target_pairs={{0,1},{1,0},{2,3},{3,2},{4,5},{5,4},{6,7},{7,6},{8,9},{9,8},{10,11... | collective-permute-start | bytes 196616 | tf_op jit(solution)/shard_map/ppermute | solution.py:299
  2.4 2.6 %collective-permute-start.1 = (bf16[4,64,128]{2,1,0:T(8,128)(2,1)S(1)}, bf16[4,64,128]{2,1,0:T(8,128)(2,1)S(1)}, u32[]{:S(2)}, u32[]{:S(2)}) collective-permute-start(bf16[4,64,128]{2,1,0:T(8,128)(2,1)S(1)} %get-tuple-element.41), channel_id=1, source_target_pairs={{0,2},{1,3},{2,0},{3,1},{4,6},{5,7},{6,4},{7,5},{8,10},{9,11},{10,... | collective-permute-start | bytes 196616 | tf_op jit(solution)/shard_map/ppermute | solution.py:299
  4.9 0.1 collective-permute-start.2
  5.0 3.9 %tree_of_maps.1 = (bf16[31,128,256]{2,1,0:T(8,128)(2,1)}, bf16[31,128,256]{2,1,0:T(8,128)(2,1)}, bf16[128,256]{1,0:T(8,128)(2,1)S(1)}) custom-call(s32[1,64]{1,0:T(1,128)S(1)} %get-tuple-element.32.levels_ref, bf16[16,128,256]{2,1,0:T(8,128)(2,1)S(1)} %get-tuple-element.35.table_ref), custom_call_target="tpu_custom_call" | custom-call | flops 1 | bytes 1 | tf_op jit(solution)/shard_map/tree_of_maps/pallas_call | solution.py:325
  8.9 0.0 collective-permute-done.refs_1_
  8.9 0.0 collective-permute-done.1.refs_2_
  8.9 0.1 collective-permute-done.2.refs_3_
  9.0 0.7 %project.1 = (bf16[128,256]{1,0:T(8,128)(2,1)}, f32[64,128]{1,0:T(8,128)S(1)}, f32[64,128]{1,0:T(8,128)S(1)}, f32[64,128]{1,0:T(8,128)S(1)}, f32[64,128]{1,0:T(8,128)S(1)}) custom-call(s32[1]{0:T(128)} %bitcast.pos_ref, bf16[128,256]{1,0:T(8,128)(2,1)S(1)} %get-tuple-element.36.total_ref, s32[16,128]{1,0:T(8,128)S(1)} %get-tuple-element.37.mode_ref, ...), custom_call_target="tpu_custom_call" | custom-call | flops 1 | bytes 1 | tf_op jit(solution)/shard_map/project/pallas_call | solution.py:335
  9.7 1.8 %collective-permute-start.3 = (f32[64,128]{1,0:T(8,128)S(1)}, f32[64,128]{1,0:T(8,128)S(1)}, u32[]{:S(2)}, u32[]{:S(2)}) collective-permute-start(f32[64,128]{1,0:T(8,128)S(1)} %get-tuple-element.46), channel_id=1, source_target_pairs={{0,4},{1,5},{2,6},{3,7},{4,0},{5,1},{6,2},{7,3},{8,12},{9,13},{10,... | collective-permute-start | bytes 98312 | tf_op jit(solution)/shard_map/ppermute | solution.py:299
  11.5 2.6 %collective-permute-start.4 = (f32[64,128]{1,0:T(8,128)S(1)}, f32[64,128]{1,0:T(8,128)S(1)}, u32[]{:S(2)}, u32[]{:S(2)}) collective-permute-start(f32[64,128]{1,0:T(8,128)S(1)} %get-tuple-element.47), channel_id=1, source_target_pairs={{0,8},{1,9},{2,10},{3,11},{4,12},{5,13},{6,14},{7,15},{8,0},{9,1},... | collective-permute-start | bytes 98312 | tf_op jit(solution)/shard_map/ppermute | solution.py:299
  14.1 0.0 collective-permute-start.5
  14.1 0.9 %collective-permute-start.8 = (bf16[128,256]{1,0:T(8,128)(2,1)}, bf16[128,256]{1,0:T(8,128)(2,1)}, u32[]{:S(2)}, u32[]{:S(2)}) collective-permute-start(bf16[128,256]{1,0:T(8,128)(2,1)} %get-tuple-element.43.total_ref.refs_0_), channel_id=1, source_target_pairs={{0,3},{1,2},{2,1},{3,0},{4,7},{5,6},{6,5},{7,4},{8,11},{9,10},{10,... | collective-permute-start | bytes 196616 | tf_op jit(solution)/shard_map/ppermute | solution.py:299
  14.9 0.9 %collective-permute-start.7 = (bf16[128,256]{1,0:T(8,128)(2,1)}, bf16[128,256]{1,0:T(8,128)(2,1)}, u32[]{:S(2)}, u32[]{:S(2)}) collective-permute-start(bf16[128,256]{1,0:T(8,128)(2,1)} %get-tuple-element.43.total_ref.refs_0_), channel_id=1, source_target_pairs={{0,2},{1,3},{2,0},{3,1},{4,6},{5,7},{6,4},{7,5},{8,10},{9,11},{10,... | collective-permute-start | bytes 196616 | tf_op jit(solution)/shard_map/ppermute | solution.py:299
  15.8 0.0 collective-permute-done.3.refs_1_
  15.8 0.1 collective-permute-start.6
  15.9 0.9 %collective-permute-done.4.refs_2_ = f32[64,128]{1,0:T(8,128)S(1)} collective-permute-done((f32[64,128]{1,0:T(8,128)S(1)}, f32[64,128]{1,0:T(8,128)S(1)}, u32[]{:S(2)}, u32[]{:S(2)}) %collective-permute-start.4) | collective-permute-done | bytes 32800 | tf_op jit(solution)/shard_map/ppermute | solution.py:299
  16.9 2.9 %collective-permute-done.5.refs_3_ = f32[64,128]{1,0:T(8,128)S(1)} collective-permute-done((f32[64,128]{1,0:T(8,128)S(1)}, f32[64,128]{1,0:T(8,128)S(1)}, u32[]{:S(2)}, u32[]{:S(2)}) %collective-permute-start.5) | collective-permute-done | bytes 32800 | tf_op jit(solution)/shard_map/ppermute | solution.py:299
  19.8 0.0 copy-start
  19.8 3.4 %local_states.1 = (f32[64,128]{1,0:T(8,128)S(1)}, f32[8,128]{1,0:T(8,128)S(1)}) custom-call(s32[1]{0:T(128)} %bitcast.pos_ref, s32[1,64]{1,0:T(1,128)S(1)} %get-tuple-element.32.levels_ref, bf16[128,128]{1,0:T(8,128)(2,1)S(1)} %get-tuple-element.34.gain_ref, f32[1,128]{1,0:T(1,128)S(1)} %get-tuple-element.33.init_ref, ...), custom_call_target="tpu_custom_call" | custom-call | flops 1099511627776 | bytes 1 | tf_op jit(solution)/shard_map/local_states/pallas_call | solution.py:351
  23.2 0.0 collective-permute-done.8.refs_3_
  23.2 0.0 collective-permute-done.7.refs_2_
  23.2 0.0 collective-permute-done.6.refs_1_
  23.2 1.4 %group_maps.1 = (bf16[4,128,256]{2,1,0:T(8,128)(2,1)S(1)}, bf16[128,256]{1,0:T(8,128)(2,1)S(1)}, bf16[128,256]{1,0:T(8,128)(2,1)S(1)}) custom-call(s32[1]{0:T(128)} %bitcast.pos_ref, f32[8,128]{1,0:T(8,128)S(1)} %get-tuple-element.49.after_ref.refs_0_, bf16[128,256]{1,0:T(8,128)(2,1)} %get-tuple-element.43.total_ref.refs_0_, ...), custom_call_target="tpu_custom_call" | custom-call | flops 1 | bytes 1 | tf_op jit(solution)/shard_map/group_maps/pallas_call | solution.py:359
  24.6 0.1 collective-permute-start.9
  24.7 0.1 collective-permute-start.12
  24.8 1.6 %collective-permute-start.11 = (f32[8,128]{1,0:T(8,128)S(1)}, f32[8,128]{1,0:T(8,128)S(1)}, u32[]{:S(2)}, u32[]{:S(2)}) collective-permute-start(f32[8,128]{1,0:T(8,128)S(1)} %get-tuple-element.49.after_ref.refs_0_), channel_id=1, source_target_pairs={{0,2},{1,3},{2,0},{3,1},{4,6},{5,7},{6,4},{7,5},{8,10},{9,11},{10,... | collective-permute-start | bytes 12296 | tf_op jit(solution)/shard_map/ppermute | solution.py:299
  26.3 0.3 collective-permute-start.10
  26.6 1.2 %collective-permute-done.12.refs_3_ = f32[8,128]{1,0:T(8,128)S(1)} collective-permute-done((f32[8,128]{1,0:T(8,128)S(1)}, f32[8,128]{1,0:T(8,128)S(1)}, u32[]{:S(2)}, u32[]{:S(2)}) %collective-permute-start.12) | collective-permute-done | bytes 4128 | tf_op jit(solution)/shard_map/ppermute | solution.py:299
  27.8 0.7 %collective-permute-done.11.refs_2_ = f32[8,128]{1,0:T(8,128)S(1)} collective-permute-done((f32[8,128]{1,0:T(8,128)S(1)}, f32[8,128]{1,0:T(8,128)S(1)}, u32[]{:S(2)}, u32[]{:S(2)}) %collective-permute-start.11) | collective-permute-done | bytes 4128 | tf_op jit(solution)/shard_map/ppermute | solution.py:299
  28.4 0.0 collective-permute-done.10.refs_1_
  28.4 0.5 %collective-permute-done.9.near_ref = bf16[128,256]{1,0:T(8,128)(2,1)S(1)} collective-permute-done((bf16[128,256]{1,0:T(8,128)(2,1)S(1)}, bf16[128,256]{1,0:T(8,128)(2,1)S(1)}, u32[]{:S(2)}, u32[]{:S(2)}) %collective-permute-start.9) | collective-permute-done | bytes 65568 | tf_op jit(solution)/shard_map/ppermute | solution.py:299
  28.9 0.6 %group_shifts.1 = (f32[8,128]{1,0:T(8,128)S(1)}, f32[8,128]{1,0:T(8,128)S(1)}, f32[8,128]{1,0:T(8,128)S(1)}, bf16[128,256]{1,0:T(8,128)(2,1)S(1)}) custom-call(s32[1]{0:T(128)} %bitcast.pos_ref, bf16[4,128,256]{2,1,0:T(8,128)(2,1)S(1)} %get-tuple-element.51.all_ref, bf16[128,256]{1,0:T(8,128)(2,1)S(1)} %collective-permute-done.9.near_ref, ...), custom_call_target="tpu_custom_call" | custom-call | flops 1 | bytes 1 | tf_op jit(solution)/shard_map/group_shifts/pallas_call | solution.py:366
  29.5 1.5 %collective-permute-start.13 = (f32[8,128]{1,0:T(8,128)S(1)}, f32[8,128]{1,0:T(8,128)S(1)}, u32[]{:S(2)}, u32[]{:S(2)}) collective-permute-start(f32[8,128]{1,0:T(8,128)S(1)} %get-tuple-element.57), channel_id=1, source_target_pairs={{0,4},{1,5},{2,6},{3,7},{4,0},{5,1},{6,2},{7,3},{8,12},{9,13},{10,... | collective-permute-start | bytes 12296 | tf_op jit(solution)/shard_map/ppermute | solution.py:299
  31.0 1.1 %collective-permute-start.15 = (f32[8,128]{1,0:T(8,128)S(1)}, f32[8,128]{1,0:T(8,128)S(1)}, u32[]{:S(2)}, u32[]{:S(2)}) collective-permute-start(f32[8,128]{1,0:T(8,128)S(1)} %get-tuple-element.58), channel_id=1, source_target_pairs={{0,12},{1,13},{2,14},{3,15},{4,8},{5,9},{6,10},{7,11},{8,4},{9,5},... | collective-permute-start | bytes 12296 | tf_op jit(solution)/shard_map/ppermute | solution.py:299
  32.1 1.0 %collective-permute-start.14 = (f32[8,128]{1,0:T(8,128)S(1)}, f32[8,128]{1,0:T(8,128)S(1)}, u32[]{:S(2)}, u32[]{:S(2)}) collective-permute-start(f32[8,128]{1,0:T(8,128)S(1)} %get-tuple-element.58), channel_id=1, source_target_pairs={{0,8},{1,9},{2,10},{3,11},{4,12},{5,13},{6,14},{7,15},{8,0},{9,1},... | collective-permute-start | bytes 12296 | tf_op jit(solution)/shard_map/ppermute | solution.py:299
  33.1 0.1 collective-permute-done.13.refs_1_
  33.2 3.2 %collective-permute-done.15.refs_3_ = f32[8,128]{1,0:T(8,128)S(1)} collective-permute-done((f32[8,128]{1,0:T(8,128)S(1)}, f32[8,128]{1,0:T(8,128)S(1)}, u32[]{:S(2)}, u32[]{:S(2)}) %collective-permute-start.15) | collective-permute-done | bytes 4128 | tf_op jit(solution)/shard_map/ppermute | solution.py:299
  36.4 0.2 collective-permute-done.14.refs_2_
  36.6 0.0 copy-done
  36.6 2.6 %estimates.1 = f32[64,128]{1,0:T(8,128)} custom-call(s32[1]{0:T(128)} %bitcast.pos_ref, s32[1,64]{1,0:T(1,128)S(1)} %get-tuple-element.32.levels_ref, f32[1,128]{1,0:T(1,128)S(1)} %get-tuple-element.33.init_ref, bf16[128,256]{1,0:T(8,128)(2,1)S(1)} %get-tuple-element.50.prefix_ref, f32[8,128]{1,0:T(8,128)S(1)} %get-tuple-element.53.before_ref, ...), custom_call_target="tpu_custom_call" | custom-call | flops 1 | bytes 1 | tf_op jit(solution)/shard_map/estimates/pallas_call | solution.py:384
Async XLA Ops:
  1.8 7.1 %collective-permute-start = (bf16[4,64,128]{2,1,0:T(8,128)(2,1)S(1)}, bf16[4,64,128]{2,1,0:T(8,128)(2,1)S(1)}, u32[]{:S(2)}, u32[]{:S(2)}) collective-permute-start(bf16[4,64,128]{2,1,0:T(8,128)(2,1)S(1)} %get-tuple-element.40), channel_id=1, source_target_pairs={{0,1},{1,0},{2,3},{3,2},{4,5},{5,4},{6,7},{7,6},{8,9},{9,8},{10,11... | collective-permute-start | bytes 196616 | tf_op jit(solution)/shard_map/ppermute | solution.py:299
  2.4 6.5 %collective-permute-start.1 = (bf16[4,64,128]{2,1,0:T(8,128)(2,1)S(1)}, bf16[4,64,128]{2,1,0:T(8,128)(2,1)S(1)}, u32[]{:S(2)}, u32[]{:S(2)}) collective-permute-start(bf16[4,64,128]{2,1,0:T(8,128)(2,1)S(1)} %get-tuple-element.41), channel_id=1, source_target_pairs={{0,2},{1,3},{2,0},{3,1},{4,6},{5,7},{6,4},{7,5},{8,10},{9,11},{10,... | collective-permute-start | bytes 196616 | tf_op jit(solution)/shard_map/ppermute | solution.py:299
  4.9 4.0 %collective-permute-start.2 = (bf16[4,64,128]{2,1,0:T(8,128)(2,1)S(1)}, bf16[4,64,128]{2,1,0:T(8,128)(2,1)S(1)}, u32[]{:S(2)}, u32[]{:S(2)}) collective-permute-start(bf16[4,64,128]{2,1,0:T(8,128)(2,1)S(1)} %get-tuple-element.42), channel_id=1, source_target_pairs={{0,3},{1,2},{2,1},{3,0},{4,7},{5,6},{6,5},{7,4},{8,11},{9,10},{10,... | collective-permute-start | bytes 196616 | tf_op jit(solution)/shard_map/ppermute | solution.py:299
  9.7 6.1 %collective-permute-start.3 = (f32[64,128]{1,0:T(8,128)S(1)}, f32[64,128]{1,0:T(8,128)S(1)}, u32[]{:S(2)}, u32[]{:S(2)}) collective-permute-start(f32[64,128]{1,0:T(8,128)S(1)} %get-tuple-element.46), channel_id=1, source_target_pairs={{0,4},{1,5},{2,6},{3,7},{4,0},{5,1},{6,2},{7,3},{8,12},{9,13},{10,... | collective-permute-start | bytes 98312 | tf_op jit(solution)/shard_map/ppermute | solution.py:299
  11.5 5.4 %collective-permute-start.4 = (f32[64,128]{1,0:T(8,128)S(1)}, f32[64,128]{1,0:T(8,128)S(1)}, u32[]{:S(2)}, u32[]{:S(2)}) collective-permute-start(f32[64,128]{1,0:T(8,128)S(1)} %get-tuple-element.47), channel_id=1, source_target_pairs={{0,8},{1,9},{2,10},{3,11},{4,12},{5,13},{6,14},{7,15},{8,0},{9,1},... | collective-permute-start | bytes 98312 | tf_op jit(solution)/shard_map/ppermute | solution.py:299
  14.1 5.7 %collective-permute-start.5 = (f32[64,128]{1,0:T(8,128)S(1)}, f32[64,128]{1,0:T(8,128)S(1)}, u32[]{:S(2)}, u32[]{:S(2)}) collective-permute-start(f32[64,128]{1,0:T(8,128)S(1)} %get-tuple-element.48), channel_id=1, source_target_pairs={{0,12},{1,13},{2,14},{3,15},{4,8},{5,9},{6,10},{7,11},{8,4},{9,5},... | collective-permute-start | bytes 98312 | tf_op jit(solution)/shard_map/ppermute | solution.py:299
  14.1 9.1 %collective-permute-start.8 = (bf16[128,256]{1,0:T(8,128)(2,1)}, bf16[128,256]{1,0:T(8,128)(2,1)}, u32[]{:S(2)}, u32[]{:S(2)}) collective-permute-start(bf16[128,256]{1,0:T(8,128)(2,1)} %get-tuple-element.43.total_ref.refs_0_), channel_id=1, source_target_pairs={{0,3},{1,2},{2,1},{3,0},{4,7},{5,6},{6,5},{7,4},{8,11},{9,10},{10,... | collective-permute-start | bytes 196616 | tf_op jit(solution)/shard_map/ppermute | solution.py:299
  14.9 8.3 %collective-permute-start.7 = (bf16[128,256]{1,0:T(8,128)(2,1)}, bf16[128,256]{1,0:T(8,128)(2,1)}, u32[]{:S(2)}, u32[]{:S(2)}) collective-permute-start(bf16[128,256]{1,0:T(8,128)(2,1)} %get-tuple-element.43.total_ref.refs_0_), channel_id=1, source_target_pairs={{0,2},{1,3},{2,0},{3,1},{4,6},{5,7},{6,4},{7,5},{8,10},{9,11},{10,... | collective-permute-start | bytes 196616 | tf_op jit(solution)/shard_map/ppermute | solution.py:299
  15.8 7.4 %collective-permute-start.6 = (bf16[128,256]{1,0:T(8,128)(2,1)}, bf16[128,256]{1,0:T(8,128)(2,1)}, u32[]{:S(2)}, u32[]{:S(2)}) collective-permute-start(bf16[128,256]{1,0:T(8,128)(2,1)} %get-tuple-element.43.total_ref.refs_0_), channel_id=1, source_target_pairs={{0,1},{1,0},{2,3},{3,2},{4,5},{5,4},{6,7},{7,6},{8,9},{9,8},{10,11... | collective-permute-start | bytes 196616 | tf_op jit(solution)/shard_map/ppermute | solution.py:299
  19.8 16.8 %copy-start = (bf16[31,128,256]{2,1,0:T(8,128)(2,1)S(1)}, bf16[31,128,256]{2,1,0:T(8,128)(2,1)}, u32[]{:S(2)}) copy-start(bf16[31,128,256]{2,1,0:T(8,128)(2,1)} %get-tuple-element.55.left_ref) | copy-start | bytes 6094852
  24.6 4.3 %collective-permute-start.9 = (bf16[128,256]{1,0:T(8,128)(2,1)S(1)}, bf16[128,256]{1,0:T(8,128)(2,1)S(1)}, u32[]{:S(2)}, u32[]{:S(2)}) collective-permute-start(bf16[128,256]{1,0:T(8,128)(2,1)S(1)} %get-tuple-element.52), channel_id=1, source_target_pairs={{0,4},{1,5},{2,6},{3,7},{4,0},{5,1},{6,2},{7,3},{8,12},{9,13},{10,... | collective-permute-start | bytes 196616 | tf_op jit(solution)/shard_map/ppermute | solution.py:299
  24.7 3.1 %collective-permute-start.12 = (f32[8,128]{1,0:T(8,128)S(1)}, f32[8,128]{1,0:T(8,128)S(1)}, u32[]{:S(2)}, u32[]{:S(2)}) collective-permute-start(f32[8,128]{1,0:T(8,128)S(1)} %get-tuple-element.49.after_ref.refs_0_), channel_id=1, source_target_pairs={{0,3},{1,2},{2,1},{3,0},{4,7},{5,6},{6,5},{7,4},{8,11},{9,10},{10,... | collective-permute-start | bytes 12296 | tf_op jit(solution)/shard_map/ppermute | solution.py:299
  24.8 3.7 %collective-permute-start.11 = (f32[8,128]{1,0:T(8,128)S(1)}, f32[8,128]{1,0:T(8,128)S(1)}, u32[]{:S(2)}, u32[]{:S(2)}) collective-permute-start(f32[8,128]{1,0:T(8,128)S(1)} %get-tuple-element.49.after_ref.refs_0_), channel_id=1, source_target_pairs={{0,2},{1,3},{2,0},{3,1},{4,6},{5,7},{6,4},{7,5},{8,10},{9,11},{10,... | collective-permute-start | bytes 12296 | tf_op jit(solution)/shard_map/ppermute | solution.py:299
  26.3 2.1 %collective-permute-start.10 = (f32[8,128]{1,0:T(8,128)S(1)}, f32[8,128]{1,0:T(8,128)S(1)}, u32[]{:S(2)}, u32[]{:S(2)}) collective-permute-start(f32[8,128]{1,0:T(8,128)S(1)} %get-tuple-element.49.after_ref.refs_0_), channel_id=1, source_target_pairs={{0,1},{1,0},{2,3},{3,2},{4,5},{5,4},{6,7},{7,6},{8,9},{9,8},{10,11... | collective-permute-start | bytes 12296 | tf_op jit(solution)/shard_map/ppermute | solution.py:299
  29.5 3.7 %collective-permute-start.13 = (f32[8,128]{1,0:T(8,128)S(1)}, f32[8,128]{1,0:T(8,128)S(1)}, u32[]{:S(2)}, u32[]{:S(2)}) collective-permute-start(f32[8,128]{1,0:T(8,128)S(1)} %get-tuple-element.57), channel_id=1, source_target_pairs={{0,4},{1,5},{2,6},{3,7},{4,0},{5,1},{6,2},{7,3},{8,12},{9,13},{10,... | collective-permute-start | bytes 12296 | tf_op jit(solution)/shard_map/ppermute | solution.py:299
  31.0 5.4 %collective-permute-start.15 = (f32[8,128]{1,0:T(8,128)S(1)}, f32[8,128]{1,0:T(8,128)S(1)}, u32[]{:S(2)}, u32[]{:S(2)}) collective-permute-start(f32[8,128]{1,0:T(8,128)S(1)} %get-tuple-element.58), channel_id=1, source_target_pairs={{0,12},{1,13},{2,14},{3,15},{4,8},{5,9},{6,10},{7,11},{8,4},{9,5},... | collective-permute-start | bytes 12296 | tf_op jit(solution)/shard_map/ppermute | solution.py:299
  32.1 4.5 %collective-permute-start.14 = (f32[8,128]{1,0:T(8,128)S(1)}, f32[8,128]{1,0:T(8,128)S(1)}, u32[]{:S(2)}, u32[]{:S(2)}) collective-permute-start(f32[8,128]{1,0:T(8,128)S(1)} %get-tuple-element.58), channel_id=1, source_target_pairs={{0,8},{1,9},{2,10},{3,11},{4,12},{5,13},{6,14},{7,15},{8,0},{9,1},... | collective-permute-start | bytes 12296 | tf_op jit(solution)/shard_map/ppermute | solution.py:299

commit v14 on v13

--- a/solution.py
+++ b/solution.py
@@ -349,7 +349,7 @@
     members = swaps(total, 1, size)
     vector = shape((8, n), F32)
     lefts, shift = call(
-        local_kernel, "local_states", 8, 1 << 40,
+        local_kernel, "local_states", 8, 1 << 30,
         out_shape=[shape((steps, n), F32), vector],
         in_specs=[SMEM, SMEM] + [VMEM] * 4 + [HBM] + [VMEM] * len(parts),
         out_specs=[VMEM] * 2,

time: 39.5 us -> 37.4 us (0.947)
  Pallas kernels: 14.4 us -> 12.3 us
    pallas_call x1, Pallas kernels: 1.39 us -> 0.45 us  [shards(): call(functools.partial(map_kernel, size), 'group_maps', 2, out_shape=[sha...]
    pallas_call x1, Pallas kernels: 0.71 us -> 0.25 us  [shards(): call(functools.partial(project_kernel, size), 'project', 4, out_shape=[on...]
    pallas_call x1, Pallas kernels: 3.4 us -> 2.94 us  [shards(): call(local_kernel, 'local_states', 8, 1 << 30, out_shape=[shape((steps, n...]
  transfers between devices with their start and end apart: 16 -> 16, of which waited for: 9 -> 9; matrix products, arithmetic and copies ran while one was open for 0% -> 0% of each run, Pallas kernels for 19% -> 18%
where the time goes in v14:
time: 37.4 us; the launch traced here: 37.3 us
  starting transfers between devices  15 us (40%)
  Pallas kernels  12.3 us (33%)
  waiting for transfers between devices  9.87 us (26%)
    ppermute x16, starting transfers between devices, swaps(): lax.ppermute(a, 'tm', [(j, j ^ r * step) for j in range(count)])  15 us
    ppermute x16, waiting for transfers between devices, swaps(): lax.ppermute(a, 'tm', [(j, j ^ r * step) for j in range(count)])  9.87 us
    pallas_call x1, Pallas kernels, shards(): call(functools.partial(tree_kernel, steps), 'tree_of_maps', 8, out_shape=...  3.89 us
    pallas_call x1, Pallas kernels, shards(): call(local_kernel, 'local_states', 8, 1 << 30, out_shape=[shape((steps, n...  2.94 us
    pallas_call x1, Pallas kernels, shards(): call(functools.partial(final_kernel, size, gather), 'estimates', 6, out_s...  2.31 us
    pallas_call x1, Pallas kernels, shards(): call(functools.partial(front_kernel, cuts, len(small), size), 'front', 5,...  1.83 us
  transfers between devices with their start and end apart: 16, of which 9 were waited for; matrix products, arithmetic and copies ran while one was open for 0% of the time, Pallas kernels for 18%

profile of v14, /device:TPU:0, one launch (start us, length us, event | category | flops | bytes accessed | tf_op | source)
XLA Modules:
  0.0 37.3 jit_solution(1731831778585125499)
XLA Ops:
  0.0 1.8 %front.1 = (bf16[16,128,256]{2,1,0:T(8,128)(2,1)S(1)}, s32[1,64]{1,0:T(1,128)S(1)}, f32[1,128]{1,0:T(1,128)S(1)}, bf16[128,128]{1,0:T(8,128)(2,1)S(1)}, s32[16,1...) custom-call(s32[1]{0:T(128)} %bitcast.pos_ref, ...), custom_call_target="tpu_custom_call" | custom-call | flops 1 | bytes 1 | tf_op jit(solution)/shard_map/front/pallas_call | solution.py:315
  1.8 0.5 %collective-permute-start = (bf16[4,64,128]{2,1,0:T(8,128)(2,1)S(1)}, bf16[4,64,128]{2,1,0:T(8,128)(2,1)S(1)}, u32[]{:S(2)}, u32[]{:S(2)}) collective-permute-start(bf16[4,64,128]{2,1,0:T(8,128)(2,1)S(1)} %get-tuple-element.40), channel_id=1, source_target_pairs={{0,1},{1,0},{2,3},{3,2},{4,5},{5,4},{6,7},{7,6},{8,9},{9,8},{10,11... | collective-permute-start | bytes 196616 | tf_op jit(solution)/shard_map/ppermute | solution.py:299
  2.4 2.6 %collective-permute-start.1 = (bf16[4,64,128]{2,1,0:T(8,128)(2,1)S(1)}, bf16[4,64,128]{2,1,0:T(8,128)(2,1)S(1)}, u32[]{:S(2)}, u32[]{:S(2)}) collective-permute-start(bf16[4,64,128]{2,1,0:T(8,128)(2,1)S(1)} %get-tuple-element.41), channel_id=1, source_target_pairs={{0,2},{1,3},{2,0},{3,1},{4,6},{5,7},{6,4},{7,5},{8,10},{9,11},{10,... | collective-permute-start | bytes 196616 | tf_op jit(solution)/shard_map/ppermute | solution.py:299
  4.9 0.1 collective-permute-start.2
  5.0 3.9 %tree_of_maps.1 = (bf16[31,128,256]{2,1,0:T(8,128)(2,1)}, bf16[31,128,256]{2,1,0:T(8,128)(2,1)}, bf16[128,256]{1,0:T(8,128)(2,1)S(1)}) custom-call(s32[1,64]{1,0:T(1,128)S(1)} %get-tuple-element.32.levels_ref, bf16[16,128,256]{2,1,0:T(8,128)(2,1)S(1)} %get-tuple-element.35.table_ref), custom_call_target="tpu_custom_call" | custom-call | flops 1 | bytes 1 | tf_op jit(solution)/shard_map/tree_of_maps/pallas_call | solution.py:325
  8.9 0.0 collective-permute-done.refs_1_
  8.9 0.0 collective-permute-done.1.refs_2_
  8.9 0.1 collective-permute-done.2.refs_3_
  9.0 0.3 project.1
  9.2 1.8 %collective-permute-start.3 = (f32[64,128]{1,0:T(8,128)S(1)}, f32[64,128]{1,0:T(8,128)S(1)}, u32[]{:S(2)}, u32[]{:S(2)}) collective-permute-start(f32[64,128]{1,0:T(8,128)S(1)} %get-tuple-element.46), channel_id=1, source_target_pairs={{0,4},{1,5},{2,6},{3,7},{4,0},{5,1},{6,2},{7,3},{8,12},{9,13},{10,... | collective-permute-start | bytes 98312 | tf_op jit(solution)/shard_map/ppermute | solution.py:299
  11.1 2.6 %collective-permute-start.4 = (f32[64,128]{1,0:T(8,128)S(1)}, f32[64,128]{1,0:T(8,128)S(1)}, u32[]{:S(2)}, u32[]{:S(2)}) collective-permute-start(f32[64,128]{1,0:T(8,128)S(1)} %get-tuple-element.47), channel_id=1, source_target_pairs={{0,8},{1,9},{2,10},{3,11},{4,12},{5,13},{6,14},{7,15},{8,0},{9,1},... | collective-permute-start | bytes 98312 | tf_op jit(solution)/shard_map/ppermute | solution.py:299
  13.7 0.0 collective-permute-start.5
  13.7 0.9 %collective-permute-start.8 = (bf16[128,256]{1,0:T(8,128)(2,1)S(1)}, bf16[128,256]{1,0:T(8,128)(2,1)S(1)}, u32[]{:S(2)}, u32[]{:S(2)}) collective-permute-start(bf16[128,256]{1,0:T(8,128)(2,1)S(1)} %get-tuple-element.43.total_ref.refs_0_), channel_id=1, source_target_pairs={{0,3},{1,2},{2,1},{3,0},{4,7},{5,6},{6,5},{7,4},{8,11},{9,10},{10,... | collective-permute-start | bytes 196616 | tf_op jit(solution)/shard_map/ppermute | solution.py:299
  14.5 0.9 %collective-permute-start.7 = (bf16[128,256]{1,0:T(8,128)(2,1)S(1)}, bf16[128,256]{1,0:T(8,128)(2,1)S(1)}, u32[]{:S(2)}, u32[]{:S(2)}) collective-permute-start(bf16[128,256]{1,0:T(8,128)(2,1)S(1)} %get-tuple-element.43.total_ref.refs_0_), channel_id=1, source_target_pairs={{0,2},{1,3},{2,0},{3,1},{4,6},{5,7},{6,4},{7,5},{8,10},{9,11},{10,... | collective-permute-start | bytes 196616 | tf_op jit(solution)/shard_map/ppermute | solution.py:299
  15.4 0.0 collective-permute-done.3.refs_1_
  15.4 0.1 collective-permute-start.6
  15.6 0.9 %collective-permute-done.4.refs_2_ = f32[64,128]{1,0:T(8,128)S(1)} collective-permute-done((f32[64,128]{1,0:T(8,128)S(1)}, f32[64,128]{1,0:T(8,128)S(1)}, u32[]{:S(2)}, u32[]{:S(2)}) %collective-permute-start.4) | collective-permute-done | bytes 32800 | tf_op jit(solution)/shard_map/ppermute | solution.py:299
  16.5 2.9 %collective-permute-done.5.refs_3_ = f32[64,128]{1,0:T(8,128)S(1)} collective-permute-done((f32[64,128]{1,0:T(8,128)S(1)}, f32[64,128]{1,0:T(8,128)S(1)}, u32[]{:S(2)}, u32[]{:S(2)}) %collective-permute-start.5) | collective-permute-done | bytes 32800 | tf_op jit(solution)/shard_map/ppermute | solution.py:299
  19.4 0.0 copy-start
  19.4 2.9 %local_states.1 = (f32[64,128]{1,0:T(8,128)S(1)}, f32[8,128]{1,0:T(8,128)S(1)}) custom-call(s32[1]{0:T(128)} %bitcast.pos_ref, s32[1,64]{1,0:T(1,128)S(1)} %get-tuple-element.32.levels_ref, bf16[128,128]{1,0:T(8,128)(2,1)S(1)} %get-tuple-element.34.gain_ref, f32[1,128]{1,0:T(1,128)S(1)} %get-tuple-element.33.init_ref, ...), custom_call_target="tpu_custom_call" | custom-call | flops 1073741824 | bytes 1 | tf_op jit(solution)/shard_map/local_states/pallas_call | solution.py:351
  22.3 0.0 collective-permute-done.8.refs_3_
  22.3 0.0 collective-permute-done.7.refs_2_
  22.3 0.0 collective-permute-done.6.refs_1_
  22.4 0.5 %group_maps.1 = (bf16[4,128,256]{2,1,0:T(8,128)(2,1)S(1)}, bf16[128,256]{1,0:T(8,128)(2,1)S(1)}, bf16[128,256]{1,0:T(8,128)(2,1)S(1)}) custom-call(s32[1]{0:T(128)} %bitcast.pos_ref, f32[8,128]{1,0:T(8,128)S(1)} %get-tuple-element.49.after_ref.refs_0_, bf16[128,256]{1,0:T(8,128)(2,1)S(1)} %get-tuple-element.43.total_ref.refs_0_, ...), custom_call_target="tpu_custom_call" | custom-call | flops 1 | bytes 1 | tf_op jit(solution)/shard_map/group_maps/pallas_call | solution.py:359
  22.8 0.1 collective-permute-start.9
  22.9 0.1 collective-permute-start.12
  23.0 1.6 %collective-permute-start.11 = (f32[8,128]{1,0:T(8,128)S(1)}, f32[8,128]{1,0:T(8,128)S(1)}, u32[]{:S(2)}, u32[]{:S(2)}) collective-permute-start(f32[8,128]{1,0:T(8,128)S(1)} %get-tuple-element.49.after_ref.refs_0_), channel_id=1, source_target_pairs={{0,2},{1,3},{2,0},{3,1},{4,6},{5,7},{6,4},{7,5},{8,10},{9,11},{10,... | collective-permute-start | bytes 12296 | tf_op jit(solution)/shard_map/ppermute | solution.py:299
  24.5 0.3 collective-permute-start.10
  24.8 1.2 %collective-permute-done.12.refs_3_ = f32[8,128]{1,0:T(8,128)S(1)} collective-permute-done((f32[8,128]{1,0:T(8,128)S(1)}, f32[8,128]{1,0:T(8,128)S(1)}, u32[]{:S(2)}, u32[]{:S(2)}) %collective-permute-start.12) | collective-permute-done | bytes 4128 | tf_op jit(solution)/shard_map/ppermute | solution.py:299
  26.0 0.7 %collective-permute-done.11.refs_2_ = f32[8,128]{1,0:T(8,128)S(1)} collective-permute-done((f32[8,128]{1,0:T(8,128)S(1)}, f32[8,128]{1,0:T(8,128)S(1)}, u32[]{:S(2)}, u32[]{:S(2)}) %collective-permute-start.11) | collective-permute-done | bytes 4128 | tf_op jit(solution)/shard_map/ppermute | solution.py:299
  26.6 0.0 collective-permute-done.10.refs_1_
  26.7 0.5 %collective-permute-done.9.near_ref = bf16[128,256]{1,0:T(8,128)(2,1)S(1)} collective-permute-done((bf16[128,256]{1,0:T(8,128)(2,1)S(1)}, bf16[128,256]{1,0:T(8,128)(2,1)S(1)}, u32[]{:S(2)}, u32[]{:S(2)}) %collective-permute-start.9) | collective-permute-done | bytes 65568 | tf_op jit(solution)/shard_map/ppermute | solution.py:299
  27.1 0.6 %group_shifts.1 = (f32[8,128]{1,0:T(8,128)S(1)}, f32[8,128]{1,0:T(8,128)S(1)}, f32[8,128]{1,0:T(8,128)S(1)}, bf16[128,256]{1,0:T(8,128)(2,1)S(1)}) custom-call(s32[1]{0:T(128)} %bitcast.pos_ref, bf16[4,128,256]{2,1,0:T(8,128)(2,1)S(1)} %get-tuple-element.51.all_ref, bf16[128,256]{1,0:T(8,128)(2,1)S(1)} %collective-permute-done.9.near_ref, ...), custom_call_target="tpu_custom_call" | custom-call | flops 1 | bytes 1 | tf_op jit(solution)/shard_map/group_shifts/pallas_call | solution.py:366
  27.7 1.5 %collective-permute-start.13 = (f32[8,128]{1,0:T(8,128)S(1)}, f32[8,128]{1,0:T(8,128)S(1)}, u32[]{:S(2)}, u32[]{:S(2)}) collective-permute-start(f32[8,128]{1,0:T(8,128)S(1)} %get-tuple-element.57), channel_id=1, source_target_pairs={{0,4},{1,5},{2,6},{3,7},{4,0},{5,1},{6,2},{7,3},{8,12},{9,13},{10,... | collective-permute-start | bytes 12296 | tf_op jit(solution)/shard_map/ppermute | solution.py:299
  29.2 1.2 %collective-permute-start.15 = (f32[8,128]{1,0:T(8,128)S(1)}, f32[8,128]{1,0:T(8,128)S(1)}, u32[]{:S(2)}, u32[]{:S(2)}) collective-permute-start(f32[8,128]{1,0:T(8,128)S(1)} %get-tuple-element.58), channel_id=1, source_target_pairs={{0,12},{1,13},{2,14},{3,15},{4,8},{5,9},{6,10},{7,11},{8,4},{9,5},... | collective-permute-start | bytes 12296 | tf_op jit(solution)/shard_map/ppermute | solution.py:299
  30.4 0.8 %collective-permute-start.14 = (f32[8,128]{1,0:T(8,128)S(1)}, f32[8,128]{1,0:T(8,128)S(1)}, u32[]{:S(2)}, u32[]{:S(2)}) collective-permute-start(f32[8,128]{1,0:T(8,128)S(1)} %get-tuple-element.58), channel_id=1, source_target_pairs={{0,8},{1,9},{2,10},{3,11},{4,12},{5,13},{6,14},{7,15},{8,0},{9,1},... | collective-permute-start | bytes 12296 | tf_op jit(solution)/shard_map/ppermute | solution.py:299
  31.3 0.1 collective-permute-done.13.refs_1_
  31.4 3.2 %collective-permute-done.15.refs_3_ = f32[8,128]{1,0:T(8,128)S(1)} collective-permute-done((f32[8,128]{1,0:T(8,128)S(1)}, f32[8,128]{1,0:T(8,128)S(1)}, u32[]{:S(2)}, u32[]{:S(2)}) %collective-permute-start.15) | collective-permute-done | bytes 4128 | tf_op jit(solution)/shard_map/ppermute | solution.py:299
  34.6 0.3 collective-permute-done.14.refs_2_
  35.0 0.0 copy-done
  35.0 2.3 %estimates.1 = f32[64,128]{1,0:T(8,128)} custom-call(s32[1]{0:T(128)} %bitcast.pos_ref, s32[1,64]{1,0:T(1,128)S(1)} %get-tuple-element.32.levels_ref, f32[1,128]{1,0:T(1,128)S(1)} %get-tuple-element.33.init_ref, bf16[128,256]{1,0:T(8,128)(2,1)S(1)} %get-tuple-element.50.prefix_ref, f32[8,128]{1,0:T(8,128)S(1)} %get-tuple-element.53.before_ref, ...), custom_call_target="tpu_custom_call" | custom-call | flops 1 | bytes 1 | tf_op jit(solution)/shard_map/estimates/pallas_call | solution.py:384
Async XLA Ops:
  1.8 7.1 %collective-permute-start = (bf16[4,64,128]{2,1,0:T(8,128)(2,1)S(1)}, bf16[4,64,128]{2,1,0:T(8,128)(2,1)S(1)}, u32[]{:S(2)}, u32[]{:S(2)}) collective-permute-start(bf16[4,64,128]{2,1,0:T(8,128)(2,1)S(1)} %get-tuple-element.40), channel_id=1, source_target_pairs={{0,1},{1,0},{2,3},{3,2},{4,5},{5,4},{6,7},{7,6},{8,9},{9,8},{10,11... | collective-permute-start | bytes 196616 | tf_op jit(solution)/shard_map/ppermute | solution.py:299
  2.4 6.5 %collective-permute-start.1 = (bf16[4,64,128]{2,1,0:T(8,128)(2,1)S(1)}, bf16[4,64,128]{2,1,0:T(8,128)(2,1)S(1)}, u32[]{:S(2)}, u32[]{:S(2)}) collective-permute-start(bf16[4,64,128]{2,1,0:T(8,128)(2,1)S(1)} %get-tuple-element.41), channel_id=1, source_target_pairs={{0,2},{1,3},{2,0},{3,1},{4,6},{5,7},{6,4},{7,5},{8,10},{9,11},{10,... | collective-permute-start | bytes 196616 | tf_op jit(solution)/shard_map/ppermute | solution.py:299
  4.9 4.0 %collective-permute-start.2 = (bf16[4,64,128]{2,1,0:T(8,128)(2,1)S(1)}, bf16[4,64,128]{2,1,0:T(8,128)(2,1)S(1)}, u32[]{:S(2)}, u32[]{:S(2)}) collective-permute-start(bf16[4,64,128]{2,1,0:T(8,128)(2,1)S(1)} %get-tuple-element.42), channel_id=1, source_target_pairs={{0,3},{1,2},{2,1},{3,0},{4,7},{5,6},{6,5},{7,4},{8,11},{9,10},{10,... | collective-permute-start | bytes 196616 | tf_op jit(solution)/shard_map/ppermute | solution.py:299
  9.2 6.2 %collective-permute-start.3 = (f32[64,128]{1,0:T(8,128)S(1)}, f32[64,128]{1,0:T(8,128)S(1)}, u32[]{:S(2)}, u32[]{:S(2)}) collective-permute-start(f32[64,128]{1,0:T(8,128)S(1)} %get-tuple-element.46), channel_id=1, source_target_pairs={{0,4},{1,5},{2,6},{3,7},{4,0},{5,1},{6,2},{7,3},{8,12},{9,13},{10,... | collective-permute-start | bytes 98312 | tf_op jit(solution)/shard_map/ppermute | solution.py:299
  11.1 5.4 %collective-permute-start.4 = (f32[64,128]{1,0:T(8,128)S(1)}, f32[64,128]{1,0:T(8,128)S(1)}, u32[]{:S(2)}, u32[]{:S(2)}) collective-permute-start(f32[64,128]{1,0:T(8,128)S(1)} %get-tuple-element.47), channel_id=1, source_target_pairs={{0,8},{1,9},{2,10},{3,11},{4,12},{5,13},{6,14},{7,15},{8,0},{9,1},... | collective-permute-start | bytes 98312 | tf_op jit(solution)/shard_map/ppermute | solution.py:299
  13.7 5.7 %collective-permute-start.5 = (f32[64,128]{1,0:T(8,128)S(1)}, f32[64,128]{1,0:T(8,128)S(1)}, u32[]{:S(2)}, u32[]{:S(2)}) collective-permute-start(f32[64,128]{1,0:T(8,128)S(1)} %get-tuple-element.48), channel_id=1, source_target_pairs={{0,12},{1,13},{2,14},{3,15},{4,8},{5,9},{6,10},{7,11},{8,4},{9,5},... | collective-permute-start | bytes 98312 | tf_op jit(solution)/shard_map/ppermute | solution.py:299
  13.7 8.6 %collective-permute-start.8 = (bf16[128,256]{1,0:T(8,128)(2,1)S(1)}, bf16[128,256]{1,0:T(8,128)(2,1)S(1)}, u32[]{:S(2)}, u32[]{:S(2)}) collective-permute-start(bf16[128,256]{1,0:T(8,128)(2,1)S(1)} %get-tuple-element.43.total_ref.refs_0_), channel_id=1, source_target_pairs={{0,3},{1,2},{2,1},{3,0},{4,7},{5,6},{6,5},{7,4},{8,11},{9,10},{10,... | collective-permute-start | bytes 196616 | tf_op jit(solution)/shard_map/ppermute | solution.py:299
  14.5 7.8 %collective-permute-start.7 = (bf16[128,256]{1,0:T(8,128)(2,1)S(1)}, bf16[128,256]{1,0:T(8,128)(2,1)S(1)}, u32[]{:S(2)}, u32[]{:S(2)}) collective-permute-start(bf16[128,256]{1,0:T(8,128)(2,1)S(1)} %get-tuple-element.43.total_ref.refs_0_), channel_id=1, source_target_pairs={{0,2},{1,3},{2,0},{3,1},{4,6},{5,7},{6,4},{7,5},{8,10},{9,11},{10,... | collective-permute-start | bytes 196616 | tf_op jit(solution)/shard_map/ppermute | solution.py:299
  15.4 6.9 %collective-permute-start.6 = (bf16[128,256]{1,0:T(8,128)(2,1)S(1)}, bf16[128,256]{1,0:T(8,128)(2,1)S(1)}, u32[]{:S(2)}, u32[]{:S(2)}) collective-permute-start(bf16[128,256]{1,0:T(8,128)(2,1)S(1)} %get-tuple-element.43.total_ref.refs_0_), channel_id=1, source_target_pairs={{0,1},{1,0},{2,3},{3,2},{4,5},{5,4},{6,7},{7,6},{8,9},{9,8},{10,11... | collective-permute-start | bytes 196616 | tf_op jit(solution)/shard_map/ppermute | solution.py:299
  19.4 15.6 %copy-start = (bf16[31,128,256]{2,1,0:T(8,128)(2,1)S(1)}, bf16[31,128,256]{2,1,0:T(8,128)(2,1)}, u32[]{:S(2)}) copy-start(bf16[31,128,256]{2,1,0:T(8,128)(2,1)} %get-tuple-element.55.left_ref) | copy-start | bytes 6094852
  22.8 4.3 %collective-permute-start.9 = (bf16[128,256]{1,0:T(8,128)(2,1)S(1)}, bf16[128,256]{1,0:T(8,128)(2,1)S(1)}, u32[]{:S(2)}, u32[]{:S(2)}) collective-permute-start(bf16[128,256]{1,0:T(8,128)(2,1)S(1)} %get-tuple-element.52), channel_id=1, source_target_pairs={{0,4},{1,5},{2,6},{3,7},{4,0},{5,1},{6,2},{7,3},{8,12},{9,13},{10,... | collective-permute-start | bytes 196616 | tf_op jit(solution)/shard_map/ppermute | solution.py:299
  22.9 3.1 %collective-permute-start.12 = (f32[8,128]{1,0:T(8,128)S(1)}, f32[8,128]{1,0:T(8,128)S(1)}, u32[]{:S(2)}, u32[]{:S(2)}) collective-permute-start(f32[8,128]{1,0:T(8,128)S(1)} %get-tuple-element.49.after_ref.refs_0_), channel_id=1, source_target_pairs={{0,3},{1,2},{2,1},{3,0},{4,7},{5,6},{6,5},{7,4},{8,11},{9,10},{10,... | collective-permute-start | bytes 12296 | tf_op jit(solution)/shard_map/ppermute | solution.py:299
  23.0 3.7 %collective-permute-start.11 = (f32[8,128]{1,0:T(8,128)S(1)}, f32[8,128]{1,0:T(8,128)S(1)}, u32[]{:S(2)}, u32[]{:S(2)}) collective-permute-start(f32[8,128]{1,0:T(8,128)S(1)} %get-tuple-element.49.after_ref.refs_0_), channel_id=1, source_target_pairs={{0,2},{1,3},{2,0},{3,1},{4,6},{5,7},{6,4},{7,5},{8,10},{9,11},{10,... | collective-permute-start | bytes 12296 | tf_op jit(solution)/shard_map/ppermute | solution.py:299
  24.5 2.1 %collective-permute-start.10 = (f32[8,128]{1,0:T(8,128)S(1)}, f32[8,128]{1,0:T(8,128)S(1)}, u32[]{:S(2)}, u32[]{:S(2)}) collective-permute-start(f32[8,128]{1,0:T(8,128)S(1)} %get-tuple-element.49.after_ref.refs_0_), channel_id=1, source_target_pairs={{0,1},{1,0},{2,3},{3,2},{4,5},{5,4},{6,7},{7,6},{8,9},{9,8},{10,11... | collective-permute-start | bytes 12296 | tf_op jit(solution)/shard_map/ppermute | solution.py:299
  27.7 3.7 %collective-permute-start.13 = (f32[8,128]{1,0:T(8,128)S(1)}, f32[8,128]{1,0:T(8,128)S(1)}, u32[]{:S(2)}, u32[]{:S(2)}) collective-permute-start(f32[8,128]{1,0:T(8,128)S(1)} %get-tuple-element.57), channel_id=1, source_target_pairs={{0,4},{1,5},{2,6},{3,7},{4,0},{5,1},{6,2},{7,3},{8,12},{9,13},{10,... | collective-permute-start | bytes 12296 | tf_op jit(solution)/shard_map/ppermute | solution.py:299
  29.2 5.4 %collective-permute-start.15 = (f32[8,128]{1,0:T(8,128)S(1)}, f32[8,128]{1,0:T(8,128)S(1)}, u32[]{:S(2)}, u32[]{:S(2)}) collective-permute-start(f32[8,128]{1,0:T(8,128)S(1)} %get-tuple-element.58), channel_id=1, source_target_pairs={{0,12},{1,13},{2,14},{3,15},{4,8},{5,9},{6,10},{7,11},{8,4},{9,5},... | collective-permute-start | bytes 12296 | tf_op jit(solution)/shard_map/ppermute | solution.py:299
  30.4 4.5 %collective-permute-start.14 = (f32[8,128]{1,0:T(8,128)S(1)}, f32[8,128]{1,0:T(8,128)S(1)}, u32[]{:S(2)}, u32[]{:S(2)}) collective-permute-start(f32[8,128]{1,0:T(8,128)S(1)} %get-tuple-element.58), channel_id=1, source_target_pairs={{0,8},{1,9},{2,10},{3,11},{4,12},{5,13},{6,14},{7,15},{8,0},{9,1},... | collective-permute-start | bytes 12296 | tf_op jit(solution)/shard_map/ppermute | solution.py:299

commit v15 on v8

--- a/solution.py
+++ b/solution.py
@@ -21,12 +21,12 @@
     return pltpu.with_memory_space_constraint(x, pltpu.HBM)
 
 
-def call(kernel, name, mib, **kw):
+def call(kernel, name, mib, flops=1, **kw):
     return pl.pallas_call(
         kernel,
         name=name,
         compiler_params=pltpu.CompilerParams(vmem_limit_bytes=mib * MIB),
-        cost_estimate=pl.CostEstimate(flops=1, bytes_accessed=1, transcendentals=0),
+        cost_estimate=pl.CostEstimate(flops=flops, bytes_accessed=1, transcendentals=0),
         **kw,
     )
 
@@ -165,16 +165,16 @@
     count, start = base // 4, base + base // 2
     while count >= 1:
         run(later_pairs, start, count)
+        store(start, count)
         start += count
         count //= 2
-    store(base + base // 2, base // 2 - 1)
     total_ref[...] = pair(node(start - 1))
     for copy in copies:
         copy.wait()
 
 
 def local_kernel(pos_ref, levels_ref, gain_ref, init_ref, total_ref, table_ref, right_hbm, *refs):
-    parts, (lefts_ref, own_ref, drive_ref, right_ref, sems) = refs[:-5], refs[-5:]
+    parts, (lefts_ref, shift_ref, drive_ref, right_ref, sems) = refs[:-5], refs[-5:]
     steps, n = drive_ref.shape
     base = steps // 4
     copies = [
@@ -204,9 +204,7 @@
         states = later
     lefts_ref[pl.ds(at, 1), :] = states[0][:1]
     first = jnp.where(pos_ref[0] == 0, row(init_ref, 0), 0.0)
-    total = total_ref[...]
-    own_ref[pl.ds(0, n), :] = total
-    own_ref[pl.ds(n, 16), :] = rows16(states[0] + vm(first, total))
+    shift_ref[...] = states[0] + vm(first, total_ref[...])
 
 
 def rows16(vec):
@@ -222,25 +220,21 @@
 
 
 def group_kernel(size, pos_ref, *refs):
-    blocks = refs[:size]
-    prefix_ref, before_ref, mine_ref, shift_ref, all_ref = refs[size:]
+    maps, shifts = refs[:size], refs[size : 2 * size]
+    prefix_ref, before_ref, mine_ref, shift_ref, map_ref, held_ref = refs[2 * size :]
     n = prefix_ref.shape[0]
     member = pos_ref[0] % size
     for r in range(size):
-        all_ref[member ^ r] = blocks[r][...]
-
-    def block(q):
-        return all_ref[q, :n, :], rows8(all_ref[q, n:, :])
-
+        map_ref[member ^ r] = maps[r][...]
+        held_ref[member ^ r] = shifts[r][...]
     rows, cols = (lax.broadcasted_iota(jnp.int32, (n, n), d) for d in (0, 1))
     prefix, before = pair((rows == cols).astype(F32)), jnp.zeros((8, n), F32)
-    run, vec = block(0)
+    run, vec = map_ref[0], held_ref[0]
     for q in range(1, size):
         here = member == q
         prefix, before = jnp.where(here, run, prefix), jnp.where(here, vec, before)
-        step, shift = block(q)
-        vec = vm(vec, step) + shift
-        run = pair(mm(run, step))
+        vec = vm(vec, map_ref[q]) + held_ref[q]
+        run = pair(mm(run, map_ref[q]))
     prefix_ref[...] = prefix
     before_ref[...] = before
     mine_ref[pl.ds(0, n), :] = run
@@ -322,7 +316,7 @@
         out_shape=[maps, maps, one_map],
         in_specs=[SMEM, VMEM],
         out_specs=[HBM, HBM, VMEM],
-        scratch_shapes=[tree, tree, dma((6,))],
+        scratch_shapes=[tree, tree, dma((2 * steps.bit_length(),))],
     )(levels, table)
 
     if turn:
@@ -341,21 +335,23 @@
         projector = jnp.where(pixel_mode[None, :] == channels[:, None], pixel_weight[None, :], jnp.zeros((), BF16))
         parts = [lax.dot_general(x, projector, (((0,), (1,)), ((), ())), preferred_element_type=F32)]
 
-    block = shape((n + 16, 2 * n), BF16)
-    lefts, own = call(
-        local_kernel, "local_states", 8,
-        out_shape=[shape((steps, n), F32), block],
+    vector = shape((8, n), F32)
+
+    members = swaps(total, 1, size)
+    lefts, shift = call(
+        local_kernel, "local_states", 8, 1 << 30,
+        out_shape=[shape((steps, n), F32), vector],
         in_specs=[SMEM, SMEM] + [VMEM] * 4 + [HBM] + [VMEM] * len(parts),
         out_specs=[VMEM] * 2,
         scratch_shapes=[pltpu.VMEM((steps, n), F32), tree, dma((2,))],
     )(position, levels, gain, initial_state, total, table, hbm(right), *parts)
     prefix, before, mine, carried = call(
         functools.partial(group_kernel, size), "group_maps", 2,
-        out_shape=[one_map, shape((8, n), F32), block, shape((16, 2 * n), BF16)],
-        in_specs=[SMEM] + [VMEM] * size,
+        out_shape=[one_map, vector, shape((n + 16, 2 * n), BF16), shape((16, 2 * n), BF16)],
+        in_specs=[SMEM] + [VMEM] * (2 * size),
         out_specs=[VMEM] * 4,
-        scratch_shapes=[pltpu.VMEM((size, n + 16, 2 * n), BF16)],
-    )(position, own, *swaps(own, 1, size))
+        scratch_shapes=[pltpu.VMEM((size, n, 2 * n), BF16), pltpu.VMEM((size, 8, n), F32)],
+    )(position, total, *members, shift, *swaps(shift, 1, size))
     got = [
         lax.ppermute(mine if r < groups - 1 else carried, "tm", [(j, (j + r * size) % count) for j in range(count)])
         for r in range(1, groups)

time: 38.8 us -> 36.4 us (0.938)
  waiting for transfers between devices: 13 us -> 9.02 us
  starting transfers between devices: 13.5 us -> 15.3 us
    ppermute x9 -> x12, waiting for transfers between devices: 10 us -> 5.71 us  [swaps(): lax.ppermute(a, 'tm', [(j, j ^ r * step) for j in range(count)])]
    ppermute x9 -> x12, starting transfers between devices: 9.54 us -> 11.4 us  [swaps(): lax.ppermute(a, 'tm', [(j, j ^ r * step) for j in range(count)])]
  transfers between devices with their start and end apart: 12 -> 15, of which waited for: 6 -> 6; matrix products, arithmetic and copies ran while one was open for 0% -> 0% of each run, Pallas kernels for 11% -> 19%
where the time goes in v15:
time: 36.4 us; the launch traced here: 36.2 us
  starting transfers between devices  15.3 us (42%)
  Pallas kernels  11.8 us (32%)
  waiting for transfers between devices  9.02 us (25%)
    ppermute x12, starting transfers between devices, swaps(): lax.ppermute(a, 'tm', [(j, j ^ r * step) for j in range(count)])  11.4 us
    ppermute x12, waiting for transfers between devices, swaps(): lax.ppermute(a, 'tm', [(j, j ^ r * step) for j in range(count)])  5.71 us
    ppermute x3, starting transfers between devices, shards(): lax.ppermute(mine if r < groups - 1 else carried, 'tm', [(j, (j + r * siz...  3.96 us
    pallas_call x1, Pallas kernels, shards(): call(functools.partial(tree_kernel, steps), 'tree_of_maps', 8, out_shape=...  3.88 us
    ppermute x3, waiting for transfers between devices, shards(): lax.ppermute(mine if r < groups - 1 else carried, 'tm', [(j, (j + r * siz...  3.3 us
    pallas_call x1, Pallas kernels, shards(): call(local_kernel, 'local_states', 8, 1 << 30, out_shape=[shape((steps, n...  2.94 us
    pallas_call x1, Pallas kernels, shards(): call(functools.partial(final_kernel, size), 'estimates', 6, out_shape=sha...  2.44 us
    pallas_call x1, Pallas kernels, shards(): call(functools.partial(front_kernel, cuts, len(small), size), 'front', 5,...  1.83 us
  transfers between devices with their start and end apart: 15, of which 6 were waited for; matrix products, arithmetic and copies ran while one was open for 0% of the time, Pallas kernels for 19%

profile of v15, /device:TPU:0, one launch (start us, length us, event | category | flops | bytes accessed | tf_op | source)
XLA Modules:
  0.0 36.2 jit_solution(9703750463199904008)
XLA Ops:
  0.0 1.8 %front.1 = (bf16[16,128,256]{2,1,0:T(8,128)(2,1)S(1)}, s32[1,64]{1,0:T(1,128)S(1)}, f32[1,128]{1,0:T(1,128)S(1)}, bf16[128,128]{1,0:T(8,128)(2,1)S(1)}, s32[16,1...) custom-call(s32[1]{0:T(128)} %bitcast.pos_ref, ...), custom_call_target="tpu_custom_call" | custom-call | flops 1 | bytes 1 | tf_op jit(solution)/shard_map/front/pallas_call | solution.py:305
  1.8 0.5 %collective-permute-start.3 = (bf16[4,64,128]{2,1,0:T(8,128)(2,1)S(1)}, bf16[4,64,128]{2,1,0:T(8,128)(2,1)S(1)}, u32[]{:S(2)}, u32[]{:S(2)}) collective-permute-start(bf16[4,64,128]{2,1,0:T(8,128)(2,1)S(1)} %get-tuple-element.37), channel_id=1, source_target_pairs={{0,1},{1,0},{2,3},{3,2},{4,5},{5,4},{6,7},{7,6},{8,9},{9,8},{10,11... | collective-permute-start | bytes 196616 | tf_op jit(solution)/shard_map/ppermute | solution.py:289
  2.4 2.6 %collective-permute-start.4 = (bf16[4,64,128]{2,1,0:T(8,128)(2,1)S(1)}, bf16[4,64,128]{2,1,0:T(8,128)(2,1)S(1)}, u32[]{:S(2)}, u32[]{:S(2)}) collective-permute-start(bf16[4,64,128]{2,1,0:T(8,128)(2,1)S(1)} %get-tuple-element.38), channel_id=1, source_target_pairs={{0,2},{1,3},{2,0},{3,1},{4,6},{5,7},{6,4},{7,5},{8,10},{9,11},{10,... | collective-permute-start | bytes 196616 | tf_op jit(solution)/shard_map/ppermute | solution.py:289
  4.9 0.1 collective-permute-start.5
  5.0 3.9 %tree_of_maps.1 = (bf16[31,128,256]{2,1,0:T(8,128)(2,1)}, bf16[31,128,256]{2,1,0:T(8,128)(2,1)}, bf16[128,256]{1,0:T(8,128)(2,1)S(1)}) custom-call(s32[1,64]{1,0:T(1,128)S(1)} %get-tuple-element.28.levels_ref, bf16[16,128,256]{2,1,0:T(8,128)(2,1)S(1)} %get-tuple-element.30.table_ref), custom_call_target="tpu_custom_call" | custom-call | flops 1 | bytes 1 | tf_op jit(solution)/shard_map/tree_of_maps/pallas_call | solution.py:314
  8.9 0.0 collective-permute-done.3.refs_1_
  8.9 0.0 collective-permute-done.4.refs_2_
  8.9 0.1 collective-permute-done.5.refs_3_
  9.0 0.2 project.1
  9.2 1.8 %collective-permute-start.6 = (f32[64,128]{1,0:T(8,128)S(1)}, f32[64,128]{1,0:T(8,128)S(1)}, u32[]{:S(2)}, u32[]{:S(2)}) collective-permute-start(f32[64,128]{1,0:T(8,128)S(1)} %get-tuple-element.41), channel_id=1, source_target_pairs={{0,4},{1,5},{2,6},{3,7},{4,0},{5,1},{6,2},{7,3},{8,12},{9,13},{10,... | collective-permute-start | bytes 98312 | tf_op jit(solution)/shard_map/ppermute | solution.py:289
  11.1 2.6 %collective-permute-start.7 = (f32[64,128]{1,0:T(8,128)S(1)}, f32[64,128]{1,0:T(8,128)S(1)}, u32[]{:S(2)}, u32[]{:S(2)}) collective-permute-start(f32[64,128]{1,0:T(8,128)S(1)} %get-tuple-element.42), channel_id=1, source_target_pairs={{0,8},{1,9},{2,10},{3,11},{4,12},{5,13},{6,14},{7,15},{8,0},{9,1},... | collective-permute-start | bytes 98312 | tf_op jit(solution)/shard_map/ppermute | solution.py:289
  13.6 0.0 collective-permute-start.8
  13.7 0.8 %collective-permute-start.2 = (bf16[128,256]{1,0:T(8,128)(2,1)S(1)}, bf16[128,256]{1,0:T(8,128)(2,1)S(1)}, u32[]{:S(2)}, u32[]{:S(2)}) collective-permute-start(bf16[128,256]{1,0:T(8,128)(2,1)S(1)} %get-tuple-element.31.after_ref.total_ref.refs_0_), channel_id=1, source_target_pairs={{0,3},{1,2},{2,1},{3,0},{4,7},{5,6},{6,5},{7,4},{8,11},{9,10},{10,... | collective-permute-start | bytes 196616 | tf_op jit(solution)/shard_map/ppermute | solution.py:289
  14.5 0.9 %collective-permute-start.1 = (bf16[128,256]{1,0:T(8,128)(2,1)S(1)}, bf16[128,256]{1,0:T(8,128)(2,1)S(1)}, u32[]{:S(2)}, u32[]{:S(2)}) collective-permute-start(bf16[128,256]{1,0:T(8,128)(2,1)S(1)} %get-tuple-element.31.after_ref.total_ref.refs_0_), channel_id=1, source_target_pairs={{0,2},{1,3},{2,0},{3,1},{4,6},{5,7},{6,4},{7,5},{8,10},{9,11},{10,... | collective-permute-start | bytes 196616 | tf_op jit(solution)/shard_map/ppermute | solution.py:289
  15.4 0.0 collective-permute-done.6.refs_1_
  15.4 0.2 collective-permute-start
  15.5 0.9 %collective-permute-done.7.refs_2_ = f32[64,128]{1,0:T(8,128)S(1)} collective-permute-done((f32[64,128]{1,0:T(8,128)S(1)}, f32[64,128]{1,0:T(8,128)S(1)}, u32[]{:S(2)}, u32[]{:S(2)}) %collective-permute-start.7) | collective-permute-done | bytes 32800 | tf_op jit(solution)/shard_map/ppermute | solution.py:289
  16.5 2.9 %collective-permute-done.8.refs_3_ = f32[64,128]{1,0:T(8,128)S(1)} collective-permute-done((f32[64,128]{1,0:T(8,128)S(1)}, f32[64,128]{1,0:T(8,128)S(1)}, u32[]{:S(2)}, u32[]{:S(2)}) %collective-permute-start.8) | collective-permute-done | bytes 32800 | tf_op jit(solution)/shard_map/ppermute | solution.py:289
  19.4 0.0 copy-start
  19.4 2.9 %local_states.1 = (f32[64,128]{1,0:T(8,128)S(1)}, f32[8,128]{1,0:T(8,128)S(1)}) custom-call(s32[1]{0:T(128)} %bitcast.pos_ref, s32[1,64]{1,0:T(1,128)S(1)} %get-tuple-element.28.levels_ref, bf16[128,128]{1,0:T(8,128)(2,1)S(1)} %get-tuple-element.32.gain_ref, f32[1,128]{1,0:T(1,128)S(1)} %get-tuple-element.29.init_ref, ...), custom_call_target="tpu_custom_call" | custom-call | flops 1073741824 | bytes 1 | tf_op jit(solution)/shard_map/local_states/pallas_call | solution.py:341
  22.3 0.1 collective-permute-start.11
  22.4 1.6 %collective-permute-start.10 = (f32[8,128]{1,0:T(8,128)S(1)}, f32[8,128]{1,0:T(8,128)S(1)}, u32[]{:S(2)}, u32[]{:S(2)}) collective-permute-start(f32[8,128]{1,0:T(8,128)S(1)} %get-tuple-element.44.refs_4_), channel_id=1, source_target_pairs={{0,2},{1,3},{2,0},{3,1},{4,6},{5,7},{6,4},{7,5},{8,10},{9,11},{10,... | collective-permute-start | bytes 12296 | tf_op jit(solution)/shard_map/ppermute | solution.py:289
  23.9 0.0 collective-permute-done.2.refs_3_
  23.9 0.3 collective-permute-start.9
  24.2 0.0 collective-permute-done.1.refs_2_
  24.2 0.0 collective-permute-done.refs_1_
  24.2 1.2 %collective-permute-done.11.refs_7_ = f32[8,128]{1,0:T(8,128)S(1)} collective-permute-done((f32[8,128]{1,0:T(8,128)S(1)}, f32[8,128]{1,0:T(8,128)S(1)}, u32[]{:S(2)}, u32[]{:S(2)}) %collective-permute-start.11) | collective-permute-done | bytes 4128 | tf_op jit(solution)/shard_map/ppermute | solution.py:289
  25.4 0.7 %collective-permute-done.10.refs_6_ = f32[8,128]{1,0:T(8,128)S(1)} collective-permute-done((f32[8,128]{1,0:T(8,128)S(1)}, f32[8,128]{1,0:T(8,128)S(1)}, u32[]{:S(2)}, u32[]{:S(2)}) %collective-permute-start.10) | collective-permute-done | bytes 4128 | tf_op jit(solution)/shard_map/ppermute | solution.py:289
  26.1 0.0 collective-permute-done.9.refs_5_
  26.1 0.4 %group_maps.1 = (bf16[128,256]{1,0:T(8,128)(2,1)S(1)}, f32[8,128]{1,0:T(8,128)S(1)}, bf16[144,256]{1,0:T(8,128)(2,1)S(1)}, bf16[16,256]{1,0:T(8,128)(2,1)S(1)}) custom-call(s32[1]{0:T(128)} %bitcast.pos_ref, bf16[128,256]{1,0:T(8,128)(2,1)S(1)} %get-tuple-element.31.after_ref.total_ref.refs_0_, bf16[128,256]{1,0:T(8,128)(2,1)S(1)} %collective-permute-done.refs_1_, ...), custom_call_target="tpu_custom_call" | custom-call | flops 1 | bytes 1 | tf_op jit(solution)/shard_map/group_maps/pallas_call | solution.py:348
  26.5 0.1 collective-permute-start.13
  26.6 1.6 %collective-permute-start.12 = (bf16[144,256]{1,0:T(8,128)(2,1)S(1)}, bf16[144,256]{1,0:T(8,128)(2,1)S(1)}, u32[]{:S(2)}, u32[]{:S(2)}) collective-permute-start(bf16[144,256]{1,0:T(8,128)(2,1)S(1)} %get-tuple-element.49), channel_id=1, source_target_pairs={{0,4},{1,5},{2,6},{3,7},{4,8},{5,9},{6,10},{7,11},{8,12},{9,13},{1... | collective-permute-start | bytes 221192 | tf_op jit(solution)/shard_map/ppermute | solution.py:356
  28.2 2.3 %collective-permute-start.14 = (bf16[16,256]{1,0:T(8,128)(2,1)S(1)}, bf16[16,256]{1,0:T(8,128)(2,1)S(1)}, u32[]{:S(2)}, u32[]{:S(2)}) collective-permute-start(bf16[16,256]{1,0:T(8,128)(2,1)S(1)} %get-tuple-element.50), channel_id=1, source_target_pairs={{0,12},{1,13},{2,14},{3,15},{4,0},{5,1},{6,2},{7,3},{8,4},{9,5},{1... | collective-permute-start | bytes 24584 | tf_op jit(solution)/shard_map/ppermute | solution.py:356
  30.5 3.3 %collective-permute-done.14.refs_2_ = bf16[16,256]{1,0:T(8,128)(2,1)S(1)} collective-permute-done((bf16[16,256]{1,0:T(8,128)(2,1)S(1)}, bf16[16,256]{1,0:T(8,128)(2,1)S(1)}, u32[]{:S(2)}, u32[]{:S(2)}) %collective-permute-start.14) | collective-permute-done | bytes 8224 | tf_op jit(solution)/shard_map/ppermute | solution.py:356
  33.8 0.0 collective-permute-done.13.refs_1_
  33.8 0.0 collective-permute-done.12.refs_0_
  33.8 0.0 copy-done
  33.8 2.4 %estimates.1 = f32[64,128]{1,0:T(8,128)} custom-call(s32[1]{0:T(128)} %bitcast.pos_ref, s32[1,64]{1,0:T(1,128)S(1)} %get-tuple-element.28.levels_ref, f32[1,128]{1,0:T(1,128)S(1)} %get-tuple-element.29.init_ref, bf16[128,256]{1,0:T(8,128)(2,1)S(1)} %get-tuple-element.45.prefix_ref, f32[8,128]{1,0:T(8,128)S(1)} %get-tuple-element.46.before_ref, ...), custom_call_target="tpu_custom_call" | custom-call | flops 1 | bytes 1 | tf_op jit(solution)/shard_map/estimates/pallas_call | solution.py:360
Async XLA Ops:
  1.8 7.0 %collective-permute-start.3 = (bf16[4,64,128]{2,1,0:T(8,128)(2,1)S(1)}, bf16[4,64,128]{2,1,0:T(8,128)(2,1)S(1)}, u32[]{:S(2)}, u32[]{:S(2)}) collective-permute-start(bf16[4,64,128]{2,1,0:T(8,128)(2,1)S(1)} %get-tuple-element.37), channel_id=1, source_target_pairs={{0,1},{1,0},{2,3},{3,2},{4,5},{5,4},{6,7},{7,6},{8,9},{9,8},{10,11... | collective-permute-start | bytes 196616 | tf_op jit(solution)/shard_map/ppermute | solution.py:289
  2.4 6.5 %collective-permute-start.4 = (bf16[4,64,128]{2,1,0:T(8,128)(2,1)S(1)}, bf16[4,64,128]{2,1,0:T(8,128)(2,1)S(1)}, u32[]{:S(2)}, u32[]{:S(2)}) collective-permute-start(bf16[4,64,128]{2,1,0:T(8,128)(2,1)S(1)} %get-tuple-element.38), channel_id=1, source_target_pairs={{0,2},{1,3},{2,0},{3,1},{4,6},{5,7},{6,4},{7,5},{8,10},{9,11},{10,... | collective-permute-start | bytes 196616 | tf_op jit(solution)/shard_map/ppermute | solution.py:289
  4.9 4.0 %collective-permute-start.5 = (bf16[4,64,128]{2,1,0:T(8,128)(2,1)S(1)}, bf16[4,64,128]{2,1,0:T(8,128)(2,1)S(1)}, u32[]{:S(2)}, u32[]{:S(2)}) collective-permute-start(bf16[4,64,128]{2,1,0:T(8,128)(2,1)S(1)} %get-tuple-element.39), channel_id=1, source_target_pairs={{0,3},{1,2},{2,1},{3,0},{4,7},{5,6},{6,5},{7,4},{8,11},{9,10},{10,... | collective-permute-start | bytes 196616 | tf_op jit(solution)/shard_map/ppermute | solution.py:289
  9.2 6.2 %collective-permute-start.6 = (f32[64,128]{1,0:T(8,128)S(1)}, f32[64,128]{1,0:T(8,128)S(1)}, u32[]{:S(2)}, u32[]{:S(2)}) collective-permute-start(f32[64,128]{1,0:T(8,128)S(1)} %get-tuple-element.41), channel_id=1, source_target_pairs={{0,4},{1,5},{2,6},{3,7},{4,0},{5,1},{6,2},{7,3},{8,12},{9,13},{10,... | collective-permute-start | bytes 98312 | tf_op jit(solution)/shard_map/ppermute | solution.py:289
  11.1 5.4 %collective-permute-start.7 = (f32[64,128]{1,0:T(8,128)S(1)}, f32[64,128]{1,0:T(8,128)S(1)}, u32[]{:S(2)}, u32[]{:S(2)}) collective-permute-start(f32[64,128]{1,0:T(8,128)S(1)} %get-tuple-element.42), channel_id=1, source_target_pairs={{0,8},{1,9},{2,10},{3,11},{4,12},{5,13},{6,14},{7,15},{8,0},{9,1},... | collective-permute-start | bytes 98312 | tf_op jit(solution)/shard_map/ppermute | solution.py:289
  13.6 5.7 %collective-permute-start.8 = (f32[64,128]{1,0:T(8,128)S(1)}, f32[64,128]{1,0:T(8,128)S(1)}, u32[]{:S(2)}, u32[]{:S(2)}) collective-permute-start(f32[64,128]{1,0:T(8,128)S(1)} %get-tuple-element.43), channel_id=1, source_target_pairs={{0,12},{1,13},{2,14},{3,15},{4,8},{5,9},{6,10},{7,11},{8,4},{9,5},... | collective-permute-start | bytes 98312 | tf_op jit(solution)/shard_map/ppermute | solution.py:289
  13.7 10.3 %collective-permute-start.2 = (bf16[128,256]{1,0:T(8,128)(2,1)S(1)}, bf16[128,256]{1,0:T(8,128)(2,1)S(1)}, u32[]{:S(2)}, u32[]{:S(2)}) collective-permute-start(bf16[128,256]{1,0:T(8,128)(2,1)S(1)} %get-tuple-element.31.after_ref.total_ref.refs_0_), channel_id=1, source_target_pairs={{0,3},{1,2},{2,1},{3,0},{4,7},{5,6},{6,5},{7,4},{8,11},{9,10},{10,... | collective-permute-start | bytes 196616 | tf_op jit(solution)/shard_map/ppermute | solution.py:289
  14.5 9.7 %collective-permute-start.1 = (bf16[128,256]{1,0:T(8,128)(2,1)S(1)}, bf16[128,256]{1,0:T(8,128)(2,1)S(1)}, u32[]{:S(2)}, u32[]{:S(2)}) collective-permute-start(bf16[128,256]{1,0:T(8,128)(2,1)S(1)} %get-tuple-element.31.after_ref.total_ref.refs_0_), channel_id=1, source_target_pairs={{0,2},{1,3},{2,0},{3,1},{4,6},{5,7},{6,4},{7,5},{8,10},{9,11},{10,... | collective-permute-start | bytes 196616 | tf_op jit(solution)/shard_map/ppermute | solution.py:289
  15.4 8.9 %collective-permute-start = (bf16[128,256]{1,0:T(8,128)(2,1)S(1)}, bf16[128,256]{1,0:T(8,128)(2,1)S(1)}, u32[]{:S(2)}, u32[]{:S(2)}) collective-permute-start(bf16[128,256]{1,0:T(8,128)(2,1)S(1)} %get-tuple-element.31.after_ref.total_ref.refs_0_), channel_id=1, source_target_pairs={{0,1},{1,0},{2,3},{3,2},{4,5},{5,4},{6,7},{7,6},{8,9},{9,8},{10,11... | collective-permute-start | bytes 196616 | tf_op jit(solution)/shard_map/ppermute | solution.py:289
  19.4 14.4 %copy-start = (bf16[31,128,256]{2,1,0:T(8,128)(2,1)S(1)}, bf16[31,128,256]{2,1,0:T(8,128)(2,1)}, u32[]{:S(2)}) copy-start(bf16[31,128,256]{2,1,0:T(8,128)(2,1)} %get-tuple-element.48.left_ref) | copy-start | bytes 6094852
  22.3 3.1 %collective-permute-start.11 = (f32[8,128]{1,0:T(8,128)S(1)}, f32[8,128]{1,0:T(8,128)S(1)}, u32[]{:S(2)}, u32[]{:S(2)}) collective-permute-start(f32[8,128]{1,0:T(8,128)S(1)} %get-tuple-element.44.refs_4_), channel_id=1, source_target_pairs={{0,3},{1,2},{2,1},{3,0},{4,7},{5,6},{6,5},{7,4},{8,11},{9,10},{10,... | collective-permute-start | bytes 12296 | tf_op jit(solution)/shard_map/ppermute | solution.py:289
  22.4 3.7 %collective-permute-start.10 = (f32[8,128]{1,0:T(8,128)S(1)}, f32[8,128]{1,0:T(8,128)S(1)}, u32[]{:S(2)}, u32[]{:S(2)}) collective-permute-start(f32[8,128]{1,0:T(8,128)S(1)} %get-tuple-element.44.refs_4_), channel_id=1, source_target_pairs={{0,2},{1,3},{2,0},{3,1},{4,6},{5,7},{6,4},{7,5},{8,10},{9,11},{10,... | collective-permute-start | bytes 12296 | tf_op jit(solution)/shard_map/ppermute | solution.py:289
  23.9 2.1 %collective-permute-start.9 = (f32[8,128]{1,0:T(8,128)S(1)}, f32[8,128]{1,0:T(8,128)S(1)}, u32[]{:S(2)}, u32[]{:S(2)}) collective-permute-start(f32[8,128]{1,0:T(8,128)S(1)} %get-tuple-element.44.refs_4_), channel_id=1, source_target_pairs={{0,1},{1,0},{2,3},{3,2},{4,5},{5,4},{6,7},{7,6},{8,9},{9,8},{10,11... | collective-permute-start | bytes 12296 | tf_op jit(solution)/shard_map/ppermute | solution.py:289
  26.5 7.3 %collective-permute-start.13 = (bf16[144,256]{1,0:T(8,128)(2,1)S(1)}, bf16[144,256]{1,0:T(8,128)(2,1)S(1)}, u32[]{:S(2)}, u32[]{:S(2)}) collective-permute-start(bf16[144,256]{1,0:T(8,128)(2,1)S(1)} %get-tuple-element.49), channel_id=1, source_target_pairs={{0,8},{1,9},{2,10},{3,11},{4,12},{5,13},{6,14},{7,15},{8,0},{9,1},... | collective-permute-start | bytes 221192 | tf_op jit(solution)/shard_map/ppermute | solution.py:356
  26.6 7.2 %collective-permute-start.12 = (bf16[144,256]{1,0:T(8,128)(2,1)S(1)}, bf16[144,256]{1,0:T(8,128)(2,1)S(1)}, u32[]{:S(2)}, u32[]{:S(2)}) collective-permute-start(bf16[144,256]{1,0:T(8,128)(2,1)S(1)} %get-tuple-element.49), channel_id=1, source_target_pairs={{0,4},{1,5},{2,6},{3,7},{4,8},{5,9},{6,10},{7,11},{8,12},{9,13},{1... | collective-permute-start | bytes 221192 | tf_op jit(solution)/shard_map/ppermute | solution.py:356
  28.2 5.6 %collective-permute-start.14 = (bf16[16,256]{1,0:T(8,128)(2,1)S(1)}, bf16[16,256]{1,0:T(8,128)(2,1)S(1)}, u32[]{:S(2)}, u32[]{:S(2)}) collective-permute-start(bf16[16,256]{1,0:T(8,128)(2,1)S(1)} %get-tuple-element.50), channel_id=1, source_target_pairs={{0,12},{1,13},{2,14},{3,15},{4,0},{5,1},{6,2},{7,3},{8,4},{9,5},{1... | collective-permute-start | bytes 24584 | tf_op jit(solution)/shard_map/ppermute | solution.py:356

commit v16 on v15

--- a/solution.py
+++ b/solution.py
@@ -177,9 +177,11 @@
     parts, (lefts_ref, shift_ref, drive_ref, right_ref, sems) = refs[:-5], refs[-5:]
     steps, n = drive_ref.shape
     base = steps // 4
+    few = base // 2
+    cuts = [(0, few), (few, few), (base, few), (base + few, few - 1)]
     copies = [
-        pltpu.make_async_copy(right_hbm.at[pl.ds(0, base)], right_ref.at[pl.ds(0, base)], sems.at[0]),
-        pltpu.make_async_copy(right_hbm.at[pl.ds(base, base - 1)], right_ref.at[pl.ds(base, base - 1)], sems.at[1]),
+        pltpu.make_async_copy(right_hbm.at[pl.ds(a, b)], right_ref.at[pl.ds(a, b)], sems.at[k])
+        for k, (a, b) in enumerate(cuts)
     ]
     for copy in copies:
         copy.start()
@@ -191,8 +193,8 @@
     states = [row(drive_ref, t) for t in range(steps)]
     at, offset = 0, 0
     for level in range(steps.bit_length() - 1):
-        if level in (1, 2):
-            copies[level - 1].wait()
+        for copy in {1: copies[:2], 2: copies[2:3], 3: copies[3:]}.get(level, []):
+            copy.wait()
         later = []
         for i in range(len(states) // 2):
             mat = table_ref[levels_ref[0, 2 * i + 1]] if level == 0 else right_ref[offset + i]
@@ -343,7 +345,7 @@
         out_shape=[shape((steps, n), F32), vector],
         in_specs=[SMEM, SMEM] + [VMEM] * 4 + [HBM] + [VMEM] * len(parts),
         out_specs=[VMEM] * 2,
-        scratch_shapes=[pltpu.VMEM((steps, n), F32), tree, dma((2,))],
+        scratch_shapes=[pltpu.VMEM((steps, n), F32), tree, dma((4,))],
     )(position, levels, gain, initial_state, total, table, hbm(right), *parts)
     prefix, before, mine, carried = call(
         functools.partial(group_kernel, size), "group_maps", 2,
@@ -353,9 +355,10 @@
         scratch_shapes=[pltpu.VMEM((size, n, 2 * n), BF16), pltpu.VMEM((size, 8, n), F32)],
     )(position, total, *members, shift, *swaps(shift, 1, size))
     got = [
-        lax.ppermute(mine if r < groups - 1 else carried, "tm", [(j, (j + r * size) % count) for j in range(count)])
-        for r in range(1, groups)
+        lax.ppermute(mine, "tm", [(j, (j + r * size) % count) for j in range(count)]) for r in range(1, groups - 1)
     ]
+    ends = lax.ppermute(carried, "tm", [(j, j ^ ((groups - 1) * size)) for j in range(count)])
+    got.append(ends)
 
     return call(
         functools.partial(final_kernel, size), "estimates", 6,

time: 36.4 us -> 36.5 us (level)
  transfers between devices with their start and end apart: 15 -> 15, of which waited for: 6 -> 7; matrix products, arithmetic and copies ran while one was open for 0% -> 0% of each run, Pallas kernels for 19% -> 19%
where the time goes in v16:
time: 36.5 us; the launch traced here: 36.3 us
  starting transfers between devices  15.3 us (42%)
  Pallas kernels  11.8 us (32%)
  waiting for transfers between devices  9.1 us (25%)
    ppermute x12, starting transfers between devices, swaps(): lax.ppermute(a, 'tm', [(j, j ^ r * step) for j in range(count)])  11.4 us
    ppermute x12, waiting for transfers between devices, swaps(): lax.ppermute(a, 'tm', [(j, j ^ r * step) for j in range(count)])  5.71 us
    pallas_call x1, Pallas kernels, shards(): call(functools.partial(tree_kernel, steps), 'tree_of_maps', 8, out_shape=...  3.88 us
    ppermute x1, waiting for transfers between devices, shards(): lax.ppermute(carried, 'tm', [(j, j ^ (groups - 1) * size) for j in range(...  3.13 us
    pallas_call x1, Pallas kernels, shards(): call(local_kernel, 'local_states', 8, 1 << 30, out_shape=[shape((steps, n...  2.97 us
    pallas_call x1, Pallas kernels, shards(): call(functools.partial(final_kernel, size), 'estimates', 6, out_shape=sha...  2.44 us
    ppermute x1, starting transfers between devices, shards(): lax.ppermute(carried, 'tm', [(j, j ^ (groups - 1) * size) for j in range(...  2.32 us
    pallas_call x1, Pallas kernels, shards(): call(functools.partial(front_kernel, cuts, len(small), size), 'front', 5,...  1.83 us
  transfers between devices with their start and end apart: 15, of which 7 were waited for; matrix products, arithmetic and copies ran while one was open for 0% of the time, Pallas kernels for 19%

profile of v16, /device:TPU:0, one launch (start us, length us, event | category | flops | bytes accessed | tf_op | source)
XLA Modules:
  0.0 36.3 jit_solution(15787543544623786310)
XLA Ops:
  0.0 1.8 %front.1 = (bf16[16,128,256]{2,1,0:T(8,128)(2,1)S(1)}, s32[1,64]{1,0:T(1,128)S(1)}, f32[1,128]{1,0:T(1,128)S(1)}, bf16[128,128]{1,0:T(8,128)(2,1)S(1)}, s32[16,1...) custom-call(s32[1]{0:T(128)} %bitcast.pos_ref, ...), custom_call_target="tpu_custom_call" | custom-call | flops 1 | bytes 1 | tf_op jit(solution)/shard_map/front/pallas_call | solution.py:307
  1.8 0.5 %collective-permute-start.3 = (bf16[4,64,128]{2,1,0:T(8,128)(2,1)S(1)}, bf16[4,64,128]{2,1,0:T(8,128)(2,1)S(1)}, u32[]{:S(2)}, u32[]{:S(2)}) collective-permute-start(bf16[4,64,128]{2,1,0:T(8,128)(2,1)S(1)} %get-tuple-element.37), channel_id=1, source_target_pairs={{0,1},{1,0},{2,3},{3,2},{4,5},{5,4},{6,7},{7,6},{8,9},{9,8},{10,11... | collective-permute-start | bytes 196616 | tf_op jit(solution)/shard_map/ppermute | solution.py:291
  2.4 2.6 %collective-permute-start.4 = (bf16[4,64,128]{2,1,0:T(8,128)(2,1)S(1)}, bf16[4,64,128]{2,1,0:T(8,128)(2,1)S(1)}, u32[]{:S(2)}, u32[]{:S(2)}) collective-permute-start(bf16[4,64,128]{2,1,0:T(8,128)(2,1)S(1)} %get-tuple-element.38), channel_id=1, source_target_pairs={{0,2},{1,3},{2,0},{3,1},{4,6},{5,7},{6,4},{7,5},{8,10},{9,11},{10,... | collective-permute-start | bytes 196616 | tf_op jit(solution)/shard_map/ppermute | solution.py:291
  4.9 0.1 collective-permute-start.5
  5.0 3.9 %tree_of_maps.1 = (bf16[31,128,256]{2,1,0:T(8,128)(2,1)}, bf16[31,128,256]{2,1,0:T(8,128)(2,1)}, bf16[128,256]{1,0:T(8,128)(2,1)S(1)}) custom-call(s32[1,64]{1,0:T(1,128)S(1)} %get-tuple-element.28.levels_ref, bf16[16,128,256]{2,1,0:T(8,128)(2,1)S(1)} %get-tuple-element.30.table_ref), custom_call_target="tpu_custom_call" | custom-call | flops 1 | bytes 1 | tf_op jit(solution)/shard_map/tree_of_maps/pallas_call | solution.py:316
  8.9 0.0 collective-permute-done.3.refs_1_
  8.9 0.0 collective-permute-done.4.refs_2_
  8.9 0.1 collective-permute-done.5.refs_3_
  9.0 0.2 project.1
  9.2 1.8 %collective-permute-start.6 = (f32[64,128]{1,0:T(8,128)S(1)}, f32[64,128]{1,0:T(8,128)S(1)}, u32[]{:S(2)}, u32[]{:S(2)}) collective-permute-start(f32[64,128]{1,0:T(8,128)S(1)} %get-tuple-element.41), channel_id=1, source_target_pairs={{0,4},{1,5},{2,6},{3,7},{4,0},{5,1},{6,2},{7,3},{8,12},{9,13},{10,... | collective-permute-start | bytes 98312 | tf_op jit(solution)/shard_map/ppermute | solution.py:291
  11.1 2.6 %collective-permute-start.7 = (f32[64,128]{1,0:T(8,128)S(1)}, f32[64,128]{1,0:T(8,128)S(1)}, u32[]{:S(2)}, u32[]{:S(2)}) collective-permute-start(f32[64,128]{1,0:T(8,128)S(1)} %get-tuple-element.42), channel_id=1, source_target_pairs={{0,8},{1,9},{2,10},{3,11},{4,12},{5,13},{6,14},{7,15},{8,0},{9,1},... | collective-permute-start | bytes 98312 | tf_op jit(solution)/shard_map/ppermute | solution.py:291
  13.6 0.0 collective-permute-start.8
  13.7 0.8 %collective-permute-start.2 = (bf16[128,256]{1,0:T(8,128)(2,1)S(1)}, bf16[128,256]{1,0:T(8,128)(2,1)S(1)}, u32[]{:S(2)}, u32[]{:S(2)}) collective-permute-start(bf16[128,256]{1,0:T(8,128)(2,1)S(1)} %get-tuple-element.31.after_ref.total_ref.refs_0_), channel_id=1, source_target_pairs={{0,3},{1,2},{2,1},{3,0},{4,7},{5,6},{6,5},{7,4},{8,11},{9,10},{10,... | collective-permute-start | bytes 196616 | tf_op jit(solution)/shard_map/ppermute | solution.py:291
  14.5 0.9 %collective-permute-start.1 = (bf16[128,256]{1,0:T(8,128)(2,1)S(1)}, bf16[128,256]{1,0:T(8,128)(2,1)S(1)}, u32[]{:S(2)}, u32[]{:S(2)}) collective-permute-start(bf16[128,256]{1,0:T(8,128)(2,1)S(1)} %get-tuple-element.31.after_ref.total_ref.refs_0_), channel_id=1, source_target_pairs={{0,2},{1,3},{2,0},{3,1},{4,6},{5,7},{6,4},{7,5},{8,10},{9,11},{10,... | collective-permute-start | bytes 196616 | tf_op jit(solution)/shard_map/ppermute | solution.py:291
  15.4 0.0 collective-permute-done.6.refs_1_
  15.4 0.2 collective-permute-start
  15.5 0.9 %collective-permute-done.7.refs_2_ = f32[64,128]{1,0:T(8,128)S(1)} collective-permute-done((f32[64,128]{1,0:T(8,128)S(1)}, f32[64,128]{1,0:T(8,128)S(1)}, u32[]{:S(2)}, u32[]{:S(2)}) %collective-permute-start.7) | collective-permute-done | bytes 32800 | tf_op jit(solution)/shard_map/ppermute | solution.py:291
  16.5 2.9 %collective-permute-done.8.refs_3_ = f32[64,128]{1,0:T(8,128)S(1)} collective-permute-done((f32[64,128]{1,0:T(8,128)S(1)}, f32[64,128]{1,0:T(8,128)S(1)}, u32[]{:S(2)}, u32[]{:S(2)}) %collective-permute-start.8) | collective-permute-done | bytes 32800 | tf_op jit(solution)/shard_map/ppermute | solution.py:291
  19.4 0.0 copy-start
  19.4 3.0 %local_states.1 = (f32[64,128]{1,0:T(8,128)S(1)}, f32[8,128]{1,0:T(8,128)S(1)}) custom-call(s32[1]{0:T(128)} %bitcast.pos_ref, s32[1,64]{1,0:T(1,128)S(1)} %get-tuple-element.28.levels_ref, bf16[128,128]{1,0:T(8,128)(2,1)S(1)} %get-tuple-element.32.gain_ref, f32[1,128]{1,0:T(1,128)S(1)} %get-tuple-element.29.init_ref, ...), custom_call_target="tpu_custom_call" | custom-call | flops 1073741824 | bytes 1 | tf_op jit(solution)/shard_map/local_states/pallas_call | solution.py:343
  22.3 0.1 collective-permute-start.11
  22.4 1.6 %collective-permute-start.10 = (f32[8,128]{1,0:T(8,128)S(1)}, f32[8,128]{1,0:T(8,128)S(1)}, u32[]{:S(2)}, u32[]{:S(2)}) collective-permute-start(f32[8,128]{1,0:T(8,128)S(1)} %get-tuple-element.44.refs_4_), channel_id=1, source_target_pairs={{0,2},{1,3},{2,0},{3,1},{4,6},{5,7},{6,4},{7,5},{8,10},{9,11},{10,... | collective-permute-start | bytes 12296 | tf_op jit(solution)/shard_map/ppermute | solution.py:291
  24.0 0.0 collective-permute-done.2.refs_3_
  24.0 0.3 collective-permute-start.9
  24.3 0.0 collective-permute-done.1.refs_2_
  24.3 0.0 collective-permute-done.refs_1_
  24.3 1.2 %collective-permute-done.11.refs_7_ = f32[8,128]{1,0:T(8,128)S(1)} collective-permute-done((f32[8,128]{1,0:T(8,128)S(1)}, f32[8,128]{1,0:T(8,128)S(1)}, u32[]{:S(2)}, u32[]{:S(2)}) %collective-permute-start.11) | collective-permute-done | bytes 4128 | tf_op jit(solution)/shard_map/ppermute | solution.py:291
  25.4 0.7 %collective-permute-done.10.refs_6_ = f32[8,128]{1,0:T(8,128)S(1)} collective-permute-done((f32[8,128]{1,0:T(8,128)S(1)}, f32[8,128]{1,0:T(8,128)S(1)}, u32[]{:S(2)}, u32[]{:S(2)}) %collective-permute-start.10) | collective-permute-done | bytes 4128 | tf_op jit(solution)/shard_map/ppermute | solution.py:291
  26.1 0.0 collective-permute-done.9.refs_5_
  26.1 0.4 %group_maps.1 = (bf16[128,256]{1,0:T(8,128)(2,1)S(1)}, f32[8,128]{1,0:T(8,128)S(1)}, bf16[144,256]{1,0:T(8,128)(2,1)S(1)}, bf16[16,256]{1,0:T(8,128)(2,1)S(1)}) custom-call(s32[1]{0:T(128)} %bitcast.pos_ref, bf16[128,256]{1,0:T(8,128)(2,1)S(1)} %get-tuple-element.31.after_ref.total_ref.refs_0_, bf16[128,256]{1,0:T(8,128)(2,1)S(1)} %collective-permute-done.refs_1_, ...), custom_call_target="tpu_custom_call" | custom-call | flops 1 | bytes 1 | tf_op jit(solution)/shard_map/group_maps/pallas_call | solution.py:350
  26.5 0.1 collective-permute-start.13
  26.6 1.6 %collective-permute-start.12 = (bf16[144,256]{1,0:T(8,128)(2,1)S(1)}, bf16[144,256]{1,0:T(8,128)(2,1)S(1)}, u32[]{:S(2)}, u32[]{:S(2)}) collective-permute-start(bf16[144,256]{1,0:T(8,128)(2,1)S(1)} %get-tuple-element.49), channel_id=1, source_target_pairs={{0,4},{1,5},{2,6},{3,7},{4,8},{5,9},{6,10},{7,11},{8,12},{9,13},{1... | collective-permute-start | bytes 221192 | tf_op jit(solution)/shard_map/ppermute | solution.py:358
  28.2 2.3 %collective-permute-start.14 = (bf16[16,256]{1,0:T(8,128)(2,1)S(1)}, bf16[16,256]{1,0:T(8,128)(2,1)S(1)}, u32[]{:S(2)}, u32[]{:S(2)}) collective-permute-start(bf16[16,256]{1,0:T(8,128)(2,1)S(1)} %get-tuple-element.50), channel_id=1, source_target_pairs={{0,12},{1,13},{2,14},{3,15},{4,8},{5,9},{6,10},{7,11},{8,4},{9,5},... | collective-permute-start | bytes 24584 | tf_op jit(solution)/shard_map/ppermute | solution.py:360
  30.5 3.1 %collective-permute-done.14.refs_2_ = bf16[16,256]{1,0:T(8,128)(2,1)S(1)} collective-permute-done((bf16[16,256]{1,0:T(8,128)(2,1)S(1)}, bf16[16,256]{1,0:T(8,128)(2,1)S(1)}, u32[]{:S(2)}, u32[]{:S(2)}) %collective-permute-start.14) | collective-permute-done | bytes 8224 | tf_op jit(solution)/shard_map/ppermute | solution.py:360
  33.6 0.3 collective-permute-done.13.refs_1_
  33.9 0.0 collective-permute-done.12.refs_0_
  33.9 0.0 copy-done
  33.9 2.4 %estimates.1 = f32[64,128]{1,0:T(8,128)} custom-call(s32[1]{0:T(128)} %bitcast.pos_ref, s32[1,64]{1,0:T(1,128)S(1)} %get-tuple-element.28.levels_ref, f32[1,128]{1,0:T(1,128)S(1)} %get-tuple-element.29.init_ref, bf16[128,256]{1,0:T(8,128)(2,1)S(1)} %get-tuple-element.45.prefix_ref, f32[8,128]{1,0:T(8,128)S(1)} %get-tuple-element.46.before_ref, ...), custom_call_target="tpu_custom_call" | custom-call | flops 1 | bytes 1 | tf_op jit(solution)/shard_map/estimates/pallas_call | solution.py:363
Async XLA Ops:
  1.8 7.0 %collective-permute-start.3 = (bf16[4,64,128]{2,1,0:T(8,128)(2,1)S(1)}, bf16[4,64,128]{2,1,0:T(8,128)(2,1)S(1)}, u32[]{:S(2)}, u32[]{:S(2)}) collective-permute-start(bf16[4,64,128]{2,1,0:T(8,128)(2,1)S(1)} %get-tuple-element.37), channel_id=1, source_target_pairs={{0,1},{1,0},{2,3},{3,2},{4,5},{5,4},{6,7},{7,6},{8,9},{9,8},{10,11... | collective-permute-start | bytes 196616 | tf_op jit(solution)/shard_map/ppermute | solution.py:291
  2.4 6.5 %collective-permute-start.4 = (bf16[4,64,128]{2,1,0:T(8,128)(2,1)S(1)}, bf16[4,64,128]{2,1,0:T(8,128)(2,1)S(1)}, u32[]{:S(2)}, u32[]{:S(2)}) collective-permute-start(bf16[4,64,128]{2,1,0:T(8,128)(2,1)S(1)} %get-tuple-element.38), channel_id=1, source_target_pairs={{0,2},{1,3},{2,0},{3,1},{4,6},{5,7},{6,4},{7,5},{8,10},{9,11},{10,... | collective-permute-start | bytes 196616 | tf_op jit(solution)/shard_map/ppermute | solution.py:291
  4.9 4.0 %collective-permute-start.5 = (bf16[4,64,128]{2,1,0:T(8,128)(2,1)S(1)}, bf16[4,64,128]{2,1,0:T(8,128)(2,1)S(1)}, u32[]{:S(2)}, u32[]{:S(2)}) collective-permute-start(bf16[4,64,128]{2,1,0:T(8,128)(2,1)S(1)} %get-tuple-element.39), channel_id=1, source_target_pairs={{0,3},{1,2},{2,1},{3,0},{4,7},{5,6},{6,5},{7,4},{8,11},{9,10},{10,... | collective-permute-start | bytes 196616 | tf_op jit(solution)/shard_map/ppermute | solution.py:291
  9.2 6.2 %collective-permute-start.6 = (f32[64,128]{1,0:T(8,128)S(1)}, f32[64,128]{1,0:T(8,128)S(1)}, u32[]{:S(2)}, u32[]{:S(2)}) collective-permute-start(f32[64,128]{1,0:T(8,128)S(1)} %get-tuple-element.41), channel_id=1, source_target_pairs={{0,4},{1,5},{2,6},{3,7},{4,0},{5,1},{6,2},{7,3},{8,12},{9,13},{10,... | collective-permute-start | bytes 98312 | tf_op jit(solution)/shard_map/ppermute | solution.py:291
  11.1 5.4 %collective-permute-start.7 = (f32[64,128]{1,0:T(8,128)S(1)}, f32[64,128]{1,0:T(8,128)S(1)}, u32[]{:S(2)}, u32[]{:S(2)}) collective-permute-start(f32[64,128]{1,0:T(8,128)S(1)} %get-tuple-element.42), channel_id=1, source_target_pairs={{0,8},{1,9},{2,10},{3,11},{4,12},{5,13},{6,14},{7,15},{8,0},{9,1},... | collective-permute-start | bytes 98312 | tf_op jit(solution)/shard_map/ppermute | solution.py:291
  13.6 5.7 %collective-permute-start.8 = (f32[64,128]{1,0:T(8,128)S(1)}, f32[64,128]{1,0:T(8,128)S(1)}, u32[]{:S(2)}, u32[]{:S(2)}) collective-permute-start(f32[64,128]{1,0:T(8,128)S(1)} %get-tuple-element.43), channel_id=1, source_target_pairs={{0,12},{1,13},{2,14},{3,15},{4,8},{5,9},{6,10},{7,11},{8,4},{9,5},... | collective-permute-start | bytes 98312 | tf_op jit(solution)/shard_map/ppermute | solution.py:291
  13.7 10.3 %collective-permute-start.2 = (bf16[128,256]{1,0:T(8,128)(2,1)S(1)}, bf16[128,256]{1,0:T(8,128)(2,1)S(1)}, u32[]{:S(2)}, u32[]{:S(2)}) collective-permute-start(bf16[128,256]{1,0:T(8,128)(2,1)S(1)} %get-tuple-element.31.after_ref.total_ref.refs_0_), channel_id=1, source_target_pairs={{0,3},{1,2},{2,1},{3,0},{4,7},{5,6},{6,5},{7,4},{8,11},{9,10},{10,... | collective-permute-start | bytes 196616 | tf_op jit(solution)/shard_map/ppermute | solution.py:291
  14.5 9.7 %collective-permute-start.1 = (bf16[128,256]{1,0:T(8,128)(2,1)S(1)}, bf16[128,256]{1,0:T(8,128)(2,1)S(1)}, u32[]{:S(2)}, u32[]{:S(2)}) collective-permute-start(bf16[128,256]{1,0:T(8,128)(2,1)S(1)} %get-tuple-element.31.after_ref.total_ref.refs_0_), channel_id=1, source_target_pairs={{0,2},{1,3},{2,0},{3,1},{4,6},{5,7},{6,4},{7,5},{8,10},{9,11},{10,... | collective-permute-start | bytes 196616 | tf_op jit(solution)/shard_map/ppermute | solution.py:291
  15.4 8.9 %collective-permute-start = (bf16[128,256]{1,0:T(8,128)(2,1)S(1)}, bf16[128,256]{1,0:T(8,128)(2,1)S(1)}, u32[]{:S(2)}, u32[]{:S(2)}) collective-permute-start(bf16[128,256]{1,0:T(8,128)(2,1)S(1)} %get-tuple-element.31.after_ref.total_ref.refs_0_), channel_id=1, source_target_pairs={{0,1},{1,0},{2,3},{3,2},{4,5},{5,4},{6,7},{7,6},{8,9},{9,8},{10,11... | collective-permute-start | bytes 196616 | tf_op jit(solution)/shard_map/ppermute | solution.py:291
  19.4 14.5 %copy-start = (bf16[31,128,256]{2,1,0:T(8,128)(2,1)S(1)}, bf16[31,128,256]{2,1,0:T(8,128)(2,1)}, u32[]{:S(2)}) copy-start(bf16[31,128,256]{2,1,0:T(8,128)(2,1)} %get-tuple-element.48.left_ref) | copy-start | bytes 6094852
  22.3 3.1 %collective-permute-start.11 = (f32[8,128]{1,0:T(8,128)S(1)}, f32[8,128]{1,0:T(8,128)S(1)}, u32[]{:S(2)}, u32[]{:S(2)}) collective-permute-start(f32[8,128]{1,0:T(8,128)S(1)} %get-tuple-element.44.refs_4_), channel_id=1, source_target_pairs={{0,3},{1,2},{2,1},{3,0},{4,7},{5,6},{6,5},{7,4},{8,11},{9,10},{10,... | collective-permute-start | bytes 12296 | tf_op jit(solution)/shard_map/ppermute | solution.py:291
  22.4 3.7 %collective-permute-start.10 = (f32[8,128]{1,0:T(8,128)S(1)}, f32[8,128]{1,0:T(8,128)S(1)}, u32[]{:S(2)}, u32[]{:S(2)}) collective-permute-start(f32[8,128]{1,0:T(8,128)S(1)} %get-tuple-element.44.refs_4_), channel_id=1, source_target_pairs={{0,2},{1,3},{2,0},{3,1},{4,6},{5,7},{6,4},{7,5},{8,10},{9,11},{10,... | collective-permute-start | bytes 12296 | tf_op jit(solution)/shard_map/ppermute | solution.py:291
  24.0 2.1 %collective-permute-start.9 = (f32[8,128]{1,0:T(8,128)S(1)}, f32[8,128]{1,0:T(8,128)S(1)}, u32[]{:S(2)}, u32[]{:S(2)}) collective-permute-start(f32[8,128]{1,0:T(8,128)S(1)} %get-tuple-element.44.refs_4_), channel_id=1, source_target_pairs={{0,1},{1,0},{2,3},{3,2},{4,5},{5,4},{6,7},{7,6},{8,9},{9,8},{10,11... | collective-permute-start | bytes 12296 | tf_op jit(solution)/shard_map/ppermute | solution.py:291
  26.5 7.4 %collective-permute-start.13 = (bf16[144,256]{1,0:T(8,128)(2,1)S(1)}, bf16[144,256]{1,0:T(8,128)(2,1)S(1)}, u32[]{:S(2)}, u32[]{:S(2)}) collective-permute-start(bf16[144,256]{1,0:T(8,128)(2,1)S(1)} %get-tuple-element.49), channel_id=1, source_target_pairs={{0,8},{1,9},{2,10},{3,11},{4,12},{5,13},{6,14},{7,15},{8,0},{9,1},... | collective-permute-start | bytes 221192 | tf_op jit(solution)/shard_map/ppermute | solution.py:358
  26.6 7.3 %collective-permute-start.12 = (bf16[144,256]{1,0:T(8,128)(2,1)S(1)}, bf16[144,256]{1,0:T(8,128)(2,1)S(1)}, u32[]{:S(2)}, u32[]{:S(2)}) collective-permute-start(bf16[144,256]{1,0:T(8,128)(2,1)S(1)} %get-tuple-element.49), channel_id=1, source_target_pairs={{0,4},{1,5},{2,6},{3,7},{4,8},{5,9},{6,10},{7,11},{8,12},{9,13},{1... | collective-permute-start | bytes 221192 | tf_op jit(solution)/shard_map/ppermute | solution.py:358
  28.2 5.5 %collective-permute-start.14 = (bf16[16,256]{1,0:T(8,128)(2,1)S(1)}, bf16[16,256]{1,0:T(8,128)(2,1)S(1)}, u32[]{:S(2)}, u32[]{:S(2)}) collective-permute-start(bf16[16,256]{1,0:T(8,128)(2,1)S(1)} %get-tuple-element.50), channel_id=1, source_target_pairs={{0,12},{1,13},{2,14},{3,15},{4,8},{5,9},{6,10},{7,11},{8,4},{9,5},... | collective-permute-start | bytes 24584 | tf_op jit(solution)/shard_map/ppermute | solution.py:360

commit v17 on v15

--- a/solution.py
+++ b/solution.py
@@ -242,9 +242,44 @@
     shift_ref[...] = rows16(vec)
 
 
-def final_kernel(size, pos_ref, levels_ref, init_ref, prefix_ref, before_ref, total_ref, lefts_ref, left_ref, table_ref, *refs):
-    got, out_ref = refs[:-1], refs[-1]
+def offsets(steps):
+    sizes = [steps >> (level + 1) for level in range(steps.bit_length() - 1)]
+    return [sum(sizes[1:k]) for k in range(len(sizes))], [sum(sizes[:k]) for k in range(len(sizes))]
+
+
+def third_kernel(levels_ref, table_ref, lefts_ref, left_hbm, maps_hbm, shifts_ref, left_ref, maps_ref, sems):
+    steps = lefts_ref.shape[0]
+    into = pltpu.make_async_copy(left_hbm, left_ref, sems.at[0])
+    into.start()
+    into.wait()
+    maps_at, shifts_at = offsets(steps)
+    k = 0
+    for level in reversed(range(0, len(maps_at), 2)):
+        for b in range(steps >> (level + 2)):
+            wide = left_ref[maps_at[level + 1] + b]
+            last = table_ref[levels_ref[0, 4 * b + 2]] if level == 0 else left_ref[maps_at[level] + 2 * b + 1]
+            maps_ref[k] = pair(mm(wide, last))
+            shift = vm(row(lefts_ref, shifts_at[level + 1] + b), last) + row(lefts_ref, shifts_at[level] + 2 * b + 1)
+            shifts_ref[pl.ds(k, 1), :] = shift[:1]
+            k += 1
+    out = pltpu.make_async_copy(maps_ref, maps_hbm, sems.at[1])
+    out.start()
+    out.wait()
+
+
+def final_kernel(size, pos_ref, levels_ref, init_ref, prefix_ref, before_ref, total_ref, lefts_ref, left_ref, table_ref, thirds_ref, maps_hbm, *refs):
+    got, (out_ref, maps_ref, sems) = refs[:-3], refs[-3:]
     steps, n = lefts_ref.shape
+    maps_at, shifts_at = offsets(steps)
+    count = maps_ref.shape[0]
+    few = steps // 16
+    cuts = [(0, count - 4 * few)] + [(count - k * few, few) for k in (4, 3, 2, 1)]
+    copies = [
+        pltpu.make_async_copy(maps_hbm.at[pl.ds(a, b)], maps_ref.at[pl.ds(a, b)], sems.at[k])
+        for k, (a, b) in enumerate(cuts)
+    ]
+    for copy in copies:
+        copy.start()
     position = pos_ref[0]
     group = position // size
     state = jnp.zeros((8, n), F32)
@@ -256,15 +291,23 @@
     first = jnp.where(position == 0, row(init_ref, 0), 0.0)
     state = vm(state, prefix_ref[...]) + before_ref[...] + first
     out_ref[pl.ds(steps - 1, 1), :] = (vm(state, total_ref[...]) + row(lefts_ref, steps - 1))[:1]
-    levels = steps.bit_length() - 1
-    starts = [state]
-    sizes = [steps >> (level + 1) for level in range(levels)]
-    for level in reversed(range(levels)):
-        at, offset = sum(sizes[:level]), sum(sizes[1:level])
+    starts, k = [state], 0
+    for level in reversed(range(0, len(maps_at), 2)):
+        if level == len(maps_at) - 2:
+            copies[0].wait()
+        if level == 0:
+            for copy in copies[1:]:
+                copy.wait()
         later = []
-        for i, x in enumerate(starts):
-            mat = table_ref[levels_ref[0, 2 * i]] if level == 0 else left_ref[offset + i]
-            later += [x, vm(x, mat) + row(lefts_ref, at + i)]
+        for b, x in enumerate(starts):
+            one = table_ref[levels_ref[0, 4 * b]] if level == 0 else left_ref[maps_at[level] + 2 * b]
+            later += [
+                x,
+                vm(x, one) + row(lefts_ref, shifts_at[level] + 2 * b),
+                vm(x, left_ref[maps_at[level + 1] + b]) + row(lefts_ref, shifts_at[level + 1] + b),
+                vm(x, maps_ref[k]) + row(thirds_ref, k),
+            ]
+            k += 1
         starts = later
     for t in range(1, steps):
         out_ref[pl.ds(t - 1, 1), :] = starts[t][:1]
@@ -357,12 +400,21 @@
         for r in range(1, groups)
     ]
 
+    nodes = (steps - 1) // 3
+    thirds_maps, thirds = call(
+        third_kernel, "third_children", 6,
+        out_shape=[pltpu.HBM((nodes, n, 2 * n), BF16), shape((nodes, n), F32)],
+        in_specs=[SMEM, VMEM, VMEM, HBM],
+        out_specs=[HBM, VMEM],
+        scratch_shapes=[tree, pltpu.VMEM((nodes, n, 2 * n), BF16), dma((2,))],
+    )(levels, table, lefts, hbm(left))
     return call(
-        functools.partial(final_kernel, size), "estimates", 6,
+        functools.partial(final_kernel, size), "estimates", 8,
         out_shape=shape((steps, n), F32),
-        in_specs=[SMEM, SMEM] + [VMEM] * (7 + len(got)),
+        in_specs=[SMEM, SMEM] + [VMEM] * 8 + [HBM] + [VMEM] * len(got),
         out_specs=VMEM,
-    )(position, levels, initial_state, prefix, before, total, lefts, left, table, *got)
+        scratch_shapes=[pltpu.VMEM((nodes, n, 2 * n), BF16), dma((5,))],
+    )(position, levels, initial_state, prefix, before, total, lefts, left, table, thirds, hbm(thirds_maps), *got)
 
 
 def solution(mesh):

time: 36.4 us -> 37.9 us (1.041)
  Pallas kernels: 11.8 us -> 16.5 us
  waiting for transfers between devices: 9.02 us -> 5.72 us
    pallas_call x1 -> x2, Pallas kernels: 2.44 us -> 7.12 us  [the longest x1 4.04 us: shards(): call(third_kernel, 'third_children', 6, out_shape=[pltpu.HBM((nodes, n, 2...]
    ppermute x3, waiting for transfers between devices: 3.3 us -> 0.01 us  [shards(): lax.ppermute(mine if r < groups - 1 else carried, 'tm', [(j, (j + r * siz...]
  transfers between devices with their start and end apart: 15 -> 15, of which waited for: 6 -> 5; matrix products, arithmetic and copies ran while one was open for 0% -> 0% of each run, Pallas kernels for 19% -> 29%
where the time goes in v17:
time: 37.9 us; the launch traced here: 37.7 us
  Pallas kernels  16.5 us (44%)
  starting transfers between devices  15.3 us (40%)
  waiting for transfers between devices  5.72 us (15%)
    ppermute x12, starting transfers between devices, swaps(): lax.ppermute(a, 'tm', [(j, j ^ r * step) for j in range(count)])  11.4 us
    ppermute x12, waiting for transfers between devices, swaps(): lax.ppermute(a, 'tm', [(j, j ^ r * step) for j in range(count)])  5.71 us
    pallas_call x1, Pallas kernels, shards(): call(third_kernel, 'third_children', 6, out_shape=[pltpu.HBM((nodes, n, 2...  4.04 us
    ppermute x3, starting transfers between devices, shards(): lax.ppermute(mine if r < groups - 1 else carried, 'tm', [(j, (j + r * siz...  3.96 us
    pallas_call x1, Pallas kernels, shards(): call(functools.partial(tree_kernel, steps), 'tree_of_maps', 8, out_shape=...  3.89 us
    pallas_call x1, Pallas kernels, shards(): call(functools.partial(final_kernel, size), 'estimates', 8, out_shape=sha...  3.08 us
    pallas_call x1, Pallas kernels, shards(): call(local_kernel, 'local_states', 8, 1 << 30, out_shape=[shape((steps, n...  2.94 us
    pallas_call x1, Pallas kernels, shards(): call(functools.partial(front_kernel, cuts, len(small), size), 'front', 5,...  1.83 us
  transfers between devices with their start and end apart: 15, of which 5 were waited for; matrix products, arithmetic and copies ran while one was open for 0% of the time, Pallas kernels for 29%

profile of v17, /device:TPU:0, one launch (start us, length us, event | category | flops | bytes accessed | tf_op | source)
XLA Modules:
  0.0 37.7 jit_solution(4958564347491498675)
XLA Ops:
  0.0 1.8 %front.1 = (bf16[16,128,256]{2,1,0:T(8,128)(2,1)S(1)}, s32[1,64]{1,0:T(1,128)S(1)}, f32[1,128]{1,0:T(1,128)S(1)}, bf16[128,128]{1,0:T(8,128)(2,1)S(1)}, s32[16,1...) custom-call(s32[1]{0:T(128)} %bitcast.pos_ref, ...), custom_call_target="tpu_custom_call" | custom-call | flops 1 | bytes 1 | tf_op jit(solution)/shard_map/front/pallas_call | solution.py:348
  1.8 0.5 %collective-permute-start.3 = (bf16[4,64,128]{2,1,0:T(8,128)(2,1)S(1)}, bf16[4,64,128]{2,1,0:T(8,128)(2,1)S(1)}, u32[]{:S(2)}, u32[]{:S(2)}) collective-permute-start(bf16[4,64,128]{2,1,0:T(8,128)(2,1)S(1)} %get-tuple-element.39), channel_id=1, source_target_pairs={{0,1},{1,0},{2,3},{3,2},{4,5},{5,4},{6,7},{7,6},{8,9},{9,8},{10,11... | collective-permute-start | bytes 196616 | tf_op jit(solution)/shard_map/ppermute | solution.py:332
  2.4 2.6 %collective-permute-start.4 = (bf16[4,64,128]{2,1,0:T(8,128)(2,1)S(1)}, bf16[4,64,128]{2,1,0:T(8,128)(2,1)S(1)}, u32[]{:S(2)}, u32[]{:S(2)}) collective-permute-start(bf16[4,64,128]{2,1,0:T(8,128)(2,1)S(1)} %get-tuple-element.40), channel_id=1, source_target_pairs={{0,2},{1,3},{2,0},{3,1},{4,6},{5,7},{6,4},{7,5},{8,10},{9,11},{10,... | collective-permute-start | bytes 196616 | tf_op jit(solution)/shard_map/ppermute | solution.py:332
  4.9 0.1 collective-permute-start.5
  5.0 3.9 %tree_of_maps.1 = (bf16[31,128,256]{2,1,0:T(8,128)(2,1)}, bf16[31,128,256]{2,1,0:T(8,128)(2,1)}, bf16[128,256]{1,0:T(8,128)(2,1)S(1)}) custom-call(s32[1,64]{1,0:T(1,128)S(1)} %get-tuple-element.30.levels_ref, bf16[16,128,256]{2,1,0:T(8,128)(2,1)S(1)} %get-tuple-element.32.table_ref), custom_call_target="tpu_custom_call" | custom-call | flops 1 | bytes 1 | tf_op jit(solution)/shard_map/tree_of_maps/pallas_call | solution.py:357
  8.9 0.0 collective-permute-done.3.refs_1_
  8.9 0.0 collective-permute-done.4.refs_2_
  8.9 0.1 collective-permute-done.5.refs_3_
  9.0 0.2 project.1
  9.2 1.8 %collective-permute-start.6 = (f32[64,128]{1,0:T(8,128)S(1)}, f32[64,128]{1,0:T(8,128)S(1)}, u32[]{:S(2)}, u32[]{:S(2)}) collective-permute-start(f32[64,128]{1,0:T(8,128)S(1)} %get-tuple-element.43), channel_id=1, source_target_pairs={{0,4},{1,5},{2,6},{3,7},{4,0},{5,1},{6,2},{7,3},{8,12},{9,13},{10,... | collective-permute-start | bytes 98312 | tf_op jit(solution)/shard_map/ppermute | solution.py:332
  11.1 2.6 %collective-permute-start.7 = (f32[64,128]{1,0:T(8,128)S(1)}, f32[64,128]{1,0:T(8,128)S(1)}, u32[]{:S(2)}, u32[]{:S(2)}) collective-permute-start(f32[64,128]{1,0:T(8,128)S(1)} %get-tuple-element.44), channel_id=1, source_target_pairs={{0,8},{1,9},{2,10},{3,11},{4,12},{5,13},{6,14},{7,15},{8,0},{9,1},... | collective-permute-start | bytes 98312 | tf_op jit(solution)/shard_map/ppermute | solution.py:332
  13.7 0.0 collective-permute-start.8
  13.7 0.9 %collective-permute-start.2 = (bf16[128,256]{1,0:T(8,128)(2,1)S(1)}, bf16[128,256]{1,0:T(8,128)(2,1)S(1)}, u32[]{:S(2)}, u32[]{:S(2)}) collective-permute-start(bf16[128,256]{1,0:T(8,128)(2,1)S(1)} %get-tuple-element.33.after_ref.total_ref.refs_0_), channel_id=1, source_target_pairs={{0,3},{1,2},{2,1},{3,0},{4,7},{5,6},{6,5},{7,4},{8,11},{9,10},{10,... | collective-permute-start | bytes 196616 | tf_op jit(solution)/shard_map/ppermute | solution.py:332
  14.5 0.9 %collective-permute-start.1 = (bf16[128,256]{1,0:T(8,128)(2,1)S(1)}, bf16[128,256]{1,0:T(8,128)(2,1)S(1)}, u32[]{:S(2)}, u32[]{:S(2)}) collective-permute-start(bf16[128,256]{1,0:T(8,128)(2,1)S(1)} %get-tuple-element.33.after_ref.total_ref.refs_0_), channel_id=1, source_target_pairs={{0,2},{1,3},{2,0},{3,1},{4,6},{5,7},{6,4},{7,5},{8,10},{9,11},{10,... | collective-permute-start | bytes 196616 | tf_op jit(solution)/shard_map/ppermute | solution.py:332
  15.4 0.0 collective-permute-done.6.refs_1_
  15.4 0.1 collective-permute-start
  15.5 0.9 %collective-permute-done.7.refs_2_ = f32[64,128]{1,0:T(8,128)S(1)} collective-permute-done((f32[64,128]{1,0:T(8,128)S(1)}, f32[64,128]{1,0:T(8,128)S(1)}, u32[]{:S(2)}, u32[]{:S(2)}) %collective-permute-start.7) | collective-permute-done | bytes 32800 | tf_op jit(solution)/shard_map/ppermute | solution.py:332
  16.5 2.9 %collective-permute-done.8.refs_3_ = f32[64,128]{1,0:T(8,128)S(1)} collective-permute-done((f32[64,128]{1,0:T(8,128)S(1)}, f32[64,128]{1,0:T(8,128)S(1)}, u32[]{:S(2)}, u32[]{:S(2)}) %collective-permute-start.8) | collective-permute-done | bytes 32800 | tf_op jit(solution)/shard_map/ppermute | solution.py:332
  19.4 2.9 %local_states.1 = (f32[64,128]{1,0:T(8,128)S(1)}, f32[8,128]{1,0:T(8,128)S(1)}) custom-call(s32[1]{0:T(128)} %bitcast.pos_ref, s32[1,64]{1,0:T(1,128)S(1)} %get-tuple-element.30.levels_ref, bf16[128,128]{1,0:T(8,128)(2,1)S(1)} %get-tuple-element.34.gain_ref, f32[1,128]{1,0:T(1,128)S(1)} %get-tuple-element.31.init_ref, ...), custom_call_target="tpu_custom_call" | custom-call | flops 1073741824 | bytes 1 | tf_op jit(solution)/shard_map/local_states/pallas_call | solution.py:384
  22.3 0.0 copy-start
  22.3 0.1 collective-permute-start.11
  22.4 1.6 %collective-permute-start.10 = (f32[8,128]{1,0:T(8,128)S(1)}, f32[8,128]{1,0:T(8,128)S(1)}, u32[]{:S(2)}, u32[]{:S(2)}) collective-permute-start(f32[8,128]{1,0:T(8,128)S(1)} %get-tuple-element.46.refs_4_), channel_id=1, source_target_pairs={{0,2},{1,3},{2,0},{3,1},{4,6},{5,7},{6,4},{7,5},{8,10},{9,11},{10,... | collective-permute-start | bytes 12296 | tf_op jit(solution)/shard_map/ppermute | solution.py:332
  24.0 0.0 collective-permute-done.2.refs_3_
  24.0 0.3 collective-permute-start.9
  24.3 0.0 collective-permute-done.1.refs_2_
  24.3 0.0 collective-permute-done.refs_1_
  24.3 1.2 %collective-permute-done.11.refs_7_ = f32[8,128]{1,0:T(8,128)S(1)} collective-permute-done((f32[8,128]{1,0:T(8,128)S(1)}, f32[8,128]{1,0:T(8,128)S(1)}, u32[]{:S(2)}, u32[]{:S(2)}) %collective-permute-start.11) | collective-permute-done | bytes 4128 | tf_op jit(solution)/shard_map/ppermute | solution.py:332
  25.4 0.7 %collective-permute-done.10.refs_6_ = f32[8,128]{1,0:T(8,128)S(1)} collective-permute-done((f32[8,128]{1,0:T(8,128)S(1)}, f32[8,128]{1,0:T(8,128)S(1)}, u32[]{:S(2)}, u32[]{:S(2)}) %collective-permute-start.10) | collective-permute-done | bytes 4128 | tf_op jit(solution)/shard_map/ppermute | solution.py:332
  26.1 0.0 collective-permute-done.9.refs_5_
  26.1 0.4 %group_maps.1 = (bf16[128,256]{1,0:T(8,128)(2,1)S(1)}, f32[8,128]{1,0:T(8,128)S(1)}, bf16[144,256]{1,0:T(8,128)(2,1)S(1)}, bf16[16,256]{1,0:T(8,128)(2,1)S(1)}) custom-call(s32[1]{0:T(128)} %bitcast.pos_ref, bf16[128,256]{1,0:T(8,128)(2,1)S(1)} %get-tuple-element.33.after_ref.total_ref.refs_0_, bf16[128,256]{1,0:T(8,128)(2,1)S(1)} %collective-permute-done.refs_1_, ...), custom_call_target="tpu_custom_call" | custom-call | flops 1 | bytes 1 | tf_op jit(solution)/shard_map/group_maps/pallas_call | solution.py:391
  26.5 0.1 collective-permute-start.13
  26.6 1.6 %collective-permute-start.12 = (bf16[144,256]{1,0:T(8,128)(2,1)S(1)}, bf16[144,256]{1,0:T(8,128)(2,1)S(1)}, u32[]{:S(2)}, u32[]{:S(2)}) collective-permute-start(bf16[144,256]{1,0:T(8,128)(2,1)S(1)} %get-tuple-element.53), channel_id=1, source_target_pairs={{0,4},{1,5},{2,6},{3,7},{4,8},{5,9},{6,10},{7,11},{8,12},{9,13},{1... | collective-permute-start | bytes 221192 | tf_op jit(solution)/shard_map/ppermute | solution.py:399
  28.2 2.3 %collective-permute-start.14 = (bf16[16,256]{1,0:T(8,128)(2,1)S(1)}, bf16[16,256]{1,0:T(8,128)(2,1)S(1)}, u32[]{:S(2)}, u32[]{:S(2)}) collective-permute-start(bf16[16,256]{1,0:T(8,128)(2,1)S(1)} %get-tuple-element.54), channel_id=1, source_target_pairs={{0,12},{1,13},{2,14},{3,15},{4,0},{5,1},{6,2},{7,3},{8,4},{9,5},{1... | collective-permute-start | bytes 24584 | tf_op jit(solution)/shard_map/ppermute | solution.py:399
  30.5 4.0 %third_children.1 = (bf16[21,128,256]{2,1,0:T(8,128)(2,1)}, f32[21,128]{1,0:T(8,128)S(1)}) custom-call(s32[1,64]{1,0:T(1,128)S(1)} %get-tuple-element.30.levels_ref, bf16[16,128,256]{2,1,0:T(8,128)(2,1)S(1)} %get-tuple-element.32.table_ref, f32[64,128]{1,0:T(8,128)S(1)} %get-tuple-element.49.lefts_ref, bf16[31,128,256]{2,1,0:T(8,128)(2,1)} %get-tuple-element.50.left_hbm.left_ref), custom_call_target="tpu_custom_call" | custom-call | flops 1 | bytes 1 | tf_op jit(solution)/shard_map/third_children/pallas_call | solution.py:404
  34.6 0.0 collective-permute-done.14.refs_2_
  34.6 0.0 collective-permute-done.13.refs_1_
  34.6 0.0 collective-permute-done.12.refs_0_
  34.6 0.0 copy-done
  34.6 3.1 %estimates.1 = f32[64,128]{1,0:T(8,128)} custom-call(s32[1]{0:T(128)} %bitcast.pos_ref, s32[1,64]{1,0:T(1,128)S(1)} %get-tuple-element.30.levels_ref, f32[1,128]{1,0:T(1,128)S(1)} %get-tuple-element.31.init_ref, bf16[128,256]{1,0:T(8,128)(2,1)S(1)} %get-tuple-element.47.prefix_ref, f32[8,128]{1,0:T(8,128)S(1)} %get-tuple-element.48.before_ref, ...), custom_call_target="tpu_custom_call" | custom-call | flops 1 | bytes 1 | tf_op jit(solution)/shard_map/estimates/pallas_call | solution.py:411
Async XLA Ops:
  1.8 7.0 %collective-permute-start.3 = (bf16[4,64,128]{2,1,0:T(8,128)(2,1)S(1)}, bf16[4,64,128]{2,1,0:T(8,128)(2,1)S(1)}, u32[]{:S(2)}, u32[]{:S(2)}) collective-permute-start(bf16[4,64,128]{2,1,0:T(8,128)(2,1)S(1)} %get-tuple-element.39), channel_id=1, source_target_pairs={{0,1},{1,0},{2,3},{3,2},{4,5},{5,4},{6,7},{7,6},{8,9},{9,8},{10,11... | collective-permute-start | bytes 196616 | tf_op jit(solution)/shard_map/ppermute | solution.py:332
  2.4 6.5 %collective-permute-start.4 = (bf16[4,64,128]{2,1,0:T(8,128)(2,1)S(1)}, bf16[4,64,128]{2,1,0:T(8,128)(2,1)S(1)}, u32[]{:S(2)}, u32[]{:S(2)}) collective-permute-start(bf16[4,64,128]{2,1,0:T(8,128)(2,1)S(1)} %get-tuple-element.40), channel_id=1, source_target_pairs={{0,2},{1,3},{2,0},{3,1},{4,6},{5,7},{6,4},{7,5},{8,10},{9,11},{10,... | collective-permute-start | bytes 196616 | tf_op jit(solution)/shard_map/ppermute | solution.py:332
  4.9 4.0 %collective-permute-start.5 = (bf16[4,64,128]{2,1,0:T(8,128)(2,1)S(1)}, bf16[4,64,128]{2,1,0:T(8,128)(2,1)S(1)}, u32[]{:S(2)}, u32[]{:S(2)}) collective-permute-start(bf16[4,64,128]{2,1,0:T(8,128)(2,1)S(1)} %get-tuple-element.41), channel_id=1, source_target_pairs={{0,3},{1,2},{2,1},{3,0},{4,7},{5,6},{6,5},{7,4},{8,11},{9,10},{10,... | collective-permute-start | bytes 196616 | tf_op jit(solution)/shard_map/ppermute | solution.py:332
  9.2 6.2 %collective-permute-start.6 = (f32[64,128]{1,0:T(8,128)S(1)}, f32[64,128]{1,0:T(8,128)S(1)}, u32[]{:S(2)}, u32[]{:S(2)}) collective-permute-start(f32[64,128]{1,0:T(8,128)S(1)} %get-tuple-element.43), channel_id=1, source_target_pairs={{0,4},{1,5},{2,6},{3,7},{4,0},{5,1},{6,2},{7,3},{8,12},{9,13},{10,... | collective-permute-start | bytes 98312 | tf_op jit(solution)/shard_map/ppermute | solution.py:332
  11.1 5.4 %collective-permute-start.7 = (f32[64,128]{1,0:T(8,128)S(1)}, f32[64,128]{1,0:T(8,128)S(1)}, u32[]{:S(2)}, u32[]{:S(2)}) collective-permute-start(f32[64,128]{1,0:T(8,128)S(1)} %get-tuple-element.44), channel_id=1, source_target_pairs={{0,8},{1,9},{2,10},{3,11},{4,12},{5,13},{6,14},{7,15},{8,0},{9,1},... | collective-permute-start | bytes 98312 | tf_op jit(solution)/shard_map/ppermute | solution.py:332
  13.7 5.7 %collective-permute-start.8 = (f32[64,128]{1,0:T(8,128)S(1)}, f32[64,128]{1,0:T(8,128)S(1)}, u32[]{:S(2)}, u32[]{:S(2)}) collective-permute-start(f32[64,128]{1,0:T(8,128)S(1)} %get-tuple-element.45), channel_id=1, source_target_pairs={{0,12},{1,13},{2,14},{3,15},{4,8},{5,9},{6,10},{7,11},{8,4},{9,5},... | collective-permute-start | bytes 98312 | tf_op jit(solution)/shard_map/ppermute | solution.py:332
  13.7 10.3 %collective-permute-start.2 = (bf16[128,256]{1,0:T(8,128)(2,1)S(1)}, bf16[128,256]{1,0:T(8,128)(2,1)S(1)}, u32[]{:S(2)}, u32[]{:S(2)}) collective-permute-start(bf16[128,256]{1,0:T(8,128)(2,1)S(1)} %get-tuple-element.33.after_ref.total_ref.refs_0_), channel_id=1, source_target_pairs={{0,3},{1,2},{2,1},{3,0},{4,7},{5,6},{6,5},{7,4},{8,11},{9,10},{10,... | collective-permute-start | bytes 196616 | tf_op jit(solution)/shard_map/ppermute | solution.py:332
  14.5 9.7 %collective-permute-start.1 = (bf16[128,256]{1,0:T(8,128)(2,1)S(1)}, bf16[128,256]{1,0:T(8,128)(2,1)S(1)}, u32[]{:S(2)}, u32[]{:S(2)}) collective-permute-start(bf16[128,256]{1,0:T(8,128)(2,1)S(1)} %get-tuple-element.33.after_ref.total_ref.refs_0_), channel_id=1, source_target_pairs={{0,2},{1,3},{2,0},{3,1},{4,6},{5,7},{6,4},{7,5},{8,10},{9,11},{10,... | collective-permute-start | bytes 196616 | tf_op jit(solution)/shard_map/ppermute | solution.py:332
  15.4 8.9 %collective-permute-start = (bf16[128,256]{1,0:T(8,128)(2,1)S(1)}, bf16[128,256]{1,0:T(8,128)(2,1)S(1)}, u32[]{:S(2)}, u32[]{:S(2)}) collective-permute-start(bf16[128,256]{1,0:T(8,128)(2,1)S(1)} %get-tuple-element.33.after_ref.total_ref.refs_0_), channel_id=1, source_target_pairs={{0,1},{1,0},{2,3},{3,2},{4,5},{5,4},{6,7},{7,6},{8,9},{9,8},{10,11... | collective-permute-start | bytes 196616 | tf_op jit(solution)/shard_map/ppermute | solution.py:332
  22.3 12.3 %copy-start = (bf16[31,128,256]{2,1,0:T(8,128)(2,1)S(1)}, bf16[31,128,256]{2,1,0:T(8,128)(2,1)}, u32[]{:S(2)}) copy-start(bf16[31,128,256]{2,1,0:T(8,128)(2,1)} %get-tuple-element.50.left_hbm.left_ref) | copy-start | bytes 6094852
  22.3 3.1 %collective-permute-start.11 = (f32[8,128]{1,0:T(8,128)S(1)}, f32[8,128]{1,0:T(8,128)S(1)}, u32[]{:S(2)}, u32[]{:S(2)}) collective-permute-start(f32[8,128]{1,0:T(8,128)S(1)} %get-tuple-element.46.refs_4_), channel_id=1, source_target_pairs={{0,3},{1,2},{2,1},{3,0},{4,7},{5,6},{6,5},{7,4},{8,11},{9,10},{10,... | collective-permute-start | bytes 12296 | tf_op jit(solution)/shard_map/ppermute | solution.py:332
  22.4 3.7 %collective-permute-start.10 = (f32[8,128]{1,0:T(8,128)S(1)}, f32[8,128]{1,0:T(8,128)S(1)}, u32[]{:S(2)}, u32[]{:S(2)}) collective-permute-start(f32[8,128]{1,0:T(8,128)S(1)} %get-tuple-element.46.refs_4_), channel_id=1, source_target_pairs={{0,2},{1,3},{2,0},{3,1},{4,6},{5,7},{6,4},{7,5},{8,10},{9,11},{10,... | collective-permute-start | bytes 12296 | tf_op jit(solution)/shard_map/ppermute | solution.py:332
  24.0 2.1 %collective-permute-start.9 = (f32[8,128]{1,0:T(8,128)S(1)}, f32[8,128]{1,0:T(8,128)S(1)}, u32[]{:S(2)}, u32[]{:S(2)}) collective-permute-start(f32[8,128]{1,0:T(8,128)S(1)} %get-tuple-element.46.refs_4_), channel_id=1, source_target_pairs={{0,1},{1,0},{2,3},{3,2},{4,5},{5,4},{6,7},{7,6},{8,9},{9,8},{10,11... | collective-permute-start | bytes 12296 | tf_op jit(solution)/shard_map/ppermute | solution.py:332
  26.5 8.0 %collective-permute-start.13 = (bf16[144,256]{1,0:T(8,128)(2,1)S(1)}, bf16[144,256]{1,0:T(8,128)(2,1)S(1)}, u32[]{:S(2)}, u32[]{:S(2)}) collective-permute-start(bf16[144,256]{1,0:T(8,128)(2,1)S(1)} %get-tuple-element.53), channel_id=1, source_target_pairs={{0,8},{1,9},{2,10},{3,11},{4,12},{5,13},{6,14},{7,15},{8,0},{9,1},... | collective-permute-start | bytes 221192 | tf_op jit(solution)/shard_map/ppermute | solution.py:399
  26.6 8.0 %collective-permute-start.12 = (bf16[144,256]{1,0:T(8,128)(2,1)S(1)}, bf16[144,256]{1,0:T(8,128)(2,1)S(1)}, u32[]{:S(2)}, u32[]{:S(2)}) collective-permute-start(bf16[144,256]{1,0:T(8,128)(2,1)S(1)} %get-tuple-element.53), channel_id=1, source_target_pairs={{0,4},{1,5},{2,6},{3,7},{4,8},{5,9},{6,10},{7,11},{8,12},{9,13},{1... | collective-permute-start | bytes 221192 | tf_op jit(solution)/shard_map/ppermute | solution.py:399
  28.2 6.4 %collective-permute-start.14 = (bf16[16,256]{1,0:T(8,128)(2,1)S(1)}, bf16[16,256]{1,0:T(8,128)(2,1)S(1)}, u32[]{:S(2)}, u32[]{:S(2)}) collective-permute-start(bf16[16,256]{1,0:T(8,128)(2,1)S(1)} %get-tuple-element.54), channel_id=1, source_target_pairs={{0,12},{1,13},{2,14},{3,15},{4,0},{5,1},{6,2},{7,3},{8,4},{9,5},{1... | collective-permute-start | bytes 24584 | tf_op jit(solution)/shard_map/ppermute | solution.py:399

commit v18 on v15

--- a/solution.py
+++ b/solution.py
@@ -140,15 +140,15 @@
             right_ref[k] = pair(b)
 
     def run(fn, start, count):
-        if count <= 4:
+        if count <= 8:
             fn(list(range(start, start + count)))
             return
 
         def body(i, c):
-            fn([start + 4 * i + k for k in range(4)])
+            fn([start + 8 * i + k for k in range(8)])
             return c
 
-        lax.fori_loop(0, count // 4, body, 0)
+        lax.fori_loop(0, count // 8, body, 0)
 
     copies = []
 

time: 36.4 us -> 36.1 us (level)
  Pallas kernels: 11.8 us -> 11.4 us
    pallas_call x1, Pallas kernels: 3.88 us -> 3.49 us  [shards(): call(functools.partial(tree_kernel, steps), 'tree_of_maps', 8, out_shape=...]
  transfers between devices with their start and end apart: 15 -> 15, of which waited for: 6 -> 6; matrix products, arithmetic and copies ran while one was open for 0% -> 0% of each run, Pallas kernels for 19% -> 18%
where the time goes in v18:
time: 36.1 us; the launch traced here: 35.9 us
  starting transfers between devices  15.3 us (42%)
  Pallas kernels  11.4 us (32%)
  waiting for transfers between devices  9.09 us (25%)
    ppermute x12, starting transfers between devices, swaps(): lax.ppermute(a, 'tm', [(j, j ^ r * step) for j in range(count)])  11.4 us
    ppermute x12, waiting for transfers between devices, swaps(): lax.ppermute(a, 'tm', [(j, j ^ r * step) for j in range(count)])  5.91 us
    ppermute x3, starting transfers between devices, shards(): lax.ppermute(mine if r < groups - 1 else carried, 'tm', [(j, (j + r * siz...  3.95 us
    pallas_call x1, Pallas kernels, shards(): call(functools.partial(tree_kernel, steps), 'tree_of_maps', 8, out_shape=...  3.49 us
    ppermute x3, waiting for transfers between devices, shards(): lax.ppermute(mine if r < groups - 1 else carried, 'tm', [(j, (j + r * siz...  3.18 us
    pallas_call x1, Pallas kernels, shards(): call(local_kernel, 'local_states', 8, 1 << 30, out_shape=[shape((steps, n...  2.94 us
    pallas_call x1, Pallas kernels, shards(): call(functools.partial(final_kernel, size), 'estimates', 6, out_shape=sha...  2.44 us
    pallas_call x1, Pallas kernels, shards(): call(functools.partial(front_kernel, cuts, len(small), size), 'front', 5,...  1.83 us
  transfers between devices with their start and end apart: 15, of which 6 were waited for; matrix products, arithmetic and copies ran while one was open for 0% of the time, Pallas kernels for 18%

profile of v18, /device:TPU:0, one launch (start us, length us, event | category | flops | bytes accessed | tf_op | source)
XLA Modules:
  0.0 35.9 jit_solution(16756510607683936629)
XLA Ops:
  0.0 1.8 %front.1 = (bf16[16,128,256]{2,1,0:T(8,128)(2,1)S(1)}, s32[1,64]{1,0:T(1,128)S(1)}, f32[1,128]{1,0:T(1,128)S(1)}, bf16[128,128]{1,0:T(8,128)(2,1)S(1)}, s32[16,1...) custom-call(s32[1]{0:T(128)} %bitcast.pos_ref, ...), custom_call_target="tpu_custom_call" | custom-call | flops 1 | bytes 1 | tf_op jit(solution)/shard_map/front/pallas_call | solution.py:305
  1.8 0.5 %collective-permute-start.3 = (bf16[4,64,128]{2,1,0:T(8,128)(2,1)S(1)}, bf16[4,64,128]{2,1,0:T(8,128)(2,1)S(1)}, u32[]{:S(2)}, u32[]{:S(2)}) collective-permute-start(bf16[4,64,128]{2,1,0:T(8,128)(2,1)S(1)} %get-tuple-element.37), channel_id=1, source_target_pairs={{0,1},{1,0},{2,3},{3,2},{4,5},{5,4},{6,7},{7,6},{8,9},{9,8},{10,11... | collective-permute-start | bytes 196616 | tf_op jit(solution)/shard_map/ppermute | solution.py:289
  2.4 2.6 %collective-permute-start.4 = (bf16[4,64,128]{2,1,0:T(8,128)(2,1)S(1)}, bf16[4,64,128]{2,1,0:T(8,128)(2,1)S(1)}, u32[]{:S(2)}, u32[]{:S(2)}) collective-permute-start(bf16[4,64,128]{2,1,0:T(8,128)(2,1)S(1)} %get-tuple-element.38), channel_id=1, source_target_pairs={{0,2},{1,3},{2,0},{3,1},{4,6},{5,7},{6,4},{7,5},{8,10},{9,11},{10,... | collective-permute-start | bytes 196616 | tf_op jit(solution)/shard_map/ppermute | solution.py:289
  4.9 0.1 collective-permute-start.5
  5.0 3.5 %tree_of_maps.1 = (bf16[31,128,256]{2,1,0:T(8,128)(2,1)}, bf16[31,128,256]{2,1,0:T(8,128)(2,1)}, bf16[128,256]{1,0:T(8,128)(2,1)S(1)}) custom-call(s32[1,64]{1,0:T(1,128)S(1)} %get-tuple-element.28.levels_ref, bf16[16,128,256]{2,1,0:T(8,128)(2,1)S(1)} %get-tuple-element.30.table_ref), custom_call_target="tpu_custom_call" | custom-call | flops 1 | bytes 1 | tf_op jit(solution)/shard_map/tree_of_maps/pallas_call | solution.py:314
  8.5 0.0 collective-permute-done.3.refs_1_
  8.5 0.0 collective-permute-done.4.refs_2_
  8.5 0.5 %collective-permute-done.5.refs_3_ = bf16[4,64,128]{2,1,0:T(8,128)(2,1)S(1)} collective-permute-done((bf16[4,64,128]{2,1,0:T(8,128)(2,1)S(1)}, bf16[4,64,128]{2,1,0:T(8,128)(2,1)S(1)}, u32[]{:S(2)}, u32[]{:S(2)}) %collective-permute-start.5) | collective-permute-done | bytes 65568 | tf_op jit(solution)/shard_map/ppermute | solution.py:289
  9.0 0.2 project.1
  9.2 1.6 %collective-permute-start.6 = (f32[64,128]{1,0:T(8,128)S(1)}, f32[64,128]{1,0:T(8,128)S(1)}, u32[]{:S(2)}, u32[]{:S(2)}) collective-permute-start(f32[64,128]{1,0:T(8,128)S(1)} %get-tuple-element.41), channel_id=1, source_target_pairs={{0,4},{1,5},{2,6},{3,7},{4,0},{5,1},{6,2},{7,3},{8,12},{9,13},{10,... | collective-permute-start | bytes 98312 | tf_op jit(solution)/shard_map/ppermute | solution.py:289
  10.9 2.6 %collective-permute-start.7 = (f32[64,128]{1,0:T(8,128)S(1)}, f32[64,128]{1,0:T(8,128)S(1)}, u32[]{:S(2)}, u32[]{:S(2)}) collective-permute-start(f32[64,128]{1,0:T(8,128)S(1)} %get-tuple-element.42), channel_id=1, source_target_pairs={{0,8},{1,9},{2,10},{3,11},{4,12},{5,13},{6,14},{7,15},{8,0},{9,1},... | collective-permute-start | bytes 98312 | tf_op jit(solution)/shard_map/ppermute | solution.py:289
  13.5 0.2 collective-permute-start.8
  13.7 0.5 %collective-permute-start.2 = (bf16[128,256]{1,0:T(8,128)(2,1)S(1)}, bf16[128,256]{1,0:T(8,128)(2,1)S(1)}, u32[]{:S(2)}, u32[]{:S(2)}) collective-permute-start(bf16[128,256]{1,0:T(8,128)(2,1)S(1)} %get-tuple-element.31.after_ref.total_ref.refs_0_), channel_id=1, source_target_pairs={{0,3},{1,2},{2,1},{3,0},{4,7},{5,6},{6,5},{7,4},{8,11},{9,10},{10,... | collective-permute-start | bytes 196616 | tf_op jit(solution)/shard_map/ppermute | solution.py:289
  14.1 0.9 %collective-permute-start.1 = (bf16[128,256]{1,0:T(8,128)(2,1)S(1)}, bf16[128,256]{1,0:T(8,128)(2,1)S(1)}, u32[]{:S(2)}, u32[]{:S(2)}) collective-permute-start(bf16[128,256]{1,0:T(8,128)(2,1)S(1)} %get-tuple-element.31.after_ref.total_ref.refs_0_), channel_id=1, source_target_pairs={{0,2},{1,3},{2,0},{3,1},{4,6},{5,7},{6,4},{7,5},{8,10},{9,11},{10,... | collective-permute-start | bytes 196616 | tf_op jit(solution)/shard_map/ppermute | solution.py:289
  15.1 0.0 collective-permute-done.6.refs_1_
  15.1 0.5 %collective-permute-start = (bf16[128,256]{1,0:T(8,128)(2,1)S(1)}, bf16[128,256]{1,0:T(8,128)(2,1)S(1)}, u32[]{:S(2)}, u32[]{:S(2)}) collective-permute-start(bf16[128,256]{1,0:T(8,128)(2,1)S(1)} %get-tuple-element.31.after_ref.total_ref.refs_0_), channel_id=1, source_target_pairs={{0,1},{1,0},{2,3},{3,2},{4,5},{5,4},{6,7},{7,6},{8,9},{9,8},{10,11... | collective-permute-start | bytes 196616 | tf_op jit(solution)/shard_map/ppermute | solution.py:289
  15.5 0.7 %collective-permute-done.7.refs_2_ = f32[64,128]{1,0:T(8,128)S(1)} collective-permute-done((f32[64,128]{1,0:T(8,128)S(1)}, f32[64,128]{1,0:T(8,128)S(1)}, u32[]{:S(2)}, u32[]{:S(2)}) %collective-permute-start.7) | collective-permute-done | bytes 32800 | tf_op jit(solution)/shard_map/ppermute | solution.py:289
  16.3 2.9 %collective-permute-done.8.refs_3_ = f32[64,128]{1,0:T(8,128)S(1)} collective-permute-done((f32[64,128]{1,0:T(8,128)S(1)}, f32[64,128]{1,0:T(8,128)S(1)}, u32[]{:S(2)}, u32[]{:S(2)}) %collective-permute-start.8) | collective-permute-done | bytes 32800 | tf_op jit(solution)/shard_map/ppermute | solution.py:289
  19.2 0.0 copy-start
  19.2 2.9 %local_states.1 = (f32[64,128]{1,0:T(8,128)S(1)}, f32[8,128]{1,0:T(8,128)S(1)}) custom-call(s32[1]{0:T(128)} %bitcast.pos_ref, s32[1,64]{1,0:T(1,128)S(1)} %get-tuple-element.28.levels_ref, bf16[128,128]{1,0:T(8,128)(2,1)S(1)} %get-tuple-element.32.gain_ref, f32[1,128]{1,0:T(1,128)S(1)} %get-tuple-element.29.init_ref, ...), custom_call_target="tpu_custom_call" | custom-call | flops 1073741824 | bytes 1 | tf_op jit(solution)/shard_map/local_states/pallas_call | solution.py:341
  22.1 0.1 collective-permute-start.11
  22.2 1.4 %collective-permute-start.10 = (f32[8,128]{1,0:T(8,128)S(1)}, f32[8,128]{1,0:T(8,128)S(1)}, u32[]{:S(2)}, u32[]{:S(2)}) collective-permute-start(f32[8,128]{1,0:T(8,128)S(1)} %get-tuple-element.44.refs_4_), channel_id=1, source_target_pairs={{0,2},{1,3},{2,0},{3,1},{4,6},{5,7},{6,4},{7,5},{8,10},{9,11},{10,... | collective-permute-start | bytes 12296 | tf_op jit(solution)/shard_map/ppermute | solution.py:289
  23.6 0.0 collective-permute-done.2.refs_3_
  23.6 0.4 %collective-permute-start.9 = (f32[8,128]{1,0:T(8,128)S(1)}, f32[8,128]{1,0:T(8,128)S(1)}, u32[]{:S(2)}, u32[]{:S(2)}) collective-permute-start(f32[8,128]{1,0:T(8,128)S(1)} %get-tuple-element.44.refs_4_), channel_id=1, source_target_pairs={{0,1},{1,0},{2,3},{3,2},{4,5},{5,4},{6,7},{7,6},{8,9},{9,8},{10,11... | collective-permute-start | bytes 12296 | tf_op jit(solution)/shard_map/ppermute | solution.py:289
  24.1 0.0 collective-permute-done.1.refs_2_
  24.1 0.0 collective-permute-done.refs_1_
  24.1 1.2 %collective-permute-done.11.refs_7_ = f32[8,128]{1,0:T(8,128)S(1)} collective-permute-done((f32[8,128]{1,0:T(8,128)S(1)}, f32[8,128]{1,0:T(8,128)S(1)}, u32[]{:S(2)}, u32[]{:S(2)}) %collective-permute-start.11) | collective-permute-done | bytes 4128 | tf_op jit(solution)/shard_map/ppermute | solution.py:289
  25.2 0.7 %collective-permute-done.10.refs_6_ = f32[8,128]{1,0:T(8,128)S(1)} collective-permute-done((f32[8,128]{1,0:T(8,128)S(1)}, f32[8,128]{1,0:T(8,128)S(1)}, u32[]{:S(2)}, u32[]{:S(2)}) %collective-permute-start.10) | collective-permute-done | bytes 4128 | tf_op jit(solution)/shard_map/ppermute | solution.py:289
  25.9 0.0 collective-permute-done.9.refs_5_
  25.9 0.4 %group_maps.1 = (bf16[128,256]{1,0:T(8,128)(2,1)S(1)}, f32[8,128]{1,0:T(8,128)S(1)}, bf16[144,256]{1,0:T(8,128)(2,1)S(1)}, bf16[16,256]{1,0:T(8,128)(2,1)S(1)}) custom-call(s32[1]{0:T(128)} %bitcast.pos_ref, bf16[128,256]{1,0:T(8,128)(2,1)S(1)} %get-tuple-element.31.after_ref.total_ref.refs_0_, bf16[128,256]{1,0:T(8,128)(2,1)S(1)} %collective-permute-done.refs_1_, ...), custom_call_target="tpu_custom_call" | custom-call | flops 1 | bytes 1 | tf_op jit(solution)/shard_map/group_maps/pallas_call | solution.py:348
  26.3 0.1 collective-permute-start.13
  26.4 1.4 %collective-permute-start.12 = (bf16[144,256]{1,0:T(8,128)(2,1)S(1)}, bf16[144,256]{1,0:T(8,128)(2,1)S(1)}, u32[]{:S(2)}, u32[]{:S(2)}) collective-permute-start(bf16[144,256]{1,0:T(8,128)(2,1)S(1)} %get-tuple-element.49), channel_id=1, source_target_pairs={{0,4},{1,5},{2,6},{3,7},{4,8},{5,9},{6,10},{7,11},{8,12},{9,13},{1... | collective-permute-start | bytes 221192 | tf_op jit(solution)/shard_map/ppermute | solution.py:356
  27.8 2.4 %collective-permute-start.14 = (bf16[16,256]{1,0:T(8,128)(2,1)S(1)}, bf16[16,256]{1,0:T(8,128)(2,1)S(1)}, u32[]{:S(2)}, u32[]{:S(2)}) collective-permute-start(bf16[16,256]{1,0:T(8,128)(2,1)S(1)} %get-tuple-element.50), channel_id=1, source_target_pairs={{0,12},{1,13},{2,14},{3,15},{4,0},{5,1},{6,2},{7,3},{8,4},{9,5},{1... | collective-permute-start | bytes 24584 | tf_op jit(solution)/shard_map/ppermute | solution.py:356
  30.3 3.2 %collective-permute-done.14.refs_2_ = bf16[16,256]{1,0:T(8,128)(2,1)S(1)} collective-permute-done((bf16[16,256]{1,0:T(8,128)(2,1)S(1)}, bf16[16,256]{1,0:T(8,128)(2,1)S(1)}, u32[]{:S(2)}, u32[]{:S(2)}) %collective-permute-start.14) | collective-permute-done | bytes 8224 | tf_op jit(solution)/shard_map/ppermute | solution.py:356
  33.5 0.0 collective-permute-done.13.refs_1_
  33.5 0.0 collective-permute-done.12.refs_0_
  33.5 0.0 copy-done
  33.5 2.4 %estimates.1 = f32[64,128]{1,0:T(8,128)} custom-call(s32[1]{0:T(128)} %bitcast.pos_ref, s32[1,64]{1,0:T(1,128)S(1)} %get-tuple-element.28.levels_ref, f32[1,128]{1,0:T(1,128)S(1)} %get-tuple-element.29.init_ref, bf16[128,256]{1,0:T(8,128)(2,1)S(1)} %get-tuple-element.45.prefix_ref, f32[8,128]{1,0:T(8,128)S(1)} %get-tuple-element.46.before_ref, ...), custom_call_target="tpu_custom_call" | custom-call | flops 1 | bytes 1 | tf_op jit(solution)/shard_map/estimates/pallas_call | solution.py:360
Async XLA Ops:
  1.8 6.7 %collective-permute-start.3 = (bf16[4,64,128]{2,1,0:T(8,128)(2,1)S(1)}, bf16[4,64,128]{2,1,0:T(8,128)(2,1)S(1)}, u32[]{:S(2)}, u32[]{:S(2)}) collective-permute-start(bf16[4,64,128]{2,1,0:T(8,128)(2,1)S(1)} %get-tuple-element.37), channel_id=1, source_target_pairs={{0,1},{1,0},{2,3},{3,2},{4,5},{5,4},{6,7},{7,6},{8,9},{9,8},{10,11... | collective-permute-start | bytes 196616 | tf_op jit(solution)/shard_map/ppermute | solution.py:289
  2.4 6.1 %collective-permute-start.4 = (bf16[4,64,128]{2,1,0:T(8,128)(2,1)S(1)}, bf16[4,64,128]{2,1,0:T(8,128)(2,1)S(1)}, u32[]{:S(2)}, u32[]{:S(2)}) collective-permute-start(bf16[4,64,128]{2,1,0:T(8,128)(2,1)S(1)} %get-tuple-element.38), channel_id=1, source_target_pairs={{0,2},{1,3},{2,0},{3,1},{4,6},{5,7},{6,4},{7,5},{8,10},{9,11},{10,... | collective-permute-start | bytes 196616 | tf_op jit(solution)/shard_map/ppermute | solution.py:289
  4.9 4.0 %collective-permute-start.5 = (bf16[4,64,128]{2,1,0:T(8,128)(2,1)S(1)}, bf16[4,64,128]{2,1,0:T(8,128)(2,1)S(1)}, u32[]{:S(2)}, u32[]{:S(2)}) collective-permute-start(bf16[4,64,128]{2,1,0:T(8,128)(2,1)S(1)} %get-tuple-element.39), channel_id=1, source_target_pairs={{0,3},{1,2},{2,1},{3,0},{4,7},{5,6},{6,5},{7,4},{8,11},{9,10},{10,... | collective-permute-start | bytes 196616 | tf_op jit(solution)/shard_map/ppermute | solution.py:289
  9.2 5.8 %collective-permute-start.6 = (f32[64,128]{1,0:T(8,128)S(1)}, f32[64,128]{1,0:T(8,128)S(1)}, u32[]{:S(2)}, u32[]{:S(2)}) collective-permute-start(f32[64,128]{1,0:T(8,128)S(1)} %get-tuple-element.41), channel_id=1, source_target_pairs={{0,4},{1,5},{2,6},{3,7},{4,0},{5,1},{6,2},{7,3},{8,12},{9,13},{10,... | collective-permute-start | bytes 98312 | tf_op jit(solution)/shard_map/ppermute | solution.py:289
  10.9 5.4 %collective-permute-start.7 = (f32[64,128]{1,0:T(8,128)S(1)}, f32[64,128]{1,0:T(8,128)S(1)}, u32[]{:S(2)}, u32[]{:S(2)}) collective-permute-start(f32[64,128]{1,0:T(8,128)S(1)} %get-tuple-element.42), channel_id=1, source_target_pairs={{0,8},{1,9},{2,10},{3,11},{4,12},{5,13},{6,14},{7,15},{8,0},{9,1},... | collective-permute-start | bytes 98312 | tf_op jit(solution)/shard_map/ppermute | solution.py:289
  13.5 5.7 %collective-permute-start.8 = (f32[64,128]{1,0:T(8,128)S(1)}, f32[64,128]{1,0:T(8,128)S(1)}, u32[]{:S(2)}, u32[]{:S(2)}) collective-permute-start(f32[64,128]{1,0:T(8,128)S(1)} %get-tuple-element.43), channel_id=1, source_target_pairs={{0,12},{1,13},{2,14},{3,15},{4,8},{5,9},{6,10},{7,11},{8,4},{9,5},... | collective-permute-start | bytes 98312 | tf_op jit(solution)/shard_map/ppermute | solution.py:289
  13.7 9.9 %collective-permute-start.2 = (bf16[128,256]{1,0:T(8,128)(2,1)S(1)}, bf16[128,256]{1,0:T(8,128)(2,1)S(1)}, u32[]{:S(2)}, u32[]{:S(2)}) collective-permute-start(bf16[128,256]{1,0:T(8,128)(2,1)S(1)} %get-tuple-element.31.after_ref.total_ref.refs_0_), channel_id=1, source_target_pairs={{0,3},{1,2},{2,1},{3,0},{4,7},{5,6},{6,5},{7,4},{8,11},{9,10},{10,... | collective-permute-start | bytes 196616 | tf_op jit(solution)/shard_map/ppermute | solution.py:289
  14.1 9.9 %collective-permute-start.1 = (bf16[128,256]{1,0:T(8,128)(2,1)S(1)}, bf16[128,256]{1,0:T(8,128)(2,1)S(1)}, u32[]{:S(2)}, u32[]{:S(2)}) collective-permute-start(bf16[128,256]{1,0:T(8,128)(2,1)S(1)} %get-tuple-element.31.after_ref.total_ref.refs_0_), channel_id=1, source_target_pairs={{0,2},{1,3},{2,0},{3,1},{4,6},{5,7},{6,4},{7,5},{8,10},{9,11},{10,... | collective-permute-start | bytes 196616 | tf_op jit(solution)/shard_map/ppermute | solution.py:289
  15.1 9.0 %collective-permute-start = (bf16[128,256]{1,0:T(8,128)(2,1)S(1)}, bf16[128,256]{1,0:T(8,128)(2,1)S(1)}, u32[]{:S(2)}, u32[]{:S(2)}) collective-permute-start(bf16[128,256]{1,0:T(8,128)(2,1)S(1)} %get-tuple-element.31.after_ref.total_ref.refs_0_), channel_id=1, source_target_pairs={{0,1},{1,0},{2,3},{3,2},{4,5},{5,4},{6,7},{7,6},{8,9},{9,8},{10,11... | collective-permute-start | bytes 196616 | tf_op jit(solution)/shard_map/ppermute | solution.py:289
  19.2 14.3 %copy-start = (bf16[31,128,256]{2,1,0:T(8,128)(2,1)S(1)}, bf16[31,128,256]{2,1,0:T(8,128)(2,1)}, u32[]{:S(2)}) copy-start(bf16[31,128,256]{2,1,0:T(8,128)(2,1)} %get-tuple-element.48.left_ref) | copy-start | bytes 6094852
  22.1 3.1 %collective-permute-start.11 = (f32[8,128]{1,0:T(8,128)S(1)}, f32[8,128]{1,0:T(8,128)S(1)}, u32[]{:S(2)}, u32[]{:S(2)}) collective-permute-start(f32[8,128]{1,0:T(8,128)S(1)} %get-tuple-element.44.refs_4_), channel_id=1, source_target_pairs={{0,3},{1,2},{2,1},{3,0},{4,7},{5,6},{6,5},{7,4},{8,11},{9,10},{10,... | collective-permute-start | bytes 12296 | tf_op jit(solution)/shard_map/ppermute | solution.py:289
  22.2 3.7 %collective-permute-start.10 = (f32[8,128]{1,0:T(8,128)S(1)}, f32[8,128]{1,0:T(8,128)S(1)}, u32[]{:S(2)}, u32[]{:S(2)}) collective-permute-start(f32[8,128]{1,0:T(8,128)S(1)} %get-tuple-element.44.refs_4_), channel_id=1, source_target_pairs={{0,2},{1,3},{2,0},{3,1},{4,6},{5,7},{6,4},{7,5},{8,10},{9,11},{10,... | collective-permute-start | bytes 12296 | tf_op jit(solution)/shard_map/ppermute | solution.py:289
  23.6 2.3 %collective-permute-start.9 = (f32[8,128]{1,0:T(8,128)S(1)}, f32[8,128]{1,0:T(8,128)S(1)}, u32[]{:S(2)}, u32[]{:S(2)}) collective-permute-start(f32[8,128]{1,0:T(8,128)S(1)} %get-tuple-element.44.refs_4_), channel_id=1, source_target_pairs={{0,1},{1,0},{2,3},{3,2},{4,5},{5,4},{6,7},{7,6},{8,9},{9,8},{10,11... | collective-permute-start | bytes 12296 | tf_op jit(solution)/shard_map/ppermute | solution.py:289
  26.3 7.1 %collective-permute-start.13 = (bf16[144,256]{1,0:T(8,128)(2,1)S(1)}, bf16[144,256]{1,0:T(8,128)(2,1)S(1)}, u32[]{:S(2)}, u32[]{:S(2)}) collective-permute-start(bf16[144,256]{1,0:T(8,128)(2,1)S(1)} %get-tuple-element.49), channel_id=1, source_target_pairs={{0,8},{1,9},{2,10},{3,11},{4,12},{5,13},{6,14},{7,15},{8,0},{9,1},... | collective-permute-start | bytes 221192 | tf_op jit(solution)/shard_map/ppermute | solution.py:356
  26.4 7.1 %collective-permute-start.12 = (bf16[144,256]{1,0:T(8,128)(2,1)S(1)}, bf16[144,256]{1,0:T(8,128)(2,1)S(1)}, u32[]{:S(2)}, u32[]{:S(2)}) collective-permute-start(bf16[144,256]{1,0:T(8,128)(2,1)S(1)} %get-tuple-element.49), channel_id=1, source_target_pairs={{0,4},{1,5},{2,6},{3,7},{4,8},{5,9},{6,10},{7,11},{8,12},{9,13},{1... | collective-permute-start | bytes 221192 | tf_op jit(solution)/shard_map/ppermute | solution.py:356
  27.8 5.6 %collective-permute-start.14 = (bf16[16,256]{1,0:T(8,128)(2,1)S(1)}, bf16[16,256]{1,0:T(8,128)(2,1)S(1)}, u32[]{:S(2)}, u32[]{:S(2)}) collective-permute-start(bf16[16,256]{1,0:T(8,128)(2,1)S(1)} %get-tuple-element.50), channel_id=1, source_target_pairs={{0,12},{1,13},{2,14},{3,15},{4,0},{5,1},{6,2},{7,3},{8,4},{9,5},{1... | collective-permute-start | bytes 24584 | tf_op jit(solution)/shard_map/ppermute | solution.py:356

commit v19 on v18

--- a/solution.py
+++ b/solution.py
@@ -328,7 +328,7 @@
             out_specs=[VMEM] * groups,
             scratch_shapes=[pltpu.VMEM((groups, steps, n), F32), pltpu.VMEM((count, pixels), F32)],
         )(position, total, mode, weight, slab, *swaps(slabs, 1, size))
-        parts = [first] + swaps(parts, size, groups)
+        parts = [first] + swaps(parts, size, groups)[::-1]
     else:
         x = lax.all_to_all(frames, "tm", split_axis=1, concat_axis=0, tiled=True)
         channels = jnp.arange(n, dtype=jnp.int32)

time: 36.1 us -> 35.9 us (level)
  waiting for transfers between devices: 9.09 us -> 7.12 us
  starting transfers between devices: 15.3 us -> 17.2 us
    ppermute x3, starting transfers between devices: 3.95 us -> 5.77 us  [shards(): lax.ppermute(mine if r < groups - 1 else carried, 'tm', [(j, (j + r * siz...]
    ppermute x12, waiting for transfers between devices: 5.91 us -> 4.59 us  [swaps(): lax.ppermute(a, 'tm', [(j, j ^ r * step) for j in range(count)])]
    ppermute x3, waiting for transfers between devices: 3.18 us -> 2.53 us  [shards(): lax.ppermute(mine if r < groups - 1 else carried, 'tm', [(j, (j + r * siz...]
where the time goes in v19:
time: 35.9 us; the launch traced here: 35.8 us
  starting transfers between devices  17.2 us (48%)
  Pallas kernels  11.4 us (32%)
  waiting for transfers between devices  7.12 us (20%)
    ppermute x12, starting transfers between devices, swaps(): lax.ppermute(a, 'tm', [(j, j ^ r * step) for j in range(count)])  11.4 us
    ppermute x3, starting transfers between devices, shards(): lax.ppermute(mine if r < groups - 1 else carried, 'tm', [(j, (j + r * siz...  5.77 us
    ppermute x12, waiting for transfers between devices, swaps(): lax.ppermute(a, 'tm', [(j, j ^ r * step) for j in range(count)])  4.59 us
    pallas_call x1, Pallas kernels, shards(): call(functools.partial(tree_kernel, steps), 'tree_of_maps', 8, out_shape=...  3.49 us
    pallas_call x1, Pallas kernels, shards(): call(local_kernel, 'local_states', 8, 1 << 30, out_shape=[shape((steps, n...  2.95 us
    ppermute x3, waiting for transfers between devices, shards(): lax.ppermute(mine if r < groups - 1 else carried, 'tm', [(j, (j + r * siz...  2.53 us
    pallas_call x1, Pallas kernels, shards(): call(functools.partial(final_kernel, size), 'estimates', 6, out_shape=sha...  2.44 us
    pallas_call x1, Pallas kernels, shards(): call(functools.partial(front_kernel, cuts, len(small), size), 'front', 5,...  1.83 us
  transfers between devices with their start and end apart: 15, of which 6 were waited for; matrix products, arithmetic and copies ran while one was open for 0% of the time, Pallas kernels for 18%

profile of v19, /device:TPU:0, one launch (start us, length us, event | category | flops | bytes accessed | tf_op | source)
XLA Modules:
  0.0 35.8 jit_solution(1933457293368540894)
XLA Ops:
  0.0 1.8 %front.1 = (bf16[16,128,256]{2,1,0:T(8,128)(2,1)S(1)}, s32[1,64]{1,0:T(1,128)S(1)}, f32[1,128]{1,0:T(1,128)S(1)}, bf16[128,128]{1,0:T(8,128)(2,1)S(1)}, s32[16,1...) custom-call(s32[1]{0:T(128)} %bitcast.pos_ref, ...), custom_call_target="tpu_custom_call" | custom-call | flops 1 | bytes 1 | tf_op jit(solution)/shard_map/front/pallas_call | solution.py:305
  1.8 0.5 %collective-permute-start.3 = (bf16[4,64,128]{2,1,0:T(8,128)(2,1)S(1)}, bf16[4,64,128]{2,1,0:T(8,128)(2,1)S(1)}, u32[]{:S(2)}, u32[]{:S(2)}) collective-permute-start(bf16[4,64,128]{2,1,0:T(8,128)(2,1)S(1)} %get-tuple-element.37), channel_id=1, source_target_pairs={{0,1},{1,0},{2,3},{3,2},{4,5},{5,4},{6,7},{7,6},{8,9},{9,8},{10,11... | collective-permute-start | bytes 196616 | tf_op jit(solution)/shard_map/ppermute | solution.py:289
  2.4 2.6 %collective-permute-start.4 = (bf16[4,64,128]{2,1,0:T(8,128)(2,1)S(1)}, bf16[4,64,128]{2,1,0:T(8,128)(2,1)S(1)}, u32[]{:S(2)}, u32[]{:S(2)}) collective-permute-start(bf16[4,64,128]{2,1,0:T(8,128)(2,1)S(1)} %get-tuple-element.38), channel_id=1, source_target_pairs={{0,2},{1,3},{2,0},{3,1},{4,6},{5,7},{6,4},{7,5},{8,10},{9,11},{10,... | collective-permute-start | bytes 196616 | tf_op jit(solution)/shard_map/ppermute | solution.py:289
  4.9 0.1 collective-permute-start.5
  5.0 3.5 %tree_of_maps.1 = (bf16[31,128,256]{2,1,0:T(8,128)(2,1)}, bf16[31,128,256]{2,1,0:T(8,128)(2,1)}, bf16[128,256]{1,0:T(8,128)(2,1)S(1)}) custom-call(s32[1,64]{1,0:T(1,128)S(1)} %get-tuple-element.28.levels_ref, bf16[16,128,256]{2,1,0:T(8,128)(2,1)S(1)} %get-tuple-element.30.table_ref), custom_call_target="tpu_custom_call" | custom-call | flops 1 | bytes 1 | tf_op jit(solution)/shard_map/tree_of_maps/pallas_call | solution.py:314
  8.5 0.0 collective-permute-done.3.refs_1_
  8.5 0.0 collective-permute-done.4.refs_2_
  8.5 0.5 %collective-permute-done.5.refs_3_ = bf16[4,64,128]{2,1,0:T(8,128)(2,1)S(1)} collective-permute-done((bf16[4,64,128]{2,1,0:T(8,128)(2,1)S(1)}, bf16[4,64,128]{2,1,0:T(8,128)(2,1)S(1)}, u32[]{:S(2)}, u32[]{:S(2)}) %collective-permute-start.5) | collective-permute-done | bytes 65568 | tf_op jit(solution)/shard_map/ppermute | solution.py:289
  9.0 0.2 project.1
  9.2 3.7 %collective-permute-start.6 = (f32[64,128]{1,0:T(8,128)S(1)}, f32[64,128]{1,0:T(8,128)S(1)}, u32[]{:S(2)}, u32[]{:S(2)}) collective-permute-start(f32[64,128]{1,0:T(8,128)S(1)} %get-tuple-element.41), channel_id=1, source_target_pairs={{0,12},{1,13},{2,14},{3,15},{4,8},{5,9},{6,10},{7,11},{8,4},{9,5},... | collective-permute-start | bytes 98312 | tf_op jit(solution)/shard_map/ppermute | solution.py:289
  12.9 0.0 collective-permute-start.7
  12.9 0.8 %collective-permute-start.8 = (f32[64,128]{1,0:T(8,128)S(1)}, f32[64,128]{1,0:T(8,128)S(1)}, u32[]{:S(2)}, u32[]{:S(2)}) collective-permute-start(f32[64,128]{1,0:T(8,128)S(1)} %get-tuple-element.43), channel_id=1, source_target_pairs={{0,4},{1,5},{2,6},{3,7},{4,0},{5,1},{6,2},{7,3},{8,12},{9,13},{10,... | collective-permute-start | bytes 98312 | tf_op jit(solution)/shard_map/ppermute | solution.py:289
  13.7 0.5 %collective-permute-start.2 = (bf16[128,256]{1,0:T(8,128)(2,1)S(1)}, bf16[128,256]{1,0:T(8,128)(2,1)S(1)}, u32[]{:S(2)}, u32[]{:S(2)}) collective-permute-start(bf16[128,256]{1,0:T(8,128)(2,1)S(1)} %get-tuple-element.31.after_ref.total_ref.refs_0_), channel_id=1, source_target_pairs={{0,3},{1,2},{2,1},{3,0},{4,7},{5,6},{6,5},{7,4},{8,11},{9,10},{10,... | collective-permute-start | bytes 196616 | tf_op jit(solution)/shard_map/ppermute | solution.py:289
  14.2 0.8 %collective-permute-start.1 = (bf16[128,256]{1,0:T(8,128)(2,1)S(1)}, bf16[128,256]{1,0:T(8,128)(2,1)S(1)}, u32[]{:S(2)}, u32[]{:S(2)}) collective-permute-start(bf16[128,256]{1,0:T(8,128)(2,1)S(1)} %get-tuple-element.31.after_ref.total_ref.refs_0_), channel_id=1, source_target_pairs={{0,2},{1,3},{2,0},{3,1},{4,6},{5,7},{6,4},{7,5},{8,10},{9,11},{10,... | collective-permute-start | bytes 196616 | tf_op jit(solution)/shard_map/ppermute | solution.py:289
  15.1 0.0 collective-permute-done.6.refs_1_
  15.1 0.5 %collective-permute-start = (bf16[128,256]{1,0:T(8,128)(2,1)S(1)}, bf16[128,256]{1,0:T(8,128)(2,1)S(1)}, u32[]{:S(2)}, u32[]{:S(2)}) collective-permute-start(bf16[128,256]{1,0:T(8,128)(2,1)S(1)} %get-tuple-element.31.after_ref.total_ref.refs_0_), channel_id=1, source_target_pairs={{0,1},{1,0},{2,3},{3,2},{4,5},{5,4},{6,7},{7,6},{8,9},{9,8},{10,11... | collective-permute-start | bytes 196616 | tf_op jit(solution)/shard_map/ppermute | solution.py:289
  15.5 2.2 %collective-permute-done.7.refs_2_ = f32[64,128]{1,0:T(8,128)S(1)} collective-permute-done((f32[64,128]{1,0:T(8,128)S(1)}, f32[64,128]{1,0:T(8,128)S(1)}, u32[]{:S(2)}, u32[]{:S(2)}) %collective-permute-start.7) | collective-permute-done | bytes 32800 | tf_op jit(solution)/shard_map/ppermute | solution.py:289
  17.7 0.0 collective-permute-done.8.refs_3_
  17.7 0.0 copy-start
  17.7 2.9 %local_states.1 = (f32[64,128]{1,0:T(8,128)S(1)}, f32[8,128]{1,0:T(8,128)S(1)}) custom-call(s32[1]{0:T(128)} %bitcast.pos_ref, s32[1,64]{1,0:T(1,128)S(1)} %get-tuple-element.28.levels_ref, bf16[128,128]{1,0:T(8,128)(2,1)S(1)} %get-tuple-element.32.gain_ref, f32[1,128]{1,0:T(1,128)S(1)} %get-tuple-element.29.init_ref, ...), custom_call_target="tpu_custom_call" | custom-call | flops 1073741824 | bytes 1 | tf_op jit(solution)/shard_map/local_states/pallas_call | solution.py:341
  20.7 0.3 collective-permute-start.11
  20.9 1.2 %collective-permute-start.10 = (f32[8,128]{1,0:T(8,128)S(1)}, f32[8,128]{1,0:T(8,128)S(1)}, u32[]{:S(2)}, u32[]{:S(2)}) collective-permute-start(f32[8,128]{1,0:T(8,128)S(1)} %get-tuple-element.44.refs_4_), channel_id=1, source_target_pairs={{0,2},{1,3},{2,0},{3,1},{4,6},{5,7},{6,4},{7,5},{8,10},{9,11},{10,... | collective-permute-start | bytes 12296 | tf_op jit(solution)/shard_map/ppermute | solution.py:289
  22.2 0.0 collective-permute-done.2.refs_3_
  22.2 0.4 %collective-permute-start.9 = (f32[8,128]{1,0:T(8,128)S(1)}, f32[8,128]{1,0:T(8,128)S(1)}, u32[]{:S(2)}, u32[]{:S(2)}) collective-permute-start(f32[8,128]{1,0:T(8,128)S(1)} %get-tuple-element.44.refs_4_), channel_id=1, source_target_pairs={{0,1},{1,0},{2,3},{3,2},{4,5},{5,4},{6,7},{7,6},{8,9},{9,8},{10,11... | collective-permute-start | bytes 12296 | tf_op jit(solution)/shard_map/ppermute | solution.py:289
  22.6 0.0 collective-permute-done.1.refs_2_
  22.6 0.0 collective-permute-done.refs_1_
  22.6 1.2 %collective-permute-done.11.refs_7_ = f32[8,128]{1,0:T(8,128)S(1)} collective-permute-done((f32[8,128]{1,0:T(8,128)S(1)}, f32[8,128]{1,0:T(8,128)S(1)}, u32[]{:S(2)}, u32[]{:S(2)}) %collective-permute-start.11) | collective-permute-done | bytes 4128 | tf_op jit(solution)/shard_map/ppermute | solution.py:289
  23.8 0.8 %collective-permute-done.10.refs_6_ = f32[8,128]{1,0:T(8,128)S(1)} collective-permute-done((f32[8,128]{1,0:T(8,128)S(1)}, f32[8,128]{1,0:T(8,128)S(1)}, u32[]{:S(2)}, u32[]{:S(2)}) %collective-permute-start.10) | collective-permute-done | bytes 4128 | tf_op jit(solution)/shard_map/ppermute | solution.py:289
  24.6 0.0 collective-permute-done.9.refs_5_
  24.6 0.4 %group_maps.1 = (bf16[128,256]{1,0:T(8,128)(2,1)S(1)}, f32[8,128]{1,0:T(8,128)S(1)}, bf16[144,256]{1,0:T(8,128)(2,1)S(1)}, bf16[16,256]{1,0:T(8,128)(2,1)S(1)}) custom-call(s32[1]{0:T(128)} %bitcast.pos_ref, bf16[128,256]{1,0:T(8,128)(2,1)S(1)} %get-tuple-element.31.after_ref.total_ref.refs_0_, bf16[128,256]{1,0:T(8,128)(2,1)S(1)} %collective-permute-done.refs_1_, ...), custom_call_target="tpu_custom_call" | custom-call | flops 1 | bytes 1 | tf_op jit(solution)/shard_map/group_maps/pallas_call | solution.py:348
  25.0 2.0 %collective-permute-start.13 = (bf16[144,256]{1,0:T(8,128)(2,1)S(1)}, bf16[144,256]{1,0:T(8,128)(2,1)S(1)}, u32[]{:S(2)}, u32[]{:S(2)}) collective-permute-start(bf16[144,256]{1,0:T(8,128)(2,1)S(1)} %get-tuple-element.49), channel_id=1, source_target_pairs={{0,8},{1,9},{2,10},{3,11},{4,12},{5,13},{6,14},{7,15},{8,0},{9,1},... | collective-permute-start | bytes 221192 | tf_op jit(solution)/shard_map/ppermute | solution.py:356
  27.0 1.2 %collective-permute-start.12 = (bf16[144,256]{1,0:T(8,128)(2,1)S(1)}, bf16[144,256]{1,0:T(8,128)(2,1)S(1)}, u32[]{:S(2)}, u32[]{:S(2)}) collective-permute-start(bf16[144,256]{1,0:T(8,128)(2,1)S(1)} %get-tuple-element.49), channel_id=1, source_target_pairs={{0,4},{1,5},{2,6},{3,7},{4,8},{5,9},{6,10},{7,11},{8,12},{9,13},{1... | collective-permute-start | bytes 221192 | tf_op jit(solution)/shard_map/ppermute | solution.py:356
  28.1 2.6 %collective-permute-start.14 = (bf16[16,256]{1,0:T(8,128)(2,1)S(1)}, bf16[16,256]{1,0:T(8,128)(2,1)S(1)}, u32[]{:S(2)}, u32[]{:S(2)}) collective-permute-start(bf16[16,256]{1,0:T(8,128)(2,1)S(1)} %get-tuple-element.50), channel_id=1, source_target_pairs={{0,12},{1,13},{2,14},{3,15},{4,0},{5,1},{6,2},{7,3},{8,4},{9,5},{1... | collective-permute-start | bytes 24584 | tf_op jit(solution)/shard_map/ppermute | solution.py:356
  30.8 1.8 %collective-permute-done.14.refs_2_ = bf16[16,256]{1,0:T(8,128)(2,1)S(1)} collective-permute-done((bf16[16,256]{1,0:T(8,128)(2,1)S(1)}, bf16[16,256]{1,0:T(8,128)(2,1)S(1)}, u32[]{:S(2)}, u32[]{:S(2)}) %collective-permute-start.14) | collective-permute-done | bytes 8224 | tf_op jit(solution)/shard_map/ppermute | solution.py:356
  32.6 0.7 %collective-permute-done.13.refs_1_ = bf16[144,256]{1,0:T(8,128)(2,1)S(1)} collective-permute-done((bf16[144,256]{1,0:T(8,128)(2,1)S(1)}, bf16[144,256]{1,0:T(8,128)(2,1)S(1)}, u32[]{:S(2)}, u32[]{:S(2)}) %collective-permute-start.13) | collective-permute-done | bytes 73760 | tf_op jit(solution)/shard_map/ppermute | solution.py:356
  33.3 0.0 collective-permute-done.12.refs_0_
  33.3 0.0 copy-done
  33.3 2.4 %estimates.1 = f32[64,128]{1,0:T(8,128)} custom-call(s32[1]{0:T(128)} %bitcast.pos_ref, s32[1,64]{1,0:T(1,128)S(1)} %get-tuple-element.28.levels_ref, f32[1,128]{1,0:T(1,128)S(1)} %get-tuple-element.29.init_ref, bf16[128,256]{1,0:T(8,128)(2,1)S(1)} %get-tuple-element.45.prefix_ref, f32[8,128]{1,0:T(8,128)S(1)} %get-tuple-element.46.before_ref, ...), custom_call_target="tpu_custom_call" | custom-call | flops 1 | bytes 1 | tf_op jit(solution)/shard_map/estimates/pallas_call | solution.py:360
Async XLA Ops:
  1.8 6.7 %collective-permute-start.3 = (bf16[4,64,128]{2,1,0:T(8,128)(2,1)S(1)}, bf16[4,64,128]{2,1,0:T(8,128)(2,1)S(1)}, u32[]{:S(2)}, u32[]{:S(2)}) collective-permute-start(bf16[4,64,128]{2,1,0:T(8,128)(2,1)S(1)} %get-tuple-element.37), channel_id=1, source_target_pairs={{0,1},{1,0},{2,3},{3,2},{4,5},{5,4},{6,7},{7,6},{8,9},{9,8},{10,11... | collective-permute-start | bytes 196616 | tf_op jit(solution)/shard_map/ppermute | solution.py:289
  2.4 6.1 %collective-permute-start.4 = (bf16[4,64,128]{2,1,0:T(8,128)(2,1)S(1)}, bf16[4,64,128]{2,1,0:T(8,128)(2,1)S(1)}, u32[]{:S(2)}, u32[]{:S(2)}) collective-permute-start(bf16[4,64,128]{2,1,0:T(8,128)(2,1)S(1)} %get-tuple-element.38), channel_id=1, source_target_pairs={{0,2},{1,3},{2,0},{3,1},{4,6},{5,7},{6,4},{7,5},{8,10},{9,11},{10,... | collective-permute-start | bytes 196616 | tf_op jit(solution)/shard_map/ppermute | solution.py:289
  4.9 4.0 %collective-permute-start.5 = (bf16[4,64,128]{2,1,0:T(8,128)(2,1)S(1)}, bf16[4,64,128]{2,1,0:T(8,128)(2,1)S(1)}, u32[]{:S(2)}, u32[]{:S(2)}) collective-permute-start(bf16[4,64,128]{2,1,0:T(8,128)(2,1)S(1)} %get-tuple-element.39), channel_id=1, source_target_pairs={{0,3},{1,2},{2,1},{3,0},{4,7},{5,6},{6,5},{7,4},{8,11},{9,10},{10,... | collective-permute-start | bytes 196616 | tf_op jit(solution)/shard_map/ppermute | solution.py:289
  9.2 5.8 %collective-permute-start.6 = (f32[64,128]{1,0:T(8,128)S(1)}, f32[64,128]{1,0:T(8,128)S(1)}, u32[]{:S(2)}, u32[]{:S(2)}) collective-permute-start(f32[64,128]{1,0:T(8,128)S(1)} %get-tuple-element.41), channel_id=1, source_target_pairs={{0,12},{1,13},{2,14},{3,15},{4,8},{5,9},{6,10},{7,11},{8,4},{9,5},... | collective-permute-start | bytes 98312 | tf_op jit(solution)/shard_map/ppermute | solution.py:289
  12.9 4.8 %collective-permute-start.7 = (f32[64,128]{1,0:T(8,128)S(1)}, f32[64,128]{1,0:T(8,128)S(1)}, u32[]{:S(2)}, u32[]{:S(2)}) collective-permute-start(f32[64,128]{1,0:T(8,128)S(1)} %get-tuple-element.42), channel_id=1, source_target_pairs={{0,8},{1,9},{2,10},{3,11},{4,12},{5,13},{6,14},{7,15},{8,0},{9,1},... | collective-permute-start | bytes 98312 | tf_op jit(solution)/shard_map/ppermute | solution.py:289
  12.9 4.8 %collective-permute-start.8 = (f32[64,128]{1,0:T(8,128)S(1)}, f32[64,128]{1,0:T(8,128)S(1)}, u32[]{:S(2)}, u32[]{:S(2)}) collective-permute-start(f32[64,128]{1,0:T(8,128)S(1)} %get-tuple-element.43), channel_id=1, source_target_pairs={{0,4},{1,5},{2,6},{3,7},{4,0},{5,1},{6,2},{7,3},{8,12},{9,13},{10,... | collective-permute-start | bytes 98312 | tf_op jit(solution)/shard_map/ppermute | solution.py:289
  13.7 8.5 %collective-permute-start.2 = (bf16[128,256]{1,0:T(8,128)(2,1)S(1)}, bf16[128,256]{1,0:T(8,128)(2,1)S(1)}, u32[]{:S(2)}, u32[]{:S(2)}) collective-permute-start(bf16[128,256]{1,0:T(8,128)(2,1)S(1)} %get-tuple-element.31.after_ref.total_ref.refs_0_), channel_id=1, source_target_pairs={{0,3},{1,2},{2,1},{3,0},{4,7},{5,6},{6,5},{7,4},{8,11},{9,10},{10,... | collective-permute-start | bytes 196616 | tf_op jit(solution)/shard_map/ppermute | solution.py:289
  14.2 8.4 %collective-permute-start.1 = (bf16[128,256]{1,0:T(8,128)(2,1)S(1)}, bf16[128,256]{1,0:T(8,128)(2,1)S(1)}, u32[]{:S(2)}, u32[]{:S(2)}) collective-permute-start(bf16[128,256]{1,0:T(8,128)(2,1)S(1)} %get-tuple-element.31.after_ref.total_ref.refs_0_), channel_id=1, source_target_pairs={{0,2},{1,3},{2,0},{3,1},{4,6},{5,7},{6,4},{7,5},{8,10},{9,11},{10,... | collective-permute-start | bytes 196616 | tf_op jit(solution)/shard_map/ppermute | solution.py:289
  15.1 7.5 %collective-permute-start = (bf16[128,256]{1,0:T(8,128)(2,1)S(1)}, bf16[128,256]{1,0:T(8,128)(2,1)S(1)}, u32[]{:S(2)}, u32[]{:S(2)}) collective-permute-start(bf16[128,256]{1,0:T(8,128)(2,1)S(1)} %get-tuple-element.31.after_ref.total_ref.refs_0_), channel_id=1, source_target_pairs={{0,1},{1,0},{2,3},{3,2},{4,5},{5,4},{6,7},{7,6},{8,9},{9,8},{10,11... | collective-permute-start | bytes 196616 | tf_op jit(solution)/shard_map/ppermute | solution.py:289
  17.7 15.6 %copy-start = (bf16[31,128,256]{2,1,0:T(8,128)(2,1)S(1)}, bf16[31,128,256]{2,1,0:T(8,128)(2,1)}, u32[]{:S(2)}) copy-start(bf16[31,128,256]{2,1,0:T(8,128)(2,1)} %get-tuple-element.48.left_ref) | copy-start | bytes 6094852
  20.7 3.1 %collective-permute-start.11 = (f32[8,128]{1,0:T(8,128)S(1)}, f32[8,128]{1,0:T(8,128)S(1)}, u32[]{:S(2)}, u32[]{:S(2)}) collective-permute-start(f32[8,128]{1,0:T(8,128)S(1)} %get-tuple-element.44.refs_4_), channel_id=1, source_target_pairs={{0,3},{1,2},{2,1},{3,0},{4,7},{5,6},{6,5},{7,4},{8,11},{9,10},{10,... | collective-permute-start | bytes 12296 | tf_op jit(solution)/shard_map/ppermute | solution.py:289
  20.9 3.6 %collective-permute-start.10 = (f32[8,128]{1,0:T(8,128)S(1)}, f32[8,128]{1,0:T(8,128)S(1)}, u32[]{:S(2)}, u32[]{:S(2)}) collective-permute-start(f32[8,128]{1,0:T(8,128)S(1)} %get-tuple-element.44.refs_4_), channel_id=1, source_target_pairs={{0,2},{1,3},{2,0},{3,1},{4,6},{5,7},{6,4},{7,5},{8,10},{9,11},{10,... | collective-permute-start | bytes 12296 | tf_op jit(solution)/shard_map/ppermute | solution.py:289
  22.2 2.4 %collective-permute-start.9 = (f32[8,128]{1,0:T(8,128)S(1)}, f32[8,128]{1,0:T(8,128)S(1)}, u32[]{:S(2)}, u32[]{:S(2)}) collective-permute-start(f32[8,128]{1,0:T(8,128)S(1)} %get-tuple-element.44.refs_4_), channel_id=1, source_target_pairs={{0,1},{1,0},{2,3},{3,2},{4,5},{5,4},{6,7},{7,6},{8,9},{9,8},{10,11... | collective-permute-start | bytes 12296 | tf_op jit(solution)/shard_map/ppermute | solution.py:289
  25.0 8.3 %collective-permute-start.13 = (bf16[144,256]{1,0:T(8,128)(2,1)S(1)}, bf16[144,256]{1,0:T(8,128)(2,1)S(1)}, u32[]{:S(2)}, u32[]{:S(2)}) collective-permute-start(bf16[144,256]{1,0:T(8,128)(2,1)S(1)} %get-tuple-element.49), channel_id=1, source_target_pairs={{0,8},{1,9},{2,10},{3,11},{4,12},{5,13},{6,14},{7,15},{8,0},{9,1},... | collective-permute-start | bytes 221192 | tf_op jit(solution)/shard_map/ppermute | solution.py:356
  27.0 6.4 %collective-permute-start.12 = (bf16[144,256]{1,0:T(8,128)(2,1)S(1)}, bf16[144,256]{1,0:T(8,128)(2,1)S(1)}, u32[]{:S(2)}, u32[]{:S(2)}) collective-permute-start(bf16[144,256]{1,0:T(8,128)(2,1)S(1)} %get-tuple-element.49), channel_id=1, source_target_pairs={{0,4},{1,5},{2,6},{3,7},{4,8},{5,9},{6,10},{7,11},{8,12},{9,13},{1... | collective-permute-start | bytes 221192 | tf_op jit(solution)/shard_map/ppermute | solution.py:356
  28.1 4.5 %collective-permute-start.14 = (bf16[16,256]{1,0:T(8,128)(2,1)S(1)}, bf16[16,256]{1,0:T(8,128)(2,1)S(1)}, u32[]{:S(2)}, u32[]{:S(2)}) collective-permute-start(bf16[16,256]{1,0:T(8,128)(2,1)S(1)} %get-tuple-element.50), channel_id=1, source_target_pairs={{0,12},{1,13},{2,14},{3,15},{4,0},{5,1},{6,2},{7,3},{8,4},{9,5},{1... | collective-permute-start | bytes 24584 | tf_op jit(solution)/shard_map/ppermute | solution.py:356

commit v20 on v18

--- a/solution.py
+++ b/solution.py
@@ -102,6 +102,7 @@
 
 def project_kernel(size, pos_ref, after_ref, mode_ref, weight_ref, *refs):
     slabs, outs, (sums, weights) = refs[:size], refs[size:-2], refs[-2:]
+    slabs = slabs[:1] + slabs[:0:-1]
     weights[...] = weight_ref[...].astype(F32)
     groups, steps, width = slabs[0].shape
     n = sums.shape[2]
@@ -327,7 +328,7 @@
             in_specs=[SMEM] + [VMEM] * (3 + size),
             out_specs=[VMEM] * groups,
             scratch_shapes=[pltpu.VMEM((groups, steps, n), F32), pltpu.VMEM((count, pixels), F32)],
-        )(position, total, mode, weight, slab, *swaps(slabs, 1, size))
+        )(position, total, mode, weight, slab, *swaps(slabs, 1, size)[::-1])
         parts = [first] + swaps(parts, size, groups)
     else:
         x = lax.all_to_all(frames, "tm", split_axis=1, concat_axis=0, tiled=True)

time: 36.1 us -> 36.4 us (level)
  no operation moved by 1% of the time
where the time goes in v20:
time: 36.4 us; the launch traced here: 36.2 us
  starting transfers between devices  15.3 us (42%)
  Pallas kernels  11.4 us (31%)
  waiting for transfers between devices  9.44 us (26%)
    ppermute x12, starting transfers between devices, swaps(): lax.ppermute(a, 'tm', [(j, j ^ r * step) for j in range(count)])  11.4 us
    ppermute x12, waiting for transfers between devices, swaps(): lax.ppermute(a, 'tm', [(j, j ^ r * step) for j in range(count)])  6.13 us
    ppermute x3, starting transfers between devices, shards(): lax.ppermute(mine if r < groups - 1 else carried, 'tm', [(j, (j + r * siz...  3.96 us
    pallas_call x1, Pallas kernels, shards(): call(functools.partial(tree_kernel, steps), 'tree_of_maps', 8, out_shape=...  3.49 us
    ppermute x3, waiting for transfers between devices, shards(): lax.ppermute(mine if r < groups - 1 else carried, 'tm', [(j, (j + r * siz...  3.3 us
    pallas_call x1, Pallas kernels, shards(): call(local_kernel, 'local_states', 8, 1 << 30, out_shape=[shape((steps, n...  2.94 us
    pallas_call x1, Pallas kernels, shards(): call(functools.partial(final_kernel, size), 'estimates', 6, out_shape=sha...  2.44 us
    pallas_call x1, Pallas kernels, shards(): call(functools.partial(front_kernel, cuts, len(small), size), 'front', 5,...  1.83 us
  transfers between devices with their start and end apart: 15, of which 6 were waited for; matrix products, arithmetic and copies ran while one was open for 0% of the time, Pallas kernels for 18%

profile of v20, /device:TPU:0, one launch (start us, length us, event | category | flops | bytes accessed | tf_op | source)
XLA Modules:
  0.0 36.2 jit_solution(16026200307548883676)
XLA Ops:
  0.0 1.8 %front.1 = (bf16[16,128,256]{2,1,0:T(8,128)(2,1)S(1)}, s32[1,64]{1,0:T(1,128)S(1)}, f32[1,128]{1,0:T(1,128)S(1)}, bf16[128,128]{1,0:T(8,128)(2,1)S(1)}, s32[16,1...) custom-call(s32[1]{0:T(128)} %bitcast.pos_ref, ...), custom_call_target="tpu_custom_call" | custom-call | flops 1 | bytes 1 | tf_op jit(solution)/shard_map/front/pallas_call | solution.py:306
  1.8 2.4 %collective-permute-start.3 = (bf16[4,64,128]{2,1,0:T(8,128)(2,1)S(1)}, bf16[4,64,128]{2,1,0:T(8,128)(2,1)S(1)}, u32[]{:S(2)}, u32[]{:S(2)}) collective-permute-start(bf16[4,64,128]{2,1,0:T(8,128)(2,1)S(1)} %get-tuple-element.37), channel_id=1, source_target_pairs={{0,3},{1,2},{2,1},{3,0},{4,7},{5,6},{6,5},{7,4},{8,11},{9,10},{10,... | collective-permute-start | bytes 196616 | tf_op jit(solution)/shard_map/ppermute | solution.py:290
  4.3 0.6 %collective-permute-start.4 = (bf16[4,64,128]{2,1,0:T(8,128)(2,1)S(1)}, bf16[4,64,128]{2,1,0:T(8,128)(2,1)S(1)}, u32[]{:S(2)}, u32[]{:S(2)}) collective-permute-start(bf16[4,64,128]{2,1,0:T(8,128)(2,1)S(1)} %get-tuple-element.38), channel_id=1, source_target_pairs={{0,2},{1,3},{2,0},{3,1},{4,6},{5,7},{6,4},{7,5},{8,10},{9,11},{10,... | collective-permute-start | bytes 196616 | tf_op jit(solution)/shard_map/ppermute | solution.py:290
  4.9 0.0 collective-permute-start.5
  5.0 3.5 %tree_of_maps.1 = (bf16[31,128,256]{2,1,0:T(8,128)(2,1)}, bf16[31,128,256]{2,1,0:T(8,128)(2,1)}, bf16[128,256]{1,0:T(8,128)(2,1)S(1)}) custom-call(s32[1,64]{1,0:T(1,128)S(1)} %get-tuple-element.28.levels_ref, bf16[16,128,256]{2,1,0:T(8,128)(2,1)S(1)} %get-tuple-element.30.table_ref), custom_call_target="tpu_custom_call" | custom-call | flops 1 | bytes 1 | tf_op jit(solution)/shard_map/tree_of_maps/pallas_call | solution.py:315
  8.5 0.0 collective-permute-done.3.refs_1_
  8.5 0.5 %collective-permute-done.4.refs_2_ = bf16[4,64,128]{2,1,0:T(8,128)(2,1)S(1)} collective-permute-done((bf16[4,64,128]{2,1,0:T(8,128)(2,1)S(1)}, bf16[4,64,128]{2,1,0:T(8,128)(2,1)S(1)}, u32[]{:S(2)}, u32[]{:S(2)}) %collective-permute-start.4) | collective-permute-done | bytes 65568 | tf_op jit(solution)/shard_map/ppermute | solution.py:290
  9.0 0.0 collective-permute-done.5.refs_3_
  9.0 0.2 project.1
  9.2 1.8 %collective-permute-start.6 = (f32[64,128]{1,0:T(8,128)S(1)}, f32[64,128]{1,0:T(8,128)S(1)}, u32[]{:S(2)}, u32[]{:S(2)}) collective-permute-start(f32[64,128]{1,0:T(8,128)S(1)} %get-tuple-element.41), channel_id=1, source_target_pairs={{0,4},{1,5},{2,6},{3,7},{4,0},{5,1},{6,2},{7,3},{8,12},{9,13},{10,... | collective-permute-start | bytes 98312 | tf_op jit(solution)/shard_map/ppermute | solution.py:290
  11.1 2.6 %collective-permute-start.7 = (f32[64,128]{1,0:T(8,128)S(1)}, f32[64,128]{1,0:T(8,128)S(1)}, u32[]{:S(2)}, u32[]{:S(2)}) collective-permute-start(f32[64,128]{1,0:T(8,128)S(1)} %get-tuple-element.42), channel_id=1, source_target_pairs={{0,8},{1,9},{2,10},{3,11},{4,12},{5,13},{6,14},{7,15},{8,0},{9,1},... | collective-permute-start | bytes 98312 | tf_op jit(solution)/shard_map/ppermute | solution.py:290
  13.6 0.0 collective-permute-start.8
  13.7 0.6 %collective-permute-start.2 = (bf16[128,256]{1,0:T(8,128)(2,1)S(1)}, bf16[128,256]{1,0:T(8,128)(2,1)S(1)}, u32[]{:S(2)}, u32[]{:S(2)}) collective-permute-start(bf16[128,256]{1,0:T(8,128)(2,1)S(1)} %get-tuple-element.31.after_ref.total_ref.refs_0_), channel_id=1, source_target_pairs={{0,3},{1,2},{2,1},{3,0},{4,7},{5,6},{6,5},{7,4},{8,11},{9,10},{10,... | collective-permute-start | bytes 196616 | tf_op jit(solution)/shard_map/ppermute | solution.py:290
  14.3 1.1 %collective-permute-start.1 = (bf16[128,256]{1,0:T(8,128)(2,1)S(1)}, bf16[128,256]{1,0:T(8,128)(2,1)S(1)}, u32[]{:S(2)}, u32[]{:S(2)}) collective-permute-start(bf16[128,256]{1,0:T(8,128)(2,1)S(1)} %get-tuple-element.31.after_ref.total_ref.refs_0_), channel_id=1, source_target_pairs={{0,2},{1,3},{2,0},{3,1},{4,6},{5,7},{6,4},{7,5},{8,10},{9,11},{10,... | collective-permute-start | bytes 196616 | tf_op jit(solution)/shard_map/ppermute | solution.py:290
  15.4 0.0 collective-permute-done.6.refs_1_
  15.4 0.1 collective-permute-start
  15.5 0.9 %collective-permute-done.7.refs_2_ = f32[64,128]{1,0:T(8,128)S(1)} collective-permute-done((f32[64,128]{1,0:T(8,128)S(1)}, f32[64,128]{1,0:T(8,128)S(1)}, u32[]{:S(2)}, u32[]{:S(2)}) %collective-permute-start.7) | collective-permute-done | bytes 32800 | tf_op jit(solution)/shard_map/ppermute | solution.py:290
  16.5 2.9 %collective-permute-done.8.refs_3_ = f32[64,128]{1,0:T(8,128)S(1)} collective-permute-done((f32[64,128]{1,0:T(8,128)S(1)}, f32[64,128]{1,0:T(8,128)S(1)}, u32[]{:S(2)}, u32[]{:S(2)}) %collective-permute-start.8) | collective-permute-done | bytes 32800 | tf_op jit(solution)/shard_map/ppermute | solution.py:290
  19.4 0.0 copy-start
  19.4 2.9 %local_states.1 = (f32[64,128]{1,0:T(8,128)S(1)}, f32[8,128]{1,0:T(8,128)S(1)}) custom-call(s32[1]{0:T(128)} %bitcast.pos_ref, s32[1,64]{1,0:T(1,128)S(1)} %get-tuple-element.28.levels_ref, bf16[128,128]{1,0:T(8,128)(2,1)S(1)} %get-tuple-element.32.gain_ref, f32[1,128]{1,0:T(1,128)S(1)} %get-tuple-element.29.init_ref, ...), custom_call_target="tpu_custom_call" | custom-call | flops 1073741824 | bytes 1 | tf_op jit(solution)/shard_map/local_states/pallas_call | solution.py:342
  22.3 0.1 collective-permute-start.11
  22.4 1.6 %collective-permute-start.10 = (f32[8,128]{1,0:T(8,128)S(1)}, f32[8,128]{1,0:T(8,128)S(1)}, u32[]{:S(2)}, u32[]{:S(2)}) collective-permute-start(f32[8,128]{1,0:T(8,128)S(1)} %get-tuple-element.44.refs_4_), channel_id=1, source_target_pairs={{0,2},{1,3},{2,0},{3,1},{4,6},{5,7},{6,4},{7,5},{8,10},{9,11},{10,... | collective-permute-start | bytes 12296 | tf_op jit(solution)/shard_map/ppermute | solution.py:290
  23.9 0.0 collective-permute-done.2.refs_3_
  23.9 0.3 collective-permute-start.9
  24.2 0.0 collective-permute-done.1.refs_2_
  24.2 0.0 collective-permute-done.refs_1_
  24.2 1.2 %collective-permute-done.11.refs_7_ = f32[8,128]{1,0:T(8,128)S(1)} collective-permute-done((f32[8,128]{1,0:T(8,128)S(1)}, f32[8,128]{1,0:T(8,128)S(1)}, u32[]{:S(2)}, u32[]{:S(2)}) %collective-permute-start.11) | collective-permute-done | bytes 4128 | tf_op jit(solution)/shard_map/ppermute | solution.py:290
  25.4 0.7 %collective-permute-done.10.refs_6_ = f32[8,128]{1,0:T(8,128)S(1)} collective-permute-done((f32[8,128]{1,0:T(8,128)S(1)}, f32[8,128]{1,0:T(8,128)S(1)}, u32[]{:S(2)}, u32[]{:S(2)}) %collective-permute-start.10) | collective-permute-done | bytes 4128 | tf_op jit(solution)/shard_map/ppermute | solution.py:290
  26.1 0.0 collective-permute-done.9.refs_5_
  26.1 0.4 %group_maps.1 = (bf16[128,256]{1,0:T(8,128)(2,1)S(1)}, f32[8,128]{1,0:T(8,128)S(1)}, bf16[144,256]{1,0:T(8,128)(2,1)S(1)}, bf16[16,256]{1,0:T(8,128)(2,1)S(1)}) custom-call(s32[1]{0:T(128)} %bitcast.pos_ref, bf16[128,256]{1,0:T(8,128)(2,1)S(1)} %get-tuple-element.31.after_ref.total_ref.refs_0_, bf16[128,256]{1,0:T(8,128)(2,1)S(1)} %collective-permute-done.refs_1_, ...), custom_call_target="tpu_custom_call" | custom-call | flops 1 | bytes 1 | tf_op jit(solution)/shard_map/group_maps/pallas_call | solution.py:349
  26.5 0.1 collective-permute-start.13
  26.6 1.6 %collective-permute-start.12 = (bf16[144,256]{1,0:T(8,128)(2,1)S(1)}, bf16[144,256]{1,0:T(8,128)(2,1)S(1)}, u32[]{:S(2)}, u32[]{:S(2)}) collective-permute-start(bf16[144,256]{1,0:T(8,128)(2,1)S(1)} %get-tuple-element.49), channel_id=1, source_target_pairs={{0,4},{1,5},{2,6},{3,7},{4,8},{5,9},{6,10},{7,11},{8,12},{9,13},{1... | collective-permute-start | bytes 221192 | tf_op jit(solution)/shard_map/ppermute | solution.py:357
  28.2 2.3 %collective-permute-start.14 = (bf16[16,256]{1,0:T(8,128)(2,1)S(1)}, bf16[16,256]{1,0:T(8,128)(2,1)S(1)}, u32[]{:S(2)}, u32[]{:S(2)}) collective-permute-start(bf16[16,256]{1,0:T(8,128)(2,1)S(1)} %get-tuple-element.50), channel_id=1, source_target_pairs={{0,12},{1,13},{2,14},{3,15},{4,0},{5,1},{6,2},{7,3},{8,4},{9,5},{1... | collective-permute-start | bytes 24584 | tf_op jit(solution)/shard_map/ppermute | solution.py:357
  30.5 3.3 %collective-permute-done.14.refs_2_ = bf16[16,256]{1,0:T(8,128)(2,1)S(1)} collective-permute-done((bf16[16,256]{1,0:T(8,128)(2,1)S(1)}, bf16[16,256]{1,0:T(8,128)(2,1)S(1)}, u32[]{:S(2)}, u32[]{:S(2)}) %collective-permute-start.14) | collective-permute-done | bytes 8224 | tf_op jit(solution)/shard_map/ppermute | solution.py:357
  33.8 0.0 collective-permute-done.13.refs_1_
  33.8 0.0 collective-permute-done.12.refs_0_
  33.8 0.0 copy-done
  33.8 2.4 %estimates.1 = f32[64,128]{1,0:T(8,128)} custom-call(s32[1]{0:T(128)} %bitcast.pos_ref, s32[1,64]{1,0:T(1,128)S(1)} %get-tuple-element.28.levels_ref, f32[1,128]{1,0:T(1,128)S(1)} %get-tuple-element.29.init_ref, bf16[128,256]{1,0:T(8,128)(2,1)S(1)} %get-tuple-element.45.prefix_ref, f32[8,128]{1,0:T(8,128)S(1)} %get-tuple-element.46.before_ref, ...), custom_call_target="tpu_custom_call" | custom-call | flops 1 | bytes 1 | tf_op jit(solution)/shard_map/estimates/pallas_call | solution.py:361
Async XLA Ops:
  1.8 6.6 %collective-permute-start.3 = (bf16[4,64,128]{2,1,0:T(8,128)(2,1)S(1)}, bf16[4,64,128]{2,1,0:T(8,128)(2,1)S(1)}, u32[]{:S(2)}, u32[]{:S(2)}) collective-permute-start(bf16[4,64,128]{2,1,0:T(8,128)(2,1)S(1)} %get-tuple-element.37), channel_id=1, source_target_pairs={{0,3},{1,2},{2,1},{3,0},{4,7},{5,6},{6,5},{7,4},{8,11},{9,10},{10,... | collective-permute-start | bytes 196616 | tf_op jit(solution)/shard_map/ppermute | solution.py:290
  4.3 4.7 %collective-permute-start.4 = (bf16[4,64,128]{2,1,0:T(8,128)(2,1)S(1)}, bf16[4,64,128]{2,1,0:T(8,128)(2,1)S(1)}, u32[]{:S(2)}, u32[]{:S(2)}) collective-permute-start(bf16[4,64,128]{2,1,0:T(8,128)(2,1)S(1)} %get-tuple-element.38), channel_id=1, source_target_pairs={{0,2},{1,3},{2,0},{3,1},{4,6},{5,7},{6,4},{7,5},{8,10},{9,11},{10,... | collective-permute-start | bytes 196616 | tf_op jit(solution)/shard_map/ppermute | solution.py:290
  4.9 4.0 %collective-permute-start.5 = (bf16[4,64,128]{2,1,0:T(8,128)(2,1)S(1)}, bf16[4,64,128]{2,1,0:T(8,128)(2,1)S(1)}, u32[]{:S(2)}, u32[]{:S(2)}) collective-permute-start(bf16[4,64,128]{2,1,0:T(8,128)(2,1)S(1)} %get-tuple-element.39), channel_id=1, source_target_pairs={{0,1},{1,0},{2,3},{3,2},{4,5},{5,4},{6,7},{7,6},{8,9},{9,8},{10,11... | collective-permute-start | bytes 196616 | tf_op jit(solution)/shard_map/ppermute | solution.py:290
  9.2 6.2 %collective-permute-start.6 = (f32[64,128]{1,0:T(8,128)S(1)}, f32[64,128]{1,0:T(8,128)S(1)}, u32[]{:S(2)}, u32[]{:S(2)}) collective-permute-start(f32[64,128]{1,0:T(8,128)S(1)} %get-tuple-element.41), channel_id=1, source_target_pairs={{0,4},{1,5},{2,6},{3,7},{4,0},{5,1},{6,2},{7,3},{8,12},{9,13},{10,... | collective-permute-start | bytes 98312 | tf_op jit(solution)/shard_map/ppermute | solution.py:290
  11.1 5.4 %collective-permute-start.7 = (f32[64,128]{1,0:T(8,128)S(1)}, f32[64,128]{1,0:T(8,128)S(1)}, u32[]{:S(2)}, u32[]{:S(2)}) collective-permute-start(f32[64,128]{1,0:T(8,128)S(1)} %get-tuple-element.42), channel_id=1, source_target_pairs={{0,8},{1,9},{2,10},{3,11},{4,12},{5,13},{6,14},{7,15},{8,0},{9,1},... | collective-permute-start | bytes 98312 | tf_op jit(solution)/shard_map/ppermute | solution.py:290
  13.6 5.7 %collective-permute-start.8 = (f32[64,128]{1,0:T(8,128)S(1)}, f32[64,128]{1,0:T(8,128)S(1)}, u32[]{:S(2)}, u32[]{:S(2)}) collective-permute-start(f32[64,128]{1,0:T(8,128)S(1)} %get-tuple-element.43), channel_id=1, source_target_pairs={{0,12},{1,13},{2,14},{3,15},{4,8},{5,9},{6,10},{7,11},{8,4},{9,5},... | collective-permute-start | bytes 98312 | tf_op jit(solution)/shard_map/ppermute | solution.py:290
  13.7 10.3 %collective-permute-start.2 = (bf16[128,256]{1,0:T(8,128)(2,1)S(1)}, bf16[128,256]{1,0:T(8,128)(2,1)S(1)}, u32[]{:S(2)}, u32[]{:S(2)}) collective-permute-start(bf16[128,256]{1,0:T(8,128)(2,1)S(1)} %get-tuple-element.31.after_ref.total_ref.refs_0_), channel_id=1, source_target_pairs={{0,3},{1,2},{2,1},{3,0},{4,7},{5,6},{6,5},{7,4},{8,11},{9,10},{10,... | collective-permute-start | bytes 196616 | tf_op jit(solution)/shard_map/ppermute | solution.py:290
  14.3 10.0 %collective-permute-start.1 = (bf16[128,256]{1,0:T(8,128)(2,1)S(1)}, bf16[128,256]{1,0:T(8,128)(2,1)S(1)}, u32[]{:S(2)}, u32[]{:S(2)}) collective-permute-start(bf16[128,256]{1,0:T(8,128)(2,1)S(1)} %get-tuple-element.31.after_ref.total_ref.refs_0_), channel_id=1, source_target_pairs={{0,2},{1,3},{2,0},{3,1},{4,6},{5,7},{6,4},{7,5},{8,10},{9,11},{10,... | collective-permute-start | bytes 196616 | tf_op jit(solution)/shard_map/ppermute | solution.py:290
  15.4 8.9 %collective-permute-start = (bf16[128,256]{1,0:T(8,128)(2,1)S(1)}, bf16[128,256]{1,0:T(8,128)(2,1)S(1)}, u32[]{:S(2)}, u32[]{:S(2)}) collective-permute-start(bf16[128,256]{1,0:T(8,128)(2,1)S(1)} %get-tuple-element.31.after_ref.total_ref.refs_0_), channel_id=1, source_target_pairs={{0,1},{1,0},{2,3},{3,2},{4,5},{5,4},{6,7},{7,6},{8,9},{9,8},{10,11... | collective-permute-start | bytes 196616 | tf_op jit(solution)/shard_map/ppermute | solution.py:290
  19.4 14.4 %copy-start = (bf16[31,128,256]{2,1,0:T(8,128)(2,1)S(1)}, bf16[31,128,256]{2,1,0:T(8,128)(2,1)}, u32[]{:S(2)}) copy-start(bf16[31,128,256]{2,1,0:T(8,128)(2,1)} %get-tuple-element.48.left_ref) | copy-start | bytes 6094852
  22.3 3.1 %collective-permute-start.11 = (f32[8,128]{1,0:T(8,128)S(1)}, f32[8,128]{1,0:T(8,128)S(1)}, u32[]{:S(2)}, u32[]{:S(2)}) collective-permute-start(f32[8,128]{1,0:T(8,128)S(1)} %get-tuple-element.44.refs_4_), channel_id=1, source_target_pairs={{0,3},{1,2},{2,1},{3,0},{4,7},{5,6},{6,5},{7,4},{8,11},{9,10},{10,... | collective-permute-start | bytes 12296 | tf_op jit(solution)/shard_map/ppermute | solution.py:290
  22.4 3.7 %collective-permute-start.10 = (f32[8,128]{1,0:T(8,128)S(1)}, f32[8,128]{1,0:T(8,128)S(1)}, u32[]{:S(2)}, u32[]{:S(2)}) collective-permute-start(f32[8,128]{1,0:T(8,128)S(1)} %get-tuple-element.44.refs_4_), channel_id=1, source_target_pairs={{0,2},{1,3},{2,0},{3,1},{4,6},{5,7},{6,4},{7,5},{8,10},{9,11},{10,... | collective-permute-start | bytes 12296 | tf_op jit(solution)/shard_map/ppermute | solution.py:290
  23.9 2.1 %collective-permute-start.9 = (f32[8,128]{1,0:T(8,128)S(1)}, f32[8,128]{1,0:T(8,128)S(1)}, u32[]{:S(2)}, u32[]{:S(2)}) collective-permute-start(f32[8,128]{1,0:T(8,128)S(1)} %get-tuple-element.44.refs_4_), channel_id=1, source_target_pairs={{0,1},{1,0},{2,3},{3,2},{4,5},{5,4},{6,7},{7,6},{8,9},{9,8},{10,11... | collective-permute-start | bytes 12296 | tf_op jit(solution)/shard_map/ppermute | solution.py:290
  26.5 7.3 %collective-permute-start.13 = (bf16[144,256]{1,0:T(8,128)(2,1)S(1)}, bf16[144,256]{1,0:T(8,128)(2,1)S(1)}, u32[]{:S(2)}, u32[]{:S(2)}) collective-permute-start(bf16[144,256]{1,0:T(8,128)(2,1)S(1)} %get-tuple-element.49), channel_id=1, source_target_pairs={{0,8},{1,9},{2,10},{3,11},{4,12},{5,13},{6,14},{7,15},{8,0},{9,1},... | collective-permute-start | bytes 221192 | tf_op jit(solution)/shard_map/ppermute | solution.py:357
  26.6 7.2 %collective-permute-start.12 = (bf16[144,256]{1,0:T(8,128)(2,1)S(1)}, bf16[144,256]{1,0:T(8,128)(2,1)S(1)}, u32[]{:S(2)}, u32[]{:S(2)}) collective-permute-start(bf16[144,256]{1,0:T(8,128)(2,1)S(1)} %get-tuple-element.49), channel_id=1, source_target_pairs={{0,4},{1,5},{2,6},{3,7},{4,8},{5,9},{6,10},{7,11},{8,12},{9,13},{1... | collective-permute-start | bytes 221192 | tf_op jit(solution)/shard_map/ppermute | solution.py:357
  28.2 5.6 %collective-permute-start.14 = (bf16[16,256]{1,0:T(8,128)(2,1)S(1)}, bf16[16,256]{1,0:T(8,128)(2,1)S(1)}, u32[]{:S(2)}, u32[]{:S(2)}) collective-permute-start(bf16[16,256]{1,0:T(8,128)(2,1)S(1)} %get-tuple-element.50), channel_id=1, source_target_pairs={{0,12},{1,13},{2,14},{3,15},{4,0},{5,1},{6,2},{7,3},{8,4},{9,5},{1... | collective-permute-start | bytes 24584 | tf_op jit(solution)/shard_map/ppermute | solution.py:357

commit v21 on v19

--- a/solution.py
+++ b/solution.py
@@ -353,9 +353,9 @@
         scratch_shapes=[pltpu.VMEM((size, n, 2 * n), BF16), pltpu.VMEM((size, 8, n), F32)],
     )(position, total, *members, shift, *swaps(shift, 1, size))
     got = [
-        lax.ppermute(mine if r < groups - 1 else carried, "tm", [(j, (j + r * size) % count) for j in range(count)])
-        for r in range(1, groups)
+        lax.ppermute(mine, "tm", [(j, (j + r * size) % count) for j in range(count)]) for r in range(1, groups - 1)
     ]
+    got.append(lax.ppermute(carried, "tm", [(j, j ^ ((groups - 1) * size)) for j in range(count)]))
 
     return call(
         functools.partial(final_kernel, size), "estimates", 6,

time: 35.9 us -> 36.2 us (level)
  transfers between devices with their start and end apart: 15 -> 15, of which waited for: 6 -> 5; matrix products, arithmetic and copies ran while one was open for 0% -> 0% of each run, Pallas kernels for 18% -> 18%
where the time goes in v21:
time: 36.2 us; the launch traced here: 36 us
  starting transfers between devices  17.2 us (48%)
  Pallas kernels  11.4 us (31%)
  waiting for transfers between devices  7.39 us (20%)
    ppermute x12, starting transfers between devices, swaps(): lax.ppermute(a, 'tm', [(j, j ^ r * step) for j in range(count)])  11.4 us
    ppermute x12, waiting for transfers between devices, swaps(): lax.ppermute(a, 'tm', [(j, j ^ r * step) for j in range(count)])  4.59 us
    pallas_call x1, Pallas kernels, shards(): call(functools.partial(tree_kernel, steps), 'tree_of_maps', 8, out_shape=...  3.49 us
    ppermute x2, starting transfers between devices, shards(): lax.ppermute(mine, 'tm', [(j, (j + r * size) % count) for j in range(coun...  3.13 us
    pallas_call x1, Pallas kernels, shards(): call(local_kernel, 'local_states', 8, 1 << 30, out_shape=[shape((steps, n...  2.95 us
    ppermute x1, waiting for transfers between devices, shards(): lax.ppermute(carried, 'tm', [(j, j ^ (groups - 1) * size) for j in range(...  2.8 us
    ppermute x1, starting transfers between devices, shards(): lax.ppermute(carried, 'tm', [(j, j ^ (groups - 1) * size) for j in range(...  2.65 us
    pallas_call x1, Pallas kernels, shards(): call(functools.partial(final_kernel, size), 'estimates', 6, out_shape=sha...  2.44 us
  transfers between devices with their start and end apart: 15, of which 5 were waited for; matrix products, arithmetic and copies ran while one was open for 0% of the time, Pallas kernels for 18%

profile of v21, /device:TPU:0, one launch (start us, length us, event | category | flops | bytes accessed | tf_op | source)
XLA Modules:
  0.0 36.0 jit_solution(12963096095517856770)
XLA Ops:
  0.0 1.8 %front.1 = (bf16[16,128,256]{2,1,0:T(8,128)(2,1)S(1)}, s32[1,64]{1,0:T(1,128)S(1)}, f32[1,128]{1,0:T(1,128)S(1)}, bf16[128,128]{1,0:T(8,128)(2,1)S(1)}, s32[16,1...) custom-call(s32[1]{0:T(128)} %bitcast.pos_ref, ...), custom_call_target="tpu_custom_call" | custom-call | flops 1 | bytes 1 | tf_op jit(solution)/shard_map/front/pallas_call | solution.py:305
  1.8 0.5 %collective-permute-start.3 = (bf16[4,64,128]{2,1,0:T(8,128)(2,1)S(1)}, bf16[4,64,128]{2,1,0:T(8,128)(2,1)S(1)}, u32[]{:S(2)}, u32[]{:S(2)}) collective-permute-start(bf16[4,64,128]{2,1,0:T(8,128)(2,1)S(1)} %get-tuple-element.37), channel_id=1, source_target_pairs={{0,1},{1,0},{2,3},{3,2},{4,5},{5,4},{6,7},{7,6},{8,9},{9,8},{10,11... | collective-permute-start | bytes 196616 | tf_op jit(solution)/shard_map/ppermute | solution.py:289
  2.4 2.6 %collective-permute-start.4 = (bf16[4,64,128]{2,1,0:T(8,128)(2,1)S(1)}, bf16[4,64,128]{2,1,0:T(8,128)(2,1)S(1)}, u32[]{:S(2)}, u32[]{:S(2)}) collective-permute-start(bf16[4,64,128]{2,1,0:T(8,128)(2,1)S(1)} %get-tuple-element.38), channel_id=1, source_target_pairs={{0,2},{1,3},{2,0},{3,1},{4,6},{5,7},{6,4},{7,5},{8,10},{9,11},{10,... | collective-permute-start | bytes 196616 | tf_op jit(solution)/shard_map/ppermute | solution.py:289
  4.9 0.1 collective-permute-start.5
  5.0 3.5 %tree_of_maps.1 = (bf16[31,128,256]{2,1,0:T(8,128)(2,1)}, bf16[31,128,256]{2,1,0:T(8,128)(2,1)}, bf16[128,256]{1,0:T(8,128)(2,1)S(1)}) custom-call(s32[1,64]{1,0:T(1,128)S(1)} %get-tuple-element.28.levels_ref, bf16[16,128,256]{2,1,0:T(8,128)(2,1)S(1)} %get-tuple-element.30.table_ref), custom_call_target="tpu_custom_call" | custom-call | flops 1 | bytes 1 | tf_op jit(solution)/shard_map/tree_of_maps/pallas_call | solution.py:314
  8.5 0.0 collective-permute-done.3.refs_1_
  8.5 0.0 collective-permute-done.4.refs_2_
  8.5 0.5 %collective-permute-done.5.refs_3_ = bf16[4,64,128]{2,1,0:T(8,128)(2,1)S(1)} collective-permute-done((bf16[4,64,128]{2,1,0:T(8,128)(2,1)S(1)}, bf16[4,64,128]{2,1,0:T(8,128)(2,1)S(1)}, u32[]{:S(2)}, u32[]{:S(2)}) %collective-permute-start.5) | collective-permute-done | bytes 65568 | tf_op jit(solution)/shard_map/ppermute | solution.py:289
  9.0 0.2 project.1
  9.2 3.7 %collective-permute-start.6 = (f32[64,128]{1,0:T(8,128)S(1)}, f32[64,128]{1,0:T(8,128)S(1)}, u32[]{:S(2)}, u32[]{:S(2)}) collective-permute-start(f32[64,128]{1,0:T(8,128)S(1)} %get-tuple-element.41), channel_id=1, source_target_pairs={{0,12},{1,13},{2,14},{3,15},{4,8},{5,9},{6,10},{7,11},{8,4},{9,5},... | collective-permute-start | bytes 98312 | tf_op jit(solution)/shard_map/ppermute | solution.py:289
  12.9 0.0 collective-permute-start.7
  12.9 0.8 %collective-permute-start.8 = (f32[64,128]{1,0:T(8,128)S(1)}, f32[64,128]{1,0:T(8,128)S(1)}, u32[]{:S(2)}, u32[]{:S(2)}) collective-permute-start(f32[64,128]{1,0:T(8,128)S(1)} %get-tuple-element.43), channel_id=1, source_target_pairs={{0,4},{1,5},{2,6},{3,7},{4,0},{5,1},{6,2},{7,3},{8,12},{9,13},{10,... | collective-permute-start | bytes 98312 | tf_op jit(solution)/shard_map/ppermute | solution.py:289
  13.7 0.5 %collective-permute-start.2 = (bf16[128,256]{1,0:T(8,128)(2,1)S(1)}, bf16[128,256]{1,0:T(8,128)(2,1)S(1)}, u32[]{:S(2)}, u32[]{:S(2)}) collective-permute-start(bf16[128,256]{1,0:T(8,128)(2,1)S(1)} %get-tuple-element.31.after_ref.total_ref.refs_0_), channel_id=1, source_target_pairs={{0,3},{1,2},{2,1},{3,0},{4,7},{5,6},{6,5},{7,4},{8,11},{9,10},{10,... | collective-permute-start | bytes 196616 | tf_op jit(solution)/shard_map/ppermute | solution.py:289
  14.2 0.8 %collective-permute-start.1 = (bf16[128,256]{1,0:T(8,128)(2,1)S(1)}, bf16[128,256]{1,0:T(8,128)(2,1)S(1)}, u32[]{:S(2)}, u32[]{:S(2)}) collective-permute-start(bf16[128,256]{1,0:T(8,128)(2,1)S(1)} %get-tuple-element.31.after_ref.total_ref.refs_0_), channel_id=1, source_target_pairs={{0,2},{1,3},{2,0},{3,1},{4,6},{5,7},{6,4},{7,5},{8,10},{9,11},{10,... | collective-permute-start | bytes 196616 | tf_op jit(solution)/shard_map/ppermute | solution.py:289
  15.1 0.0 collective-permute-done.6.refs_1_
  15.1 0.5 %collective-permute-start = (bf16[128,256]{1,0:T(8,128)(2,1)S(1)}, bf16[128,256]{1,0:T(8,128)(2,1)S(1)}, u32[]{:S(2)}, u32[]{:S(2)}) collective-permute-start(bf16[128,256]{1,0:T(8,128)(2,1)S(1)} %get-tuple-element.31.after_ref.total_ref.refs_0_), channel_id=1, source_target_pairs={{0,1},{1,0},{2,3},{3,2},{4,5},{5,4},{6,7},{7,6},{8,9},{9,8},{10,11... | collective-permute-start | bytes 196616 | tf_op jit(solution)/shard_map/ppermute | solution.py:289
  15.5 2.2 %collective-permute-done.7.refs_2_ = f32[64,128]{1,0:T(8,128)S(1)} collective-permute-done((f32[64,128]{1,0:T(8,128)S(1)}, f32[64,128]{1,0:T(8,128)S(1)}, u32[]{:S(2)}, u32[]{:S(2)}) %collective-permute-start.7) | collective-permute-done | bytes 32800 | tf_op jit(solution)/shard_map/ppermute | solution.py:289
  17.7 0.0 collective-permute-done.8.refs_3_
  17.7 0.0 copy-start
  17.7 2.9 %local_states.1 = (f32[64,128]{1,0:T(8,128)S(1)}, f32[8,128]{1,0:T(8,128)S(1)}) custom-call(s32[1]{0:T(128)} %bitcast.pos_ref, s32[1,64]{1,0:T(1,128)S(1)} %get-tuple-element.28.levels_ref, bf16[128,128]{1,0:T(8,128)(2,1)S(1)} %get-tuple-element.32.gain_ref, f32[1,128]{1,0:T(1,128)S(1)} %get-tuple-element.29.init_ref, ...), custom_call_target="tpu_custom_call" | custom-call | flops 1073741824 | bytes 1 | tf_op jit(solution)/shard_map/local_states/pallas_call | solution.py:341
  20.7 0.3 collective-permute-start.11
  20.9 1.2 %collective-permute-start.10 = (f32[8,128]{1,0:T(8,128)S(1)}, f32[8,128]{1,0:T(8,128)S(1)}, u32[]{:S(2)}, u32[]{:S(2)}) collective-permute-start(f32[8,128]{1,0:T(8,128)S(1)} %get-tuple-element.44.refs_4_), channel_id=1, source_target_pairs={{0,2},{1,3},{2,0},{3,1},{4,6},{5,7},{6,4},{7,5},{8,10},{9,11},{10,... | collective-permute-start | bytes 12296 | tf_op jit(solution)/shard_map/ppermute | solution.py:289
  22.2 0.0 collective-permute-done.2.refs_3_
  22.2 0.4 %collective-permute-start.9 = (f32[8,128]{1,0:T(8,128)S(1)}, f32[8,128]{1,0:T(8,128)S(1)}, u32[]{:S(2)}, u32[]{:S(2)}) collective-permute-start(f32[8,128]{1,0:T(8,128)S(1)} %get-tuple-element.44.refs_4_), channel_id=1, source_target_pairs={{0,1},{1,0},{2,3},{3,2},{4,5},{5,4},{6,7},{7,6},{8,9},{9,8},{10,11... | collective-permute-start | bytes 12296 | tf_op jit(solution)/shard_map/ppermute | solution.py:289
  22.6 0.0 collective-permute-done.1.refs_2_
  22.6 0.0 collective-permute-done.refs_1_
  22.6 1.2 %collective-permute-done.11.refs_7_ = f32[8,128]{1,0:T(8,128)S(1)} collective-permute-done((f32[8,128]{1,0:T(8,128)S(1)}, f32[8,128]{1,0:T(8,128)S(1)}, u32[]{:S(2)}, u32[]{:S(2)}) %collective-permute-start.11) | collective-permute-done | bytes 4128 | tf_op jit(solution)/shard_map/ppermute | solution.py:289
  23.8 0.8 %collective-permute-done.10.refs_6_ = f32[8,128]{1,0:T(8,128)S(1)} collective-permute-done((f32[8,128]{1,0:T(8,128)S(1)}, f32[8,128]{1,0:T(8,128)S(1)}, u32[]{:S(2)}, u32[]{:S(2)}) %collective-permute-start.10) | collective-permute-done | bytes 4128 | tf_op jit(solution)/shard_map/ppermute | solution.py:289
  24.6 0.0 collective-permute-done.9.refs_5_
  24.6 0.4 %group_maps.1 = (bf16[128,256]{1,0:T(8,128)(2,1)S(1)}, f32[8,128]{1,0:T(8,128)S(1)}, bf16[144,256]{1,0:T(8,128)(2,1)S(1)}, bf16[16,256]{1,0:T(8,128)(2,1)S(1)}) custom-call(s32[1]{0:T(128)} %bitcast.pos_ref, bf16[128,256]{1,0:T(8,128)(2,1)S(1)} %get-tuple-element.31.after_ref.total_ref.refs_0_, bf16[128,256]{1,0:T(8,128)(2,1)S(1)} %collective-permute-done.refs_1_, ...), custom_call_target="tpu_custom_call" | custom-call | flops 1 | bytes 1 | tf_op jit(solution)/shard_map/group_maps/pallas_call | solution.py:348
  25.0 2.0 %collective-permute-start.13 = (bf16[144,256]{1,0:T(8,128)(2,1)S(1)}, bf16[144,256]{1,0:T(8,128)(2,1)S(1)}, u32[]{:S(2)}, u32[]{:S(2)}) collective-permute-start(bf16[144,256]{1,0:T(8,128)(2,1)S(1)} %get-tuple-element.49), channel_id=1, source_target_pairs={{0,8},{1,9},{2,10},{3,11},{4,12},{5,13},{6,14},{7,15},{8,0},{9,1},... | collective-permute-start | bytes 221192 | tf_op jit(solution)/shard_map/ppermute | solution.py:356
  27.0 1.2 %collective-permute-start.12 = (bf16[144,256]{1,0:T(8,128)(2,1)S(1)}, bf16[144,256]{1,0:T(8,128)(2,1)S(1)}, u32[]{:S(2)}, u32[]{:S(2)}) collective-permute-start(bf16[144,256]{1,0:T(8,128)(2,1)S(1)} %get-tuple-element.49), channel_id=1, source_target_pairs={{0,4},{1,5},{2,6},{3,7},{4,8},{5,9},{6,10},{7,11},{8,12},{9,13},{1... | collective-permute-start | bytes 221192 | tf_op jit(solution)/shard_map/ppermute | solution.py:356
  28.1 2.6 %collective-permute-start.14 = (bf16[16,256]{1,0:T(8,128)(2,1)S(1)}, bf16[16,256]{1,0:T(8,128)(2,1)S(1)}, u32[]{:S(2)}, u32[]{:S(2)}) collective-permute-start(bf16[16,256]{1,0:T(8,128)(2,1)S(1)} %get-tuple-element.50), channel_id=1, source_target_pairs={{0,12},{1,13},{2,14},{3,15},{4,8},{5,9},{6,10},{7,11},{8,4},{9,5},... | collective-permute-start | bytes 24584 | tf_op jit(solution)/shard_map/ppermute | solution.py:358
  30.8 2.8 %collective-permute-done.14.refs_2_ = bf16[16,256]{1,0:T(8,128)(2,1)S(1)} collective-permute-done((bf16[16,256]{1,0:T(8,128)(2,1)S(1)}, bf16[16,256]{1,0:T(8,128)(2,1)S(1)}, u32[]{:S(2)}, u32[]{:S(2)}) %collective-permute-start.14) | collective-permute-done | bytes 8224 | tf_op jit(solution)/shard_map/ppermute | solution.py:358
  33.6 0.0 collective-permute-done.13.refs_1_
  33.6 0.0 collective-permute-done.12.refs_0_
  33.6 0.0 copy-done
  33.6 2.4 %estimates.1 = f32[64,128]{1,0:T(8,128)} custom-call(s32[1]{0:T(128)} %bitcast.pos_ref, s32[1,64]{1,0:T(1,128)S(1)} %get-tuple-element.28.levels_ref, f32[1,128]{1,0:T(1,128)S(1)} %get-tuple-element.29.init_ref, bf16[128,256]{1,0:T(8,128)(2,1)S(1)} %get-tuple-element.45.prefix_ref, f32[8,128]{1,0:T(8,128)S(1)} %get-tuple-element.46.before_ref, ...), custom_call_target="tpu_custom_call" | custom-call | flops 1 | bytes 1 | tf_op jit(solution)/shard_map/estimates/pallas_call | solution.py:360
Async XLA Ops:
  1.8 6.7 %collective-permute-start.3 = (bf16[4,64,128]{2,1,0:T(8,128)(2,1)S(1)}, bf16[4,64,128]{2,1,0:T(8,128)(2,1)S(1)}, u32[]{:S(2)}, u32[]{:S(2)}) collective-permute-start(bf16[4,64,128]{2,1,0:T(8,128)(2,1)S(1)} %get-tuple-element.37), channel_id=1, source_target_pairs={{0,1},{1,0},{2,3},{3,2},{4,5},{5,4},{6,7},{7,6},{8,9},{9,8},{10,11... | collective-permute-start | bytes 196616 | tf_op jit(solution)/shard_map/ppermute | solution.py:289
  2.4 6.1 %collective-permute-start.4 = (bf16[4,64,128]{2,1,0:T(8,128)(2,1)S(1)}, bf16[4,64,128]{2,1,0:T(8,128)(2,1)S(1)}, u32[]{:S(2)}, u32[]{:S(2)}) collective-permute-start(bf16[4,64,128]{2,1,0:T(8,128)(2,1)S(1)} %get-tuple-element.38), channel_id=1, source_target_pairs={{0,2},{1,3},{2,0},{3,1},{4,6},{5,7},{6,4},{7,5},{8,10},{9,11},{10,... | collective-permute-start | bytes 196616 | tf_op jit(solution)/shard_map/ppermute | solution.py:289
  4.9 4.0 %collective-permute-start.5 = (bf16[4,64,128]{2,1,0:T(8,128)(2,1)S(1)}, bf16[4,64,128]{2,1,0:T(8,128)(2,1)S(1)}, u32[]{:S(2)}, u32[]{:S(2)}) collective-permute-start(bf16[4,64,128]{2,1,0:T(8,128)(2,1)S(1)} %get-tuple-element.39), channel_id=1, source_target_pairs={{0,3},{1,2},{2,1},{3,0},{4,7},{5,6},{6,5},{7,4},{8,11},{9,10},{10,... | collective-permute-start | bytes 196616 | tf_op jit(solution)/shard_map/ppermute | solution.py:289
  9.2 5.8 %collective-permute-start.6 = (f32[64,128]{1,0:T(8,128)S(1)}, f32[64,128]{1,0:T(8,128)S(1)}, u32[]{:S(2)}, u32[]{:S(2)}) collective-permute-start(f32[64,128]{1,0:T(8,128)S(1)} %get-tuple-element.41), channel_id=1, source_target_pairs={{0,12},{1,13},{2,14},{3,15},{4,8},{5,9},{6,10},{7,11},{8,4},{9,5},... | collective-permute-start | bytes 98312 | tf_op jit(solution)/shard_map/ppermute | solution.py:289
  12.9 4.8 %collective-permute-start.7 = (f32[64,128]{1,0:T(8,128)S(1)}, f32[64,128]{1,0:T(8,128)S(1)}, u32[]{:S(2)}, u32[]{:S(2)}) collective-permute-start(f32[64,128]{1,0:T(8,128)S(1)} %get-tuple-element.42), channel_id=1, source_target_pairs={{0,8},{1,9},{2,10},{3,11},{4,12},{5,13},{6,14},{7,15},{8,0},{9,1},... | collective-permute-start | bytes 98312 | tf_op jit(solution)/shard_map/ppermute | solution.py:289
  12.9 4.8 %collective-permute-start.8 = (f32[64,128]{1,0:T(8,128)S(1)}, f32[64,128]{1,0:T(8,128)S(1)}, u32[]{:S(2)}, u32[]{:S(2)}) collective-permute-start(f32[64,128]{1,0:T(8,128)S(1)} %get-tuple-element.43), channel_id=1, source_target_pairs={{0,4},{1,5},{2,6},{3,7},{4,0},{5,1},{6,2},{7,3},{8,12},{9,13},{10,... | collective-permute-start | bytes 98312 | tf_op jit(solution)/shard_map/ppermute | solution.py:289
  13.7 8.5 %collective-permute-start.2 = (bf16[128,256]{1,0:T(8,128)(2,1)S(1)}, bf16[128,256]{1,0:T(8,128)(2,1)S(1)}, u32[]{:S(2)}, u32[]{:S(2)}) collective-permute-start(bf16[128,256]{1,0:T(8,128)(2,1)S(1)} %get-tuple-element.31.after_ref.total_ref.refs_0_), channel_id=1, source_target_pairs={{0,3},{1,2},{2,1},{3,0},{4,7},{5,6},{6,5},{7,4},{8,11},{9,10},{10,... | collective-permute-start | bytes 196616 | tf_op jit(solution)/shard_map/ppermute | solution.py:289
  14.2 8.4 %collective-permute-start.1 = (bf16[128,256]{1,0:T(8,128)(2,1)S(1)}, bf16[128,256]{1,0:T(8,128)(2,1)S(1)}, u32[]{:S(2)}, u32[]{:S(2)}) collective-permute-start(bf16[128,256]{1,0:T(8,128)(2,1)S(1)} %get-tuple-element.31.after_ref.total_ref.refs_0_), channel_id=1, source_target_pairs={{0,2},{1,3},{2,0},{3,1},{4,6},{5,7},{6,4},{7,5},{8,10},{9,11},{10,... | collective-permute-start | bytes 196616 | tf_op jit(solution)/shard_map/ppermute | solution.py:289
  15.1 7.5 %collective-permute-start = (bf16[128,256]{1,0:T(8,128)(2,1)S(1)}, bf16[128,256]{1,0:T(8,128)(2,1)S(1)}, u32[]{:S(2)}, u32[]{:S(2)}) collective-permute-start(bf16[128,256]{1,0:T(8,128)(2,1)S(1)} %get-tuple-element.31.after_ref.total_ref.refs_0_), channel_id=1, source_target_pairs={{0,1},{1,0},{2,3},{3,2},{4,5},{5,4},{6,7},{7,6},{8,9},{9,8},{10,11... | collective-permute-start | bytes 196616 | tf_op jit(solution)/shard_map/ppermute | solution.py:289
  17.7 15.9 %copy-start = (bf16[31,128,256]{2,1,0:T(8,128)(2,1)S(1)}, bf16[31,128,256]{2,1,0:T(8,128)(2,1)}, u32[]{:S(2)}) copy-start(bf16[31,128,256]{2,1,0:T(8,128)(2,1)} %get-tuple-element.48.left_ref) | copy-start | bytes 6094852
  20.7 3.1 %collective-permute-start.11 = (f32[8,128]{1,0:T(8,128)S(1)}, f32[8,128]{1,0:T(8,128)S(1)}, u32[]{:S(2)}, u32[]{:S(2)}) collective-permute-start(f32[8,128]{1,0:T(8,128)S(1)} %get-tuple-element.44.refs_4_), channel_id=1, source_target_pairs={{0,3},{1,2},{2,1},{3,0},{4,7},{5,6},{6,5},{7,4},{8,11},{9,10},{10,... | collective-permute-start | bytes 12296 | tf_op jit(solution)/shard_map/ppermute | solution.py:289
  20.9 3.6 %collective-permute-start.10 = (f32[8,128]{1,0:T(8,128)S(1)}, f32[8,128]{1,0:T(8,128)S(1)}, u32[]{:S(2)}, u32[]{:S(2)}) collective-permute-start(f32[8,128]{1,0:T(8,128)S(1)} %get-tuple-element.44.refs_4_), channel_id=1, source_target_pairs={{0,2},{1,3},{2,0},{3,1},{4,6},{5,7},{6,4},{7,5},{8,10},{9,11},{10,... | collective-permute-start | bytes 12296 | tf_op jit(solution)/shard_map/ppermute | solution.py:289
  22.2 2.4 %collective-permute-start.9 = (f32[8,128]{1,0:T(8,128)S(1)}, f32[8,128]{1,0:T(8,128)S(1)}, u32[]{:S(2)}, u32[]{:S(2)}) collective-permute-start(f32[8,128]{1,0:T(8,128)S(1)} %get-tuple-element.44.refs_4_), channel_id=1, source_target_pairs={{0,1},{1,0},{2,3},{3,2},{4,5},{5,4},{6,7},{7,6},{8,9},{9,8},{10,11... | collective-permute-start | bytes 12296 | tf_op jit(solution)/shard_map/ppermute | solution.py:289
  25.0 8.6 %collective-permute-start.13 = (bf16[144,256]{1,0:T(8,128)(2,1)S(1)}, bf16[144,256]{1,0:T(8,128)(2,1)S(1)}, u32[]{:S(2)}, u32[]{:S(2)}) collective-permute-start(bf16[144,256]{1,0:T(8,128)(2,1)S(1)} %get-tuple-element.49), channel_id=1, source_target_pairs={{0,8},{1,9},{2,10},{3,11},{4,12},{5,13},{6,14},{7,15},{8,0},{9,1},... | collective-permute-start | bytes 221192 | tf_op jit(solution)/shard_map/ppermute | solution.py:356
  27.0 6.6 %collective-permute-start.12 = (bf16[144,256]{1,0:T(8,128)(2,1)S(1)}, bf16[144,256]{1,0:T(8,128)(2,1)S(1)}, u32[]{:S(2)}, u32[]{:S(2)}) collective-permute-start(bf16[144,256]{1,0:T(8,128)(2,1)S(1)} %get-tuple-element.49), channel_id=1, source_target_pairs={{0,4},{1,5},{2,6},{3,7},{4,8},{5,9},{6,10},{7,11},{8,12},{9,13},{1... | collective-permute-start | bytes 221192 | tf_op jit(solution)/shard_map/ppermute | solution.py:356
  28.1 5.4 %collective-permute-start.14 = (bf16[16,256]{1,0:T(8,128)(2,1)S(1)}, bf16[16,256]{1,0:T(8,128)(2,1)S(1)}, u32[]{:S(2)}, u32[]{:S(2)}) collective-permute-start(bf16[16,256]{1,0:T(8,128)(2,1)S(1)} %get-tuple-element.50), channel_id=1, source_target_pairs={{0,12},{1,13},{2,14},{3,15},{4,8},{5,9},{6,10},{7,11},{8,4},{9,5},... | collective-permute-start | bytes 24584 | tf_op jit(solution)/shard_map/ppermute | solution.py:358
